TPU v7x, 32 devices: a whole 2x2x4 slice. The times are simulated.
32 devices in a mesh: groups: 2 (over y), streams: 8 (over z, x), segment: 2 (over core).
Axes of the slice: x: 2, y: 2, z: 4, core: 2. Of those that a mesh axis runs over, the one named last changes fastest.
Arguments:
- latent: bfloat16 [4096, 1024], P(('groups', 'streams'), 'segment'), parts along dimension 0, may hold values from -6 to 6
- conv_weight: bfloat16 [1024, 16, 512], P('streams', None, 'segment'), may hold values from -0.1875 to 0.1875
- conv_bias: float32 [512], P('segment'), may hold values from -3 to 3
- tail_cache: bfloat16 [128, 8, 512], P(('groups', 'streams'), None, 'segment'), parts along dimension 0, may hold values from -6 to 6
- input_cache: bfloat16 [128, 2, 512], P(('groups', 'streams'), None, 'segment'), parts along dimension 0, may hold values from -0.8984375 to 2
- resume_slot: int32 [128], P(('groups', 'streams')), parts along dimension 0, may hold values from -1 to 255, as said below
- res_weight: bfloat16 [3, 512, 256], P(None, 'segment'), may hold values from -0.15625 to 0.15625
- res_bias: float32 [256], replicated, may hold values from -3 to 3
- skip_weight: bfloat16 [256, 512], P(None, 'segment'), may hold values from -0.375 to 0.375
- skip_bias: float32 [512], P('segment'), may hold values from -3 to 3
Outputs:
- decoded: bfloat16 [4096, 8, 512], P(('groups', 'streams'), None, 'segment'), parts along dimension 0
- new_tail: bfloat16 [4096, 8, 512], P(('groups', 'streams'), None, 'segment'), parts along dimension 0
There are 2 independent parts, one for each index of `groups`. A program takes and returns all parts, laid end to end along the dimension named above; an argument that names none is the same for every part. Nothing has to cross between parts.
Inputs may be any that keep to these rules, and one draw needn't show every extreme that they name: `resume_slot`: slot k of an owner device's store serves decoder device k // 1 of the same index range; an entry is -1 (slot unused) or the position, among that decoder device's 256 rows in decoder order, of the session that resumes from it. No decoder row is named by two slots. In every draw there is one decoder device all of whose reserved slots are in use (none is -1).
All inputs are finite; a program needn't handle non-finite values.
Results may differ from a plain program's by a relative error of at most 0.0042.
Values may be sent and summed in bfloat16 or wider, within the bound.
No kernel may reach another device: no remote copies, remote signals or barrier semaphores. Data moves between devices by JAX's collectives and lax.ppermute only.
A program may use at most 64 MiB of HBM per device.

v0:
```python
import functools

import jax
import jax.numpy as jnp
from jax import lax
from jax.experimental import pallas as pl
from jax.experimental.pallas import tpu as pltpu
from jax.sharding import PartitionSpec as P

VMEM_LIMIT = 48 * 1024 * 1024
F32 = jnp.float32
BF16 = jnp.bfloat16
VMEM = pl.BlockSpec(memory_space=pltpu.VMEM)


def apply_elu(values):
    return jnp.where(values > 0, values, jnp.exp(jnp.minimum(values, 0.0)) - 1.0)


def ring_order(count):
    return [2 * p if p < count // 2 else 2 * (count - 1 - p) + 1 for p in range(count)]


def ring_place(stream, count):
    return jnp.where(stream % 2 == 0, stream // 2, count - 1 - stream // 2)


def ring_stream(place, count):
    return jnp.where(place < count // 2, 2 * place, 2 * (count - 1 - place) + 1)


def spread_kernel(count, steps, *refs):
    blocks = refs[: len(steps)]
    sides, (home_ref, away_ref) = refs[len(steps) : len(steps) + 4], refs[len(steps) + 4 : -3]
    kernel_rows, inputs, sems = refs[-3:]
    taps = kernel_rows.shape[0]
    rows = blocks[0].shape[-2]
    core = lax.axis_index("segment")
    place = ring_place(lax.axis_index("streams"), count)
    copies = []
    for slot, (step, block) in enumerate(zip(steps, blocks)):
        if step is None:
            source, target = block, kernel_rows
        else:
            distance, passed = step
            taker = 1 - core if passed else core
            stream = ring_stream(
                lax.rem(place + (2 * taker - 1) * distance + count, count), count
            )
            source = block if len(block.shape) == 3 else block.at[0]
            part = source.shape[0]
            first = 0 if part == taps else taker * part
            target = kernel_rows.at[
                pl.ds(first, part), pl.ds(pl.multiple_of(stream * rows, rows), rows), :
            ]
        copy = pltpu.make_async_copy(source, target, sems.at[slot])
        copy.start()
        copies.append(copy)
    half = sides[0].shape[1]
    for index, side in enumerate(sides):
        column = core if index % 2 == 0 else 1 - core
        inputs[index // 2, :, pl.ds(pl.multiple_of(column * half, half), half)] = side[...]
    for copy in copies:
        copy.wait()

    @pl.loop(0, taps)
    def _(tap):
        weights = kernel_rows[tap]
        home_ref[tap] = jnp.dot(inputs[0], weights, preferred_element_type=F32).astype(
            home_ref.dtype
        )
        away_ref[tap] = jnp.dot(inputs[1], weights, preferred_element_type=F32).astype(
            away_ref.dtype
        )


def spread_taps(sides, blocks, steps, count, home_type):
    taps, _, width = blocks[0].shape
    sessions, depth = sides[0].shape[0], 2 * sides[0].shape[1]
    return pl.pallas_call(
        functools.partial(spread_kernel, count, steps),
        out_shape=(
            jax.ShapeDtypeStruct((taps, sessions, width), home_type),
            jax.ShapeDtypeStruct((taps, sessions, width), BF16),
        ),
        in_specs=[pl.BlockSpec(memory_space=pl.ANY)] * len(blocks) + [VMEM] * 4,
        out_specs=(VMEM, VMEM),
        scratch_shapes=[
            pltpu.VMEM((taps, depth, width), BF16),
            pltpu.VMEM((2, sessions, depth), BF16),
            pltpu.SemaphoreType.DMA((len(blocks),)),
        ],
        compiler_params=pltpu.CompilerParams(vmem_limit_bytes=VMEM_LIMIT),
        cost_estimate=pl.CostEstimate(
            flops=4 * taps * sessions * depth * width,
            bytes_accessed=2 * taps * depth * width + 4 * sessions * depth + 6 * taps * sessions * width,
            transcendentals=0,
        ),
    )(*blocks, *sides)


def excite_kernel(group_ref, own_ref, other_ref, prev_ref, bias_ref, up_ref, window_ref):
    taps = own_ref.shape[0]
    bias = bias_ref[...]
    group = group_ref[0]
    history = prev_ref.shape[0] - 2 * taps
    for step in range(history):
        window_ref[step] = prev_ref[2 * taps + step]
    for half in range(2):
        for tap in range(taps):
            value = jnp.where(group == half, own_ref[tap], other_ref[tap].astype(F32))
            step = half * taps + tap
            up = value + prev_ref[step].astype(F32) + bias
            up_ref[step] = up
            window_ref[history + step] = apply_elu(up).astype(BF16)


def excite(group, own, other, prev, bias):
    taps, sessions, width = own.shape
    return pl.pallas_call(
        excite_kernel,
        out_shape=(
            jax.ShapeDtypeStruct((2 * taps, sessions, width), F32),
            jax.ShapeDtypeStruct((prev.shape[0], sessions, width), BF16),
        ),
        in_specs=[pl.BlockSpec(memory_space=pltpu.SMEM), VMEM, VMEM, VMEM, VMEM],
        out_specs=(VMEM, VMEM),
        compiler_params=pltpu.CompilerParams(vmem_limit_bytes=VMEM_LIMIT),
        cost_estimate=pl.CostEstimate(
            flops=20 * taps * sessions * width,
            bytes_accessed=40 * taps * sessions * width,
            transcendentals=2 * taps * sessions * width,
        ),
    )(group, own, other, prev, bias)


def residual_kernel(
    up_ref, mine_ref, theirs_ref, res_mine_ref, res_theirs_ref, res_bias_ref, skip_ref, skip_bias_ref, out_ref, frames
):
    steps, block, width = up_ref.shape
    branch = None
    for source, weights in ((mine_ref, res_mine_ref), (theirs_ref, res_theirs_ref)):
        for offset in range(weights.shape[0]):
            term = jnp.dot(
                source[offset : offset + steps].reshape(steps * block, width),
                weights[offset],
                preferred_element_type=F32,
            )
            branch = term if branch is None else branch + term
    hidden = apply_elu(branch + res_bias_ref[...]).astype(BF16)
    projected = jnp.dot(hidden, skip_ref[...], preferred_element_type=F32)
    mixed = up_ref[...] + projected.reshape(steps, block, width) + skip_bias_ref[...]
    for step in range(steps):
        for part in range(width // 128):
            frames.at[part][pl.ds(step, block, stride=steps), :] = mixed[
                step, :, part * 128 : (part + 1) * 128
            ]
    for part in range(width // 128):
        out_ref[:, part * 128 : (part + 1) * 128] = frames[part].astype(BF16)


def residual(up, mine, theirs, res_mine, res_theirs, res_bias, skip_weight, skip_bias):
    steps, sessions, width = up.shape
    window, block = mine.shape[0], sessions // 4
    frames = pl.BlockSpec((window, block, width), lambda i: (0, i, 0))
    return pl.pallas_call(
        residual_kernel,
        out_shape=jax.ShapeDtypeStruct((sessions * steps, width), BF16),
        grid=(4,),
        in_specs=[pl.BlockSpec((steps, block, width), lambda i: (0, i, 0)), frames, frames]
        + [VMEM] * 5,
        out_specs=pl.BlockSpec((block * steps, width), lambda i: (i, 0)),
        scratch_shapes=[pltpu.VMEM((width // 128, block * steps, 128), F32)],
        compiler_params=pltpu.CompilerParams(vmem_limit_bytes=VMEM_LIMIT),
        cost_estimate=pl.CostEstimate(
            flops=2 * up.size * (2 * res_mine.shape[0] + 1) * res_mine.shape[2],
            bytes_accessed=12 * up.size,
            transcendentals=up.size,
        ),
    )(up, mine, theirs, res_mine, res_theirs, res_bias, skip_weight, skip_bias)


def weave_kernel(group_ref, own_ref, other_ref, out_ref, frames):
    group = group_ref[0]
    taps, block, width = own_ref.shape
    for half in range(2):
        for tap in range(taps):
            value = jnp.where(
                group == half, own_ref[tap].astype(F32), other_ref[tap].astype(F32)
            )
            step = half * taps + tap
            for part in range(width // 128):
                frames.at[part][pl.ds(step, block, stride=2 * taps), :] = value[
                    :, part * 128 : (part + 1) * 128
                ]
    for part in range(width // 128):
        out_ref[:, part * 128 : (part + 1) * 128] = frames[part].astype(BF16)


def weave(group, own, other):
    taps, sessions, width = own.shape
    steps, block = 2 * taps, sessions // 4
    part = pl.BlockSpec((taps, block, width), lambda i: (0, i, 0))
    return pl.pallas_call(
        weave_kernel,
        out_shape=jax.ShapeDtypeStruct((sessions * steps, width), BF16),
        grid=(4,),
        in_specs=[pl.BlockSpec(memory_space=pltpu.SMEM), part, part],
        out_specs=pl.BlockSpec((block * steps, width), lambda i: (i, 0)),
        scratch_shapes=[pltpu.VMEM((width // 128, block * steps, 128), F32)],
        compiler_params=pltpu.CompilerParams(vmem_limit_bytes=VMEM_LIMIT),
        cost_estimate=pl.CostEstimate(
            flops=0, bytes_accessed=4 * sessions * steps * width, transcendentals=0
        ),
    )(group, own, other)


def swap(value, axis):
    return lax.ppermute(value, axis, [(0, 1), (1, 0)])


def after(value, earlier):
    return lax.optimization_barrier((value, earlier))[0]


class Ring:
    def __init__(self, count, own, other):
        order = ring_order(count)
        self.count = count
        self.pairs = []
        for p in range(count):
            here, there = order[p], order[(p + 1) % count]
            self.pairs += [(2 * here, 2 * there), (2 * there + 1, 2 * here + 1)]
        self.item = jnp.stack([own, other])
        self.blocks, self.steps, self.rounds = [own], [(0, 0)], 0

    def round(self, earlier=None):
        self.rounds += 1
        item = self.item
        if 2 * self.rounds == self.count:
            part = item.shape[1] // 2
            item = lax.dynamic_slice_in_dim(item, lax.axis_index("segment") * part, part, axis=1)
        if earlier is not None:
            item = after(item, earlier)
        item = lax.ppermute(item, ("streams", "segment"), self.pairs)
        self.item = item
        self.blocks += [item, swap(item[1], "segment")]
        self.steps += [(self.rounds, 0), (self.rounds, 1)]
        return item


def local(
    count,
    latent,
    conv_weight,
    conv_bias,
    tail_cache,
    input_cache,
    resume_slot,
    res_weight,
    res_bias,
    skip_weight,
    skip_bias,
):
    group = lax.axis_index("groups")
    group_word = group[None].astype(jnp.int32)
    rows, tap_count, width = conv_weight.shape
    sessions = latent.shape[0]
    taps = tap_count // 4

    halves = []
    for first in (0, tap_count // 2):
        part = lax.dynamic_slice_in_dim(conv_weight, first + group * taps, taps, axis=1)
        halves.append(part.transpose(1, 0, 2))
    own = jnp.concatenate(halves, axis=0)
    cuts = ((0, taps), (taps, 2 * taps))

    if rows % 128 == 0 and count % 2 == 0:
        other = swap(own, "segment")
        rings = [Ring(count, own[a:b], other[a:b]) for a, b in cuts]
        up_ring, tail_ring = rings
        first_done = up_ring.round()
        behind = None
        for _ in range(2, count // 2 + 1):
            ahead = up_ring.round(behind)
            behind = tail_ring.round(behind_of_ahead) if tail_ring.rounds else tail_ring.round()
            behind_of_ahead = ahead
        nearly_done = behind
        tail_ring.round(behind_of_ahead)
        gathered = [(ring.blocks, ring.steps) for ring in rings]
    else:
        gathered = [
            ([lax.all_gather(own[a:b], "streams", axis=1, tiled=True)], [None]) for a, b in cuts
        ]
        first_done = nearly_done = own

    portion = sessions // count
    cap = tail_cache.shape[0] // count
    half_taps, history = tail_cache.shape[1], input_cache.shape[1]
    slot_step = jnp.broadcast_to(
        resume_slot.astype(BF16)[:, None, None], (count * cap, 1, width)
    )
    filler = jnp.zeros((count * cap, half_taps - history - 1, width), BF16)
    beside = jnp.concatenate([input_cache, slot_step, filler], axis=1)
    stored = jnp.concatenate([tail_cache, beside], axis=2).reshape(count, cap * half_taps, 2 * width)
    parcel = jnp.concatenate([latent.reshape(count, portion, 2 * width), stored], axis=1)
    parcel = after(parcel, first_done)
    parcel = lax.all_to_all(parcel, "streams", split_axis=0, concat_axis=0, tiled=True)
    handed = parcel[:, :portion].reshape(sessions, 2 * width)
    stored = parcel[:, portion:].reshape(count * cap, half_taps, 2 * width)

    near_half = apply_elu(handed.astype(F32)).astype(BF16)
    far_half = swap(near_half, "groups")
    sides = (near_half, swap(near_half, "segment"), far_half, swap(far_half, "segment"))

    slots = stored[:, history, width:].astype(jnp.int32)[:, :1]
    one_hot = (slots == jnp.arange(sessions, dtype=jnp.int32)[None, :]).astype(BF16)
    packed = jnp.concatenate([stored[:, :, :width], stored[:, :history, width:]], axis=1)
    prev = jnp.einsum("js,jkc->ksc", one_hot, packed, preferred_element_type=F32).astype(BF16)

    res_theirs = swap(res_weight, "segment")

    own_up, away_up = spread_taps(sides, *gathered[0], count, F32)
    other_up = swap(after(away_up, nearly_done), "groups")
    own_tail, away_tail = spread_taps(sides, *gathered[1], count, BF16)
    other_tail = swap(away_tail, "groups")

    own_up = after(own_up, away_tail)
    up, mine = excite(group_word, own_up, other_up, prev, conv_bias[None])
    theirs = swap(mine, "segment")
    decoded = residual(
        up, mine, theirs, res_weight, res_theirs, res_bias[None], skip_weight, skip_bias[None]
    )
    decoded, other_tail = lax.optimization_barrier((decoded, other_tail))
    new_tail = weave(group_word, own_tail, other_tail)
    shape = (sessions, half_taps, width)
    return decoded.reshape(shape), new_tail.reshape(shape)


def solution(mesh):
    placed = (
        P(("groups", "streams"), "segment"),
        P("streams", None, "segment"),
        P("segment"),
        P(("groups", "streams"), None, "segment"),
        P(("groups", "streams"), None, "segment"),
        P(("groups", "streams")),
        P(None, "segment", None),
        P(),
        P(None, "segment"),
        P("segment"),
    )
    return jax.shard_map(
        functools.partial(local, mesh.shape["streams"]),
        mesh=mesh,
        in_specs=placed,
        out_specs=(
            P(("groups", "streams"), None, "segment"),
            P(("groups", "streams"), None, "segment"),
        ),
        check_vma=False,
    )
```

profile of v0, /device:TPU:0, one launch (start us, length us, event | category | flops | bytes accessed | tf_op | source)
XLA Modules:
  0.0 95.3 jit_solution(829926642875443612)
XLA Ops:
  0.6 1.5 %constant_dynamic-slice_fusion.2 = (bf16[128,4,256]{2,1,0:T(4,128)(2,1)S(1)}, bf16[128,4,256]{2,1,0:T(4,128)(2,1)S(1)}) fusion(bf16[128,16,256]{2,1,0:T(8,128)(2,1)} %param.11, s32[]{:T(128)S(6)} %select_n.15, s32[]{:T(128)S(6)} %select_n.14), kind=kLoop, calls=%fused_computation.35 | loop fusion | bytes 1048584 | tf_op jit(solution)/shard_map/dynamic_slice | solution.py:273
  2.1 0.1 copy_bitcast_fusion
  2.3 0.5 collective-permute-start
  2.8 1.5 %collective-permute-done = bf16[8,128,256]{2,1,0:T(8,128)(2,1)S(1)} collective-permute-done((bf16[8,128,256]{2,1,0:T(8,128)(2,1)S(1)}, bf16[8,128,256]{2,1,0:T(8,128)(2,1)S(1)}, u32[]{:S(2)}, u32[]{:S(2)}) %collective-permute-start) | collective-permute-done | bytes 524320 | tf_op jit(solution)/shard_map/ppermute | solution.py:219
  4.5 3.0 %collective-permute-start.1 = (bf16[2,4,128,256]{3,2,1,0:T(8,128)(2,1)S(1)}, bf16[2,4,128,256]{3,2,1,0:T(8,128)(2,1)S(1)}, u32[]{:S(2)}, u32[]{:S(2)}) collective-permute-start(bf16[2,4,128,256]{3,2,1,0:T(8,128)(2,1)S(1)} %pad_maximum_fusion.1), channel_id=1, source_target_pairs={{0,4},{5,1},{4,8},{9,5},{8,12},{13,9},{12,14},{15,13},{14,10},{11,... | collective-permute-start | bytes 1572872 | tf_op jit(solution)/shard_map/ppermute | solution.py:245
  7.6 1.6 %collective-permute-start.5 = (bf16[2,4,128,256]{3,2,1,0:T(8,128)(2,1)S(1)}, bf16[2,4,128,256]{3,2,1,0:T(8,128)(2,1)S(1)}, u32[]{:S(2)}, u32[]{:S(2)}) collective-permute-start(bf16[2,4,128,256]{3,2,1,0:T(8,128)(2,1)S(1)} %pad_maximum_fusion.2), channel_id=1, source_target_pairs={{0,4},{5,1},{4,8},{9,5},{8,12},{13,9},{12,14},{15,13},{14,10},{11,... | collective-permute-start | bytes 1572872 | tf_op jit(solution)/shard_map/ppermute | solution.py:245
  9.2 5.4 %collective-permute-done.1.refs_1_ = bf16[2,4,128,256]{3,2,1,0:T(8,128)(2,1)S(1)} collective-permute-done((bf16[2,4,128,256]{3,2,1,0:T(8,128)(2,1)S(1)}, bf16[2,4,128,256]{3,2,1,0:T(8,128)(2,1)S(1)}, u32[]{:S(2)}, u32[]{:S(2)}) %collective-permute-start.1) | collective-permute-done | bytes 524320 | tf_op jit(solution)/shard_map/ppermute | solution.py:245
  14.6 2.1 %collective-permute-start.3 = (bf16[2,4,128,256]{3,2,1,0:T(8,128)(2,1)S(1)}, bf16[2,4,128,256]{3,2,1,0:T(8,128)(2,1)S(1)}, u32[]{:S(2)}, u32[]{:S(2)}) collective-permute-start(bf16[2,4,128,256]{3,2,1,0:T(8,128)(2,1)S(1)} %collective-permute-done.1.refs_1_), channel_id=1, source_target_pairs={{0,4},{5,1},{4,8},{9,5},{8,12},{13,9},{12,14},{15,13},{14,10},{11,... | collective-permute-start | bytes 1572872 | tf_op jit(solution)/shard_map/ppermute | solution.py:245
  16.7 0.1 broadcast_in_dim.23
  16.8 0.8 maximum_maximum_fusion
  17.6 4.8 %all-to-all-start = ((bf16[8,40,512]{2,1,0:T(8,128)(2,1)}), bf16[8,40,512]{2,1,0:T(8,128)(2,1)}, u32[]{:S(2)}, u32[]{:S(2)}) async-start(bf16[8,40,512]{2,1,0:T(8,128)(2,1)} %maximum_maximum_fusion), calls=%async_computation | async-start | bytes 655360 | tf_op jit(solution)/shard_map/all_to_all | solution.py:308
  22.4 0.7 slice_bitcast_fusion.6
  23.1 4.9 %collective-permute-done.3.refs_3_ = bf16[2,4,128,256]{3,2,1,0:T(8,128)(2,1)S(1)} collective-permute-done((bf16[2,4,128,256]{3,2,1,0:T(8,128)(2,1)S(1)}, bf16[2,4,128,256]{3,2,1,0:T(8,128)(2,1)S(1)}, u32[]{:S(2)}, u32[]{:S(2)}) %collective-permute-start.3) | collective-permute-done | bytes 524320 | tf_op jit(solution)/shard_map/ppermute | solution.py:245
  28.1 3.4 %collective-permute-start.6 = (bf16[2,4,128,256]{3,2,1,0:T(8,128)(2,1)S(1)}, bf16[2,4,128,256]{3,2,1,0:T(8,128)(2,1)S(1)}, u32[]{:S(2)}, u32[]{:S(2)}) collective-permute-start(bf16[2,4,128,256]{3,2,1,0:T(8,128)(2,1)S(1)} %collective-permute-done.3.refs_3_), channel_id=1, source_target_pairs={{0,4},{5,1},{4,8},{9,5},{8,12},{13,9},{12,14},{15,13},{14,10},{11,... | collective-permute-start | bytes 1572872 | tf_op jit(solution)/shard_map/ppermute | solution.py:245
  31.4 0.7 slice_bitcast_fusion.2
  32.2 3.3 %collective-permute-start.8 = (bf16[2,4,128,256]{3,2,1,0:T(8,128)(2,1)S(1)}, bf16[2,4,128,256]{3,2,1,0:T(8,128)(2,1)S(1)}, u32[]{:S(2)}, u32[]{:S(2)}) collective-permute-start(bf16[2,4,128,256]{3,2,1,0:T(8,128)(2,1)S(1)} %collective-permute-done.5.refs_1_), channel_id=1, source_target_pairs={{0,4},{5,1},{4,8},{9,5},{8,12},{13,9},{12,14},{15,13},{14,10},{11,... | collective-permute-start | bytes 1572872 | tf_op jit(solution)/shard_map/ppermute | solution.py:245
  35.5 0.7 slice_bitcast_fusion.5
  36.2 1.0 %slice.71 = bf16[8,32,512]{2,1,0:T(8,128)(2,1)S(1)} slice(bf16[8,40,512]{2,1,0:T(8,128)(2,1)} %all-to-all-done), slice={[0:8], [0:32], [0:512]} | slice | bytes 524288 | tf_op jit(solution)/shard_map/slice | solution.py:309
  37.2 0.1 fusion.3.refs_9_
  37.4 1.6 %collective-permute-start.12 = (bf16[256,512]{1,0:T(8,128)(2,1)S(1)}, bf16[256,512]{1,0:T(8,128)(2,1)S(1)}, u32[]{:S(2)}, u32[]{:S(2)}) collective-permute-start(bf16[256,512]{1,0:T(8,128)(2,1)S(1)} %fusion.3.refs_9_), channel_id=1, source_target_pairs={{0,16},{16,0},{1,17},{17,1},{2,18},{18,2},{3,19},{19,3},{4,20},{20... | collective-permute-start | bytes 786440 | tf_op jit(solution)/shard_map/ppermute | solution.py:219
  38.9 0.8 slice.78
  39.8 4.0 %collective-permute-done.8.refs_3_ = bf16[2,4,128,256]{3,2,1,0:T(8,128)(2,1)S(1)} collective-permute-done((bf16[2,4,128,256]{3,2,1,0:T(8,128)(2,1)S(1)}, bf16[2,4,128,256]{3,2,1,0:T(8,128)(2,1)S(1)}, u32[]{:S(2)}, u32[]{:S(2)}) %collective-permute-start.8) | collective-permute-done | bytes 524320 | tf_op jit(solution)/shard_map/ppermute | solution.py:245
  43.8 3.3 %collective-permute-start.9 = (bf16[2,2,128,256]{3,2,1,0:T(8,128)(2,1)S(1)}, bf16[2,2,128,256]{3,2,1,0:T(8,128)(2,1)S(1)}, u32[]{:S(2)}, u32[]{:S(2)}) collective-permute-start(bf16[2,2,128,256]{3,2,1,0:T(8,128)(2,1)S(1)} %constant_dynamic-slice_fusion.1), channel_id=1, source_target_pairs={{0,4},{5,1},{4,8},{9,5},{8,12},{13,9},{12,14},{15,13},{14,10},{11,... | collective-permute-start | bytes 786440 | tf_op jit(solution)/shard_map/ppermute | solution.py:245
  47.1 2.5 %collective-permute-start.16 = (bf16[2,4,128,256]{3,2,1,0:T(8,128)(2,1)S(1)}, bf16[2,4,128,256]{3,2,1,0:T(8,128)(2,1)S(1)}, u32[]{:S(2)}, u32[]{:S(2)}) collective-permute-start(bf16[2,4,128,256]{3,2,1,0:T(8,128)(2,1)S(1)} %collective-permute-done.8.refs_3_), channel_id=1, source_target_pairs={{0,4},{5,1},{4,8},{9,5},{8,12},{13,9},{12,14},{15,13},{14,10},{11,... | collective-permute-start | bytes 1572872 | tf_op jit(solution)/shard_map/ppermute | solution.py:245
  49.6 0.1 convert_reduce_fusion
  49.7 0.8 slice.77
  50.5 0.8 slice.76
  51.4 0.5 collective-permute-start.13
  51.9 0.2 collective-permute-start.7
  52.0 4.6 %collective-permute-done.16.refs_5_ = bf16[2,4,128,256]{3,2,1,0:T(8,128)(2,1)S(1)} collective-permute-done((bf16[2,4,128,256]{3,2,1,0:T(8,128)(2,1)S(1)}, bf16[2,4,128,256]{3,2,1,0:T(8,128)(2,1)S(1)}, u32[]{:S(2)}, u32[]{:S(2)}) %collective-permute-start.16) | collective-permute-done | bytes 524320 | tf_op jit(solution)/shard_map/ppermute | solution.py:245
  56.7 0.6 collective-permute-start.14
  57.2 0.1 collective-permute-start.15
  57.3 2.5 %collective-permute-start.18 = (bf16[2,2,128,256]{3,2,1,0:T(8,128)(2,1)S(1)}, bf16[2,2,128,256]{3,2,1,0:T(8,128)(2,1)S(1)}, u32[]{:S(2)}, u32[]{:S(2)}) collective-permute-start(bf16[2,2,128,256]{3,2,1,0:T(8,128)(2,1)S(1)} %constant_dynamic-slice_fusion), channel_id=1, source_target_pairs={{0,4},{5,1},{4,8},{9,5},{8,12},{13,9},{12,14},{15,13},{14,10},{11,... | collective-permute-start | bytes 786440 | tf_op jit(solution)/shard_map/ppermute | solution.py:245
  59.8 2.9 %shard_map.113 = (f32[4,256,256]{2,1,0:T(8,128)S(1)}, bf16[4,256,256]{2,1,0:T(8,128)(2,1)S(1)}) custom-call(bf16[4,128,256]{2,1,0:T(8,128)(2,1)S(1)} %get-tuple-element.42.refs_0_, bf16[2,4,128,256]{3,2,1,0:T(8,128)(2,1)S(1)} %collective-permute-done.1.refs_1_, bf16[4,128,256]{2,1,0:T(8,128)(2,1)S(1)} %collective-permute-done.2.refs_2_, ...), custom_call_target="tpu_custom_call" | custom-call | flops 1073741824 | bytes 4718592 | tf_op jit(solution)/shard_map/pallas_call | solution.py:80
  62.8 1.6 %collective-permute-start.20 = (bf16[4,256,256]{2,1,0:T(8,128)(2,1)S(1)}, bf16[4,256,256]{2,1,0:T(8,128)(2,1)S(1)}, u32[]{:S(2)}, u32[]{:S(2)}) collective-permute-start(bf16[4,256,256]{2,1,0:T(8,128)(2,1)S(1)} %get-tuple-element.28), channel_id=1, source_target_pairs={{0,16},{16,0},{1,17},{17,1},{2,18},{18,2},{3,19},{19,3},{4,20},{20... | collective-permute-start | bytes 1572872 | tf_op jit(solution)/shard_map/ppermute | solution.py:219
  64.4 0.2 collective-permute-start.19
  64.7 0.6 fusion.prev_ref
  65.3 0.5 collective-permute-done.19.refs_8_
  65.9 2.3 %shard_map.114 = (bf16[4,256,256]{2,1,0:T(8,128)(2,1)S(1)}, bf16[4,256,256]{2,1,0:T(8,128)(2,1)S(1)}) custom-call(bf16[4,128,256]{2,1,0:T(8,128)(2,1)S(1)} %get-tuple-element.39.refs_0_, bf16[2,4,128,256]{3,2,1,0:T(8,128)(2,1)S(1)} %collective-permute-done.5.refs_1_, bf16[4,128,256]{2,1,0:T(8,128)(2,1)S(1)} %collective-permute-done.14.refs_2_, ...), custom_call_target="tpu_custom_call" | custom-call | flops 1073741824 | bytes 4718592 | tf_op jit(solution)/shard_map/pallas_call | solution.py:80
  68.1 9.0 %collective-permute-done.20.other_ref = bf16[4,256,256]{2,1,0:T(8,128)(2,1)S(1)} collective-permute-done((bf16[4,256,256]{2,1,0:T(8,128)(2,1)S(1)}, bf16[4,256,256]{2,1,0:T(8,128)(2,1)S(1)}, u32[]{:S(2)}, u32[]{:S(2)}) %collective-permute-start.20) | collective-permute-done | bytes 524320 | tf_op jit(solution)/shard_map/ppermute | solution.py:219
  77.2 1.7 %shard_map.115 = (f32[8,256,256]{2,1,0:T(8,128)}, bf16[10,256,256]{2,1,0:T(8,128)(2,1)S(1)}) custom-call(s32[1]{0:T(128)} %bitcast.group_ref, f32[4,256,256]{2,1,0:T(8,128)S(1)} %get-tuple-element.26.own_ref, bf16[4,256,256]{2,1,0:T(8,128)(2,1)S(1)} %collective-permute-done.20.other_ref, bf16[10,256,256]{2,1,0:T(8,128)(2,1)S(1)} %fusion.prev_ref, ...), custom_call_target="tpu_custom_call" | custom-call | flops 5242880 | bytes 10485760 | tf_op jit(solution)/shard_map/pallas_call | solution.py:120
  78.9 0.5 collective-permute-start.22
  79.4 1.5 %collective-permute-start.23 = (bf16[4,256,256]{2,1,0:T(8,128)(2,1)S(1)}, bf16[4,256,256]{2,1,0:T(8,128)(2,1)S(1)}, u32[]{:S(2)}, u32[]{:S(2)}) collective-permute-start(bf16[4,256,256]{2,1,0:T(8,128)(2,1)S(1)} %get-tuple-element.25), channel_id=1, source_target_pairs={{0,16},{16,0},{1,17},{17,1},{2,18},{18,2},{3,19},{19,3},{4,20},{20... | collective-permute-start | bytes 1572872 | tf_op jit(solution)/shard_map/ppermute | solution.py:219
  80.9 1.6 %collective-permute-done.22.res_theirs_ref = bf16[3,256,256]{2,1,0:T(8,128)(2,1)S(1)} collective-permute-done((bf16[3,256,256]{2,1,0:T(8,128)(2,1)S(1)}, bf16[3,256,256]{2,1,0:T(8,128)(2,1)S(1)}, u32[]{:S(2)}, u32[]{:S(2)}) %collective-permute-start.22) | collective-permute-done | bytes 393248 | tf_op jit(solution)/shard_map/ppermute | solution.py:219
  82.5 1.6 %copy-done.1 = f32[8,256,256]{2,1,0:T(8,128)S(1)} copy-done((f32[8,256,256]{2,1,0:T(8,128)S(1)}, f32[8,256,256]{2,1,0:T(8,128)}, u32[]{:S(2)}) %copy-start.1) | copy-done | bytes 2097176
  84.1 4.4 %shard_map.116 = bf16[2048,256]{1,0:T(8,128)(2,1)} custom-call(f32[8,256,256]{2,1,0:T(8,128)S(1)} %copy-done.1, bf16[10,256,256]{2,1,0:T(8,128)(2,1)S(1)} %get-tuple-element.30.mine_ref, bf16[10,256,256]{2,1,0:T(8,128)(2,1)S(1)} %collective-permute-done.21.theirs_ref, bf16[3,256,256]{2,1,0:T(8,128)(2,1)S(1)} %copy-done.2, ...), custom_call_target="tpu_custom_call" | custom-call | flops 1879048192 | bytes 6291456 | tf_op jit(solution)/shard_map/pallas_call | solution.py:166
  88.6 4.7 %collective-permute-done.23.other_ref = bf16[4,256,256]{2,1,0:T(8,128)(2,1)S(1)} collective-permute-done((bf16[4,256,256]{2,1,0:T(8,128)(2,1)S(1)}, bf16[4,256,256]{2,1,0:T(8,128)(2,1)S(1)}, u32[]{:S(2)}, u32[]{:S(2)}) %collective-permute-start.23) | collective-permute-done | bytes 524320 | tf_op jit(solution)/shard_map/ppermute | solution.py:219
  93.3 2.0 %shard_map.117 = bf16[2048,256]{1,0:T(8,128)(2,1)} custom-call(s32[1]{0:T(128)} %bitcast.group_ref, bf16[4,256,256]{2,1,0:T(8,128)(2,1)S(1)} %get-tuple-element.32.own_ref, bf16[4,256,256]{2,1,0:T(8,128)(2,1)S(1)} %collective-permute-done.23.other_ref), custom_call_target="tpu_custom_call" | custom-call | bytes 2097152 | tf_op jit(solution)/shard_map/pallas_call | solution.py:204
  (60 shorter events, 0.6 us)
Async XLA Ops:
  2.3 2.1 %collective-permute-start = (bf16[8,128,256]{2,1,0:T(8,128)(2,1)S(1)}, bf16[8,128,256]{2,1,0:T(8,128)(2,1)S(1)}, u32[]{:S(2)}, u32[]{:S(2)}) collective-permute-start(bf16[8,128,256]{2,1,0:T(8,128)(2,1)S(1)} %pad_maximum_fusion), channel_id=1, source_target_pairs={{0,1},{1,0},{2,3},{3,2},{4,5},{5,4},{6,7},{7,6},{8,9},{9,8},{10,11... | collective-permute-start | bytes 1572872 | tf_op jit(solution)/shard_map/ppermute | solution.py:219
  4.4 12.3 %copy-start.10 = (s32[8]{0:T(128)S(1)}, s32[8]{0:T(128)}, u32[]{:S(2)}) copy-start(s32[8]{0:T(128)} %param.15) | copy-start | bytes 100
  4.4 12.4 %copy-start.7 = (bf16[256,512]{1,0:T(8,128)(2,1)S(1)}, bf16[256,512]{1,0:T(8,128)(2,1)}, u32[]{:S(2)}) copy-start(bf16[256,512]{1,0:T(8,128)(2,1)} %param.10) | copy-start | bytes 786436
  4.4 12.4 %copy-start.8 = (bf16[8,8,256]{2,1,0:T(8,128)(2,1)S(1)}, bf16[8,8,256]{2,1,0:T(8,128)(2,1)}, u32[]{:S(2)}) copy-start(bf16[8,8,256]{2,1,0:T(8,128)(2,1)} %param.13) | copy-start | bytes 98308
  4.4 12.4 %copy-start.9 = (bf16[8,2,256]{2,1,0:T(2,128)(2,1)S(1)}, bf16[8,2,256]{2,1,0:T(2,128)(2,1)}, u32[]{:S(2)}) copy-start(bf16[8,2,256]{2,1,0:T(2,128)(2,1)} %param.14) | copy-start | bytes 24580
  4.5 10.1 %collective-permute-start.1 = (bf16[2,4,128,256]{3,2,1,0:T(8,128)(2,1)S(1)}, bf16[2,4,128,256]{3,2,1,0:T(8,128)(2,1)S(1)}, u32[]{:S(2)}, u32[]{:S(2)}) collective-permute-start(bf16[2,4,128,256]{3,2,1,0:T(8,128)(2,1)S(1)} %pad_maximum_fusion.1), channel_id=1, source_target_pairs={{0,4},{5,1},{4,8},{9,5},{8,12},{13,9},{12,14},{15,13},{14,10},{11,... | collective-permute-start | bytes 1572872 | tf_op jit(solution)/shard_map/ppermute | solution.py:245
  7.6 15.6 %collective-permute-start.5 = (bf16[2,4,128,256]{3,2,1,0:T(8,128)(2,1)S(1)}, bf16[2,4,128,256]{3,2,1,0:T(8,128)(2,1)S(1)}, u32[]{:S(2)}, u32[]{:S(2)}) collective-permute-start(bf16[2,4,128,256]{3,2,1,0:T(8,128)(2,1)S(1)} %pad_maximum_fusion.2), channel_id=1, source_target_pairs={{0,4},{5,1},{4,8},{9,5},{8,12},{13,9},{12,14},{15,13},{14,10},{11,... | collective-permute-start | bytes 1572872 | tf_op jit(solution)/shard_map/ppermute | solution.py:245
  14.6 13.5 %collective-permute-start.3 = (bf16[2,4,128,256]{3,2,1,0:T(8,128)(2,1)S(1)}, bf16[2,4,128,256]{3,2,1,0:T(8,128)(2,1)S(1)}, u32[]{:S(2)}, u32[]{:S(2)}) collective-permute-start(bf16[2,4,128,256]{3,2,1,0:T(8,128)(2,1)S(1)} %collective-permute-done.1.refs_1_), channel_id=1, source_target_pairs={{0,4},{5,1},{4,8},{9,5},{8,12},{13,9},{12,14},{15,13},{14,10},{11,... | collective-permute-start | bytes 1572872 | tf_op jit(solution)/shard_map/ppermute | solution.py:245
  17.6 18.6 %all-to-all-start = ((bf16[8,40,512]{2,1,0:T(8,128)(2,1)}), bf16[8,40,512]{2,1,0:T(8,128)(2,1)}, u32[]{:S(2)}, u32[]{:S(2)}) async-start(bf16[8,40,512]{2,1,0:T(8,128)(2,1)} %maximum_maximum_fusion), calls=%async_computation | async-start | bytes 655360 | tf_op jit(solution)/shard_map/all_to_all | solution.py:308
  23.1 28.7 %collective-permute-start.2 = (bf16[4,128,256]{2,1,0:T(8,128)(2,1)}, bf16[4,128,256]{2,1,0:T(8,128)(2,1)S(1)}, u32[]{:S(2)}, u32[]{:S(2)}) collective-permute-start(bf16[4,128,256]{2,1,0:T(8,128)(2,1)} %slice_bitcast_fusion.6), channel_id=1, source_target_pairs={{0,1},{1,0},{2,3},{3,2},{4,5},{5,4},{6,7},{7,6},{8,9},{9,8},{10,11... | collective-permute-start | bytes 786440 | tf_op jit(solution)/shard_map/ppermute | solution.py:219
  28.1 11.7 %collective-permute-start.6 = (bf16[2,4,128,256]{3,2,1,0:T(8,128)(2,1)S(1)}, bf16[2,4,128,256]{3,2,1,0:T(8,128)(2,1)S(1)}, u32[]{:S(2)}, u32[]{:S(2)}) collective-permute-start(bf16[2,4,128,256]{3,2,1,0:T(8,128)(2,1)S(1)} %collective-permute-done.3.refs_3_), channel_id=1, source_target_pairs={{0,4},{5,1},{4,8},{9,5},{8,12},{13,9},{12,14},{15,13},{14,10},{11,... | collective-permute-start | bytes 1572872 | tf_op jit(solution)/shard_map/ppermute | solution.py:245
  32.2 11.6 %collective-permute-start.8 = (bf16[2,4,128,256]{3,2,1,0:T(8,128)(2,1)S(1)}, bf16[2,4,128,256]{3,2,1,0:T(8,128)(2,1)S(1)}, u32[]{:S(2)}, u32[]{:S(2)}) collective-permute-start(bf16[2,4,128,256]{3,2,1,0:T(8,128)(2,1)S(1)} %collective-permute-done.5.refs_1_), channel_id=1, source_target_pairs={{0,4},{5,1},{4,8},{9,5},{8,12},{13,9},{12,14},{15,13},{14,10},{11,... | collective-permute-start | bytes 1572872 | tf_op jit(solution)/shard_map/ppermute | solution.py:245
  36.2 20.4 %collective-permute-start.4 = (bf16[4,128,256]{2,1,0:T(8,128)(2,1)}, bf16[4,128,256]{2,1,0:T(8,128)(2,1)}, u32[]{:S(2)}, u32[]{:S(2)}) collective-permute-start(bf16[4,128,256]{2,1,0:T(8,128)(2,1)} %slice_bitcast_fusion.5), channel_id=1, source_target_pairs={{0,1},{1,0},{2,3},{3,2},{4,5},{5,4},{6,7},{7,6},{8,9},{9,8},{10,11... | collective-permute-start | bytes 786440 | tf_op jit(solution)/shard_map/ppermute | solution.py:219
  37.3 19.3 %copy-start.6 = (bf16[4,128,256]{2,1,0:T(8,128)(2,1)S(1)}, bf16[4,128,256]{2,1,0:T(8,128)(2,1)}, u32[]{:S(2)}) copy-start(bf16[4,128,256]{2,1,0:T(8,128)(2,1)} %slice_bitcast_fusion.2) | copy-start | bytes 786436
  37.4 13.9 %collective-permute-start.12 = (bf16[256,512]{1,0:T(8,128)(2,1)S(1)}, bf16[256,512]{1,0:T(8,128)(2,1)S(1)}, u32[]{:S(2)}, u32[]{:S(2)}) collective-permute-start(bf16[256,512]{1,0:T(8,128)(2,1)S(1)} %fusion.3.refs_9_), channel_id=1, source_target_pairs={{0,16},{16,0},{1,17},{17,1},{2,18},{18,2},{3,19},{19,3},{4,20},{20... | collective-permute-start | bytes 786440 | tf_op jit(solution)/shard_map/ppermute | solution.py:219
  43.8 7.6 %collective-permute-start.9 = (bf16[2,2,128,256]{3,2,1,0:T(8,128)(2,1)S(1)}, bf16[2,2,128,256]{3,2,1,0:T(8,128)(2,1)S(1)}, u32[]{:S(2)}, u32[]{:S(2)}) collective-permute-start(bf16[2,2,128,256]{3,2,1,0:T(8,128)(2,1)S(1)} %constant_dynamic-slice_fusion.1), channel_id=1, source_target_pairs={{0,4},{5,1},{4,8},{9,5},{8,12},{13,9},{12,14},{15,13},{14,10},{11,... | collective-permute-start | bytes 786440 | tf_op jit(solution)/shard_map/ppermute | solution.py:245
  47.1 9.5 %collective-permute-start.16 = (bf16[2,4,128,256]{3,2,1,0:T(8,128)(2,1)S(1)}, bf16[2,4,128,256]{3,2,1,0:T(8,128)(2,1)S(1)}, u32[]{:S(2)}, u32[]{:S(2)}) collective-permute-start(bf16[2,4,128,256]{3,2,1,0:T(8,128)(2,1)S(1)} %collective-permute-done.8.refs_3_), channel_id=1, source_target_pairs={{0,4},{5,1},{4,8},{9,5},{8,12},{13,9},{12,14},{15,13},{14,10},{11,... | collective-permute-start | bytes 1572872 | tf_op jit(solution)/shard_map/ppermute | solution.py:245
  51.3 6.0 %collective-permute-start.11 = (bf16[256,512]{1,0:T(8,128)(2,1)S(1)}, bf16[256,512]{1,0:T(8,128)(2,1)S(1)}, u32[]{:S(2)}, u32[]{:S(2)}) collective-permute-start(bf16[256,512]{1,0:T(8,128)(2,1)S(1)} %fusion.3.refs_9_), channel_id=1, source_target_pairs={{0,1},{1,0},{2,3},{3,2},{4,5},{5,4},{6,7},{7,6},{8,9},{9,8},{10,11... | collective-permute-start | bytes 786440 | tf_op jit(solution)/shard_map/ppermute | solution.py:219
  51.4 6.0 %collective-permute-start.13 = (bf16[256,512]{1,0:T(8,128)(2,1)S(1)}, bf16[256,512]{1,0:T(8,128)(2,1)S(1)}, u32[]{:S(2)}, u32[]{:S(2)}) collective-permute-start(bf16[256,512]{1,0:T(8,128)(2,1)S(1)} %collective-permute-done.12.refs_11_), channel_id=1, source_target_pairs={{0,1},{1,0},{2,3},{3,2},{4,5},{5,4},{6,7},{7,6},{8,9},{9,8},{10,11... | collective-permute-start | bytes 786440 | tf_op jit(solution)/shard_map/ppermute | solution.py:219
  51.9 8.0 %collective-permute-start.7 = (bf16[4,128,256]{2,1,0:T(8,128)(2,1)S(1)}, bf16[4,128,256]{2,1,0:T(8,128)(2,1)S(1)}, u32[]{:S(2)}, u32[]{:S(2)}) collective-permute-start(bf16[4,128,256]{2,1,0:T(8,128)(2,1)S(1)} %slice_bitcast_fusion.3), channel_id=1, source_target_pairs={{0,1},{1,0},{2,3},{3,2},{4,5},{5,4},{6,7},{7,6},{8,9},{9,8},{10,11... | collective-permute-start | bytes 786440 | tf_op jit(solution)/shard_map/ppermute | solution.py:219
  56.6 3.2 %collective-permute-start.10 = (bf16[2,128,256]{2,1,0:T(8,128)(2,1)S(1)}, bf16[2,128,256]{2,1,0:T(8,128)(2,1)S(1)}, u32[]{:S(2)}, u32[]{:S(2)}) collective-permute-start(bf16[2,128,256]{2,1,0:T(8,128)(2,1)S(1)} %slice_bitcast_fusion.9), channel_id=1, source_target_pairs={{0,1},{1,0},{2,3},{3,2},{4,5},{5,4},{6,7},{7,6},{8,9},{9,8},{10,11... | collective-permute-start | bytes 393224 | tf_op jit(solution)/shard_map/ppermute | solution.py:219
  56.7 8.6 %collective-permute-start.14 = (bf16[4,128,256]{2,1,0:T(8,128)(2,1)S(1)}, bf16[4,128,256]{2,1,0:T(8,128)(2,1)S(1)}, u32[]{:S(2)}, u32[]{:S(2)}) collective-permute-start(bf16[4,128,256]{2,1,0:T(8,128)(2,1)S(1)} %copy-done.6), channel_id=1, source_target_pairs={{0,1},{1,0},{2,3},{3,2},{4,5},{5,4},{6,7},{7,6},{8,9},{9,8},{10,11... | collective-permute-start | bytes 786440 | tf_op jit(solution)/shard_map/ppermute | solution.py:219
  57.2 8.1 %collective-permute-start.15 = (bf16[4,128,256]{2,1,0:T(8,128)(2,1)S(1)}, bf16[4,128,256]{2,1,0:T(8,128)(2,1)S(1)}, u32[]{:S(2)}, u32[]{:S(2)}) collective-permute-start(bf16[4,128,256]{2,1,0:T(8,128)(2,1)S(1)} %slice_bitcast_fusion.1), channel_id=1, source_target_pairs={{0,1},{1,0},{2,3},{3,2},{4,5},{5,4},{6,7},{7,6},{8,9},{9,8},{10,11... | collective-permute-start | bytes 786440 | tf_op jit(solution)/shard_map/ppermute | solution.py:219
  57.3 7.1 %collective-permute-start.18 = (bf16[2,2,128,256]{3,2,1,0:T(8,128)(2,1)S(1)}, bf16[2,2,128,256]{3,2,1,0:T(8,128)(2,1)S(1)}, u32[]{:S(2)}, u32[]{:S(2)}) collective-permute-start(bf16[2,2,128,256]{3,2,1,0:T(8,128)(2,1)S(1)} %constant_dynamic-slice_fusion), channel_id=1, source_target_pairs={{0,4},{5,1},{4,8},{9,5},{8,12},{13,9},{12,14},{15,13},{14,10},{11,... | collective-permute-start | bytes 786440 | tf_op jit(solution)/shard_map/ppermute | solution.py:245
  62.8 2.6 %collective-permute-start.17 = (bf16[4,128,256]{2,1,0:T(8,128)(2,1)S(1)}, bf16[4,128,256]{2,1,0:T(8,128)(2,1)S(1)}, u32[]{:S(2)}, u32[]{:S(2)}) collective-permute-start(bf16[4,128,256]{2,1,0:T(8,128)(2,1)S(1)} %slice_bitcast_fusion), channel_id=1, source_target_pairs={{0,1},{1,0},{2,3},{3,2},{4,5},{5,4},{6,7},{7,6},{8,9},{9,8},{10,11... | collective-permute-start | bytes 786440 | tf_op jit(solution)/shard_map/ppermute | solution.py:219
  62.8 14.3 %collective-permute-start.20 = (bf16[4,256,256]{2,1,0:T(8,128)(2,1)S(1)}, bf16[4,256,256]{2,1,0:T(8,128)(2,1)S(1)}, u32[]{:S(2)}, u32[]{:S(2)}) collective-permute-start(bf16[4,256,256]{2,1,0:T(8,128)(2,1)S(1)} %get-tuple-element.28), channel_id=1, source_target_pairs={{0,16},{16,0},{1,17},{17,1},{2,18},{18,2},{3,19},{19,3},{4,20},{20... | collective-permute-start | bytes 1572872 | tf_op jit(solution)/shard_map/ppermute | solution.py:219
  64.4 1.4 %collective-permute-start.19 = (bf16[2,128,256]{2,1,0:T(8,128)(2,1)S(1)}, bf16[2,128,256]{2,1,0:T(8,128)(2,1)S(1)}, u32[]{:S(2)}, u32[]{:S(2)}) collective-permute-start(bf16[2,128,256]{2,1,0:T(8,128)(2,1)S(1)} %slice_bitcast_fusion.8), channel_id=1, source_target_pairs={{0,1},{1,0},{2,3},{3,2},{4,5},{5,4},{6,7},{7,6},{8,9},{9,8},{10,11... | collective-permute-start | bytes 393224 | tf_op jit(solution)/shard_map/ppermute | solution.py:219
  65.3 11.9 %copy-start = (f32[256]{0:T(256)S(1)}, f32[256]{0:T(256)}, u32[]{:S(2)}) copy-start(f32[256]{0:T(256)} %param.12) | copy-start | bytes 3076
  77.2 1.7 %copy-start.2 = (bf16[3,256,256]{2,1,0:T(8,128)(2,1)S(1)}, bf16[3,256,256]{2,1,0:T(8,128)(2,1)}, u32[]{:S(2)}) copy-start(bf16[3,256,256]{2,1,0:T(8,128)(2,1)} %res_mine_ref.1) | copy-start | bytes 1179652
  77.2 5.3 %copy-start.3 = (bf16[256,256]{1,0:T(8,128)(2,1)S(1)}, bf16[256,256]{1,0:T(8,128)(2,1)}, u32[]{:S(2)}) copy-start(bf16[256,256]{1,0:T(8,128)(2,1)} %skip_ref.1) | copy-start | bytes 393220
  77.2 5.3 %copy-start.4 = (f32[256]{0:T(256)S(1)}, f32[256]{0:T(256)}, u32[]{:S(2)}) copy-start(f32[256]{0:T(256)} %param.17) | copy-start | bytes 3076
  77.2 5.3 %copy-start.5 = (f32[256]{0:T(256)S(1)}, f32[256]{0:T(256)}, u32[]{:S(2)}) copy-start(f32[256]{0:T(256)} %param.19) | copy-start | bytes 3076
  78.9 3.6 %collective-permute-start.21 = (bf16[10,256,256]{2,1,0:T(8,128)(2,1)S(1)}, bf16[10,256,256]{2,1,0:T(8,128)(2,1)S(1)}, u32[]{:S(2)}, u32[]{:S(2)}) collective-permute-start(bf16[10,256,256]{2,1,0:T(8,128)(2,1)S(1)} %get-tuple-element.30.mine_ref), channel_id=1, source_target_pairs={{0,1},{1,0},{2,3},{3,2},{4,5},{5,4},{6,7},{7,6},{8,9},{9,8},{10,11... | collective-permute-start | bytes 3932168 | tf_op jit(solution)/shard_map/ppermute | solution.py:219
  78.9 3.6 %collective-permute-start.22 = (bf16[3,256,256]{2,1,0:T(8,128)(2,1)S(1)}, bf16[3,256,256]{2,1,0:T(8,128)(2,1)S(1)}, u32[]{:S(2)}, u32[]{:S(2)}) collective-permute-start(bf16[3,256,256]{2,1,0:T(8,128)(2,1)S(1)} %copy-done.2), channel_id=1, source_target_pairs={{0,1},{1,0},{2,3},{3,2},{4,5},{5,4},{6,7},{7,6},{8,9},{9,8},{10,11... | collective-permute-start | bytes 1179656 | tf_op jit(solution)/shard_map/ppermute | solution.py:219
  79.4 13.8 %collective-permute-start.23 = (bf16[4,256,256]{2,1,0:T(8,128)(2,1)S(1)}, bf16[4,256,256]{2,1,0:T(8,128)(2,1)S(1)}, u32[]{:S(2)}, u32[]{:S(2)}) collective-permute-start(bf16[4,256,256]{2,1,0:T(8,128)(2,1)S(1)} %get-tuple-element.25), channel_id=1, source_target_pairs={{0,16},{16,0},{1,17},{17,1},{2,18},{18,2},{3,19},{19,3},{4,20},{20... | collective-permute-start | bytes 1572872 | tf_op jit(solution)/shard_map/ppermute | solution.py:219
  82.5 1.6 %copy-start.1 = (f32[8,256,256]{2,1,0:T(8,128)S(1)}, f32[8,256,256]{2,1,0:T(8,128)}, u32[]{:S(2)}) copy-start(f32[8,256,256]{2,1,0:T(8,128)} %get-tuple-element.29.up_ref) | copy-start | bytes 6291460
where the time goes:
time: 95.8 us; the launch traced here: 95.3 us
  waiting for transfers between devices  36.3 us (38%)
  starting transfers between devices  33.9 us (35%)
  Pallas kernels  13.4 us (14%)
  local copies, waits for them, and re-layouts  8.94 us (9%)
  other arithmetic  1.22 us (1%)
  between operations  0.97 us (1%)
    ppermute x8, starting transfers between devices, round(): item = lax.ppermute(item, ('streams', 'segment'), self.pairs)  21.7 us
    ppermute x8, waiting for transfers between devices, round(): item = lax.ppermute(item, ('streams', 'segment'), self.pairs)  18.9 us
    ppermute x16, waiting for transfers between devices, swap(): return lax.ppermute(value, axis, [(0, 1), (1, 0)])  17.4 us
    ppermute x16, starting transfers between devices, swap(): return lax.ppermute(value, axis, [(0, 1), (1, 0)])  7.4 us
    pallas_call x2, Pallas kernels, spread_taps(): pl.pallas_call(functools.partial(spread_kernel, count, steps), out_shape=...  5.19 us
    all_to_all x1, starting transfers between devices, local(): lax.all_to_all(parcel, 'streams', split_axis=0, concat_axis=0, tiled=True)  4.79 us
    pallas_call x1, Pallas kernels, residual(): pl.pallas_call(residual_kernel, out_shape=jax.ShapeDtypeStruct((sessions...  4.44 us
    squeeze x8, local copies, waits for them, and re-layouts, round(): self.blocks += [item, swap(item[1], 'segment')]  2.25 us
  transfers between devices with their start and end apart: 25, of which 9 were waited for; matrix products, arithmetic and copies ran while one was open for 8% of the time, Pallas kernels for 10%

commit v1 on v0

--- a/solution.py
+++ b/solution.py
@@ -47,7 +47,7 @@
             stream = ring_stream(
                 lax.rem(place + (2 * taker - 1) * distance + count, count), count
             )
-            source = block if len(block.shape) == 3 else block.at[0]
+            source = block if len(block.shape) == 3 else block.at[passed]
             part = source.shape[0]
             first = 0 if part == taps else taker * part
             target = kernel_rows.at[
@@ -91,53 +91,53 @@
             pltpu.SemaphoreType.DMA((len(blocks),)),
         ],
         compiler_params=pltpu.CompilerParams(vmem_limit_bytes=VMEM_LIMIT),
-        cost_estimate=pl.CostEstimate(
-            flops=4 * taps * sessions * depth * width,
-            bytes_accessed=2 * taps * depth * width + 4 * sessions * depth + 6 * taps * sessions * width,
-            transcendentals=0,
-        ),
     )(*blocks, *sides)
 
 
-def excite_kernel(group_ref, own_ref, other_ref, prev_ref, bias_ref, up_ref, window_ref):
-    taps = own_ref.shape[0]
-    bias = bias_ref[...]
-    group = group_ref[0]
-    history = prev_ref.shape[0] - 2 * taps
+def upsampled(group, own_ref, other_ref, prev_ref, bias, step):
+    half, tap = divmod(step, own_ref.shape[0])
+    value = jnp.where(group == half, own_ref[tap], other_ref[tap].astype(F32))
+    return value + prev_ref[step].astype(F32) + bias
+
+
+def excite_kernel(group_ref, own_ref, other_ref, prev_ref, bias_ref, window_ref):
+    steps = 2 * own_ref.shape[0]
+    history = prev_ref.shape[0] - steps
     for step in range(history):
-        window_ref[step] = prev_ref[2 * taps + step]
-    for half in range(2):
-        for tap in range(taps):
-            value = jnp.where(group == half, own_ref[tap], other_ref[tap].astype(F32))
-            step = half * taps + tap
-            up = value + prev_ref[step].astype(F32) + bias
-            up_ref[step] = up
-            window_ref[history + step] = apply_elu(up).astype(BF16)
+        window_ref[step] = prev_ref[steps + step]
+    for step in range(steps):
+        up = upsampled(group_ref[0], own_ref, other_ref, prev_ref, bias_ref[...], step)
+        window_ref[history + step] = apply_elu(up).astype(BF16)
 
 
 def excite(group, own, other, prev, bias):
-    taps, sessions, width = own.shape
     return pl.pallas_call(
         excite_kernel,
-        out_shape=(
-            jax.ShapeDtypeStruct((2 * taps, sessions, width), F32),
-            jax.ShapeDtypeStruct((prev.shape[0], sessions, width), BF16),
-        ),
+        out_shape=jax.ShapeDtypeStruct(prev.shape, BF16),
         in_specs=[pl.BlockSpec(memory_space=pltpu.SMEM), VMEM, VMEM, VMEM, VMEM],
-        out_specs=(VMEM, VMEM),
+        out_specs=VMEM,
         compiler_params=pltpu.CompilerParams(vmem_limit_bytes=VMEM_LIMIT),
-        cost_estimate=pl.CostEstimate(
-            flops=20 * taps * sessions * width,
-            bytes_accessed=40 * taps * sessions * width,
-            transcendentals=2 * taps * sessions * width,
-        ),
     )(group, own, other, prev, bias)
 
 
 def residual_kernel(
-    up_ref, mine_ref, theirs_ref, res_mine_ref, res_theirs_ref, res_bias_ref, skip_ref, skip_bias_ref, out_ref, frames
+    group_ref,
+    own_ref,
+    other_ref,
+    prev_ref,
+    mine_ref,
+    theirs_ref,
+    bias_ref,
+    res_mine_ref,
+    res_theirs_ref,
+    res_bias_ref,
+    skip_ref,
+    skip_bias_ref,
+    out_ref,
+    frames,
 ):
-    steps, block, width = up_ref.shape
+    taps, block, width = own_ref.shape
+    steps = 2 * taps
     branch = None
     for source, weights in ((mine_ref, res_mine_ref), (theirs_ref, res_theirs_ref)):
         for offset in range(weights.shape[0]):
@@ -149,35 +149,36 @@
             branch = term if branch is None else branch + term
     hidden = apply_elu(branch + res_bias_ref[...]).astype(BF16)
     projected = jnp.dot(hidden, skip_ref[...], preferred_element_type=F32)
-    mixed = up_ref[...] + projected.reshape(steps, block, width) + skip_bias_ref[...]
     for step in range(steps):
+        up = upsampled(group_ref[0], own_ref, other_ref, prev_ref, bias_ref[...], step)
+        mixed = up + projected[step * block : (step + 1) * block] + skip_bias_ref[...]
         for part in range(width // 128):
             frames.at[part][pl.ds(step, block, stride=steps), :] = mixed[
-                step, :, part * 128 : (part + 1) * 128
+                :, part * 128 : (part + 1) * 128
             ]
     for part in range(width // 128):
         out_ref[:, part * 128 : (part + 1) * 128] = frames[part].astype(BF16)
 
 
-def residual(up, mine, theirs, res_mine, res_theirs, res_bias, skip_weight, skip_bias):
-    steps, sessions, width = up.shape
-    window, block = mine.shape[0], sessions // 4
-    frames = pl.BlockSpec((window, block, width), lambda i: (0, i, 0))
+def residual(group, own, other, prev, mine, theirs, *parameters):
+    taps, sessions, width = own.shape
+    steps, block = 2 * taps, sessions // 4
+
+    def blocks(array):
+        return pl.BlockSpec((array.shape[0], block, width), lambda i: (0, i, 0))
+
+    arrays = (own, other, prev, mine, theirs)
     return pl.pallas_call(
         residual_kernel,
         out_shape=jax.ShapeDtypeStruct((sessions * steps, width), BF16),
         grid=(4,),
-        in_specs=[pl.BlockSpec((steps, block, width), lambda i: (0, i, 0)), frames, frames]
-        + [VMEM] * 5,
+        in_specs=[pl.BlockSpec(memory_space=pltpu.SMEM)]
+        + [blocks(array) for array in arrays]
+        + [VMEM] * len(parameters),
         out_specs=pl.BlockSpec((block * steps, width), lambda i: (i, 0)),
         scratch_shapes=[pltpu.VMEM((width // 128, block * steps, 128), F32)],
         compiler_params=pltpu.CompilerParams(vmem_limit_bytes=VMEM_LIMIT),
-        cost_estimate=pl.CostEstimate(
-            flops=2 * up.size * (2 * res_mine.shape[0] + 1) * res_mine.shape[2],
-            bytes_accessed=12 * up.size,
-            transcendentals=up.size,
-        ),
-    )(up, mine, theirs, res_mine, res_theirs, res_bias, skip_weight, skip_bias)
+    )(group, *arrays, *parameters)
 
 
 def weave_kernel(group_ref, own_ref, other_ref, out_ref, frames):
@@ -209,9 +210,6 @@
         out_specs=pl.BlockSpec((block * steps, width), lambda i: (i, 0)),
         scratch_shapes=[pltpu.VMEM((width // 128, block * steps, 128), F32)],
         compiler_params=pltpu.CompilerParams(vmem_limit_bytes=VMEM_LIMIT),
-        cost_estimate=pl.CostEstimate(
-            flops=0, bytes_accessed=4 * sessions * steps * width, transcendentals=0
-        ),
     )(group, own, other)
 
 
@@ -244,7 +242,7 @@
             item = after(item, earlier)
         item = lax.ppermute(item, ("streams", "segment"), self.pairs)
         self.item = item
-        self.blocks += [item, swap(item[1], "segment")]
+        self.blocks += [item, swap(item, "segment")]
         self.steps += [(self.rounds, 0), (self.rounds, 1)]
         return item
 
@@ -279,14 +277,13 @@
         other = swap(own, "segment")
         rings = [Ring(count, own[a:b], other[a:b]) for a, b in cuts]
         up_ring, tail_ring = rings
-        first_done = up_ring.round()
-        behind = None
-        for _ in range(2, count // 2 + 1):
-            ahead = up_ring.round(behind)
-            behind = tail_ring.round(behind_of_ahead) if tail_ring.rounds else tail_ring.round()
-            behind_of_ahead = ahead
-        nearly_done = behind
-        tail_ring.round(behind_of_ahead)
+        up_seen, tail_seen = [], []
+        for _ in range(count // 2):
+            up_seen.append(up_ring.round())
+            tail_seen.append(tail_ring.round())
+        first_done = up_seen[0]
+        up_ring.blocks[0] = after(up_ring.blocks[0], tail_seen[-2])
+        nearly_done = tail_seen[-1]
         gathered = [(ring.blocks, ring.steps) for ring in rings]
     else:
         gathered = [
@@ -325,11 +322,23 @@
     own_tail, away_tail = spread_taps(sides, *gathered[1], count, BF16)
     other_tail = swap(away_tail, "groups")
 
-    own_up = after(own_up, away_tail)
-    up, mine = excite(group_word, own_up, other_up, prev, conv_bias[None])
+    own_up = after(own_up, (away_tail, res_theirs))
+    bias = conv_bias[None]
+    mine = excite(group_word, own_up, other_up, prev, bias)
     theirs = swap(mine, "segment")
     decoded = residual(
-        up, mine, theirs, res_weight, res_theirs, res_bias[None], skip_weight, skip_bias[None]
+        group_word,
+        own_up,
+        other_up,
+        prev,
+        mine,
+        theirs,
+        bias,
+        res_weight,
+        res_theirs,
+        res_bias[None],
+        skip_weight,
+        skip_bias[None],
     )
     decoded, other_tail = lax.optimization_barrier((decoded, other_tail))
     new_tail = weave(group_word, own_tail, other_tail)

time: 95.8 us -> 90.5 us (0.945)
  local copies, waits for them, and re-layouts: 8.94 us -> 2.96 us
  Pallas kernels: 13.4 us -> 14.7 us
  waiting for transfers between devices: 36.3 us -> 35.2 us
    ppermute x8, waiting for transfers between devices: 18.9 us -> 15.7 us  [round(): item = lax.ppermute(item, ('streams', 'segment'), self.pairs)]
    squeeze x8 -> x0, local copies, waits for them, and re-layouts: 2.25 us -> none  [round(): self.blocks += [item, swap(item[1], 'segment')]]
    ppermute x16, waiting for transfers between devices: 17.4 us -> 19.5 us  [swap(): return lax.ppermute(value, axis, [(0, 1), (1, 0)])]
    pallas_call x2, Pallas kernels: 5.19 us -> 6.32 us  [spread_taps(): pl.pallas_call(functools.partial(spread_kernel, count, steps), out_shape=...]
    pallas_call x1, Pallas kernels: 4.44 us -> 5.54 us  [residual(): pl.pallas_call(residual_kernel, out_shape=jax.ShapeDtypeStruct((sessions...]
  transfers between devices with their start and end apart: 25 -> 25, of which waited for: 9 -> 11; matrix products, arithmetic and copies ran while one was open for 8% -> 2% of each run, Pallas kernels for 10% -> 13%
where the time goes in v1:
time: 90.5 us; the launch traced here: 90.2 us
  waiting for transfers between devices  35.2 us (39%)
  starting transfers between devices  34.5 us (38%)
  Pallas kernels  14.7 us (16%)
  local copies, waits for them, and re-layouts  2.96 us (3%)
  other arithmetic  1.22 us (1%)
  between operations  0.94 us (1%)
    ppermute x8, starting transfers between devices, round(): item = lax.ppermute(item, ('streams', 'segment'), self.pairs)  22.3 us
    ppermute x16, waiting for transfers between devices, swap(): return lax.ppermute(value, axis, [(0, 1), (1, 0)])  19.5 us
    ppermute x8, waiting for transfers between devices, round(): item = lax.ppermute(item, ('streams', 'segment'), self.pairs)  15.7 us
    ppermute x16, starting transfers between devices, swap(): return lax.ppermute(value, axis, [(0, 1), (1, 0)])  7.45 us
    pallas_call x2, Pallas kernels, spread_taps(): pl.pallas_call(functools.partial(spread_kernel, count, steps), out_shape=...  6.32 us
    pallas_call x1, Pallas kernels, residual(): pl.pallas_call(residual_kernel, out_shape=jax.ShapeDtypeStruct((sessions...  5.54 us
    all_to_all x1, starting transfers between devices, local(): lax.all_to_all(parcel, 'streams', split_axis=0, concat_axis=0, tiled=True)  4.79 us
    pallas_call x1, Pallas kernels, weave(): pl.pallas_call(weave_kernel, out_shape=jax.ShapeDtypeStruct((sessions * s...  2.03 us
  transfers between devices with their start and end apart: 25, of which 11 were waited for; matrix products, arithmetic and copies ran while one was open for 2% of the time, Pallas kernels for 13%

profile of v1, /device:TPU:0, one launch (start us, length us, event | category | flops | bytes accessed | tf_op | source)
XLA Modules:
  0.0 90.2 jit_solution(12837825103165949685)
XLA Ops:
  0.6 1.5 %constant_dynamic-slice_fusion.2 = (bf16[128,4,256]{2,1,0:T(4,128)(2,1)S(1)}, bf16[128,4,256]{2,1,0:T(4,128)(2,1)S(1)}) fusion(bf16[128,16,256]{2,1,0:T(8,128)(2,1)} %param.11, s32[]{:T(128)S(6)} %select_n.15, s32[]{:T(128)S(6)} %select_n.14), kind=kLoop, calls=%fused_computation.27 | loop fusion | bytes 1048584 | tf_op jit(solution)/shard_map/dynamic_slice | solution.py:271
  2.1 0.1 copy_bitcast_fusion
  2.3 0.5 collective-permute-start
  2.8 1.5 %collective-permute-done = bf16[8,128,256]{2,1,0:T(8,128)(2,1)S(1)} collective-permute-done((bf16[8,128,256]{2,1,0:T(8,128)(2,1)S(1)}, bf16[8,128,256]{2,1,0:T(8,128)(2,1)S(1)}, u32[]{:S(2)}, u32[]{:S(2)}) %collective-permute-start) | collective-permute-done | bytes 524320 | tf_op jit(solution)/shard_map/ppermute | solution.py:217
  4.4 0.0 copy-start.7
  4.4 0.0 copy-start.8
  4.4 0.1 pad_maximum_fusion.2
  4.5 3.0 %collective-permute-start.4 = (bf16[2,4,128,256]{3,2,1,0:T(8,128)(2,1)S(1)}, bf16[2,4,128,256]{3,2,1,0:T(8,128)(2,1)}, u32[]{:S(2)}, u32[]{:S(2)}) collective-permute-start(bf16[2,4,128,256]{3,2,1,0:T(8,128)(2,1)S(1)} %pad_maximum_fusion.2), channel_id=1, source_target_pairs={{0,4},{5,1},{4,8},{9,5},{8,12},{13,9},{12,14},{15,13},{14,10},{11,... | collective-permute-start | bytes 1572872 | tf_op jit(solution)/shard_map/ppermute | solution.py:243
  7.5 0.1 pad_maximum_fusion.1
  7.6 1.6 %collective-permute-start.1 = (bf16[2,4,128,256]{3,2,1,0:T(8,128)(2,1)S(1)}, bf16[2,4,128,256]{3,2,1,0:T(8,128)(2,1)S(1)}, u32[]{:S(2)}, u32[]{:S(2)}) collective-permute-start(bf16[2,4,128,256]{3,2,1,0:T(8,128)(2,1)S(1)} %pad_maximum_fusion.1), channel_id=1, source_target_pairs={{0,4},{5,1},{4,8},{9,5},{8,12},{13,9},{12,14},{15,13},{14,10},{11,... | collective-permute-start | bytes 1572872 | tf_op jit(solution)/shard_map/ppermute | solution.py:243
  9.2 5.5 %collective-permute-done.4.refs_1_ = bf16[2,4,128,256]{3,2,1,0:T(8,128)(2,1)} collective-permute-done((bf16[2,4,128,256]{3,2,1,0:T(8,128)(2,1)S(1)}, bf16[2,4,128,256]{3,2,1,0:T(8,128)(2,1)}, u32[]{:S(2)}, u32[]{:S(2)}) %collective-permute-start.4) | collective-permute-done | bytes 524320 | tf_op jit(solution)/shard_map/ppermute | solution.py:243
  14.7 2.1 %collective-permute-start.6 = (bf16[2,4,128,256]{3,2,1,0:T(8,128)(2,1)}, bf16[2,4,128,256]{3,2,1,0:T(8,128)(2,1)}, u32[]{:S(2)}, u32[]{:S(2)}) collective-permute-start(bf16[2,4,128,256]{3,2,1,0:T(8,128)(2,1)} %collective-permute-done.4.refs_1_), channel_id=1, source_target_pairs={{0,4},{5,1},{4,8},{9,5},{8,12},{13,9},{12,14},{15,13},{14,10},{11,... | collective-permute-start | bytes 1572872 | tf_op jit(solution)/shard_map/ppermute | solution.py:243
  16.8 0.1 broadcast_in_dim.23
  16.9 0.8 maximum_maximum_fusion
  17.7 4.8 %all-to-all-start = ((bf16[8,40,512]{2,1,0:T(8,128)(2,1)}), bf16[8,40,512]{2,1,0:T(8,128)(2,1)S(1)}, u32[]{:S(2)}, u32[]{:S(2)}) async-start(bf16[8,40,512]{2,1,0:T(8,128)(2,1)} %maximum_maximum_fusion), calls=%async_computation | async-start | bytes 655360 | tf_op jit(solution)/shard_map/all_to_all | solution.py:305
  22.5 2.0 %collective-permute-start.2 = (bf16[2,4,128,256]{3,2,1,0:T(8,128)(2,1)S(1)}, bf16[2,4,128,256]{3,2,1,0:T(8,128)(2,1)S(1)}, u32[]{:S(2)}, u32[]{:S(2)}) collective-permute-start(bf16[2,4,128,256]{3,2,1,0:T(8,128)(2,1)S(1)} %collective-permute-done.1.refs_1_), channel_id=1, source_target_pairs={{0,4},{5,1},{4,8},{9,5},{8,12},{13,9},{12,14},{15,13},{14,10},{11,... | collective-permute-start | bytes 1572872 | tf_op jit(solution)/shard_map/ppermute | solution.py:243
  24.5 3.7 %collective-permute-done.6.refs_3_ = bf16[2,4,128,256]{3,2,1,0:T(8,128)(2,1)} collective-permute-done((bf16[2,4,128,256]{3,2,1,0:T(8,128)(2,1)}, bf16[2,4,128,256]{3,2,1,0:T(8,128)(2,1)}, u32[]{:S(2)}, u32[]{:S(2)}) %collective-permute-start.6) | collective-permute-done | bytes 524320 | tf_op jit(solution)/shard_map/ppermute | solution.py:243
  28.2 3.4 %collective-permute-start.8 = (bf16[2,4,128,256]{3,2,1,0:T(8,128)(2,1)}, bf16[2,4,128,256]{3,2,1,0:T(8,128)(2,1)S(1)}, u32[]{:S(2)}, u32[]{:S(2)}) collective-permute-start(bf16[2,4,128,256]{3,2,1,0:T(8,128)(2,1)} %collective-permute-done.6.refs_3_), channel_id=1, source_target_pairs={{0,4},{5,1},{4,8},{9,5},{8,12},{13,9},{12,14},{15,13},{14,10},{11,... | collective-permute-start | bytes 1572872 | tf_op jit(solution)/shard_map/ppermute | solution.py:243
  31.5 4.8 %collective-permute-done.2.refs_3_ = bf16[2,4,128,256]{3,2,1,0:T(8,128)(2,1)S(1)} collective-permute-done((bf16[2,4,128,256]{3,2,1,0:T(8,128)(2,1)S(1)}, bf16[2,4,128,256]{3,2,1,0:T(8,128)(2,1)S(1)}, u32[]{:S(2)}, u32[]{:S(2)}) %collective-permute-start.2) | collective-permute-done | bytes 524320 | tf_op jit(solution)/shard_map/ppermute | solution.py:243
  36.3 3.3 %collective-permute-start.3 = (bf16[2,4,128,256]{3,2,1,0:T(8,128)(2,1)S(1)}, bf16[2,4,128,256]{3,2,1,0:T(8,128)(2,1)S(1)}, u32[]{:S(2)}, u32[]{:S(2)}) collective-permute-start(bf16[2,4,128,256]{3,2,1,0:T(8,128)(2,1)S(1)} %collective-permute-done.2.refs_3_), channel_id=1, source_target_pairs={{0,4},{5,1},{4,8},{9,5},{8,12},{13,9},{12,14},{15,13},{14,10},{11,... | collective-permute-start | bytes 1572872 | tf_op jit(solution)/shard_map/ppermute | solution.py:243
  39.7 0.1 fusion.3.refs_9_
  39.8 0.1 collective-permute-start.12
  39.9 0.5 collective-permute-start.7
  40.4 1.6 %collective-permute-done.8.refs_5_ = bf16[2,4,128,256]{3,2,1,0:T(8,128)(2,1)S(1)} collective-permute-done((bf16[2,4,128,256]{3,2,1,0:T(8,128)(2,1)}, bf16[2,4,128,256]{3,2,1,0:T(8,128)(2,1)S(1)}, u32[]{:S(2)}, u32[]{:S(2)}) %collective-permute-start.8) | collective-permute-done | bytes 524320 | tf_op jit(solution)/shard_map/ppermute | solution.py:243
  42.0 1.5 %collective-permute-start.13 = (bf16[256,512]{1,0:T(8,128)(2,1)S(1)}, bf16[256,512]{1,0:T(8,128)(2,1)S(1)}, u32[]{:S(2)}, u32[]{:S(2)}) collective-permute-start(bf16[256,512]{1,0:T(8,128)(2,1)S(1)} %fusion.3.refs_9_), channel_id=1, source_target_pairs={{0,16},{16,0},{1,17},{17,1},{2,18},{18,2},{3,19},{19,3},{4,20},{20... | collective-permute-start | bytes 786440 | tf_op jit(solution)/shard_map/ppermute | solution.py:217
  43.6 3.4 %collective-permute-start.10 = (bf16[2,2,128,256]{3,2,1,0:T(8,128)(2,1)S(1)}, bf16[2,2,128,256]{3,2,1,0:T(8,128)(2,1)S(1)}, u32[]{:S(2)}, u32[]{:S(2)}) collective-permute-start(bf16[2,2,128,256]{3,2,1,0:T(8,128)(2,1)S(1)} %constant_dynamic-slice_fusion.1), channel_id=1, source_target_pairs={{0,4},{5,1},{4,8},{9,5},{8,12},{13,9},{12,14},{15,13},{14,10},{11,... | collective-permute-start | bytes 786440 | tf_op jit(solution)/shard_map/ppermute | solution.py:243
  47.0 3.2 %collective-permute-done.13.refs_11_ = bf16[256,512]{1,0:T(8,128)(2,1)S(1)} collective-permute-done((bf16[256,512]{1,0:T(8,128)(2,1)S(1)}, bf16[256,512]{1,0:T(8,128)(2,1)S(1)}, u32[]{:S(2)}, u32[]{:S(2)}) %collective-permute-start.13) | collective-permute-done | bytes 262176 | tf_op jit(solution)/shard_map/ppermute | solution.py:217
  50.2 0.5 collective-permute-start.14
  50.7 0.2 collective-permute-done.10.refs_7_
  50.9 3.4 %collective-permute-start.18 = (bf16[2,2,128,256]{3,2,1,0:T(8,128)(2,1)S(1)}, bf16[2,2,128,256]{3,2,1,0:T(8,128)(2,1)S(1)}, u32[]{:S(2)}, u32[]{:S(2)}) collective-permute-start(bf16[2,2,128,256]{3,2,1,0:T(8,128)(2,1)S(1)} %constant_dynamic-slice_fusion), channel_id=1, source_target_pairs={{0,4},{5,1},{4,8},{9,5},{8,12},{13,9},{12,14},{15,13},{14,10},{11,... | collective-permute-start | bytes 786440 | tf_op jit(solution)/shard_map/ppermute | solution.py:243
  54.4 0.5 collective-permute-start.17
  54.9 4.0 %shard_map.113 = (f32[4,256,256]{2,1,0:T(8,128)}, bf16[4,256,256]{2,1,0:T(8,128)(2,1)S(1)}) custom-call(bf16[4,128,256]{2,1,0:T(8,128)(2,1)S(1)} %get-tuple-element.12.refs_0_, bf16[2,4,128,256]{3,2,1,0:T(8,128)(2,1)} %collective-permute-done.4.refs_1_, bf16[2,4,128,256]{3,2,1,0:T(8,128)(2,1)} %collective-permute-done.5.refs_2_, ...), custom_call_target="tpu_custom_call" | custom-call | tf_op jit(solution)/shard_map/pallas_call | solution.py:80
  58.9 1.6 %collective-permute-start.21 = (bf16[4,256,256]{2,1,0:T(8,128)(2,1)S(1)}, bf16[4,256,256]{2,1,0:T(8,128)(2,1)S(1)}, u32[]{:S(2)}, u32[]{:S(2)}) collective-permute-start(bf16[4,256,256]{2,1,0:T(8,128)(2,1)S(1)} %get-tuple-element.18), channel_id=1, source_target_pairs={{0,16},{16,0},{1,17},{17,1},{2,18},{18,2},{3,19},{19,3},{4,20},{20... | collective-permute-start | bytes 1572872 | tf_op jit(solution)/shard_map/ppermute | solution.py:217
  60.6 0.6 collective-permute-start.19
  61.1 0.1 convert_reduce_fusion
  61.3 0.6 fusion.prev_ref
  61.9 0.7 collective-permute-done.19.refs_8_
  62.6 2.3 %shard_map.114 = (bf16[4,256,256]{2,1,0:T(8,128)(2,1)S(1)}, bf16[4,256,256]{2,1,0:T(8,128)(2,1)S(1)}) custom-call(bf16[4,128,256]{2,1,0:T(8,128)(2,1)S(1)} %get-tuple-element.29.refs_0_, bf16[2,4,128,256]{3,2,1,0:T(8,128)(2,1)S(1)} %collective-permute-done.1.refs_1_, bf16[2,4,128,256]{3,2,1,0:T(8,128)(2,1)S(1)} %collective-permute-done.15.refs_2_, ...), custom_call_target="tpu_custom_call" | custom-call | tf_op jit(solution)/shard_map/pallas_call | solution.py:80
  64.9 8.0 %collective-permute-done.21.other_ref = bf16[4,256,256]{2,1,0:T(8,128)(2,1)S(1)} collective-permute-done((bf16[4,256,256]{2,1,0:T(8,128)(2,1)S(1)}, bf16[4,256,256]{2,1,0:T(8,128)(2,1)S(1)}, u32[]{:S(2)}, u32[]{:S(2)}) %collective-permute-start.21) | collective-permute-done | bytes 524320 | tf_op jit(solution)/shard_map/ppermute | solution.py:217
  72.9 0.0 copy-start.5
  72.9 0.8 shard_map.115.mine_ref
  73.7 0.1 collective-permute-start.22
  73.8 1.6 %collective-permute-start.23 = (bf16[4,256,256]{2,1,0:T(8,128)(2,1)S(1)}, bf16[4,256,256]{2,1,0:T(8,128)(2,1)S(1)}, u32[]{:S(2)}, u32[]{:S(2)}) collective-permute-start(bf16[4,256,256]{2,1,0:T(8,128)(2,1)S(1)} %get-tuple-element.15), channel_id=1, source_target_pairs={{0,16},{16,0},{1,17},{17,1},{2,18},{18,2},{3,19},{19,3},{4,20},{20... | collective-permute-start | bytes 1572872 | tf_op jit(solution)/shard_map/ppermute | solution.py:217
  75.4 1.4 %collective-permute-done.22.theirs_ref = bf16[10,256,256]{2,1,0:T(8,128)(2,1)S(1)} collective-permute-done((bf16[10,256,256]{2,1,0:T(8,128)(2,1)S(1)}, bf16[10,256,256]{2,1,0:T(8,128)(2,1)S(1)}, u32[]{:S(2)}, u32[]{:S(2)}) %collective-permute-start.22) | collective-permute-done | bytes 1310752 | tf_op jit(solution)/shard_map/ppermute | solution.py:217
  76.8 1.1 %copy-done.6 = bf16[10,256,256]{2,1,0:T(8,128)(2,1)} copy-done((bf16[10,256,256]{2,1,0:T(8,128)(2,1)}, bf16[10,256,256]{2,1,0:T(8,128)(2,1)S(1)}, u32[]{:S(2)}) %copy-start.6) | copy-done | bytes 1310744
  77.9 5.5 %shard_map.116 = bf16[2048,256]{1,0:T(8,128)(2,1)} custom-call(s32[1]{0:T(128)} %bitcast.group_ref, f32[4,256,256]{2,1,0:T(8,128)S(1)} %copy-done, bf16[4,256,256]{2,1,0:T(8,128)(2,1)S(1)} %collective-permute-done.21.other_ref, bf16[10,256,256]{2,1,0:T(8,128)(2,1)S(1)} %fusion.prev_ref, bf16[10,256,256]{2,1,0:T(8,128)(2,1)S(1)} %shard_map.115.mine_ref, ...), custom_call_target="tpu_custom_call" | custom-call | tf_op jit(solution)/shard_map/pallas_call | solution.py:171
  83.5 4.7 %collective-permute-done.23.other_ref = bf16[4,256,256]{2,1,0:T(8,128)(2,1)S(1)} collective-permute-done((bf16[4,256,256]{2,1,0:T(8,128)(2,1)S(1)}, bf16[4,256,256]{2,1,0:T(8,128)(2,1)S(1)}, u32[]{:S(2)}, u32[]{:S(2)}) %collective-permute-start.23) | collective-permute-done | bytes 524320 | tf_op jit(solution)/shard_map/ppermute | solution.py:217
  88.1 2.0 %shard_map.117 = bf16[2048,256]{1,0:T(8,128)(2,1)} custom-call(s32[1]{0:T(128)} %bitcast.group_ref, bf16[4,256,256]{2,1,0:T(8,128)(2,1)S(1)} %get-tuple-element.20.own_ref, bf16[4,256,256]{2,1,0:T(8,128)(2,1)S(1)} %collective-permute-done.23.other_ref), custom_call_target="tpu_custom_call" | custom-call | tf_op jit(solution)/shard_map/pallas_call | solution.py:205
  (52 shorter events, 0.3 us)
Async XLA Ops:
  2.3 2.1 %collective-permute-start = (bf16[8,128,256]{2,1,0:T(8,128)(2,1)S(1)}, bf16[8,128,256]{2,1,0:T(8,128)(2,1)S(1)}, u32[]{:S(2)}, u32[]{:S(2)}) collective-permute-start(bf16[8,128,256]{2,1,0:T(8,128)(2,1)S(1)} %pad_maximum_fusion), channel_id=1, source_target_pairs={{0,1},{1,0},{2,3},{3,2},{4,5},{5,4},{6,7},{7,6},{8,9},{9,8},{10,11... | collective-permute-start | bytes 1572872 | tf_op jit(solution)/shard_map/ppermute | solution.py:217
  4.4 4.8 %copy-start.10 = (s32[8]{0:T(128)S(1)}, s32[8]{0:T(128)}, u32[]{:S(2)}) copy-start(s32[8]{0:T(128)} %param.15) | copy-start | bytes 100
  4.4 12.5 %copy-start.7 = (bf16[256,512]{1,0:T(8,128)(2,1)S(1)}, bf16[256,512]{1,0:T(8,128)(2,1)}, u32[]{:S(2)}) copy-start(bf16[256,512]{1,0:T(8,128)(2,1)} %param.10) | copy-start | bytes 786436
  4.4 12.4 %copy-start.8 = (bf16[8,8,256]{2,1,0:T(8,128)(2,1)S(1)}, bf16[8,8,256]{2,1,0:T(8,128)(2,1)}, u32[]{:S(2)}) copy-start(bf16[8,8,256]{2,1,0:T(8,128)(2,1)} %param.13) | copy-start | bytes 98308
  4.4 12.4 %copy-start.9 = (bf16[8,2,256]{2,1,0:T(2,128)(2,1)S(1)}, bf16[8,2,256]{2,1,0:T(2,128)(2,1)}, u32[]{:S(2)}) copy-start(bf16[8,2,256]{2,1,0:T(2,128)(2,1)} %param.14) | copy-start | bytes 24580
  4.5 10.2 %collective-permute-start.4 = (bf16[2,4,128,256]{3,2,1,0:T(8,128)(2,1)S(1)}, bf16[2,4,128,256]{3,2,1,0:T(8,128)(2,1)}, u32[]{:S(2)}, u32[]{:S(2)}) collective-permute-start(bf16[2,4,128,256]{3,2,1,0:T(8,128)(2,1)S(1)} %pad_maximum_fusion.2), channel_id=1, source_target_pairs={{0,4},{5,1},{4,8},{9,5},{8,12},{13,9},{12,14},{15,13},{14,10},{11,... | collective-permute-start | bytes 1572872 | tf_op jit(solution)/shard_map/ppermute | solution.py:243
  7.6 14.9 %collective-permute-start.1 = (bf16[2,4,128,256]{3,2,1,0:T(8,128)(2,1)S(1)}, bf16[2,4,128,256]{3,2,1,0:T(8,128)(2,1)S(1)}, u32[]{:S(2)}, u32[]{:S(2)}) collective-permute-start(bf16[2,4,128,256]{3,2,1,0:T(8,128)(2,1)S(1)} %pad_maximum_fusion.1), channel_id=1, source_target_pairs={{0,4},{5,1},{4,8},{9,5},{8,12},{13,9},{12,14},{15,13},{14,10},{11,... | collective-permute-start | bytes 1572872 | tf_op jit(solution)/shard_map/ppermute | solution.py:243
  14.7 13.5 %collective-permute-start.6 = (bf16[2,4,128,256]{3,2,1,0:T(8,128)(2,1)}, bf16[2,4,128,256]{3,2,1,0:T(8,128)(2,1)}, u32[]{:S(2)}, u32[]{:S(2)}) collective-permute-start(bf16[2,4,128,256]{3,2,1,0:T(8,128)(2,1)} %collective-permute-done.4.refs_1_), channel_id=1, source_target_pairs={{0,4},{5,1},{4,8},{9,5},{8,12},{13,9},{12,14},{15,13},{14,10},{11,... | collective-permute-start | bytes 1572872 | tf_op jit(solution)/shard_map/ppermute | solution.py:243
  17.7 22.0 %all-to-all-start = ((bf16[8,40,512]{2,1,0:T(8,128)(2,1)}), bf16[8,40,512]{2,1,0:T(8,128)(2,1)S(1)}, u32[]{:S(2)}, u32[]{:S(2)}) async-start(bf16[8,40,512]{2,1,0:T(8,128)(2,1)} %maximum_maximum_fusion), calls=%async_computation | async-start | bytes 655360 | tf_op jit(solution)/shard_map/all_to_all | solution.py:305
  22.5 13.8 %collective-permute-start.2 = (bf16[2,4,128,256]{3,2,1,0:T(8,128)(2,1)S(1)}, bf16[2,4,128,256]{3,2,1,0:T(8,128)(2,1)S(1)}, u32[]{:S(2)}, u32[]{:S(2)}) collective-permute-start(bf16[2,4,128,256]{3,2,1,0:T(8,128)(2,1)S(1)} %collective-permute-done.1.refs_1_), channel_id=1, source_target_pairs={{0,4},{5,1},{4,8},{9,5},{8,12},{13,9},{12,14},{15,13},{14,10},{11,... | collective-permute-start | bytes 1572872 | tf_op jit(solution)/shard_map/ppermute | solution.py:243
  28.2 13.9 %collective-permute-start.8 = (bf16[2,4,128,256]{3,2,1,0:T(8,128)(2,1)}, bf16[2,4,128,256]{3,2,1,0:T(8,128)(2,1)S(1)}, u32[]{:S(2)}, u32[]{:S(2)}) collective-permute-start(bf16[2,4,128,256]{3,2,1,0:T(8,128)(2,1)} %collective-permute-done.6.refs_3_), channel_id=1, source_target_pairs={{0,4},{5,1},{4,8},{9,5},{8,12},{13,9},{12,14},{15,13},{14,10},{11,... | collective-permute-start | bytes 1572872 | tf_op jit(solution)/shard_map/ppermute | solution.py:243
  31.5 12.0 %collective-permute-start.5 = (bf16[2,4,128,256]{3,2,1,0:T(8,128)(2,1)}, bf16[2,4,128,256]{3,2,1,0:T(8,128)(2,1)}, u32[]{:S(2)}, u32[]{:S(2)}) collective-permute-start(bf16[2,4,128,256]{3,2,1,0:T(8,128)(2,1)} %collective-permute-done.4.refs_1_), channel_id=1, source_target_pairs={{0,1},{1,0},{2,3},{3,2},{4,5},{5,4},{6,7},{7,6},{8,9},{9,8},{10,11... | collective-permute-start | bytes 1572872 | tf_op jit(solution)/shard_map/ppermute | solution.py:217
  36.3 13.9 %collective-permute-start.3 = (bf16[2,4,128,256]{3,2,1,0:T(8,128)(2,1)S(1)}, bf16[2,4,128,256]{3,2,1,0:T(8,128)(2,1)S(1)}, u32[]{:S(2)}, u32[]{:S(2)}) collective-permute-start(bf16[2,4,128,256]{3,2,1,0:T(8,128)(2,1)S(1)} %collective-permute-done.2.refs_3_), channel_id=1, source_target_pairs={{0,4},{5,1},{4,8},{9,5},{8,12},{13,9},{12,14},{15,13},{14,10},{11,... | collective-permute-start | bytes 1572872 | tf_op jit(solution)/shard_map/ppermute | solution.py:243
  39.8 7.1 %collective-permute-start.12 = (bf16[256,512]{1,0:T(8,128)(2,1)S(1)}, bf16[256,512]{1,0:T(8,128)(2,1)S(1)}, u32[]{:S(2)}, u32[]{:S(2)}) collective-permute-start(bf16[256,512]{1,0:T(8,128)(2,1)S(1)} %fusion.3.refs_9_), channel_id=1, source_target_pairs={{0,1},{1,0},{2,3},{3,2},{4,5},{5,4},{6,7},{7,6},{8,9},{9,8},{10,11... | collective-permute-start | bytes 786440 | tf_op jit(solution)/shard_map/ppermute | solution.py:217
  39.9 11.0 %collective-permute-start.7 = (bf16[2,4,128,256]{3,2,1,0:T(8,128)(2,1)}, bf16[2,4,128,256]{3,2,1,0:T(8,128)(2,1)}, u32[]{:S(2)}, u32[]{:S(2)}) collective-permute-start(bf16[2,4,128,256]{3,2,1,0:T(8,128)(2,1)} %collective-permute-done.6.refs_3_), channel_id=1, source_target_pairs={{0,1},{1,0},{2,3},{3,2},{4,5},{5,4},{6,7},{7,6},{8,9},{9,8},{10,11... | collective-permute-start | bytes 1572872 | tf_op jit(solution)/shard_map/ppermute | solution.py:217
  42.0 8.1 %collective-permute-start.13 = (bf16[256,512]{1,0:T(8,128)(2,1)S(1)}, bf16[256,512]{1,0:T(8,128)(2,1)S(1)}, u32[]{:S(2)}, u32[]{:S(2)}) collective-permute-start(bf16[256,512]{1,0:T(8,128)(2,1)S(1)} %fusion.3.refs_9_), channel_id=1, source_target_pairs={{0,16},{16,0},{1,17},{17,1},{2,18},{18,2},{3,19},{19,3},{4,20},{20... | collective-permute-start | bytes 786440 | tf_op jit(solution)/shard_map/ppermute | solution.py:217
  43.6 7.3 %collective-permute-start.10 = (bf16[2,2,128,256]{3,2,1,0:T(8,128)(2,1)S(1)}, bf16[2,2,128,256]{3,2,1,0:T(8,128)(2,1)S(1)}, u32[]{:S(2)}, u32[]{:S(2)}) collective-permute-start(bf16[2,2,128,256]{3,2,1,0:T(8,128)(2,1)S(1)} %constant_dynamic-slice_fusion.1), channel_id=1, source_target_pairs={{0,4},{5,1},{4,8},{9,5},{8,12},{13,9},{12,14},{15,13},{14,10},{11,... | collective-permute-start | bytes 786440 | tf_op jit(solution)/shard_map/ppermute | solution.py:243
  47.0 7.9 %collective-permute-start.9 = (bf16[2,4,128,256]{3,2,1,0:T(8,128)(2,1)S(1)}, bf16[2,4,128,256]{3,2,1,0:T(8,128)(2,1)S(1)}, u32[]{:S(2)}, u32[]{:S(2)}) collective-permute-start(bf16[2,4,128,256]{3,2,1,0:T(8,128)(2,1)S(1)} %collective-permute-done.8.refs_5_), channel_id=1, source_target_pairs={{0,1},{1,0},{2,3},{3,2},{4,5},{5,4},{6,7},{7,6},{8,9},{9,8},{10,11... | collective-permute-start | bytes 1572872 | tf_op jit(solution)/shard_map/ppermute | solution.py:217
  50.2 10.4 %collective-permute-start.15 = (bf16[2,4,128,256]{3,2,1,0:T(8,128)(2,1)S(1)}, bf16[2,4,128,256]{3,2,1,0:T(8,128)(2,1)S(1)}, u32[]{:S(2)}, u32[]{:S(2)}) collective-permute-start(bf16[2,4,128,256]{3,2,1,0:T(8,128)(2,1)S(1)} %collective-permute-done.1.refs_1_), channel_id=1, source_target_pairs={{0,1},{1,0},{2,3},{3,2},{4,5},{5,4},{6,7},{7,6},{8,9},{9,8},{10,11... | collective-permute-start | bytes 1572872 | tf_op jit(solution)/shard_map/ppermute | solution.py:217
  50.2 4.2 %collective-permute-start.14 = (bf16[256,512]{1,0:T(8,128)(2,1)S(1)}, bf16[256,512]{1,0:T(8,128)(2,1)S(1)}, u32[]{:S(2)}, u32[]{:S(2)}) collective-permute-start(bf16[256,512]{1,0:T(8,128)(2,1)S(1)} %collective-permute-done.13.refs_11_), channel_id=1, source_target_pairs={{0,1},{1,0},{2,3},{3,2},{4,5},{5,4},{6,7},{7,6},{8,9},{9,8},{10,11... | collective-permute-start | bytes 786440 | tf_op jit(solution)/shard_map/ppermute | solution.py:217
  50.9 3.5 %collective-permute-start.11 = (bf16[2,2,128,256]{3,2,1,0:T(8,128)(2,1)S(1)}, bf16[2,2,128,256]{3,2,1,0:T(8,128)(2,1)S(1)}, u32[]{:S(2)}, u32[]{:S(2)}) collective-permute-start(bf16[2,2,128,256]{3,2,1,0:T(8,128)(2,1)S(1)} %collective-permute-done.10.refs_7_), channel_id=1, source_target_pairs={{0,1},{1,0},{2,3},{3,2},{4,5},{5,4},{6,7},{7,6},{8,9},{9,8},{10,11... | collective-permute-start | bytes 786440 | tf_op jit(solution)/shard_map/ppermute | solution.py:217
  50.9 9.6 %copy-start.1 = (bf16[3,256,256]{2,1,0:T(8,128)(2,1)S(1)}, bf16[3,256,256]{2,1,0:T(8,128)(2,1)}, u32[]{:S(2)}) copy-start(bf16[3,256,256]{2,1,0:T(8,128)(2,1)} %res_mine_ref.1) | copy-start | bytes 1179652
  50.9 8.0 %collective-permute-start.18 = (bf16[2,2,128,256]{3,2,1,0:T(8,128)(2,1)S(1)}, bf16[2,2,128,256]{3,2,1,0:T(8,128)(2,1)S(1)}, u32[]{:S(2)}, u32[]{:S(2)}) collective-permute-start(bf16[2,2,128,256]{3,2,1,0:T(8,128)(2,1)S(1)} %constant_dynamic-slice_fusion), channel_id=1, source_target_pairs={{0,4},{5,1},{4,8},{9,5},{8,12},{13,9},{12,14},{15,13},{14,10},{11,... | collective-permute-start | bytes 786440 | tf_op jit(solution)/shard_map/ppermute | solution.py:243
  54.4 7.6 %collective-permute-start.16 = (bf16[2,4,128,256]{3,2,1,0:T(8,128)(2,1)S(1)}, bf16[2,4,128,256]{3,2,1,0:T(8,128)(2,1)S(1)}, u32[]{:S(2)}, u32[]{:S(2)}) collective-permute-start(bf16[2,4,128,256]{3,2,1,0:T(8,128)(2,1)S(1)} %collective-permute-done.2.refs_3_), channel_id=1, source_target_pairs={{0,1},{1,0},{2,3},{3,2},{4,5},{5,4},{6,7},{7,6},{8,9},{9,8},{10,11... | collective-permute-start | bytes 1572872 | tf_op jit(solution)/shard_map/ppermute | solution.py:217
  54.4 8.2 %collective-permute-start.17 = (bf16[2,4,128,256]{3,2,1,0:T(8,128)(2,1)S(1)}, bf16[2,4,128,256]{3,2,1,0:T(8,128)(2,1)S(1)}, u32[]{:S(2)}, u32[]{:S(2)}) collective-permute-start(bf16[2,4,128,256]{3,2,1,0:T(8,128)(2,1)S(1)} %collective-permute-done.3.refs_5_), channel_id=1, source_target_pairs={{0,1},{1,0},{2,3},{3,2},{4,5},{5,4},{6,7},{7,6},{8,9},{9,8},{10,11... | collective-permute-start | bytes 1572872 | tf_op jit(solution)/shard_map/ppermute | solution.py:217
  58.9 14.0 %collective-permute-start.21 = (bf16[4,256,256]{2,1,0:T(8,128)(2,1)S(1)}, bf16[4,256,256]{2,1,0:T(8,128)(2,1)S(1)}, u32[]{:S(2)}, u32[]{:S(2)}) collective-permute-start(bf16[4,256,256]{2,1,0:T(8,128)(2,1)S(1)} %get-tuple-element.18), channel_id=1, source_target_pairs={{0,16},{16,0},{1,17},{17,1},{2,18},{18,2},{3,19},{19,3},{4,20},{20... | collective-permute-start | bytes 1572872 | tf_op jit(solution)/shard_map/ppermute | solution.py:217
  60.5 4.4 %collective-permute-start.20 = (bf16[3,256,256]{2,1,0:T(8,128)(2,1)S(1)}, bf16[3,256,256]{2,1,0:T(8,128)(2,1)S(1)}, u32[]{:S(2)}, u32[]{:S(2)}) collective-permute-start(bf16[3,256,256]{2,1,0:T(8,128)(2,1)S(1)} %copy-done.1), channel_id=1, source_target_pairs={{0,1},{1,0},{2,3},{3,2},{4,5},{5,4},{6,7},{7,6},{8,9},{9,8},{10,11... | collective-permute-start | bytes 1179656 | tf_op jit(solution)/shard_map/ppermute | solution.py:217
  60.6 2.1 %collective-permute-start.19 = (bf16[2,2,128,256]{3,2,1,0:T(8,128)(2,1)S(1)}, bf16[2,2,128,256]{3,2,1,0:T(8,128)(2,1)S(1)}, u32[]{:S(2)}, u32[]{:S(2)}) collective-permute-start(bf16[2,2,128,256]{3,2,1,0:T(8,128)(2,1)S(1)} %collective-permute-done.18.refs_7_), channel_id=1, source_target_pairs={{0,1},{1,0},{2,3},{3,2},{4,5},{5,4},{6,7},{7,6},{8,9},{9,8},{10,11... | collective-permute-start | bytes 786440 | tf_op jit(solution)/shard_map/ppermute | solution.py:217
  61.9 11.0 %copy-start = (f32[4,256,256]{2,1,0:T(8,128)S(1)}, f32[4,256,256]{2,1,0:T(8,128)}, u32[]{:S(2)}) copy-start(f32[4,256,256]{2,1,0:T(8,128)} %get-tuple-element.16.own_ref) | copy-start | bytes 3145732
  61.9 11.0 %copy-start.3 = (f32[256]{0:T(256)S(1)}, f32[256]{0:T(256)}, u32[]{:S(2)}) copy-start(f32[256]{0:T(256)} %param.12) | copy-start | bytes 3076
  72.9 5.0 %copy-start.2 = (bf16[256,256]{1,0:T(8,128)(2,1)S(1)}, bf16[256,256]{1,0:T(8,128)(2,1)}, u32[]{:S(2)}) copy-start(bf16[256,256]{1,0:T(8,128)(2,1)} %skip_ref.1) | copy-start | bytes 393220
  72.9 5.0 %copy-start.4 = (f32[256]{0:T(256)S(1)}, f32[256]{0:T(256)}, u32[]{:S(2)}) copy-start(f32[256]{0:T(256)} %param.17) | copy-start | bytes 3076
  72.9 5.0 %copy-start.5 = (f32[256]{0:T(256)S(1)}, f32[256]{0:T(256)}, u32[]{:S(2)}) copy-start(f32[256]{0:T(256)} %param.19) | copy-start | bytes 3076
  73.7 3.1 %collective-permute-start.22 = (bf16[10,256,256]{2,1,0:T(8,128)(2,1)S(1)}, bf16[10,256,256]{2,1,0:T(8,128)(2,1)S(1)}, u32[]{:S(2)}, u32[]{:S(2)}) collective-permute-start(bf16[10,256,256]{2,1,0:T(8,128)(2,1)S(1)} %shard_map.115.mine_ref), channel_id=1, source_target_pairs={{0,1},{1,0},{2,3},{3,2},{4,5},{5,4},{6,7},{7,6},{8,9},{9,8},{10,11... | collective-permute-start | bytes 3932168 | tf_op jit(solution)/shard_map/ppermute | solution.py:217
  73.8 14.3 %collective-permute-start.23 = (bf16[4,256,256]{2,1,0:T(8,128)(2,1)S(1)}, bf16[4,256,256]{2,1,0:T(8,128)(2,1)S(1)}, u32[]{:S(2)}, u32[]{:S(2)}) collective-permute-start(bf16[4,256,256]{2,1,0:T(8,128)(2,1)S(1)} %get-tuple-element.15), channel_id=1, source_target_pairs={{0,16},{16,0},{1,17},{17,1},{2,18},{18,2},{3,19},{19,3},{4,20},{20... | collective-permute-start | bytes 1572872 | tf_op jit(solution)/shard_map/ppermute | solution.py:217
  76.8 1.1 %copy-start.6 = (bf16[10,256,256]{2,1,0:T(8,128)(2,1)}, bf16[10,256,256]{2,1,0:T(8,128)(2,1)S(1)}, u32[]{:S(2)}) copy-start(bf16[10,256,256]{2,1,0:T(8,128)(2,1)S(1)} %collective-permute-done.22.theirs_ref) | copy-start | bytes 3932164

commit v2 on v1

--- a/solution.py
+++ b/solution.py
@@ -94,10 +94,12 @@
     )(*blocks, *sides)
 
 
-def upsampled(group, own_ref, other_ref, prev_ref, bias, step):
-    half, tap = divmod(step, own_ref.shape[0])
-    value = jnp.where(group == half, own_ref[tap], other_ref[tap].astype(F32))
-    return value + prev_ref[step].astype(F32) + bias
+def each_step(group, own_ref, other_ref):
+    taps = own_ref.shape[0]
+    for index, source in enumerate((own_ref, other_ref)):
+        first = (group if index == 0 else 1 - group) * taps
+        for tap in range(taps):
+            yield first + tap, source[tap].astype(F32)
 
 
 def excite_kernel(group_ref, own_ref, other_ref, prev_ref, bias_ref, window_ref):
@@ -105,8 +107,8 @@
     history = prev_ref.shape[0] - steps
     for step in range(history):
         window_ref[step] = prev_ref[steps + step]
-    for step in range(steps):
-        up = upsampled(group_ref[0], own_ref, other_ref, prev_ref, bias_ref[...], step)
+    for step, value in each_step(group_ref[0], own_ref, other_ref):
+        up = value + prev_ref[step].astype(F32) + bias_ref[...]
         window_ref[history + step] = apply_elu(up).astype(BF16)
 
 
@@ -134,6 +136,7 @@
     skip_ref,
     skip_bias_ref,
     out_ref,
+    products,
     frames,
 ):
     taps, block, width = own_ref.shape
@@ -149,9 +152,10 @@
             branch = term if branch is None else branch + term
     hidden = apply_elu(branch + res_bias_ref[...]).astype(BF16)
     projected = jnp.dot(hidden, skip_ref[...], preferred_element_type=F32)
-    for step in range(steps):
-        up = upsampled(group_ref[0], own_ref, other_ref, prev_ref, bias_ref[...], step)
-        mixed = up + projected[step * block : (step + 1) * block] + skip_bias_ref[...]
+    products[...] = projected.reshape(products.shape)
+    for step, value in each_step(group_ref[0], own_ref, other_ref):
+        up = value + prev_ref[step].astype(F32) + bias_ref[...]
+        mixed = up + products[step] + skip_bias_ref[...]
         for part in range(width // 128):
             frames.at[part][pl.ds(step, block, stride=steps), :] = mixed[
                 :, part * 128 : (part + 1) * 128
@@ -176,24 +180,21 @@
         + [blocks(array) for array in arrays]
         + [VMEM] * len(parameters),
         out_specs=pl.BlockSpec((block * steps, width), lambda i: (i, 0)),
-        scratch_shapes=[pltpu.VMEM((width // 128, block * steps, 128), F32)],
+        scratch_shapes=[
+            pltpu.VMEM((steps, block, width), F32),
+            pltpu.VMEM((width // 128, block * steps, 128), F32),
+        ],
         compiler_params=pltpu.CompilerParams(vmem_limit_bytes=VMEM_LIMIT),
     )(group, *arrays, *parameters)
 
 
 def weave_kernel(group_ref, own_ref, other_ref, out_ref, frames):
-    group = group_ref[0]
     taps, block, width = own_ref.shape
-    for half in range(2):
-        for tap in range(taps):
-            value = jnp.where(
-                group == half, own_ref[tap].astype(F32), other_ref[tap].astype(F32)
-            )
-            step = half * taps + tap
-            for part in range(width // 128):
-                frames.at[part][pl.ds(step, block, stride=2 * taps), :] = value[
-                    :, part * 128 : (part + 1) * 128
-                ]
+    for step, value in each_step(group_ref[0], own_ref, other_ref):
+        for part in range(width // 128):
+            frames.at[part][pl.ds(step, block, stride=2 * taps), :] = value[
+                :, part * 128 : (part + 1) * 128
+            ]
     for part in range(width // 128):
         out_ref[:, part * 128 : (part + 1) * 128] = frames[part].astype(BF16)
 
@@ -270,26 +271,20 @@
     for first in (0, tap_count // 2):
         part = lax.dynamic_slice_in_dim(conv_weight, first + group * taps, taps, axis=1)
         halves.append(part.transpose(1, 0, 2))
-    own = jnp.concatenate(halves, axis=0)
-    cuts = ((0, taps), (taps, 2 * taps))
 
     if rows % 128 == 0 and count % 2 == 0:
-        other = swap(own, "segment")
-        rings = [Ring(count, own[a:b], other[a:b]) for a, b in cuts]
-        up_ring, tail_ring = rings
-        up_seen, tail_seen = [], []
-        for _ in range(count // 2):
+        up_ring, tail_ring = (Ring(count, own, swap(own, "segment")) for own in halves)
+        up_seen, tail_seen = [up_ring.round()], []
+        tail_seen.append(tail_ring.round(up_seen[0]))
+        for _ in range(2, count // 2):
             up_seen.append(up_ring.round())
             tail_seen.append(tail_ring.round())
-        first_done = up_seen[0]
+        up_ring.round()
         up_ring.blocks[0] = after(up_ring.blocks[0], tail_seen[-2])
-        nearly_done = tail_seen[-1]
-        gathered = [(ring.blocks, ring.steps) for ring in rings]
+        first_done, nearly_done = up_seen[0], tail_seen[-1]
     else:
-        gathered = [
-            ([lax.all_gather(own[a:b], "streams", axis=1, tiled=True)], [None]) for a, b in cuts
-        ]
-        first_done = nearly_done = own
+        tail_ring = None
+        first_done = nearly_done = halves[0]
 
     portion = sessions // count
     cap = tail_cache.shape[0] // count
@@ -317,9 +312,16 @@
 
     res_theirs = swap(res_weight, "segment")
 
-    own_up, away_up = spread_taps(sides, *gathered[0], count, F32)
-    other_up = swap(after(away_up, nearly_done), "groups")
-    own_tail, away_tail = spread_taps(sides, *gathered[1], count, BF16)
+    if tail_ring is None:
+        whole = [lax.all_gather(own, "streams", axis=1, tiled=True) for own in halves]
+        own_up, away_up = spread_taps(sides, [whole[0]], [None], count, F32)
+        other_up = swap(away_up, "groups")
+        own_tail, away_tail = spread_taps(sides, [whole[1]], [None], count, BF16)
+    else:
+        own_up, away_up = spread_taps(sides, up_ring.blocks, up_ring.steps, count, F32)
+        tail_ring.round(away_up)
+        other_up = swap(after(away_up, nearly_done), "groups")
+        own_tail, away_tail = spread_taps(sides, tail_ring.blocks, tail_ring.steps, count, BF16)
     other_tail = swap(away_tail, "groups")
 
     own_up = after(own_up, (away_tail, res_theirs))

time: 90.5 us -> 93.1 us (1.029)
  waiting for transfers between devices: 35.2 us -> 41.1 us
  starting transfers between devices: 34.5 us -> 31.3 us
    ppermute x8, waiting for transfers between devices: 15.7 us -> 26.7 us  [round(): item = lax.ppermute(item, ('streams', 'segment'), self.pairs)]
    ppermute x16 -> x17, waiting for transfers between devices: 19.5 us -> 14.5 us  [swap(): return lax.ppermute(value, axis, [(0, 1), (1, 0)])]
    ppermute x8, starting transfers between devices: 22.3 us -> 17.5 us  [round(): item = lax.ppermute(item, ('streams', 'segment'), self.pairs)]
    all_to_all x1, starting transfers between devices: 4.79 us -> 6.34 us  [local(): lax.all_to_all(parcel, 'streams', split_axis=0, concat_axis=0, tiled=True)]
    ppermute x16 -> x17, starting transfers between devices: 7.45 us -> 7.48 us  [swap(): return lax.ppermute(value, axis, [(0, 1), (1, 0)])]
  transfers between devices with their start and end apart: 25 -> 26, of which waited for: 11 -> 14; matrix products, arithmetic and copies ran while one was open for 2% -> 2% of each run, Pallas kernels for 13% -> 13%
where the time goes in v2:
time: 93.1 us; the launch traced here: 92.8 us
  waiting for transfers between devices  41.1 us (44%)
  starting transfers between devices  31.3 us (34%)
  Pallas kernels  14.8 us (16%)
  local copies, waits for them, and re-layouts  2.85 us (3%)
  other arithmetic  1.17 us (1%)
    ppermute x8, waiting for transfers between devices, round(): item = lax.ppermute(item, ('streams', 'segment'), self.pairs)  26.7 us
    ppermute x8, starting transfers between devices, round(): item = lax.ppermute(item, ('streams', 'segment'), self.pairs)  17.5 us
    ppermute x17, waiting for transfers between devices, swap(): return lax.ppermute(value, axis, [(0, 1), (1, 0)])  14.5 us
    ppermute x17, starting transfers between devices, swap(): return lax.ppermute(value, axis, [(0, 1), (1, 0)])  7.48 us
    all_to_all x1, starting transfers between devices, local(): lax.all_to_all(parcel, 'streams', split_axis=0, concat_axis=0, tiled=True)  6.34 us
    pallas_call x2, Pallas kernels, spread_taps(): pl.pallas_call(functools.partial(spread_kernel, count, steps), out_shape=...  6.26 us
    pallas_call x1, Pallas kernels, residual(): pl.pallas_call(residual_kernel, out_shape=jax.ShapeDtypeStruct((sessions...  5.89 us
    pallas_call x1, Pallas kernels, weave(): pl.pallas_call(weave_kernel, out_shape=jax.ShapeDtypeStruct((sessions * s...  1.99 us
  transfers between devices with their start and end apart: 26, of which 14 were waited for; matrix products, arithmetic and copies ran while one was open for 2% of the time, Pallas kernels for 13%

profile of v2, /device:TPU:0, one launch (start us, length us, event | category | flops | bytes accessed | tf_op | source)
XLA Modules:
  0.0 92.8 jit_solution(59752188010773180)
XLA Ops:
  0.6 1.5 %constant_dynamic-slice_fusion.2 = (bf16[128,4,256]{2,1,0:T(4,128)(2,1)S(1)}, bf16[128,4,256]{2,1,0:T(4,128)(2,1)S(1)}) fusion(bf16[128,16,256]{2,1,0:T(8,128)(2,1)} %param.11, s32[]{:T(128)S(6)} %select_n.15, s32[]{:T(128)S(6)} %select_n.14), kind=kLoop, calls=%fused_computation.24 | loop fusion | bytes 1048584 | tf_op jit(solution)/shard_map/dynamic_slice | solution.py:272
  2.1 0.0 copy-start.8
  2.2 0.0 copy-start.9
  2.2 0.5 collective-permute-start.1
  2.7 1.2 %collective-permute-done.1 = bf16[4,128,256]{2,1,0:T(8,128)(2,1)S(1)} collective-permute-done((bf16[4,128,256]{2,1,0:T(8,128)(2,1)S(1)}, bf16[4,128,256]{2,1,0:T(8,128)(2,1)S(1)}, u32[]{:S(2)}, u32[]{:S(2)}) %collective-permute-start.1) | collective-permute-done | bytes 262176 | tf_op jit(solution)/shard_map/ppermute | solution.py:218
  3.9 0.1 pad_maximum_fusion.1
  3.9 3.0 %collective-permute-start.2 = (bf16[2,4,128,256]{3,2,1,0:T(8,128)(2,1)S(1)}, bf16[2,4,128,256]{3,2,1,0:T(8,128)(2,1)S(1)}, u32[]{:S(2)}, u32[]{:S(2)}) collective-permute-start(bf16[2,4,128,256]{3,2,1,0:T(8,128)(2,1)S(1)} %pad_maximum_fusion.1), channel_id=1, source_target_pairs={{0,4},{5,1},{4,8},{9,5},{8,12},{13,9},{12,14},{15,13},{14,10},{11,... | collective-permute-start | bytes 1572872 | tf_op jit(solution)/shard_map/ppermute | solution.py:244
  7.0 0.1 collective-permute-start
  7.1 0.1 broadcast_in_dim.23
  7.2 0.8 maximum_maximum_fusion
  8.0 6.0 %collective-permute-done.2.refs_1_ = bf16[2,4,128,256]{3,2,1,0:T(8,128)(2,1)S(1)} collective-permute-done((bf16[2,4,128,256]{3,2,1,0:T(8,128)(2,1)S(1)}, bf16[2,4,128,256]{3,2,1,0:T(8,128)(2,1)S(1)}, u32[]{:S(2)}, u32[]{:S(2)}) %collective-permute-start.2) | collective-permute-done | bytes 524320 | tf_op jit(solution)/shard_map/ppermute | solution.py:244
  14.0 6.3 %all-to-all-start = ((bf16[8,40,512]{2,1,0:T(8,128)(2,1)}), bf16[8,40,512]{2,1,0:T(8,128)(2,1)S(1)}, u32[]{:S(2)}, u32[]{:S(2)}) async-start(bf16[8,40,512]{2,1,0:T(8,128)(2,1)} %maximum_maximum_fusion), calls=%async_computation | async-start | bytes 655360 | tf_op jit(solution)/shard_map/all_to_all | solution.py:300
  20.3 2.0 %collective-permute-start.6 = (bf16[2,4,128,256]{3,2,1,0:T(8,128)(2,1)S(1)}, bf16[2,4,128,256]{3,2,1,0:T(8,128)(2,1)}, u32[]{:S(2)}, u32[]{:S(2)}) collective-permute-start(bf16[2,4,128,256]{3,2,1,0:T(8,128)(2,1)S(1)} %collective-permute-done.2.refs_1_), channel_id=1, source_target_pairs={{0,4},{5,1},{4,8},{9,5},{8,12},{13,9},{12,14},{15,13},{14,10},{11,... | collective-permute-start | bytes 1572872 | tf_op jit(solution)/shard_map/ppermute | solution.py:244
  22.4 0.1 pad_maximum_fusion
  22.4 1.5 %collective-permute-start.3 = (bf16[2,4,128,256]{3,2,1,0:T(8,128)(2,1)S(1)}, bf16[2,4,128,256]{3,2,1,0:T(8,128)(2,1)S(1)}, u32[]{:S(2)}, u32[]{:S(2)}) collective-permute-start(bf16[2,4,128,256]{3,2,1,0:T(8,128)(2,1)S(1)} %pad_maximum_fusion), channel_id=1, source_target_pairs={{0,4},{5,1},{4,8},{9,5},{8,12},{13,9},{12,14},{15,13},{14,10},{11,... | collective-permute-start | bytes 1572872 | tf_op jit(solution)/shard_map/ppermute | solution.py:244
  23.9 8.4 %collective-permute-done.6.refs_3_ = bf16[2,4,128,256]{3,2,1,0:T(8,128)(2,1)} collective-permute-done((bf16[2,4,128,256]{3,2,1,0:T(8,128)(2,1)S(1)}, bf16[2,4,128,256]{3,2,1,0:T(8,128)(2,1)}, u32[]{:S(2)}, u32[]{:S(2)}) %collective-permute-start.6) | collective-permute-done | bytes 524320 | tf_op jit(solution)/shard_map/ppermute | solution.py:244
  32.3 1.7 %collective-permute-start.8 = (bf16[2,4,128,256]{3,2,1,0:T(8,128)(2,1)}, bf16[2,4,128,256]{3,2,1,0:T(8,128)(2,1)S(1)}, u32[]{:S(2)}, u32[]{:S(2)}) collective-permute-start(bf16[2,4,128,256]{3,2,1,0:T(8,128)(2,1)} %collective-permute-done.6.refs_3_), channel_id=1, source_target_pairs={{0,4},{5,1},{4,8},{9,5},{8,12},{13,9},{12,14},{15,13},{14,10},{11,... | collective-permute-start | bytes 1572872 | tf_op jit(solution)/shard_map/ppermute | solution.py:244
  34.1 3.8 %collective-permute-done.3.refs_1_ = bf16[2,4,128,256]{3,2,1,0:T(8,128)(2,1)S(1)} collective-permute-done((bf16[2,4,128,256]{3,2,1,0:T(8,128)(2,1)S(1)}, bf16[2,4,128,256]{3,2,1,0:T(8,128)(2,1)S(1)}, u32[]{:S(2)}, u32[]{:S(2)}) %collective-permute-start.3) | collective-permute-done | bytes 524320 | tf_op jit(solution)/shard_map/ppermute | solution.py:244
  37.8 1.9 %collective-permute-start.4 = (bf16[2,4,128,256]{3,2,1,0:T(8,128)(2,1)S(1)}, bf16[2,4,128,256]{3,2,1,0:T(8,128)(2,1)S(1)}, u32[]{:S(2)}, u32[]{:S(2)}) collective-permute-start(bf16[2,4,128,256]{3,2,1,0:T(8,128)(2,1)S(1)} %collective-permute-done.3.refs_1_), channel_id=1, source_target_pairs={{0,4},{5,1},{4,8},{9,5},{8,12},{13,9},{12,14},{15,13},{14,10},{11,... | collective-permute-start | bytes 1572872 | tf_op jit(solution)/shard_map/ppermute | solution.py:244
  39.7 0.1 fusion.3.refs_9_
  39.9 1.6 %collective-permute-start.13 = (bf16[256,512]{1,0:T(8,128)(2,1)S(1)}, bf16[256,512]{1,0:T(8,128)(2,1)S(1)}, u32[]{:S(2)}, u32[]{:S(2)}) collective-permute-start(bf16[256,512]{1,0:T(8,128)(2,1)S(1)} %fusion.3.refs_9_), channel_id=1, source_target_pairs={{0,16},{16,0},{1,17},{17,1},{2,18},{18,2},{3,19},{19,3},{4,20},{20... | collective-permute-start | bytes 786440 | tf_op jit(solution)/shard_map/ppermute | solution.py:218
  41.4 2.0 %collective-permute-done.8.refs_5_ = bf16[2,4,128,256]{3,2,1,0:T(8,128)(2,1)S(1)} collective-permute-done((bf16[2,4,128,256]{3,2,1,0:T(8,128)(2,1)}, bf16[2,4,128,256]{3,2,1,0:T(8,128)(2,1)S(1)}, u32[]{:S(2)}, u32[]{:S(2)}) %collective-permute-start.8) | collective-permute-done | bytes 524320 | tf_op jit(solution)/shard_map/ppermute | solution.py:244
  43.4 0.9 %collective-permute-start.12 = (bf16[256,512]{1,0:T(8,128)(2,1)S(1)}, bf16[256,512]{1,0:T(8,128)(2,1)S(1)}, u32[]{:S(2)}, u32[]{:S(2)}) collective-permute-start(bf16[256,512]{1,0:T(8,128)(2,1)S(1)} %fusion.3.refs_9_), channel_id=1, source_target_pairs={{0,1},{1,0},{2,3},{3,2},{4,5},{5,4},{6,7},{7,6},{8,9},{9,8},{10,11... | collective-permute-start | bytes 786440 | tf_op jit(solution)/shard_map/ppermute | solution.py:218
  44.4 3.3 %collective-permute-start.10 = (bf16[2,2,128,256]{3,2,1,0:T(8,128)(2,1)S(1)}, bf16[2,2,128,256]{3,2,1,0:T(8,128)(2,1)S(1)}, u32[]{:S(2)}, u32[]{:S(2)}) collective-permute-start(bf16[2,2,128,256]{3,2,1,0:T(8,128)(2,1)S(1)} %constant_dynamic-slice_fusion.1), channel_id=1, source_target_pairs={{0,4},{5,1},{4,8},{9,5},{8,12},{13,9},{12,14},{15,13},{14,10},{11,... | collective-permute-start | bytes 786440 | tf_op jit(solution)/shard_map/ppermute | solution.py:244
  47.8 1.3 %collective-permute-done.4.refs_3_ = bf16[2,4,128,256]{3,2,1,0:T(8,128)(2,1)S(1)} collective-permute-done((bf16[2,4,128,256]{3,2,1,0:T(8,128)(2,1)S(1)}, bf16[2,4,128,256]{3,2,1,0:T(8,128)(2,1)S(1)}, u32[]{:S(2)}, u32[]{:S(2)}) %collective-permute-start.4) | collective-permute-done | bytes 524320 | tf_op jit(solution)/shard_map/ppermute | solution.py:244
  49.0 1.9 %collective-permute-start.17 = (bf16[2,4,128,256]{3,2,1,0:T(8,128)(2,1)S(1)}, bf16[2,4,128,256]{3,2,1,0:T(8,128)(2,1)S(1)}, u32[]{:S(2)}, u32[]{:S(2)}) collective-permute-start(bf16[2,4,128,256]{3,2,1,0:T(8,128)(2,1)S(1)} %collective-permute-done.4.refs_3_), channel_id=1, source_target_pairs={{0,4},{5,1},{4,8},{9,5},{8,12},{13,9},{12,14},{15,13},{14,10},{11,... | collective-permute-start | bytes 1572872 | tf_op jit(solution)/shard_map/ppermute | solution.py:244
  50.9 0.9 %collective-permute-done.10.refs_7_ = bf16[2,2,128,256]{3,2,1,0:T(8,128)(2,1)S(1)} collective-permute-done((bf16[2,2,128,256]{3,2,1,0:T(8,128)(2,1)S(1)}, bf16[2,2,128,256]{3,2,1,0:T(8,128)(2,1)S(1)}, u32[]{:S(2)}, u32[]{:S(2)}) %collective-permute-start.10) | collective-permute-done | bytes 262176 | tf_op jit(solution)/shard_map/ppermute | solution.py:244
  51.9 0.7 collective-permute-start.11
  52.5 1.1 %collective-permute-done.11.refs_8_ = bf16[2,2,128,256]{3,2,1,0:T(8,128)(2,1)S(1)} collective-permute-done((bf16[2,2,128,256]{3,2,1,0:T(8,128)(2,1)S(1)}, bf16[2,2,128,256]{3,2,1,0:T(8,128)(2,1)S(1)}, u32[]{:S(2)}, u32[]{:S(2)}) %collective-permute-start.11) | collective-permute-done | bytes 262176 | tf_op jit(solution)/shard_map/ppermute | solution.py:218
  53.7 4.0 %shard_map.113 = (f32[4,256,256]{2,1,0:T(8,128)}, bf16[4,256,256]{2,1,0:T(8,128)(2,1)S(1)}) custom-call(bf16[4,128,256]{2,1,0:T(8,128)(2,1)S(1)} %bitcast.37, bf16[2,4,128,256]{3,2,1,0:T(8,128)(2,1)S(1)} %collective-permute-done.2.refs_1_, bf16[2,4,128,256]{3,2,1,0:T(8,128)(2,1)} %collective-permute-done.5.refs_2_, ...), custom_call_target="tpu_custom_call" | custom-call | tf_op jit(solution)/shard_map/pallas_call | solution.py:80
  57.7 1.5 %collective-permute-done.17.refs_5_ = bf16[2,4,128,256]{3,2,1,0:T(8,128)(2,1)S(1)} collective-permute-done((bf16[2,4,128,256]{3,2,1,0:T(8,128)(2,1)S(1)}, bf16[2,4,128,256]{3,2,1,0:T(8,128)(2,1)S(1)}, u32[]{:S(2)}, u32[]{:S(2)}) %collective-permute-start.17) | collective-permute-done | bytes 524320 | tf_op jit(solution)/shard_map/ppermute | solution.py:244
  59.2 2.1 %collective-permute-start.19 = (bf16[2,2,128,256]{3,2,1,0:T(8,128)(2,1)S(1)}, bf16[2,2,128,256]{3,2,1,0:T(8,128)(2,1)S(1)}, u32[]{:S(2)}, u32[]{:S(2)}) collective-permute-start(bf16[2,2,128,256]{3,2,1,0:T(8,128)(2,1)S(1)} %constant_dynamic-slice_fusion), channel_id=1, source_target_pairs={{0,4},{5,1},{4,8},{9,5},{8,12},{13,9},{12,14},{15,13},{14,10},{11,... | collective-permute-start | bytes 786440 | tf_op jit(solution)/shard_map/ppermute | solution.py:244
  61.3 0.5 collective-permute-start.18
  61.8 1.5 %collective-permute-start.22 = (bf16[4,256,256]{2,1,0:T(8,128)(2,1)S(1)}, bf16[4,256,256]{2,1,0:T(8,128)(2,1)S(1)}, u32[]{:S(2)}, u32[]{:S(2)}) collective-permute-start(bf16[4,256,256]{2,1,0:T(8,128)(2,1)S(1)} %get-tuple-element.22), channel_id=1, source_target_pairs={{0,16},{16,0},{1,17},{17,1},{2,18},{18,2},{3,19},{19,3},{4,20},{20... | collective-permute-start | bytes 1572872 | tf_op jit(solution)/shard_map/ppermute | solution.py:218
  63.4 2.8 %collective-permute-done.19.refs_7_ = bf16[2,2,128,256]{3,2,1,0:T(8,128)(2,1)S(1)} collective-permute-done((bf16[2,2,128,256]{3,2,1,0:T(8,128)(2,1)S(1)}, bf16[2,2,128,256]{3,2,1,0:T(8,128)(2,1)S(1)}, u32[]{:S(2)}, u32[]{:S(2)}) %collective-permute-start.19) | collective-permute-done | bytes 262176 | tf_op jit(solution)/shard_map/ppermute | solution.py:244
  66.2 0.1 convert_reduce_fusion
  66.4 0.6 fusion.prev_ref
  67.0 0.7 collective-permute-done.20.refs_8_
  67.7 2.3 %shard_map.114 = (bf16[4,256,256]{2,1,0:T(8,128)(2,1)S(1)}, bf16[4,256,256]{2,1,0:T(8,128)(2,1)S(1)}) custom-call(bf16[4,128,256]{2,1,0:T(8,128)(2,1)S(1)} %bitcast.34, bf16[2,4,128,256]{3,2,1,0:T(8,128)(2,1)S(1)} %collective-permute-done.3.refs_1_, bf16[2,4,128,256]{3,2,1,0:T(8,128)(2,1)S(1)} %collective-permute-done.15.refs_2_, ...), custom_call_target="tpu_custom_call" | custom-call | tf_op jit(solution)/shard_map/pallas_call | solution.py:80
  70.0 5.6 %collective-permute-done.22.other_ref = bf16[4,256,256]{2,1,0:T(8,128)(2,1)S(1)} collective-permute-done((bf16[4,256,256]{2,1,0:T(8,128)(2,1)S(1)}, bf16[4,256,256]{2,1,0:T(8,128)(2,1)S(1)}, u32[]{:S(2)}, u32[]{:S(2)}) %collective-permute-start.22) | collective-permute-done | bytes 524320 | tf_op jit(solution)/shard_map/ppermute | solution.py:218
  75.7 0.7 shard_map.115.mine_ref
  76.4 0.1 collective-permute-start.23
  76.5 1.6 %collective-permute-start.24 = (bf16[4,256,256]{2,1,0:T(8,128)(2,1)S(1)}, bf16[4,256,256]{2,1,0:T(8,128)(2,1)S(1)}, u32[]{:S(2)}, u32[]{:S(2)}) collective-permute-start(bf16[4,256,256]{2,1,0:T(8,128)(2,1)S(1)} %get-tuple-element.20), channel_id=1, source_target_pairs={{0,16},{16,0},{1,17},{17,1},{2,18},{18,2},{3,19},{19,3},{4,20},{20... | collective-permute-start | bytes 1572872 | tf_op jit(solution)/shard_map/ppermute | solution.py:218
  78.1 1.4 %collective-permute-done.23.theirs_ref = bf16[10,256,256]{2,1,0:T(8,128)(2,1)S(1)} collective-permute-done((bf16[10,256,256]{2,1,0:T(8,128)(2,1)S(1)}, bf16[10,256,256]{2,1,0:T(8,128)(2,1)S(1)}, u32[]{:S(2)}, u32[]{:S(2)}) %collective-permute-start.23) | collective-permute-done | bytes 1310752 | tf_op jit(solution)/shard_map/ppermute | solution.py:218
  79.5 1.1 %copy-done.6 = bf16[10,256,256]{2,1,0:T(8,128)(2,1)} copy-done((bf16[10,256,256]{2,1,0:T(8,128)(2,1)}, bf16[10,256,256]{2,1,0:T(8,128)(2,1)S(1)}, u32[]{:S(2)}) %copy-start.6) | copy-done | bytes 1310744
  80.6 5.9 %shard_map.116 = bf16[2048,256]{1,0:T(8,128)(2,1)} custom-call(s32[1]{0:T(128)} %bitcast.group_ref, f32[4,256,256]{2,1,0:T(8,128)S(1)} %copy-done, bf16[4,256,256]{2,1,0:T(8,128)(2,1)S(1)} %collective-permute-done.22.other_ref, bf16[10,256,256]{2,1,0:T(8,128)(2,1)S(1)} %fusion.prev_ref, bf16[10,256,256]{2,1,0:T(8,128)(2,1)S(1)} %shard_map.115.mine_ref, ...), custom_call_target="tpu_custom_call" | custom-call | tf_op jit(solution)/shard_map/pallas_call | solution.py:175
  86.5 4.4 %collective-permute-done.24.other_ref = bf16[4,256,256]{2,1,0:T(8,128)(2,1)S(1)} collective-permute-done((bf16[4,256,256]{2,1,0:T(8,128)(2,1)S(1)}, bf16[4,256,256]{2,1,0:T(8,128)(2,1)S(1)}, u32[]{:S(2)}, u32[]{:S(2)}) %collective-permute-start.24) | collective-permute-done | bytes 524320 | tf_op jit(solution)/shard_map/ppermute | solution.py:218
  90.8 2.0 %shard_map.117 = bf16[2048,256]{1,0:T(8,128)(2,1)} custom-call(s32[1]{0:T(128)} %bitcast.group_ref, bf16[4,256,256]{2,1,0:T(8,128)(2,1)S(1)} %get-tuple-element.24.own_ref, bf16[4,256,256]{2,1,0:T(8,128)(2,1)S(1)} %collective-permute-done.24.other_ref), custom_call_target="tpu_custom_call" | custom-call | tf_op jit(solution)/shard_map/pallas_call | solution.py:206
  (53 shorter events, 0.3 us)
Async XLA Ops:
  2.1 4.9 %copy-start.10 = (s32[8]{0:T(128)S(1)}, s32[8]{0:T(128)}, u32[]{:S(2)}) copy-start(s32[8]{0:T(128)} %param.15) | copy-start | bytes 100
  2.1 5.0 %copy-start.7 = (bf16[256,512]{1,0:T(8,128)(2,1)S(1)}, bf16[256,512]{1,0:T(8,128)(2,1)}, u32[]{:S(2)}) copy-start(bf16[256,512]{1,0:T(8,128)(2,1)} %param.10) | copy-start | bytes 786436
  2.1 5.0 %copy-start.8 = (bf16[8,8,256]{2,1,0:T(8,128)(2,1)S(1)}, bf16[8,8,256]{2,1,0:T(8,128)(2,1)}, u32[]{:S(2)}) copy-start(bf16[8,8,256]{2,1,0:T(8,128)(2,1)} %param.13) | copy-start | bytes 98308
  2.2 5.0 %copy-start.9 = (bf16[8,2,256]{2,1,0:T(2,128)(2,1)S(1)}, bf16[8,2,256]{2,1,0:T(2,128)(2,1)}, u32[]{:S(2)}) copy-start(bf16[8,2,256]{2,1,0:T(2,128)(2,1)} %param.14) | copy-start | bytes 24580
  2.2 1.7 %collective-permute-start.1 = (bf16[4,128,256]{2,1,0:T(8,128)(2,1)S(1)}, bf16[4,128,256]{2,1,0:T(8,128)(2,1)S(1)}, u32[]{:S(2)}, u32[]{:S(2)}) collective-permute-start(bf16[4,128,256]{2,1,0:T(8,128)(2,1)S(1)} %bitcast.35), channel_id=1, source_target_pairs={{0,1},{1,0},{2,3},{3,2},{4,5},{5,4},{6,7},{7,6},{8,9},{9,8},{10,11... | collective-permute-start | bytes 786440 | tf_op jit(solution)/shard_map/ppermute | solution.py:218
  3.9 10.1 %collective-permute-start.2 = (bf16[2,4,128,256]{3,2,1,0:T(8,128)(2,1)S(1)}, bf16[2,4,128,256]{3,2,1,0:T(8,128)(2,1)S(1)}, u32[]{:S(2)}, u32[]{:S(2)}) collective-permute-start(bf16[2,4,128,256]{3,2,1,0:T(8,128)(2,1)S(1)} %pad_maximum_fusion.1), channel_id=1, source_target_pairs={{0,4},{5,1},{4,8},{9,5},{8,12},{13,9},{12,14},{15,13},{14,10},{11,... | collective-permute-start | bytes 1572872 | tf_op jit(solution)/shard_map/ppermute | solution.py:244
  7.0 15.4 %collective-permute-start = (bf16[4,128,256]{2,1,0:T(8,128)(2,1)S(1)}, bf16[4,128,256]{2,1,0:T(8,128)(2,1)S(1)}, u32[]{:S(2)}, u32[]{:S(2)}) collective-permute-start(bf16[4,128,256]{2,1,0:T(8,128)(2,1)S(1)} %bitcast.32), channel_id=1, source_target_pairs={{0,1},{1,0},{2,3},{3,2},{4,5},{5,4},{6,7},{7,6},{8,9},{9,8},{10,11... | collective-permute-start | bytes 786440 | tf_op jit(solution)/shard_map/ppermute | solution.py:218
  14.0 25.7 %all-to-all-start = ((bf16[8,40,512]{2,1,0:T(8,128)(2,1)}), bf16[8,40,512]{2,1,0:T(8,128)(2,1)S(1)}, u32[]{:S(2)}, u32[]{:S(2)}) async-start(bf16[8,40,512]{2,1,0:T(8,128)(2,1)} %maximum_maximum_fusion), calls=%async_computation | async-start | bytes 655360 | tf_op jit(solution)/shard_map/all_to_all | solution.py:300
  20.3 12.0 %collective-permute-start.6 = (bf16[2,4,128,256]{3,2,1,0:T(8,128)(2,1)S(1)}, bf16[2,4,128,256]{3,2,1,0:T(8,128)(2,1)}, u32[]{:S(2)}, u32[]{:S(2)}) collective-permute-start(bf16[2,4,128,256]{3,2,1,0:T(8,128)(2,1)S(1)} %collective-permute-done.2.refs_1_), channel_id=1, source_target_pairs={{0,4},{5,1},{4,8},{9,5},{8,12},{13,9},{12,14},{15,13},{14,10},{11,... | collective-permute-start | bytes 1572872 | tf_op jit(solution)/shard_map/ppermute | solution.py:244
  22.4 15.4 %collective-permute-start.3 = (bf16[2,4,128,256]{3,2,1,0:T(8,128)(2,1)S(1)}, bf16[2,4,128,256]{3,2,1,0:T(8,128)(2,1)S(1)}, u32[]{:S(2)}, u32[]{:S(2)}) collective-permute-start(bf16[2,4,128,256]{3,2,1,0:T(8,128)(2,1)S(1)} %pad_maximum_fusion), channel_id=1, source_target_pairs={{0,4},{5,1},{4,8},{9,5},{8,12},{13,9},{12,14},{15,13},{14,10},{11,... | collective-permute-start | bytes 1572872 | tf_op jit(solution)/shard_map/ppermute | solution.py:244
  32.3 11.1 %collective-permute-start.8 = (bf16[2,4,128,256]{3,2,1,0:T(8,128)(2,1)}, bf16[2,4,128,256]{3,2,1,0:T(8,128)(2,1)S(1)}, u32[]{:S(2)}, u32[]{:S(2)}) collective-permute-start(bf16[2,4,128,256]{3,2,1,0:T(8,128)(2,1)} %collective-permute-done.6.refs_3_), channel_id=1, source_target_pairs={{0,4},{5,1},{4,8},{9,5},{8,12},{13,9},{12,14},{15,13},{14,10},{11,... | collective-permute-start | bytes 1572872 | tf_op jit(solution)/shard_map/ppermute | solution.py:244
  34.1 10.4 %collective-permute-start.5 = (bf16[2,4,128,256]{3,2,1,0:T(8,128)(2,1)S(1)}, bf16[2,4,128,256]{3,2,1,0:T(8,128)(2,1)}, u32[]{:S(2)}, u32[]{:S(2)}) collective-permute-start(bf16[2,4,128,256]{3,2,1,0:T(8,128)(2,1)S(1)} %collective-permute-done.2.refs_1_), channel_id=1, source_target_pairs={{0,1},{1,0},{2,3},{3,2},{4,5},{5,4},{6,7},{7,6},{8,9},{9,8},{10,11... | collective-permute-start | bytes 1572872 | tf_op jit(solution)/shard_map/ppermute | solution.py:218
  37.8 11.2 %collective-permute-start.4 = (bf16[2,4,128,256]{3,2,1,0:T(8,128)(2,1)S(1)}, bf16[2,4,128,256]{3,2,1,0:T(8,128)(2,1)S(1)}, u32[]{:S(2)}, u32[]{:S(2)}) collective-permute-start(bf16[2,4,128,256]{3,2,1,0:T(8,128)(2,1)S(1)} %collective-permute-done.3.refs_1_), channel_id=1, source_target_pairs={{0,4},{5,1},{4,8},{9,5},{8,12},{13,9},{12,14},{15,13},{14,10},{11,... | collective-permute-start | bytes 1572872 | tf_op jit(solution)/shard_map/ppermute | solution.py:244
  39.9 7.9 %collective-permute-start.13 = (bf16[256,512]{1,0:T(8,128)(2,1)S(1)}, bf16[256,512]{1,0:T(8,128)(2,1)S(1)}, u32[]{:S(2)}, u32[]{:S(2)}) collective-permute-start(bf16[256,512]{1,0:T(8,128)(2,1)S(1)} %fusion.3.refs_9_), channel_id=1, source_target_pairs={{0,16},{16,0},{1,17},{17,1},{2,18},{18,2},{3,19},{19,3},{4,20},{20... | collective-permute-start | bytes 786440 | tf_op jit(solution)/shard_map/ppermute | solution.py:218
  41.4 11.1 %collective-permute-start.7 = (bf16[2,4,128,256]{3,2,1,0:T(8,128)(2,1)}, bf16[2,4,128,256]{3,2,1,0:T(8,128)(2,1)}, u32[]{:S(2)}, u32[]{:S(2)}) collective-permute-start(bf16[2,4,128,256]{3,2,1,0:T(8,128)(2,1)} %collective-permute-done.6.refs_3_), channel_id=1, source_target_pairs={{0,1},{1,0},{2,3},{3,2},{4,5},{5,4},{6,7},{7,6},{8,9},{9,8},{10,11... | collective-permute-start | bytes 1572872 | tf_op jit(solution)/shard_map/ppermute | solution.py:218
  43.4 7.5 %collective-permute-start.12 = (bf16[256,512]{1,0:T(8,128)(2,1)S(1)}, bf16[256,512]{1,0:T(8,128)(2,1)S(1)}, u32[]{:S(2)}, u32[]{:S(2)}) collective-permute-start(bf16[256,512]{1,0:T(8,128)(2,1)S(1)} %fusion.3.refs_9_), channel_id=1, source_target_pairs={{0,1},{1,0},{2,3},{3,2},{4,5},{5,4},{6,7},{7,6},{8,9},{9,8},{10,11... | collective-permute-start | bytes 786440 | tf_op jit(solution)/shard_map/ppermute | solution.py:218
  44.4 19.0 %copy-start.1 = (bf16[3,256,256]{2,1,0:T(8,128)(2,1)S(1)}, bf16[3,256,256]{2,1,0:T(8,128)(2,1)}, u32[]{:S(2)}) copy-start(bf16[3,256,256]{2,1,0:T(8,128)(2,1)} %res_mine_ref.1) | copy-start | bytes 1179652
  44.4 7.4 %collective-permute-start.10 = (bf16[2,2,128,256]{3,2,1,0:T(8,128)(2,1)S(1)}, bf16[2,2,128,256]{3,2,1,0:T(8,128)(2,1)S(1)}, u32[]{:S(2)}, u32[]{:S(2)}) collective-permute-start(bf16[2,2,128,256]{3,2,1,0:T(8,128)(2,1)S(1)} %constant_dynamic-slice_fusion.1), channel_id=1, source_target_pairs={{0,4},{5,1},{4,8},{9,5},{8,12},{13,9},{12,14},{15,13},{14,10},{11,... | collective-permute-start | bytes 786440 | tf_op jit(solution)/shard_map/ppermute | solution.py:244
  47.7 5.9 %collective-permute-start.9 = (bf16[2,4,128,256]{3,2,1,0:T(8,128)(2,1)S(1)}, bf16[2,4,128,256]{3,2,1,0:T(8,128)(2,1)S(1)}, u32[]{:S(2)}, u32[]{:S(2)}) collective-permute-start(bf16[2,4,128,256]{3,2,1,0:T(8,128)(2,1)S(1)} %collective-permute-done.8.refs_5_), channel_id=1, source_target_pairs={{0,1},{1,0},{2,3},{3,2},{4,5},{5,4},{6,7},{7,6},{8,9},{9,8},{10,11... | collective-permute-start | bytes 1572872 | tf_op jit(solution)/shard_map/ppermute | solution.py:218
  49.0 10.1 %collective-permute-start.17 = (bf16[2,4,128,256]{3,2,1,0:T(8,128)(2,1)S(1)}, bf16[2,4,128,256]{3,2,1,0:T(8,128)(2,1)S(1)}, u32[]{:S(2)}, u32[]{:S(2)}) collective-permute-start(bf16[2,4,128,256]{3,2,1,0:T(8,128)(2,1)S(1)} %collective-permute-done.4.refs_3_), channel_id=1, source_target_pairs={{0,4},{5,1},{4,8},{9,5},{8,12},{13,9},{12,14},{15,13},{14,10},{11,... | collective-permute-start | bytes 1572872 | tf_op jit(solution)/shard_map/ppermute | solution.py:244
  50.9 1.6 %collective-permute-start.14 = (bf16[256,512]{1,0:T(8,128)(2,1)S(1)}, bf16[256,512]{1,0:T(8,128)(2,1)S(1)}, u32[]{:S(2)}, u32[]{:S(2)}) collective-permute-start(bf16[256,512]{1,0:T(8,128)(2,1)S(1)} %collective-permute-done.13.refs_11_), channel_id=1, source_target_pairs={{0,1},{1,0},{2,3},{3,2},{4,5},{5,4},{6,7},{7,6},{8,9},{9,8},{10,11... | collective-permute-start | bytes 786440 | tf_op jit(solution)/shard_map/ppermute | solution.py:218
  51.9 1.8 %collective-permute-start.11 = (bf16[2,2,128,256]{3,2,1,0:T(8,128)(2,1)S(1)}, bf16[2,2,128,256]{3,2,1,0:T(8,128)(2,1)S(1)}, u32[]{:S(2)}, u32[]{:S(2)}) collective-permute-start(bf16[2,2,128,256]{3,2,1,0:T(8,128)(2,1)S(1)} %collective-permute-done.10.refs_7_), channel_id=1, source_target_pairs={{0,1},{1,0},{2,3},{3,2},{4,5},{5,4},{6,7},{7,6},{8,9},{9,8},{10,11... | collective-permute-start | bytes 786440 | tf_op jit(solution)/shard_map/ppermute | solution.py:218
  52.5 10.8 %collective-permute-start.15 = (bf16[2,4,128,256]{3,2,1,0:T(8,128)(2,1)S(1)}, bf16[2,4,128,256]{3,2,1,0:T(8,128)(2,1)S(1)}, u32[]{:S(2)}, u32[]{:S(2)}) collective-permute-start(bf16[2,4,128,256]{3,2,1,0:T(8,128)(2,1)S(1)} %collective-permute-done.3.refs_1_), channel_id=1, source_target_pairs={{0,1},{1,0},{2,3},{3,2},{4,5},{5,4},{6,7},{7,6},{8,9},{9,8},{10,11... | collective-permute-start | bytes 1572872 | tf_op jit(solution)/shard_map/ppermute | solution.py:218
  59.2 7.0 %collective-permute-start.19 = (bf16[2,2,128,256]{3,2,1,0:T(8,128)(2,1)S(1)}, bf16[2,2,128,256]{3,2,1,0:T(8,128)(2,1)S(1)}, u32[]{:S(2)}, u32[]{:S(2)}) collective-permute-start(bf16[2,2,128,256]{3,2,1,0:T(8,128)(2,1)S(1)} %constant_dynamic-slice_fusion), channel_id=1, source_target_pairs={{0,4},{5,1},{4,8},{9,5},{8,12},{13,9},{12,14},{15,13},{14,10},{11,... | collective-permute-start | bytes 786440 | tf_op jit(solution)/shard_map/ppermute | solution.py:244
  61.3 5.7 %collective-permute-start.16 = (bf16[2,4,128,256]{3,2,1,0:T(8,128)(2,1)S(1)}, bf16[2,4,128,256]{3,2,1,0:T(8,128)(2,1)S(1)}, u32[]{:S(2)}, u32[]{:S(2)}) collective-permute-start(bf16[2,4,128,256]{3,2,1,0:T(8,128)(2,1)S(1)} %collective-permute-done.4.refs_3_), channel_id=1, source_target_pairs={{0,1},{1,0},{2,3},{3,2},{4,5},{5,4},{6,7},{7,6},{8,9},{9,8},{10,11... | collective-permute-start | bytes 1572872 | tf_op jit(solution)/shard_map/ppermute | solution.py:218
  61.3 6.4 %collective-permute-start.18 = (bf16[2,4,128,256]{3,2,1,0:T(8,128)(2,1)S(1)}, bf16[2,4,128,256]{3,2,1,0:T(8,128)(2,1)S(1)}, u32[]{:S(2)}, u32[]{:S(2)}) collective-permute-start(bf16[2,4,128,256]{3,2,1,0:T(8,128)(2,1)S(1)} %collective-permute-done.17.refs_5_), channel_id=1, source_target_pairs={{0,1},{1,0},{2,3},{3,2},{4,5},{5,4},{6,7},{7,6},{8,9},{9,8},{10,11... | collective-permute-start | bytes 1572872 | tf_op jit(solution)/shard_map/ppermute | solution.py:218
  61.8 13.8 %collective-permute-start.22 = (bf16[4,256,256]{2,1,0:T(8,128)(2,1)S(1)}, bf16[4,256,256]{2,1,0:T(8,128)(2,1)S(1)}, u32[]{:S(2)}, u32[]{:S(2)}) collective-permute-start(bf16[4,256,256]{2,1,0:T(8,128)(2,1)S(1)} %get-tuple-element.22), channel_id=1, source_target_pairs={{0,16},{16,0},{1,17},{17,1},{2,18},{18,2},{3,19},{19,3},{4,20},{20... | collective-permute-start | bytes 1572872 | tf_op jit(solution)/shard_map/ppermute | solution.py:218
  63.4 6.7 %collective-permute-start.21 = (bf16[3,256,256]{2,1,0:T(8,128)(2,1)S(1)}, bf16[3,256,256]{2,1,0:T(8,128)(2,1)S(1)}, u32[]{:S(2)}, u32[]{:S(2)}) collective-permute-start(bf16[3,256,256]{2,1,0:T(8,128)(2,1)S(1)} %copy-done.1), channel_id=1, source_target_pairs={{0,1},{1,0},{2,3},{3,2},{4,5},{5,4},{6,7},{7,6},{8,9},{9,8},{10,11... | collective-permute-start | bytes 1179656 | tf_op jit(solution)/shard_map/ppermute | solution.py:218
  66.2 1.5 %collective-permute-start.20 = (bf16[2,2,128,256]{3,2,1,0:T(8,128)(2,1)S(1)}, bf16[2,2,128,256]{3,2,1,0:T(8,128)(2,1)S(1)}, u32[]{:S(2)}, u32[]{:S(2)}) collective-permute-start(bf16[2,2,128,256]{3,2,1,0:T(8,128)(2,1)S(1)} %collective-permute-done.19.refs_7_), channel_id=1, source_target_pairs={{0,1},{1,0},{2,3},{3,2},{4,5},{5,4},{6,7},{7,6},{8,9},{9,8},{10,11... | collective-permute-start | bytes 786440 | tf_op jit(solution)/shard_map/ppermute | solution.py:218
  67.0 8.7 %copy-start = (f32[4,256,256]{2,1,0:T(8,128)S(1)}, f32[4,256,256]{2,1,0:T(8,128)}, u32[]{:S(2)}) copy-start(f32[4,256,256]{2,1,0:T(8,128)} %get-tuple-element.21.own_ref) | copy-start | bytes 3145732
  67.0 8.7 %copy-start.3 = (f32[256]{0:T(256)S(1)}, f32[256]{0:T(256)}, u32[]{:S(2)}) copy-start(f32[256]{0:T(256)} %param.12) | copy-start | bytes 3076
  75.7 4.9 %copy-start.2 = (bf16[256,256]{1,0:T(8,128)(2,1)S(1)}, bf16[256,256]{1,0:T(8,128)(2,1)}, u32[]{:S(2)}) copy-start(bf16[256,256]{1,0:T(8,128)(2,1)} %skip_ref.1) | copy-start | bytes 393220
  75.7 4.9 %copy-start.4 = (f32[256]{0:T(256)S(1)}, f32[256]{0:T(256)}, u32[]{:S(2)}) copy-start(f32[256]{0:T(256)} %param.17) | copy-start | bytes 3076
  75.7 4.9 %copy-start.5 = (f32[256]{0:T(256)S(1)}, f32[256]{0:T(256)}, u32[]{:S(2)}) copy-start(f32[256]{0:T(256)} %param.19) | copy-start | bytes 3076
  76.4 3.1 %collective-permute-start.23 = (bf16[10,256,256]{2,1,0:T(8,128)(2,1)S(1)}, bf16[10,256,256]{2,1,0:T(8,128)(2,1)S(1)}, u32[]{:S(2)}, u32[]{:S(2)}) collective-permute-start(bf16[10,256,256]{2,1,0:T(8,128)(2,1)S(1)} %shard_map.115.mine_ref), channel_id=1, source_target_pairs={{0,1},{1,0},{2,3},{3,2},{4,5},{5,4},{6,7},{7,6},{8,9},{9,8},{10,11... | collective-permute-start | bytes 3932168 | tf_op jit(solution)/shard_map/ppermute | solution.py:218
  76.5 14.3 %collective-permute-start.24 = (bf16[4,256,256]{2,1,0:T(8,128)(2,1)S(1)}, bf16[4,256,256]{2,1,0:T(8,128)(2,1)S(1)}, u32[]{:S(2)}, u32[]{:S(2)}) collective-permute-start(bf16[4,256,256]{2,1,0:T(8,128)(2,1)S(1)} %get-tuple-element.20), channel_id=1, source_target_pairs={{0,16},{16,0},{1,17},{17,1},{2,18},{18,2},{3,19},{19,3},{4,20},{20... | collective-permute-start | bytes 1572872 | tf_op jit(solution)/shard_map/ppermute | solution.py:218
  79.5 1.1 %copy-start.6 = (bf16[10,256,256]{2,1,0:T(8,128)(2,1)}, bf16[10,256,256]{2,1,0:T(8,128)(2,1)S(1)}, u32[]{:S(2)}) copy-start(bf16[10,256,256]{2,1,0:T(8,128)(2,1)S(1)} %collective-permute-done.23.theirs_ref) | copy-start | bytes 3932164

commit v3 on v2

--- a/solution.py
+++ b/solution.py
@@ -7,7 +7,7 @@
 from jax.experimental.pallas import tpu as pltpu
 from jax.sharding import PartitionSpec as P
 
-VMEM_LIMIT = 48 * 1024 * 1024
+VMEM_LIMIT = 16 * 1024 * 1024
 F32 = jnp.float32
 BF16 = jnp.bfloat16
 VMEM = pl.BlockSpec(memory_space=pltpu.VMEM)
@@ -56,22 +56,19 @@
         copy = pltpu.make_async_copy(source, target, sems.at[slot])
         copy.start()
         copies.append(copy)
-    half = sides[0].shape[1]
+    sessions, half = sides[0].shape
     for index, side in enumerate(sides):
         column = core if index % 2 == 0 else 1 - core
-        inputs[index // 2, :, pl.ds(pl.multiple_of(column * half, half), half)] = side[...]
+        first = index // 2 * sessions
+        inputs[first : first + sessions, pl.ds(pl.multiple_of(column * half, half), half)] = side[...]
     for copy in copies:
         copy.wait()
 
     @pl.loop(0, taps)
     def _(tap):
-        weights = kernel_rows[tap]
-        home_ref[tap] = jnp.dot(inputs[0], weights, preferred_element_type=F32).astype(
-            home_ref.dtype
-        )
-        away_ref[tap] = jnp.dot(inputs[1], weights, preferred_element_type=F32).astype(
-            away_ref.dtype
-        )
+        product = jnp.dot(inputs[...], kernel_rows[tap], preferred_element_type=F32)
+        home_ref[tap] = product[:sessions].astype(home_ref.dtype)
+        away_ref[tap] = product[sessions:].astype(away_ref.dtype)
 
 
 def spread_taps(sides, blocks, steps, count, home_type):
@@ -87,10 +84,15 @@
         out_specs=(VMEM, VMEM),
         scratch_shapes=[
             pltpu.VMEM((taps, depth, width), BF16),
-            pltpu.VMEM((2, sessions, depth), BF16),
+            pltpu.VMEM((2 * sessions, depth), BF16),
             pltpu.SemaphoreType.DMA((len(blocks),)),
         ],
         compiler_params=pltpu.CompilerParams(vmem_limit_bytes=VMEM_LIMIT),
+        cost_estimate=pl.CostEstimate(
+            flops=4 * taps * sessions * depth * width,
+            bytes_accessed=2 * taps * depth * width + 4 * sessions * depth + 6 * taps * sessions * width,
+            transcendentals=0,
+        ),
     )(*blocks, *sides)
 
 
@@ -116,7 +118,7 @@
     return pl.pallas_call(
         excite_kernel,
         out_shape=jax.ShapeDtypeStruct(prev.shape, BF16),
-        in_specs=[pl.BlockSpec(memory_space=pltpu.SMEM), VMEM, VMEM, VMEM, VMEM],
+        in_specs=[pl.BlockSpec(memory_space=pltpu.SMEM)] + [VMEM] * 4,
         out_specs=VMEM,
         compiler_params=pltpu.CompilerParams(vmem_limit_bytes=VMEM_LIMIT),
     )(group, own, other, prev, bias)
@@ -202,12 +204,12 @@
 def weave(group, own, other):
     taps, sessions, width = own.shape
     steps, block = 2 * taps, sessions // 4
-    part = pl.BlockSpec((taps, block, width), lambda i: (0, i, 0))
+    taken = pl.BlockSpec((taps, block, width), lambda i: (0, i, 0))
     return pl.pallas_call(
         weave_kernel,
         out_shape=jax.ShapeDtypeStruct((sessions * steps, width), BF16),
         grid=(4,),
-        in_specs=[pl.BlockSpec(memory_space=pltpu.SMEM), part, part],
+        in_specs=[pl.BlockSpec(memory_space=pltpu.SMEM), taken, taken],
         out_specs=pl.BlockSpec((block * steps, width), lambda i: (i, 0)),
         scratch_shapes=[pltpu.VMEM((width // 128, block * steps, 128), F32)],
         compiler_params=pltpu.CompilerParams(vmem_limit_bytes=VMEM_LIMIT),
@@ -272,19 +274,13 @@
         part = lax.dynamic_slice_in_dim(conv_weight, first + group * taps, taps, axis=1)
         halves.append(part.transpose(1, 0, 2))
 
-    if rows % 128 == 0 and count % 2 == 0:
-        up_ring, tail_ring = (Ring(count, own, swap(own, "segment")) for own in halves)
-        up_seen, tail_seen = [up_ring.round()], []
-        tail_seen.append(tail_ring.round(up_seen[0]))
-        for _ in range(2, count // 2):
-            up_seen.append(up_ring.round())
-            tail_seen.append(tail_ring.round())
-        up_ring.round()
-        up_ring.blocks[0] = after(up_ring.blocks[0], tail_seen[-2])
-        first_done, nearly_done = up_seen[0], tail_seen[-1]
+    use_ring = rows % 128 == 0 and count % 2 == 0
+    if use_ring:
+        other = swap(halves[0], "segment")
+        prepared = swap(after(halves[1], other), "segment")
+        up_ring, tail_ring = Ring(count, halves[0], other), Ring(count, halves[1], prepared)
     else:
-        tail_ring = None
-        first_done = nearly_done = halves[0]
+        prepared = halves[1]
 
     portion = sessions // count
     cap = tail_cache.shape[0] // count
@@ -296,7 +292,7 @@
     beside = jnp.concatenate([input_cache, slot_step, filler], axis=1)
     stored = jnp.concatenate([tail_cache, beside], axis=2).reshape(count, cap * half_taps, 2 * width)
     parcel = jnp.concatenate([latent.reshape(count, portion, 2 * width), stored], axis=1)
-    parcel = after(parcel, first_done)
+    parcel = after(parcel, prepared)
     parcel = lax.all_to_all(parcel, "streams", split_axis=0, concat_axis=0, tiled=True)
     handed = parcel[:, :portion].reshape(sessions, 2 * width)
     stored = parcel[:, portion:].reshape(count * cap, half_taps, 2 * width)
@@ -312,16 +308,21 @@
 
     res_theirs = swap(res_weight, "segment")
 
-    if tail_ring is None:
-        whole = [lax.all_gather(own, "streams", axis=1, tiled=True) for own in halves]
-        own_up, away_up = spread_taps(sides, [whole[0]], [None], count, F32)
-        other_up = swap(away_up, "groups")
-        own_tail, away_tail = spread_taps(sides, [whole[1]], [None], count, BF16)
+    if use_ring:
+        for r in range(count // 2):
+            up_ring.round()
+            seen = tail_ring.round(far_half if r == count // 2 - 2 else None)
+            if r == count // 2 - 2:
+                nearly_done = seen
+        up_ring.blocks[0] = after(up_ring.blocks[0], nearly_done)
+        gathered = [(ring.blocks, ring.steps) for ring in (up_ring, tail_ring)]
     else:
-        own_up, away_up = spread_taps(sides, up_ring.blocks, up_ring.steps, count, F32)
-        tail_ring.round(away_up)
-        other_up = swap(after(away_up, nearly_done), "groups")
-        own_tail, away_tail = spread_taps(sides, tail_ring.blocks, tail_ring.steps, count, BF16)
+        gathered = [
+            ([lax.all_gather(own, "streams", axis=1, tiled=True)], [None]) for own in halves
+        ]
+    own_up, away_up = spread_taps(sides, *gathered[0], count, F32)
+    own_tail, away_tail = spread_taps(sides, *gathered[1], count, BF16)
+    other_up = swap(away_up, "groups")
     other_tail = swap(away_tail, "groups")
 
     own_up = after(own_up, (away_tail, res_theirs))

time: 93.1 us -> 91.2 us (0.980)
  waiting for transfers between devices: 41.1 us -> 44 us
  Pallas kernels: 14.8 us -> 13 us
  starting transfers between devices: 31.3 us -> 29.5 us
  local copies, waits for them, and re-layouts: 2.85 us -> 1.77 us
    ppermute x17, waiting for transfers between devices: 14.5 us -> 24.1 us  [swap(): return lax.ppermute(value, axis, [(0, 1), (1, 0)])]
    ppermute x8, waiting for transfers between devices: 26.7 us -> 19.9 us  [round(): item = lax.ppermute(item, ('streams', 'segment'), self.pairs)]
    all_to_all x1, starting transfers between devices: 6.34 us -> 4.79 us  [local(): lax.all_to_all(parcel, 'streams', split_axis=0, concat_axis=0, tiled=True)]
    unnamed x27 -> x23, local copies, waits for them, and re-layouts: 1.21 us -> 0.13 us
    pallas_call x2, Pallas kernels: 6.26 us -> 5.26 us  [spread_taps(): pl.pallas_call(functools.partial(spread_kernel, count, steps), out_shape=...]
  transfers between devices with their start and end apart: 26 -> 26, of which waited for: 14 -> 12; matrix products, arithmetic and copies ran while one was open for 2% -> 2% of each run, Pallas kernels for 13% -> 11%
where the time goes in v3:
time: 91.2 us; the launch traced here: 91 us
  waiting for transfers between devices  44 us (48%)
  starting transfers between devices  29.5 us (32%)
  Pallas kernels  13 us (14%)
  local copies, waits for them, and re-layouts  1.77 us (2%)
  other arithmetic  1.17 us (1%)
  between operations  0.93 us (1%)
    ppermute x17, waiting for transfers between devices, swap(): return lax.ppermute(value, axis, [(0, 1), (1, 0)])  24.1 us
    ppermute x8, waiting for transfers between devices, round(): item = lax.ppermute(item, ('streams', 'segment'), self.pairs)  19.9 us
    ppermute x8, starting transfers between devices, round(): item = lax.ppermute(item, ('streams', 'segment'), self.pairs)  17.5 us
    ppermute x17, starting transfers between devices, swap(): return lax.ppermute(value, axis, [(0, 1), (1, 0)])  7.14 us
    pallas_call x2, Pallas kernels, spread_taps(): pl.pallas_call(functools.partial(spread_kernel, count, steps), out_shape=...  5.26 us
    pallas_call x1, Pallas kernels, residual(): pl.pallas_call(residual_kernel, out_shape=jax.ShapeDtypeStruct((sessions...  5.08 us
    all_to_all x1, starting transfers between devices, local(): lax.all_to_all(parcel, 'streams', split_axis=0, concat_axis=0, tiled=True)  4.79 us
    pallas_call x1, Pallas kernels, weave(): pl.pallas_call(weave_kernel, out_shape=jax.ShapeDtypeStruct((sessions * s...  1.99 us
  transfers between devices with their start and end apart: 26, of which 12 were waited for; matrix products, arithmetic and copies ran while one was open for 2% of the time, Pallas kernels for 11%

profile of v3, /device:TPU:0, one launch (start us, length us, event | category | flops | bytes accessed | tf_op | source)
XLA Modules:
  0.0 91.0 jit_solution(17379917765795196652)
XLA Ops:
  0.6 1.5 %constant_dynamic-slice_fusion.2 = (bf16[128,4,256]{2,1,0:T(4,128)(2,1)S(1)}, bf16[128,4,256]{2,1,0:T(4,128)(2,1)S(1)}) fusion(bf16[128,16,256]{2,1,0:T(8,128)(2,1)} %param.11, s32[]{:T(128)S(6)} %select_n.15, s32[]{:T(128)S(6)} %select_n.14), kind=kLoop, calls=%fused_computation.24 | loop fusion | bytes 1048584 | tf_op jit(solution)/shard_map/dynamic_slice | solution.py:274
  2.1 0.0 copy-start.8
  2.1 0.0 copy-start.5
  2.1 0.0 copy-start.6
  2.2 0.5 collective-permute-start
  2.7 1.2 %collective-permute-done = bf16[4,128,256]{2,1,0:T(8,128)(2,1)S(1)} collective-permute-done((bf16[4,128,256]{2,1,0:T(8,128)(2,1)S(1)}, bf16[4,128,256]{2,1,0:T(8,128)(2,1)S(1)}, u32[]{:S(2)}, u32[]{:S(2)}) %collective-permute-start) | collective-permute-done | bytes 262176 | tf_op jit(solution)/shard_map/ppermute | solution.py:220
  3.9 0.1 pad_maximum_fusion.1
  3.9 3.0 %collective-permute-start.6 = (bf16[2,4,128,256]{3,2,1,0:T(8,128)(2,1)S(1)}, bf16[2,4,128,256]{3,2,1,0:T(8,128)(2,1)}, u32[]{:S(2)}, u32[]{:S(2)}) collective-permute-start(bf16[2,4,128,256]{3,2,1,0:T(8,128)(2,1)S(1)} %pad_maximum_fusion.1), channel_id=1, source_target_pairs={{0,4},{5,1},{4,8},{9,5},{8,12},{13,9},{12,14},{15,13},{14,10},{11,... | collective-permute-start | bytes 1572872 | tf_op jit(solution)/shard_map/ppermute | solution.py:246
  7.0 0.1 collective-permute-start.1
  7.1 0.1 broadcast_in_dim.23
  7.2 0.8 maximum_maximum_fusion
  8.0 0.6 collective-permute-done.1
  8.6 4.8 %all-to-all-start = ((bf16[8,40,512]{2,1,0:T(8,128)(2,1)}), bf16[8,40,512]{2,1,0:T(8,128)(2,1)S(1)}, u32[]{:S(2)}, u32[]{:S(2)}) async-start(bf16[8,40,512]{2,1,0:T(8,128)(2,1)} %maximum_maximum_fusion), calls=%async_computation | async-start | bytes 655360 | tf_op jit(solution)/shard_map/all_to_all | solution.py:296
  13.4 0.1 pad_maximum_fusion
  13.4 2.1 %collective-permute-start.2 = (bf16[2,4,128,256]{3,2,1,0:T(8,128)(2,1)S(1)}, bf16[2,4,128,256]{3,2,1,0:T(8,128)(2,1)S(1)}, u32[]{:S(2)}, u32[]{:S(2)}) collective-permute-start(bf16[2,4,128,256]{3,2,1,0:T(8,128)(2,1)S(1)} %pad_maximum_fusion), channel_id=1, source_target_pairs={{0,4},{5,1},{4,8},{9,5},{8,12},{13,9},{12,14},{15,13},{14,10},{11,... | collective-permute-start | bytes 1572872 | tf_op jit(solution)/shard_map/ppermute | solution.py:246
  15.5 1.5 %collective-permute-start.8 = (bf16[2,4,128,256]{3,2,1,0:T(8,128)(2,1)}, bf16[2,4,128,256]{3,2,1,0:T(8,128)(2,1)}, u32[]{:S(2)}, u32[]{:S(2)}) collective-permute-start(bf16[2,4,128,256]{3,2,1,0:T(8,128)(2,1)} %collective-permute-done.6.refs_1_), channel_id=1, source_target_pairs={{0,4},{5,1},{4,8},{9,5},{8,12},{13,9},{12,14},{15,13},{14,10},{11,... | collective-permute-start | bytes 1572872 | tf_op jit(solution)/shard_map/ppermute | solution.py:246
  17.0 8.9 %collective-permute-done.2.refs_1_ = bf16[2,4,128,256]{3,2,1,0:T(8,128)(2,1)S(1)} collective-permute-done((bf16[2,4,128,256]{3,2,1,0:T(8,128)(2,1)S(1)}, bf16[2,4,128,256]{3,2,1,0:T(8,128)(2,1)S(1)}, u32[]{:S(2)}, u32[]{:S(2)}) %collective-permute-start.2) | collective-permute-done | bytes 524320 | tf_op jit(solution)/shard_map/ppermute | solution.py:246
  25.8 2.1 %collective-permute-start.3 = (bf16[2,4,128,256]{3,2,1,0:T(8,128)(2,1)S(1)}, bf16[2,4,128,256]{3,2,1,0:T(8,128)(2,1)S(1)}, u32[]{:S(2)}, u32[]{:S(2)}) collective-permute-start(bf16[2,4,128,256]{3,2,1,0:T(8,128)(2,1)S(1)} %collective-permute-done.2.refs_1_), channel_id=1, source_target_pairs={{0,4},{5,1},{4,8},{9,5},{8,12},{13,9},{12,14},{15,13},{14,10},{11,... | collective-permute-start | bytes 1572872 | tf_op jit(solution)/shard_map/ppermute | solution.py:246
  28.0 3.5 %collective-permute-done.8.refs_3_ = bf16[2,4,128,256]{3,2,1,0:T(8,128)(2,1)} collective-permute-done((bf16[2,4,128,256]{3,2,1,0:T(8,128)(2,1)}, bf16[2,4,128,256]{3,2,1,0:T(8,128)(2,1)}, u32[]{:S(2)}, u32[]{:S(2)}) %collective-permute-start.8) | collective-permute-done | bytes 524320 | tf_op jit(solution)/shard_map/ppermute | solution.py:246
  31.5 2.1 %collective-permute-start.10 = (bf16[2,4,128,256]{3,2,1,0:T(8,128)(2,1)}, bf16[2,4,128,256]{3,2,1,0:T(8,128)(2,1)S(1)}, u32[]{:S(2)}, u32[]{:S(2)}) collective-permute-start(bf16[2,4,128,256]{3,2,1,0:T(8,128)(2,1)} %collective-permute-done.8.refs_3_), channel_id=1, source_target_pairs={{0,4},{5,1},{4,8},{9,5},{8,12},{13,9},{12,14},{15,13},{14,10},{11,... | collective-permute-start | bytes 1572872 | tf_op jit(solution)/shard_map/ppermute | solution.py:246
  33.7 0.1 fusion.3.refs_9_
  33.8 1.6 %collective-permute-start.4 = (bf16[256,512]{1,0:T(8,128)(2,1)S(1)}, bf16[256,512]{1,0:T(8,128)(2,1)S(1)}, u32[]{:S(2)}, u32[]{:S(2)}) collective-permute-start(bf16[256,512]{1,0:T(8,128)(2,1)S(1)} %fusion.3.refs_9_), channel_id=1, source_target_pairs={{0,16},{16,0},{1,17},{17,1},{2,18},{18,2},{3,19},{19,3},{4,20},{20... | collective-permute-start | bytes 786440 | tf_op jit(solution)/shard_map/ppermute | solution.py:220
  35.4 5.6 %collective-permute-done.4.refs_11_ = bf16[256,512]{1,0:T(8,128)(2,1)S(1)} collective-permute-done((bf16[256,512]{1,0:T(8,128)(2,1)S(1)}, bf16[256,512]{1,0:T(8,128)(2,1)S(1)}, u32[]{:S(2)}, u32[]{:S(2)}) %collective-permute-start.4) | collective-permute-done | bytes 262176 | tf_op jit(solution)/shard_map/ppermute | solution.py:220
  41.1 3.2 %collective-permute-start.5 = (bf16[2,4,128,256]{3,2,1,0:T(8,128)(2,1)S(1)}, bf16[2,4,128,256]{3,2,1,0:T(8,128)(2,1)S(1)}, u32[]{:S(2)}, u32[]{:S(2)}) collective-permute-start(bf16[2,4,128,256]{3,2,1,0:T(8,128)(2,1)S(1)} %collective-permute-done.3.refs_3_), channel_id=1, source_target_pairs={{0,4},{5,1},{4,8},{9,5},{8,12},{13,9},{12,14},{15,13},{14,10},{11,... | collective-permute-start | bytes 1572872 | tf_op jit(solution)/shard_map/ppermute | solution.py:246
  44.3 0.5 collective-permute-start.9
  44.8 1.0 %collective-permute-start.12 = (bf16[2,2,128,256]{3,2,1,0:T(8,128)(2,1)S(1)}, bf16[2,2,128,256]{3,2,1,0:T(8,128)(2,1)S(1)}, u32[]{:S(2)}, u32[]{:S(2)}) collective-permute-start(bf16[2,2,128,256]{3,2,1,0:T(8,128)(2,1)S(1)} %constant_dynamic-slice_fusion.1), channel_id=1, source_target_pairs={{0,4},{5,1},{4,8},{9,5},{8,12},{13,9},{12,14},{15,13},{14,10},{11,... | collective-permute-start | bytes 786440 | tf_op jit(solution)/shard_map/ppermute | solution.py:246
  45.8 0.4 collective-permute-done.14.refs_10_
  46.2 0.1 collective-permute-start.16
  46.3 4.7 %collective-permute-done.5.refs_5_ = bf16[2,4,128,256]{3,2,1,0:T(8,128)(2,1)S(1)} collective-permute-done((bf16[2,4,128,256]{3,2,1,0:T(8,128)(2,1)S(1)}, bf16[2,4,128,256]{3,2,1,0:T(8,128)(2,1)S(1)}, u32[]{:S(2)}, u32[]{:S(2)}) %collective-permute-start.5) | collective-permute-done | bytes 524320 | tf_op jit(solution)/shard_map/ppermute | solution.py:246
  51.0 2.8 %collective-permute-done.12.refs_7_ = bf16[2,2,128,256]{3,2,1,0:T(8,128)(2,1)S(1)} collective-permute-done((bf16[2,2,128,256]{3,2,1,0:T(8,128)(2,1)S(1)}, bf16[2,2,128,256]{3,2,1,0:T(8,128)(2,1)S(1)}, u32[]{:S(2)}, u32[]{:S(2)}) %collective-permute-start.12) | collective-permute-done | bytes 262176 | tf_op jit(solution)/shard_map/ppermute | solution.py:246
  53.8 2.5 %collective-permute-start.19 = (bf16[2,2,128,256]{3,2,1,0:T(8,128)(2,1)S(1)}, bf16[2,2,128,256]{3,2,1,0:T(8,128)(2,1)S(1)}, u32[]{:S(2)}, u32[]{:S(2)}) collective-permute-start(bf16[2,2,128,256]{3,2,1,0:T(8,128)(2,1)S(1)} %constant_dynamic-slice_fusion), channel_id=1, source_target_pairs={{0,4},{5,1},{4,8},{9,5},{8,12},{13,9},{12,14},{15,13},{14,10},{11,... | collective-permute-start | bytes 786440 | tf_op jit(solution)/shard_map/ppermute | solution.py:246
  56.4 0.5 collective-permute-start.18
  56.9 3.0 %shard_map.113 = (f32[4,256,256]{2,1,0:T(8,128)S(1)}, bf16[4,256,256]{2,1,0:T(8,128)(2,1)S(1)}) custom-call(bf16[4,128,256]{2,1,0:T(8,128)(2,1)S(1)} %bitcast.37, bf16[2,4,128,256]{3,2,1,0:T(8,128)(2,1)} %collective-permute-done.6.refs_1_, bf16[2,4,128,256]{3,2,1,0:T(8,128)(2,1)} %collective-permute-done.7.refs_2_, ...), custom_call_target="tpu_custom_call" | custom-call | flops 1073741824 | bytes 4718592 | tf_op jit(solution)/shard_map/pallas_call | solution.py:77
  59.9 1.6 %collective-permute-start.22 = (bf16[4,256,256]{2,1,0:T(8,128)(2,1)S(1)}, bf16[4,256,256]{2,1,0:T(8,128)(2,1)S(1)}, u32[]{:S(2)}, u32[]{:S(2)}) collective-permute-start(bf16[4,256,256]{2,1,0:T(8,128)(2,1)S(1)} %get-tuple-element.20), channel_id=1, source_target_pairs={{0,16},{16,0},{1,17},{17,1},{2,18},{18,2},{3,19},{19,3},{4,20},{20... | collective-permute-start | bytes 1572872 | tf_op jit(solution)/shard_map/ppermute | solution.py:220
  61.5 0.1 collective-permute-start.21
  61.6 0.5 collective-permute-start.20
  62.1 0.1 convert_reduce_fusion
  62.3 0.6 fusion.prev_ref
  62.9 0.8 collective-permute-done.20.refs_8_
  63.7 2.3 %shard_map.114 = (bf16[4,256,256]{2,1,0:T(8,128)(2,1)S(1)}, bf16[4,256,256]{2,1,0:T(8,128)(2,1)S(1)}) custom-call(bf16[4,128,256]{2,1,0:T(8,128)(2,1)S(1)} %bitcast.34, bf16[2,4,128,256]{3,2,1,0:T(8,128)(2,1)S(1)} %collective-permute-done.2.refs_1_, bf16[2,4,128,256]{3,2,1,0:T(8,128)(2,1)S(1)} %collective-permute-done.16.refs_2_, ...), custom_call_target="tpu_custom_call" | custom-call | flops 1073741824 | bytes 4718592 | tf_op jit(solution)/shard_map/pallas_call | solution.py:77
  66.0 7.9 %collective-permute-done.22.other_ref = bf16[4,256,256]{2,1,0:T(8,128)(2,1)S(1)} collective-permute-done((bf16[4,256,256]{2,1,0:T(8,128)(2,1)S(1)}, bf16[4,256,256]{2,1,0:T(8,128)(2,1)S(1)}, u32[]{:S(2)}, u32[]{:S(2)}) %collective-permute-start.22) | collective-permute-done | bytes 524320 | tf_op jit(solution)/shard_map/ppermute | solution.py:220
  73.9 0.7 shard_map.115.mine_ref
  74.6 0.1 collective-permute-start.23
  74.7 1.6 %collective-permute-start.24 = (bf16[4,256,256]{2,1,0:T(8,128)(2,1)S(1)}, bf16[4,256,256]{2,1,0:T(8,128)(2,1)S(1)}, u32[]{:S(2)}, u32[]{:S(2)}) collective-permute-start(bf16[4,256,256]{2,1,0:T(8,128)(2,1)S(1)} %get-tuple-element.18), channel_id=1, source_target_pairs={{0,16},{16,0},{1,17},{17,1},{2,18},{18,2},{3,19},{19,3},{4,20},{20... | collective-permute-start | bytes 1572872 | tf_op jit(solution)/shard_map/ppermute | solution.py:220
  76.2 1.4 %collective-permute-done.23.theirs_ref = bf16[10,256,256]{2,1,0:T(8,128)(2,1)S(1)} collective-permute-done((bf16[10,256,256]{2,1,0:T(8,128)(2,1)S(1)}, bf16[10,256,256]{2,1,0:T(8,128)(2,1)S(1)}, u32[]{:S(2)}, u32[]{:S(2)}) %collective-permute-start.23) | collective-permute-done | bytes 1310752 | tf_op jit(solution)/shard_map/ppermute | solution.py:220
  77.7 5.1 %shard_map.116 = bf16[2048,256]{1,0:T(8,128)(2,1)} custom-call(s32[1]{0:T(128)} %bitcast.group_ref, f32[4,256,256]{2,1,0:T(8,128)S(1)} %get-tuple-element.19.own_ref, bf16[4,256,256]{2,1,0:T(8,128)(2,1)S(1)} %collective-permute-done.22.other_ref, bf16[10,256,256]{2,1,0:T(8,128)(2,1)S(1)} %fusion.prev_ref, bf16[10,256,256]{2,1,0:T(8,128)(2,1)S(1)} %shard_map.115.mine_ref, ...), custom_call_target="tpu_custom_call" | custom-call | tf_op jit(solution)/shard_map/pallas_call | solution.py:177
  82.8 6.2 %collective-permute-done.24.other_ref = bf16[4,256,256]{2,1,0:T(8,128)(2,1)S(1)} collective-permute-done((bf16[4,256,256]{2,1,0:T(8,128)(2,1)S(1)}, bf16[4,256,256]{2,1,0:T(8,128)(2,1)S(1)}, u32[]{:S(2)}, u32[]{:S(2)}) %collective-permute-start.24) | collective-permute-done | bytes 524320 | tf_op jit(solution)/shard_map/ppermute | solution.py:220
  89.0 2.0 %shard_map.117 = bf16[2048,256]{1,0:T(8,128)(2,1)} custom-call(s32[1]{0:T(128)} %bitcast.group_ref, bf16[4,256,256]{2,1,0:T(8,128)(2,1)S(1)} %get-tuple-element.22.own_ref, bf16[4,256,256]{2,1,0:T(8,128)(2,1)S(1)} %collective-permute-done.24.other_ref), custom_call_target="tpu_custom_call" | custom-call | tf_op jit(solution)/shard_map/pallas_call | solution.py:208
  (49 shorter events, 0.3 us)
Async XLA Ops:
  2.1 4.9 %copy-start.8 = (s32[8]{0:T(128)S(1)}, s32[8]{0:T(128)}, u32[]{:S(2)}) copy-start(s32[8]{0:T(128)} %param.15) | copy-start | bytes 100
  2.1 5.0 %copy-start.5 = (bf16[256,512]{1,0:T(8,128)(2,1)S(1)}, bf16[256,512]{1,0:T(8,128)(2,1)}, u32[]{:S(2)}) copy-start(bf16[256,512]{1,0:T(8,128)(2,1)} %param.10) | copy-start | bytes 786436
  2.1 5.0 %copy-start.6 = (bf16[8,8,256]{2,1,0:T(8,128)(2,1)S(1)}, bf16[8,8,256]{2,1,0:T(8,128)(2,1)}, u32[]{:S(2)}) copy-start(bf16[8,8,256]{2,1,0:T(8,128)(2,1)} %param.13) | copy-start | bytes 98308
  2.2 5.0 %copy-start.7 = (bf16[8,2,256]{2,1,0:T(2,128)(2,1)S(1)}, bf16[8,2,256]{2,1,0:T(2,128)(2,1)}, u32[]{:S(2)}) copy-start(bf16[8,2,256]{2,1,0:T(2,128)(2,1)} %param.14) | copy-start | bytes 24580
  2.2 1.7 %collective-permute-start = (bf16[4,128,256]{2,1,0:T(8,128)(2,1)S(1)}, bf16[4,128,256]{2,1,0:T(8,128)(2,1)S(1)}, u32[]{:S(2)}, u32[]{:S(2)}) collective-permute-start(bf16[4,128,256]{2,1,0:T(8,128)(2,1)S(1)} %bitcast.35), channel_id=1, source_target_pairs={{0,1},{1,0},{2,3},{3,2},{4,5},{5,4},{6,7},{7,6},{8,9},{9,8},{10,11... | collective-permute-start | bytes 786440 | tf_op jit(solution)/shard_map/ppermute | solution.py:220
  3.9 11.6 %collective-permute-start.6 = (bf16[2,4,128,256]{3,2,1,0:T(8,128)(2,1)S(1)}, bf16[2,4,128,256]{3,2,1,0:T(8,128)(2,1)}, u32[]{:S(2)}, u32[]{:S(2)}) collective-permute-start(bf16[2,4,128,256]{3,2,1,0:T(8,128)(2,1)S(1)} %pad_maximum_fusion.1), channel_id=1, source_target_pairs={{0,4},{5,1},{4,8},{9,5},{8,12},{13,9},{12,14},{15,13},{14,10},{11,... | collective-permute-start | bytes 1572872 | tf_op jit(solution)/shard_map/ppermute | solution.py:246
  7.0 1.6 %collective-permute-start.1 = (bf16[4,128,256]{2,1,0:T(8,128)(2,1)S(1)}, bf16[4,128,256]{2,1,0:T(8,128)(2,1)S(1)}, u32[]{:S(2)}, u32[]{:S(2)}) collective-permute-start(bf16[4,128,256]{2,1,0:T(8,128)(2,1)S(1)} %bitcast.32), channel_id=1, source_target_pairs={{0,1},{1,0},{2,3},{3,2},{4,5},{5,4},{6,7},{7,6},{8,9},{9,8},{10,11... | collective-permute-start | bytes 786440 | tf_op jit(solution)/shard_map/ppermute | solution.py:220
  8.6 19.4 %all-to-all-start = ((bf16[8,40,512]{2,1,0:T(8,128)(2,1)}), bf16[8,40,512]{2,1,0:T(8,128)(2,1)S(1)}, u32[]{:S(2)}, u32[]{:S(2)}) async-start(bf16[8,40,512]{2,1,0:T(8,128)(2,1)} %maximum_maximum_fusion), calls=%async_computation | async-start | bytes 655360 | tf_op jit(solution)/shard_map/all_to_all | solution.py:296
  13.4 12.4 %collective-permute-start.2 = (bf16[2,4,128,256]{3,2,1,0:T(8,128)(2,1)S(1)}, bf16[2,4,128,256]{3,2,1,0:T(8,128)(2,1)S(1)}, u32[]{:S(2)}, u32[]{:S(2)}) collective-permute-start(bf16[2,4,128,256]{3,2,1,0:T(8,128)(2,1)S(1)} %pad_maximum_fusion), channel_id=1, source_target_pairs={{0,4},{5,1},{4,8},{9,5},{8,12},{13,9},{12,14},{15,13},{14,10},{11,... | collective-permute-start | bytes 1572872 | tf_op jit(solution)/shard_map/ppermute | solution.py:246
  15.5 16.0 %collective-permute-start.8 = (bf16[2,4,128,256]{3,2,1,0:T(8,128)(2,1)}, bf16[2,4,128,256]{3,2,1,0:T(8,128)(2,1)}, u32[]{:S(2)}, u32[]{:S(2)}) collective-permute-start(bf16[2,4,128,256]{3,2,1,0:T(8,128)(2,1)} %collective-permute-done.6.refs_1_), channel_id=1, source_target_pairs={{0,4},{5,1},{4,8},{9,5},{8,12},{13,9},{12,14},{15,13},{14,10},{11,... | collective-permute-start | bytes 1572872 | tf_op jit(solution)/shard_map/ppermute | solution.py:246
  25.8 15.2 %collective-permute-start.3 = (bf16[2,4,128,256]{3,2,1,0:T(8,128)(2,1)S(1)}, bf16[2,4,128,256]{3,2,1,0:T(8,128)(2,1)S(1)}, u32[]{:S(2)}, u32[]{:S(2)}) collective-permute-start(bf16[2,4,128,256]{3,2,1,0:T(8,128)(2,1)S(1)} %collective-permute-done.2.refs_1_), channel_id=1, source_target_pairs={{0,4},{5,1},{4,8},{9,5},{8,12},{13,9},{12,14},{15,13},{14,10},{11,... | collective-permute-start | bytes 1572872 | tf_op jit(solution)/shard_map/ppermute | solution.py:246
  31.5 13.3 %collective-permute-start.10 = (bf16[2,4,128,256]{3,2,1,0:T(8,128)(2,1)}, bf16[2,4,128,256]{3,2,1,0:T(8,128)(2,1)S(1)}, u32[]{:S(2)}, u32[]{:S(2)}) collective-permute-start(bf16[2,4,128,256]{3,2,1,0:T(8,128)(2,1)} %collective-permute-done.8.refs_3_), channel_id=1, source_target_pairs={{0,4},{5,1},{4,8},{9,5},{8,12},{13,9},{12,14},{15,13},{14,10},{11,... | collective-permute-start | bytes 1572872 | tf_op jit(solution)/shard_map/ppermute | solution.py:246
  33.8 7.2 %collective-permute-start.4 = (bf16[256,512]{1,0:T(8,128)(2,1)S(1)}, bf16[256,512]{1,0:T(8,128)(2,1)S(1)}, u32[]{:S(2)}, u32[]{:S(2)}) collective-permute-start(bf16[256,512]{1,0:T(8,128)(2,1)S(1)} %fusion.3.refs_9_), channel_id=1, source_target_pairs={{0,16},{16,0},{1,17},{17,1},{2,18},{18,2},{3,19},{19,3},{4,20},{20... | collective-permute-start | bytes 786440 | tf_op jit(solution)/shard_map/ppermute | solution.py:220
  35.4 10.4 %collective-permute-start.7 = (bf16[2,4,128,256]{3,2,1,0:T(8,128)(2,1)}, bf16[2,4,128,256]{3,2,1,0:T(8,128)(2,1)}, u32[]{:S(2)}, u32[]{:S(2)}) collective-permute-start(bf16[2,4,128,256]{3,2,1,0:T(8,128)(2,1)} %collective-permute-done.6.refs_1_), channel_id=1, source_target_pairs={{0,1},{1,0},{2,3},{3,2},{4,5},{5,4},{6,7},{7,6},{8,9},{9,8},{10,11... | collective-permute-start | bytes 1572872 | tf_op jit(solution)/shard_map/ppermute | solution.py:220
  41.1 9.9 %collective-permute-start.5 = (bf16[2,4,128,256]{3,2,1,0:T(8,128)(2,1)S(1)}, bf16[2,4,128,256]{3,2,1,0:T(8,128)(2,1)S(1)}, u32[]{:S(2)}, u32[]{:S(2)}) collective-permute-start(bf16[2,4,128,256]{3,2,1,0:T(8,128)(2,1)S(1)} %collective-permute-done.3.refs_3_), channel_id=1, source_target_pairs={{0,4},{5,1},{4,8},{9,5},{8,12},{13,9},{12,14},{15,13},{14,10},{11,... | collective-permute-start | bytes 1572872 | tf_op jit(solution)/shard_map/ppermute | solution.py:246
  44.3 1.9 %collective-permute-start.14 = (bf16[256,512]{1,0:T(8,128)(2,1)S(1)}, bf16[256,512]{1,0:T(8,128)(2,1)S(1)}, u32[]{:S(2)}, u32[]{:S(2)}) collective-permute-start(bf16[256,512]{1,0:T(8,128)(2,1)S(1)} %fusion.3.refs_9_), channel_id=1, source_target_pairs={{0,1},{1,0},{2,3},{3,2},{4,5},{5,4},{6,7},{7,6},{8,9},{9,8},{10,11... | collective-permute-start | bytes 786440 | tf_op jit(solution)/shard_map/ppermute | solution.py:220
  44.3 12.1 %collective-permute-start.9 = (bf16[2,4,128,256]{3,2,1,0:T(8,128)(2,1)}, bf16[2,4,128,256]{3,2,1,0:T(8,128)(2,1)S(1)}, u32[]{:S(2)}, u32[]{:S(2)}) collective-permute-start(bf16[2,4,128,256]{3,2,1,0:T(8,128)(2,1)} %collective-permute-done.8.refs_3_), channel_id=1, source_target_pairs={{0,1},{1,0},{2,3},{3,2},{4,5},{5,4},{6,7},{7,6},{8,9},{9,8},{10,11... | collective-permute-start | bytes 1572872 | tf_op jit(solution)/shard_map/ppermute | solution.py:220
  44.8 9.0 %collective-permute-start.12 = (bf16[2,2,128,256]{3,2,1,0:T(8,128)(2,1)S(1)}, bf16[2,2,128,256]{3,2,1,0:T(8,128)(2,1)S(1)}, u32[]{:S(2)}, u32[]{:S(2)}) collective-permute-start(bf16[2,2,128,256]{3,2,1,0:T(8,128)(2,1)S(1)} %constant_dynamic-slice_fusion.1), channel_id=1, source_target_pairs={{0,4},{5,1},{4,8},{9,5},{8,12},{13,9},{12,14},{15,13},{14,10},{11,... | collective-permute-start | bytes 786440 | tf_op jit(solution)/shard_map/ppermute | solution.py:246
  45.8 11.1 %collective-permute-start.11 = (bf16[2,4,128,256]{3,2,1,0:T(8,128)(2,1)S(1)}, bf16[2,4,128,256]{3,2,1,0:T(8,128)(2,1)S(1)}, u32[]{:S(2)}, u32[]{:S(2)}) collective-permute-start(bf16[2,4,128,256]{3,2,1,0:T(8,128)(2,1)S(1)} %collective-permute-done.10.refs_5_), channel_id=1, source_target_pairs={{0,1},{1,0},{2,3},{3,2},{4,5},{5,4},{6,7},{7,6},{8,9},{9,8},{10,11... | collective-permute-start | bytes 1572872 | tf_op jit(solution)/shard_map/ppermute | solution.py:220
  46.2 15.3 %collective-permute-start.16 = (bf16[2,4,128,256]{3,2,1,0:T(8,128)(2,1)S(1)}, bf16[2,4,128,256]{3,2,1,0:T(8,128)(2,1)S(1)}, u32[]{:S(2)}, u32[]{:S(2)}) collective-permute-start(bf16[2,4,128,256]{3,2,1,0:T(8,128)(2,1)S(1)} %collective-permute-done.2.refs_1_), channel_id=1, source_target_pairs={{0,1},{1,0},{2,3},{3,2},{4,5},{5,4},{6,7},{7,6},{8,9},{9,8},{10,11... | collective-permute-start | bytes 1572872 | tf_op jit(solution)/shard_map/ppermute | solution.py:220
  51.0 2.8 %collective-permute-start.15 = (bf16[256,512]{1,0:T(8,128)(2,1)S(1)}, bf16[256,512]{1,0:T(8,128)(2,1)S(1)}, u32[]{:S(2)}, u32[]{:S(2)}) collective-permute-start(bf16[256,512]{1,0:T(8,128)(2,1)S(1)} %collective-permute-done.4.refs_11_), channel_id=1, source_target_pairs={{0,1},{1,0},{2,3},{3,2},{4,5},{5,4},{6,7},{7,6},{8,9},{9,8},{10,11... | collective-permute-start | bytes 786440 | tf_op jit(solution)/shard_map/ppermute | solution.py:220
  53.8 2.6 %collective-permute-start.13 = (bf16[2,2,128,256]{3,2,1,0:T(8,128)(2,1)S(1)}, bf16[2,2,128,256]{3,2,1,0:T(8,128)(2,1)S(1)}, u32[]{:S(2)}, u32[]{:S(2)}) collective-permute-start(bf16[2,2,128,256]{3,2,1,0:T(8,128)(2,1)S(1)} %collective-permute-done.12.refs_7_), channel_id=1, source_target_pairs={{0,1},{1,0},{2,3},{3,2},{4,5},{5,4},{6,7},{7,6},{8,9},{9,8},{10,11... | collective-permute-start | bytes 786440 | tf_op jit(solution)/shard_map/ppermute | solution.py:220
  53.8 7.7 %copy-start = (bf16[3,256,256]{2,1,0:T(8,128)(2,1)S(1)}, bf16[3,256,256]{2,1,0:T(8,128)(2,1)}, u32[]{:S(2)}) copy-start(bf16[3,256,256]{2,1,0:T(8,128)(2,1)} %res_mine_ref.1) | copy-start | bytes 1179652
  53.8 7.8 %collective-permute-start.19 = (bf16[2,2,128,256]{3,2,1,0:T(8,128)(2,1)S(1)}, bf16[2,2,128,256]{3,2,1,0:T(8,128)(2,1)S(1)}, u32[]{:S(2)}, u32[]{:S(2)}) collective-permute-start(bf16[2,2,128,256]{3,2,1,0:T(8,128)(2,1)S(1)} %constant_dynamic-slice_fusion), channel_id=1, source_target_pairs={{0,4},{5,1},{4,8},{9,5},{8,12},{13,9},{12,14},{15,13},{14,10},{11,... | collective-permute-start | bytes 786440 | tf_op jit(solution)/shard_map/ppermute | solution.py:246
  56.4 6.5 %collective-permute-start.17 = (bf16[2,4,128,256]{3,2,1,0:T(8,128)(2,1)S(1)}, bf16[2,4,128,256]{3,2,1,0:T(8,128)(2,1)S(1)}, u32[]{:S(2)}, u32[]{:S(2)}) collective-permute-start(bf16[2,4,128,256]{3,2,1,0:T(8,128)(2,1)S(1)} %collective-permute-done.3.refs_3_), channel_id=1, source_target_pairs={{0,1},{1,0},{2,3},{3,2},{4,5},{5,4},{6,7},{7,6},{8,9},{9,8},{10,11... | collective-permute-start | bytes 1572872 | tf_op jit(solution)/shard_map/ppermute | solution.py:220
  56.4 7.3 %collective-permute-start.18 = (bf16[2,4,128,256]{3,2,1,0:T(8,128)(2,1)S(1)}, bf16[2,4,128,256]{3,2,1,0:T(8,128)(2,1)S(1)}, u32[]{:S(2)}, u32[]{:S(2)}) collective-permute-start(bf16[2,4,128,256]{3,2,1,0:T(8,128)(2,1)S(1)} %collective-permute-done.5.refs_5_), channel_id=1, source_target_pairs={{0,1},{1,0},{2,3},{3,2},{4,5},{5,4},{6,7},{7,6},{8,9},{9,8},{10,11... | collective-permute-start | bytes 1572872 | tf_op jit(solution)/shard_map/ppermute | solution.py:220
  59.9 14.0 %collective-permute-start.22 = (bf16[4,256,256]{2,1,0:T(8,128)(2,1)S(1)}, bf16[4,256,256]{2,1,0:T(8,128)(2,1)S(1)}, u32[]{:S(2)}, u32[]{:S(2)}) collective-permute-start(bf16[4,256,256]{2,1,0:T(8,128)(2,1)S(1)} %get-tuple-element.20), channel_id=1, source_target_pairs={{0,16},{16,0},{1,17},{17,1},{2,18},{18,2},{3,19},{19,3},{4,20},{20... | collective-permute-start | bytes 1572872 | tf_op jit(solution)/shard_map/ppermute | solution.py:220
  61.5 4.5 %collective-permute-start.21 = (bf16[3,256,256]{2,1,0:T(8,128)(2,1)S(1)}, bf16[3,256,256]{2,1,0:T(8,128)(2,1)S(1)}, u32[]{:S(2)}, u32[]{:S(2)}) collective-permute-start(bf16[3,256,256]{2,1,0:T(8,128)(2,1)S(1)} %copy-done), channel_id=1, source_target_pairs={{0,1},{1,0},{2,3},{3,2},{4,5},{5,4},{6,7},{7,6},{8,9},{9,8},{10,11... | collective-permute-start | bytes 1179656 | tf_op jit(solution)/shard_map/ppermute | solution.py:220
  61.6 2.1 %collective-permute-start.20 = (bf16[2,2,128,256]{3,2,1,0:T(8,128)(2,1)S(1)}, bf16[2,2,128,256]{3,2,1,0:T(8,128)(2,1)S(1)}, u32[]{:S(2)}, u32[]{:S(2)}) collective-permute-start(bf16[2,2,128,256]{3,2,1,0:T(8,128)(2,1)S(1)} %collective-permute-done.19.refs_7_), channel_id=1, source_target_pairs={{0,1},{1,0},{2,3},{3,2},{4,5},{5,4},{6,7},{7,6},{8,9},{9,8},{10,11... | collective-permute-start | bytes 786440 | tf_op jit(solution)/shard_map/ppermute | solution.py:220
  62.9 11.0 %copy-start.2 = (f32[256]{0:T(256)S(1)}, f32[256]{0:T(256)}, u32[]{:S(2)}) copy-start(f32[256]{0:T(256)} %param.12) | copy-start | bytes 3076
  73.9 3.8 %copy-start.1 = (bf16[256,256]{1,0:T(8,128)(2,1)S(1)}, bf16[256,256]{1,0:T(8,128)(2,1)}, u32[]{:S(2)}) copy-start(bf16[256,256]{1,0:T(8,128)(2,1)} %skip_ref.1) | copy-start | bytes 393220
  73.9 3.8 %copy-start.3 = (f32[256]{0:T(256)S(1)}, f32[256]{0:T(256)}, u32[]{:S(2)}) copy-start(f32[256]{0:T(256)} %param.17) | copy-start | bytes 3076
  73.9 3.8 %copy-start.4 = (f32[256]{0:T(256)S(1)}, f32[256]{0:T(256)}, u32[]{:S(2)}) copy-start(f32[256]{0:T(256)} %param.19) | copy-start | bytes 3076
  74.6 3.1 %collective-permute-start.23 = (bf16[10,256,256]{2,1,0:T(8,128)(2,1)S(1)}, bf16[10,256,256]{2,1,0:T(8,128)(2,1)S(1)}, u32[]{:S(2)}, u32[]{:S(2)}) collective-permute-start(bf16[10,256,256]{2,1,0:T(8,128)(2,1)S(1)} %shard_map.115.mine_ref), channel_id=1, source_target_pairs={{0,1},{1,0},{2,3},{3,2},{4,5},{5,4},{6,7},{7,6},{8,9},{9,8},{10,11... | collective-permute-start | bytes 3932168 | tf_op jit(solution)/shard_map/ppermute | solution.py:220
  74.7 14.3 %collective-permute-start.24 = (bf16[4,256,256]{2,1,0:T(8,128)(2,1)S(1)}, bf16[4,256,256]{2,1,0:T(8,128)(2,1)S(1)}, u32[]{:S(2)}, u32[]{:S(2)}) collective-permute-start(bf16[4,256,256]{2,1,0:T(8,128)(2,1)S(1)} %get-tuple-element.18), channel_id=1, source_target_pairs={{0,16},{16,0},{1,17},{17,1},{2,18},{18,2},{3,19},{19,3},{4,20},{20... | collective-permute-start | bytes 1572872 | tf_op jit(solution)/shard_map/ppermute | solution.py:220

commit v4 on v3

--- a/solution.py
+++ b/solution.py
@@ -298,8 +298,9 @@
     stored = parcel[:, portion:].reshape(count * cap, half_taps, 2 * width)
 
     near_half = apply_elu(handed.astype(F32)).astype(BF16)
-    far_half = swap(near_half, "groups")
-    sides = (near_half, swap(near_half, "segment"), far_half, swap(far_half, "segment"))
+    near_other = swap(near_half, "segment")
+    far_half = swap(after(near_half, near_other), "groups")
+    sides = (near_half, near_other, far_half, swap(far_half, "segment"))
 
     slots = stored[:, history, width:].astype(jnp.int32)[:, :1]
     one_hot = (slots == jnp.arange(sessions, dtype=jnp.int32)[None, :]).astype(BF16)
@@ -310,8 +311,8 @@
 
     if use_ring:
         for r in range(count // 2):
-            up_ring.round()
-            seen = tail_ring.round(far_half if r == count // 2 - 2 else None)
+            up_ring.round(far_half if r == count // 2 - 1 else None)
+            seen = tail_ring.round()
             if r == count // 2 - 2:
                 nearly_done = seen
         up_ring.blocks[0] = after(up_ring.blocks[0], nearly_done)

time: 91.2 us -> 90.4 us (level)
  waiting for transfers between devices: 44 us -> 36.7 us
  starting transfers between devices: 29.5 us -> 33.4 us
  local copies, waits for them, and re-layouts: 1.77 us -> 4.05 us
    ppermute x17, waiting for transfers between devices: 24.1 us -> 17.9 us  [swap(): return lax.ppermute(value, axis, [(0, 1), (1, 0)])]
    ppermute x17, starting transfers between devices: 7.14 us -> 9.59 us  [swap(): return lax.ppermute(value, axis, [(0, 1), (1, 0)])]
    ppermute x8, starting transfers between devices: 17.5 us -> 19 us  [round(): item = lax.ppermute(item, ('streams', 'segment'), self.pairs)]
    ppermute x8, waiting for transfers between devices: 19.9 us -> 18.8 us  [round(): item = lax.ppermute(item, ('streams', 'segment'), self.pairs)]
  transfers between devices with their start and end apart: 26 -> 26, of which waited for: 12 -> 13; matrix products, arithmetic and copies ran while one was open for 2% -> 5% of each run, Pallas kernels for 11% -> 12%
where the time goes in v4:
time: 90.4 us; the launch traced here: 89.9 us
  waiting for transfers between devices  36.7 us (41%)
  starting transfers between devices  33.4 us (37%)
  Pallas kernels  13.1 us (14%)
  local copies, waits for them, and re-layouts  4.05 us (4%)
  other arithmetic  1.17 us (1%)
  between operations  0.94 us (1%)
    ppermute x8, starting transfers between devices, round(): item = lax.ppermute(item, ('streams', 'segment'), self.pairs)  19 us
    ppermute x8, waiting for transfers between devices, round(): item = lax.ppermute(item, ('streams', 'segment'), self.pairs)  18.8 us
    ppermute x17, waiting for transfers between devices, swap(): return lax.ppermute(value, axis, [(0, 1), (1, 0)])  17.9 us
    ppermute x17, starting transfers between devices, swap(): return lax.ppermute(value, axis, [(0, 1), (1, 0)])  9.59 us
    pallas_call x2, Pallas kernels, spread_taps(): pl.pallas_call(functools.partial(spread_kernel, count, steps), out_shape=...  5.3 us
    pallas_call x1, Pallas kernels, residual(): pl.pallas_call(residual_kernel, out_shape=jax.ShapeDtypeStruct((sessions...  5.08 us
    all_to_all x1, starting transfers between devices, local(): lax.all_to_all(parcel, 'streams', split_axis=0, concat_axis=0, tiled=True)  4.79 us
    pallas_call x1, Pallas kernels, weave(): pl.pallas_call(weave_kernel, out_shape=jax.ShapeDtypeStruct((sessions * s...  1.99 us
  transfers between devices with their start and end apart: 26, of which 13 were waited for; matrix products, arithmetic and copies ran while one was open for 5% of the time, Pallas kernels for 12%

profile of v4, /device:TPU:0, one launch (start us, length us, event | category | flops | bytes accessed | tf_op | source)
XLA Modules:
  0.0 89.9 jit_solution(18331706680858634774)
XLA Ops:
  0.6 1.5 %constant_dynamic-slice_fusion.2 = (bf16[128,4,256]{2,1,0:T(4,128)(2,1)S(1)}, bf16[128,4,256]{2,1,0:T(4,128)(2,1)S(1)}) fusion(bf16[128,16,256]{2,1,0:T(8,128)(2,1)} %param.11, s32[]{:T(128)S(6)} %select_n.15, s32[]{:T(128)S(6)} %select_n.14), kind=kLoop, calls=%fused_computation.24 | loop fusion | bytes 1048584 | tf_op jit(solution)/shard_map/dynamic_slice | solution.py:274
  2.2 0.5 collective-permute-start
  2.7 1.2 %collective-permute-done = bf16[4,128,256]{2,1,0:T(8,128)(2,1)S(1)} collective-permute-done((bf16[4,128,256]{2,1,0:T(8,128)(2,1)S(1)}, bf16[4,128,256]{2,1,0:T(8,128)(2,1)S(1)}, u32[]{:S(2)}, u32[]{:S(2)}) %collective-permute-start) | collective-permute-done | bytes 262176 | tf_op jit(solution)/shard_map/ppermute | solution.py:220
  3.9 3.0 %collective-permute-start.5 = (bf16[2,4,128,256]{3,2,1,0:T(8,128)(2,1)S(1)}, bf16[2,4,128,256]{3,2,1,0:T(8,128)(2,1)}, u32[]{:S(2)}, u32[]{:S(2)}) collective-permute-start(bf16[2,4,128,256]{3,2,1,0:T(8,128)(2,1)S(1)} %pad_maximum_fusion.1), channel_id=1, source_target_pairs={{0,4},{5,1},{4,8},{9,5},{8,12},{13,9},{12,14},{15,13},{14,10},{11,... | collective-permute-start | bytes 1572872 | tf_op jit(solution)/shard_map/ppermute | solution.py:246
  7.1 0.1 broadcast_in_dim.23
  7.2 0.8 maximum_maximum_fusion
  8.0 0.6 collective-permute-done.1
  8.6 4.8 %all-to-all-start = ((bf16[8,40,512]{2,1,0:T(8,128)(2,1)}), bf16[8,40,512]{2,1,0:T(8,128)(2,1)S(1)}, u32[]{:S(2)}, u32[]{:S(2)}) async-start(bf16[8,40,512]{2,1,0:T(8,128)(2,1)} %maximum_maximum_fusion), calls=%async_computation | async-start | bytes 655360 | tf_op jit(solution)/shard_map/all_to_all | solution.py:296
  13.4 2.1 %collective-permute-start.2 = (bf16[2,4,128,256]{3,2,1,0:T(8,128)(2,1)S(1)}, bf16[2,4,128,256]{3,2,1,0:T(8,128)(2,1)S(1)}, u32[]{:S(2)}, u32[]{:S(2)}) collective-permute-start(bf16[2,4,128,256]{3,2,1,0:T(8,128)(2,1)S(1)} %pad_maximum_fusion), channel_id=1, source_target_pairs={{0,4},{5,1},{4,8},{9,5},{8,12},{13,9},{12,14},{15,13},{14,10},{11,... | collective-permute-start | bytes 1572872 | tf_op jit(solution)/shard_map/ppermute | solution.py:246
  15.5 1.5 %collective-permute-start.7 = (bf16[2,4,128,256]{3,2,1,0:T(8,128)(2,1)}, bf16[2,4,128,256]{3,2,1,0:T(8,128)(2,1)}, u32[]{:S(2)}, u32[]{:S(2)}) collective-permute-start(bf16[2,4,128,256]{3,2,1,0:T(8,128)(2,1)} %collective-permute-done.5.refs_1_), channel_id=1, source_target_pairs={{0,4},{5,1},{4,8},{9,5},{8,12},{13,9},{12,14},{15,13},{14,10},{11,... | collective-permute-start | bytes 1572872 | tf_op jit(solution)/shard_map/ppermute | solution.py:246
  17.0 8.9 %collective-permute-done.2.refs_1_ = bf16[2,4,128,256]{3,2,1,0:T(8,128)(2,1)S(1)} collective-permute-done((bf16[2,4,128,256]{3,2,1,0:T(8,128)(2,1)S(1)}, bf16[2,4,128,256]{3,2,1,0:T(8,128)(2,1)S(1)}, u32[]{:S(2)}, u32[]{:S(2)}) %collective-permute-start.2) | collective-permute-done | bytes 524320 | tf_op jit(solution)/shard_map/ppermute | solution.py:246
  25.8 2.1 %collective-permute-start.3 = (bf16[2,4,128,256]{3,2,1,0:T(8,128)(2,1)S(1)}, bf16[2,4,128,256]{3,2,1,0:T(8,128)(2,1)S(1)}, u32[]{:S(2)}, u32[]{:S(2)}) collective-permute-start(bf16[2,4,128,256]{3,2,1,0:T(8,128)(2,1)S(1)} %collective-permute-done.2.refs_1_), channel_id=1, source_target_pairs={{0,4},{5,1},{4,8},{9,5},{8,12},{13,9},{12,14},{15,13},{14,10},{11,... | collective-permute-start | bytes 1572872 | tf_op jit(solution)/shard_map/ppermute | solution.py:246
  28.0 3.5 %collective-permute-done.7.refs_3_ = bf16[2,4,128,256]{3,2,1,0:T(8,128)(2,1)} collective-permute-done((bf16[2,4,128,256]{3,2,1,0:T(8,128)(2,1)}, bf16[2,4,128,256]{3,2,1,0:T(8,128)(2,1)}, u32[]{:S(2)}, u32[]{:S(2)}) %collective-permute-start.7) | collective-permute-done | bytes 524320 | tf_op jit(solution)/shard_map/ppermute | solution.py:246
  31.5 2.1 %collective-permute-start.9 = (bf16[2,4,128,256]{3,2,1,0:T(8,128)(2,1)}, bf16[2,4,128,256]{3,2,1,0:T(8,128)(2,1)S(1)}, u32[]{:S(2)}, u32[]{:S(2)}) collective-permute-start(bf16[2,4,128,256]{3,2,1,0:T(8,128)(2,1)} %collective-permute-done.7.refs_3_), channel_id=1, source_target_pairs={{0,4},{5,1},{4,8},{9,5},{8,12},{13,9},{12,14},{15,13},{14,10},{11,... | collective-permute-start | bytes 1572872 | tf_op jit(solution)/shard_map/ppermute | solution.py:246
  33.7 0.1 fusion.3.refs_9_
  33.8 0.1 collective-permute-start.11
  33.9 0.5 collective-permute-start.6
  34.4 1.0 %collective-permute-done.11.refs_10_ = bf16[256,512]{1,0:T(8,128)(2,1)S(1)} collective-permute-done((bf16[256,512]{1,0:T(8,128)(2,1)S(1)}, bf16[256,512]{1,0:T(8,128)(2,1)S(1)}, u32[]{:S(2)}, u32[]{:S(2)}) %collective-permute-start.11) | collective-permute-done | bytes 262176 | tf_op jit(solution)/shard_map/ppermute | solution.py:220
  35.4 1.5 %collective-permute-start.12 = (bf16[256,512]{1,0:T(8,128)(2,1)S(1)}, bf16[256,512]{1,0:T(8,128)(2,1)S(1)}, u32[]{:S(2)}, u32[]{:S(2)}) collective-permute-start(bf16[256,512]{1,0:T(8,128)(2,1)S(1)} %fusion.3.refs_9_), channel_id=1, source_target_pairs={{0,16},{16,0},{1,17},{17,1},{2,18},{18,2},{3,19},{19,3},{4,20},{20... | collective-permute-start | bytes 786440 | tf_op jit(solution)/shard_map/ppermute | solution.py:220
  37.0 0.1 collective-permute-done.3.refs_3_
  37.1 2.4 %collective-permute-start.4 = (bf16[2,4,128,256]{3,2,1,0:T(8,128)(2,1)S(1)}, bf16[2,4,128,256]{3,2,1,0:T(8,128)(2,1)S(1)}, u32[]{:S(2)}, u32[]{:S(2)}) collective-permute-start(bf16[2,4,128,256]{3,2,1,0:T(8,128)(2,1)S(1)} %collective-permute-done.3.refs_3_), channel_id=1, source_target_pairs={{0,4},{5,1},{4,8},{9,5},{8,12},{13,9},{12,14},{15,13},{14,10},{11,... | collective-permute-start | bytes 1572872 | tf_op jit(solution)/shard_map/ppermute | solution.py:246
  39.5 3.2 %collective-permute-done.9.refs_5_ = bf16[2,4,128,256]{3,2,1,0:T(8,128)(2,1)S(1)} collective-permute-done((bf16[2,4,128,256]{3,2,1,0:T(8,128)(2,1)}, bf16[2,4,128,256]{3,2,1,0:T(8,128)(2,1)S(1)}, u32[]{:S(2)}, u32[]{:S(2)}) %collective-permute-start.9) | collective-permute-done | bytes 524320 | tf_op jit(solution)/shard_map/ppermute | solution.py:246
  42.7 1.1 %collective-permute-done.12.refs_11_ = bf16[256,512]{1,0:T(8,128)(2,1)S(1)} collective-permute-done((bf16[256,512]{1,0:T(8,128)(2,1)S(1)}, bf16[256,512]{1,0:T(8,128)(2,1)S(1)}, u32[]{:S(2)}, u32[]{:S(2)}) %collective-permute-start.12) | collective-permute-done | bytes 262176 | tf_op jit(solution)/shard_map/ppermute | solution.py:220
  43.8 2.5 %collective-permute-start.13 = (bf16[2,2,128,256]{3,2,1,0:T(8,128)(2,1)S(1)}, bf16[2,2,128,256]{3,2,1,0:T(8,128)(2,1)S(1)}, u32[]{:S(2)}, u32[]{:S(2)}) collective-permute-start(bf16[2,2,128,256]{3,2,1,0:T(8,128)(2,1)S(1)} %constant_dynamic-slice_fusion.1), channel_id=1, source_target_pairs={{0,4},{5,1},{4,8},{9,5},{8,12},{13,9},{12,14},{15,13},{14,10},{11,... | collective-permute-start | bytes 786440 | tf_op jit(solution)/shard_map/ppermute | solution.py:246
  46.3 0.5 collective-permute-start.16
  46.8 1.5 %collective-permute-done.4.refs_5_ = bf16[2,4,128,256]{3,2,1,0:T(8,128)(2,1)S(1)} collective-permute-done((bf16[2,4,128,256]{3,2,1,0:T(8,128)(2,1)S(1)}, bf16[2,4,128,256]{3,2,1,0:T(8,128)(2,1)S(1)}, u32[]{:S(2)}, u32[]{:S(2)}) %collective-permute-start.4) | collective-permute-done | bytes 524320 | tf_op jit(solution)/shard_map/ppermute | solution.py:246
  48.3 1.2 %collective-permute-start.15 = (bf16[256,512]{1,0:T(8,128)(2,1)S(1)}, bf16[256,512]{1,0:T(8,128)(2,1)S(1)}, u32[]{:S(2)}, u32[]{:S(2)}) collective-permute-start(bf16[256,512]{1,0:T(8,128)(2,1)S(1)} %collective-permute-done.12.refs_11_), channel_id=1, source_target_pairs={{0,1},{1,0},{2,3},{3,2},{4,5},{5,4},{6,7},{7,6},{8,9},{9,8},{10,11... | collective-permute-start | bytes 786440 | tf_op jit(solution)/shard_map/ppermute | solution.py:220
  49.5 1.6 %collective-permute-done.13.refs_7_ = bf16[2,2,128,256]{3,2,1,0:T(8,128)(2,1)S(1)} collective-permute-done((bf16[2,2,128,256]{3,2,1,0:T(8,128)(2,1)S(1)}, bf16[2,2,128,256]{3,2,1,0:T(8,128)(2,1)S(1)}, u32[]{:S(2)}, u32[]{:S(2)}) %collective-permute-start.13) | collective-permute-done | bytes 262176 | tf_op jit(solution)/shard_map/ppermute | solution.py:246
  51.1 0.9 %collective-permute-start.14 = (bf16[2,2,128,256]{3,2,1,0:T(8,128)(2,1)S(1)}, bf16[2,2,128,256]{3,2,1,0:T(8,128)(2,1)S(1)}, u32[]{:S(2)}, u32[]{:S(2)}) collective-permute-start(bf16[2,2,128,256]{3,2,1,0:T(8,128)(2,1)S(1)} %collective-permute-done.13.refs_7_), channel_id=1, source_target_pairs={{0,1},{1,0},{2,3},{3,2},{4,5},{5,4},{6,7},{7,6},{8,9},{9,8},{10,11... | collective-permute-start | bytes 786440 | tf_op jit(solution)/shard_map/ppermute | solution.py:220
  52.0 3.3 %collective-permute-start.19 = (bf16[2,2,128,256]{3,2,1,0:T(8,128)(2,1)S(1)}, bf16[2,2,128,256]{3,2,1,0:T(8,128)(2,1)S(1)}, u32[]{:S(2)}, u32[]{:S(2)}) collective-permute-start(bf16[2,2,128,256]{3,2,1,0:T(8,128)(2,1)S(1)} %constant_dynamic-slice_fusion), channel_id=1, source_target_pairs={{0,4},{5,1},{4,8},{9,5},{8,12},{13,9},{12,14},{15,13},{14,10},{11,... | collective-permute-start | bytes 786440 | tf_op jit(solution)/shard_map/ppermute | solution.py:246
  55.3 0.5 collective-permute-start.18
  55.8 3.0 %shard_map.113 = (f32[4,256,256]{2,1,0:T(8,128)S(1)}, bf16[4,256,256]{2,1,0:T(8,128)(2,1)S(1)}) custom-call(bf16[4,128,256]{2,1,0:T(8,128)(2,1)S(1)} %bitcast.37, bf16[2,4,128,256]{3,2,1,0:T(8,128)(2,1)} %collective-permute-done.5.refs_1_, bf16[2,4,128,256]{3,2,1,0:T(8,128)(2,1)} %collective-permute-done.6.refs_2_, ...), custom_call_target="tpu_custom_call" | custom-call | flops 1073741824 | bytes 4718592 | tf_op jit(solution)/shard_map/pallas_call | solution.py:77
  58.8 1.6 %collective-permute-start.22 = (bf16[4,256,256]{2,1,0:T(8,128)(2,1)S(1)}, bf16[4,256,256]{2,1,0:T(8,128)(2,1)S(1)}, u32[]{:S(2)}, u32[]{:S(2)}) collective-permute-start(bf16[4,256,256]{2,1,0:T(8,128)(2,1)S(1)} %get-tuple-element.22), channel_id=1, source_target_pairs={{0,16},{16,0},{1,17},{17,1},{2,18},{18,2},{3,19},{19,3},{4,20},{20... | collective-permute-start | bytes 1572872 | tf_op jit(solution)/shard_map/ppermute | solution.py:220
  60.4 0.8 slice.28
  61.2 0.1 collective-permute-start.21
  61.3 0.5 collective-permute-start.20
  61.8 0.1 convert_reduce_fusion
  61.9 0.8 slice.26
  62.7 0.8 slice.27
  63.5 0.6 fusion.prev_ref
  64.1 2.3 %shard_map.114 = (bf16[4,256,256]{2,1,0:T(8,128)(2,1)S(1)}, bf16[4,256,256]{2,1,0:T(8,128)(2,1)S(1)}) custom-call(bf16[4,128,256]{2,1,0:T(8,128)(2,1)S(1)} %bitcast.34, bf16[2,4,128,256]{3,2,1,0:T(8,128)(2,1)S(1)} %collective-permute-done.2.refs_1_, bf16[2,4,128,256]{3,2,1,0:T(8,128)(2,1)S(1)} %collective-permute-done.16.refs_2_, ...), custom_call_target="tpu_custom_call" | custom-call | flops 1073741824 | bytes 4718592 | tf_op jit(solution)/shard_map/pallas_call | solution.py:77
  66.5 6.3 %collective-permute-done.22.other_ref = bf16[4,256,256]{2,1,0:T(8,128)(2,1)S(1)} collective-permute-done((bf16[4,256,256]{2,1,0:T(8,128)(2,1)S(1)}, bf16[4,256,256]{2,1,0:T(8,128)(2,1)S(1)}, u32[]{:S(2)}, u32[]{:S(2)}) %collective-permute-start.22) | collective-permute-done | bytes 524320 | tf_op jit(solution)/shard_map/ppermute | solution.py:220
  72.8 0.7 shard_map.115.mine_ref
  73.6 1.6 %collective-permute-start.24 = (bf16[4,256,256]{2,1,0:T(8,128)(2,1)S(1)}, bf16[4,256,256]{2,1,0:T(8,128)(2,1)S(1)}, u32[]{:S(2)}, u32[]{:S(2)}) collective-permute-start(bf16[4,256,256]{2,1,0:T(8,128)(2,1)S(1)} %get-tuple-element.20), channel_id=1, source_target_pairs={{0,16},{16,0},{1,17},{17,1},{2,18},{18,2},{3,19},{19,3},{4,20},{20... | collective-permute-start | bytes 1572872 | tf_op jit(solution)/shard_map/ppermute | solution.py:220
  75.2 1.4 %collective-permute-done.23.theirs_ref = bf16[10,256,256]{2,1,0:T(8,128)(2,1)S(1)} collective-permute-done((bf16[10,256,256]{2,1,0:T(8,128)(2,1)S(1)}, bf16[10,256,256]{2,1,0:T(8,128)(2,1)S(1)}, u32[]{:S(2)}, u32[]{:S(2)}) %collective-permute-start.23) | collective-permute-done | bytes 1310752 | tf_op jit(solution)/shard_map/ppermute | solution.py:220
  76.6 5.1 %shard_map.116 = bf16[2048,256]{1,0:T(8,128)(2,1)} custom-call(s32[1]{0:T(128)} %bitcast.group_ref, f32[4,256,256]{2,1,0:T(8,128)S(1)} %get-tuple-element.21.own_ref, bf16[4,256,256]{2,1,0:T(8,128)(2,1)S(1)} %collective-permute-done.22.other_ref, bf16[10,256,256]{2,1,0:T(8,128)(2,1)S(1)} %fusion.prev_ref, bf16[10,256,256]{2,1,0:T(8,128)(2,1)S(1)} %shard_map.115.mine_ref, ...), custom_call_target="tpu_custom_call" | custom-call | tf_op jit(solution)/shard_map/pallas_call | solution.py:177
  81.7 6.2 %collective-permute-done.24.other_ref = bf16[4,256,256]{2,1,0:T(8,128)(2,1)S(1)} collective-permute-done((bf16[4,256,256]{2,1,0:T(8,128)(2,1)S(1)}, bf16[4,256,256]{2,1,0:T(8,128)(2,1)S(1)}, u32[]{:S(2)}, u32[]{:S(2)}) %collective-permute-start.24) | collective-permute-done | bytes 524320 | tf_op jit(solution)/shard_map/ppermute | solution.py:220
  87.9 2.0 %shard_map.117 = bf16[2048,256]{1,0:T(8,128)(2,1)} custom-call(s32[1]{0:T(128)} %bitcast.group_ref, bf16[4,256,256]{2,1,0:T(8,128)(2,1)S(1)} %get-tuple-element.24.own_ref, bf16[4,256,256]{2,1,0:T(8,128)(2,1)S(1)} %collective-permute-done.24.other_ref), custom_call_target="tpu_custom_call" | custom-call | tf_op jit(solution)/shard_map/pallas_call | solution.py:208
  (51 shorter events, 0.5 us)
Async XLA Ops:
  2.1 4.9 %copy-start.9 = (s32[8]{0:T(128)S(1)}, s32[8]{0:T(128)}, u32[]{:S(2)}) copy-start(s32[8]{0:T(128)} %param.15) | copy-start | bytes 100
  2.1 5.0 %copy-start.6 = (bf16[256,512]{1,0:T(8,128)(2,1)S(1)}, bf16[256,512]{1,0:T(8,128)(2,1)}, u32[]{:S(2)}) copy-start(bf16[256,512]{1,0:T(8,128)(2,1)} %param.10) | copy-start | bytes 786436
  2.1 5.0 %copy-start.7 = (bf16[8,8,256]{2,1,0:T(8,128)(2,1)S(1)}, bf16[8,8,256]{2,1,0:T(8,128)(2,1)}, u32[]{:S(2)}) copy-start(bf16[8,8,256]{2,1,0:T(8,128)(2,1)} %param.13) | copy-start | bytes 98308
  2.2 5.0 %copy-start.8 = (bf16[8,2,256]{2,1,0:T(2,128)(2,1)S(1)}, bf16[8,2,256]{2,1,0:T(2,128)(2,1)}, u32[]{:S(2)}) copy-start(bf16[8,2,256]{2,1,0:T(2,128)(2,1)} %param.14) | copy-start | bytes 24580
  2.2 1.7 %collective-permute-start = (bf16[4,128,256]{2,1,0:T(8,128)(2,1)S(1)}, bf16[4,128,256]{2,1,0:T(8,128)(2,1)S(1)}, u32[]{:S(2)}, u32[]{:S(2)}) collective-permute-start(bf16[4,128,256]{2,1,0:T(8,128)(2,1)S(1)} %bitcast.35), channel_id=1, source_target_pairs={{0,1},{1,0},{2,3},{3,2},{4,5},{5,4},{6,7},{7,6},{8,9},{9,8},{10,11... | collective-permute-start | bytes 786440 | tf_op jit(solution)/shard_map/ppermute | solution.py:220
  3.9 11.6 %collective-permute-start.5 = (bf16[2,4,128,256]{3,2,1,0:T(8,128)(2,1)S(1)}, bf16[2,4,128,256]{3,2,1,0:T(8,128)(2,1)}, u32[]{:S(2)}, u32[]{:S(2)}) collective-permute-start(bf16[2,4,128,256]{3,2,1,0:T(8,128)(2,1)S(1)} %pad_maximum_fusion.1), channel_id=1, source_target_pairs={{0,4},{5,1},{4,8},{9,5},{8,12},{13,9},{12,14},{15,13},{14,10},{11,... | collective-permute-start | bytes 1572872 | tf_op jit(solution)/shard_map/ppermute | solution.py:246
  7.0 1.6 %collective-permute-start.1 = (bf16[4,128,256]{2,1,0:T(8,128)(2,1)S(1)}, bf16[4,128,256]{2,1,0:T(8,128)(2,1)S(1)}, u32[]{:S(2)}, u32[]{:S(2)}) collective-permute-start(bf16[4,128,256]{2,1,0:T(8,128)(2,1)S(1)} %bitcast.32), channel_id=1, source_target_pairs={{0,1},{1,0},{2,3},{3,2},{4,5},{5,4},{6,7},{7,6},{8,9},{9,8},{10,11... | collective-permute-start | bytes 786440 | tf_op jit(solution)/shard_map/ppermute | solution.py:220
  8.6 19.4 %all-to-all-start = ((bf16[8,40,512]{2,1,0:T(8,128)(2,1)}), bf16[8,40,512]{2,1,0:T(8,128)(2,1)S(1)}, u32[]{:S(2)}, u32[]{:S(2)}) async-start(bf16[8,40,512]{2,1,0:T(8,128)(2,1)} %maximum_maximum_fusion), calls=%async_computation | async-start | bytes 655360 | tf_op jit(solution)/shard_map/all_to_all | solution.py:296
  13.4 12.4 %collective-permute-start.2 = (bf16[2,4,128,256]{3,2,1,0:T(8,128)(2,1)S(1)}, bf16[2,4,128,256]{3,2,1,0:T(8,128)(2,1)S(1)}, u32[]{:S(2)}, u32[]{:S(2)}) collective-permute-start(bf16[2,4,128,256]{3,2,1,0:T(8,128)(2,1)S(1)} %pad_maximum_fusion), channel_id=1, source_target_pairs={{0,4},{5,1},{4,8},{9,5},{8,12},{13,9},{12,14},{15,13},{14,10},{11,... | collective-permute-start | bytes 1572872 | tf_op jit(solution)/shard_map/ppermute | solution.py:246
  15.5 16.0 %collective-permute-start.7 = (bf16[2,4,128,256]{3,2,1,0:T(8,128)(2,1)}, bf16[2,4,128,256]{3,2,1,0:T(8,128)(2,1)}, u32[]{:S(2)}, u32[]{:S(2)}) collective-permute-start(bf16[2,4,128,256]{3,2,1,0:T(8,128)(2,1)} %collective-permute-done.5.refs_1_), channel_id=1, source_target_pairs={{0,4},{5,1},{4,8},{9,5},{8,12},{13,9},{12,14},{15,13},{14,10},{11,... | collective-permute-start | bytes 1572872 | tf_op jit(solution)/shard_map/ppermute | solution.py:246
  25.8 11.2 %collective-permute-start.3 = (bf16[2,4,128,256]{3,2,1,0:T(8,128)(2,1)S(1)}, bf16[2,4,128,256]{3,2,1,0:T(8,128)(2,1)S(1)}, u32[]{:S(2)}, u32[]{:S(2)}) collective-permute-start(bf16[2,4,128,256]{3,2,1,0:T(8,128)(2,1)S(1)} %collective-permute-done.2.refs_1_), channel_id=1, source_target_pairs={{0,4},{5,1},{4,8},{9,5},{8,12},{13,9},{12,14},{15,13},{14,10},{11,... | collective-permute-start | bytes 1572872 | tf_op jit(solution)/shard_map/ppermute | solution.py:246
  28.0 9.0 %copy-start.5 = (bf16[8,40,512]{2,1,0:T(8,128)(2,1)}, bf16[8,40,512]{2,1,0:T(8,128)(2,1)S(1)}, u32[]{:S(2)}) copy-start(bf16[8,40,512]{2,1,0:T(8,128)(2,1)S(1)} %all-to-all-done) | copy-start | bytes 983044
  31.5 11.1 %collective-permute-start.9 = (bf16[2,4,128,256]{3,2,1,0:T(8,128)(2,1)}, bf16[2,4,128,256]{3,2,1,0:T(8,128)(2,1)S(1)}, u32[]{:S(2)}, u32[]{:S(2)}) collective-permute-start(bf16[2,4,128,256]{3,2,1,0:T(8,128)(2,1)} %collective-permute-done.7.refs_3_), channel_id=1, source_target_pairs={{0,4},{5,1},{4,8},{9,5},{8,12},{13,9},{12,14},{15,13},{14,10},{11,... | collective-permute-start | bytes 1572872 | tf_op jit(solution)/shard_map/ppermute | solution.py:246
  33.8 1.6 %collective-permute-start.11 = (bf16[256,512]{1,0:T(8,128)(2,1)S(1)}, bf16[256,512]{1,0:T(8,128)(2,1)S(1)}, u32[]{:S(2)}, u32[]{:S(2)}) collective-permute-start(bf16[256,512]{1,0:T(8,128)(2,1)S(1)} %fusion.3.refs_9_), channel_id=1, source_target_pairs={{0,1},{1,0},{2,3},{3,2},{4,5},{5,4},{6,7},{7,6},{8,9},{9,8},{10,11... | collective-permute-start | bytes 786440 | tf_op jit(solution)/shard_map/ppermute | solution.py:220
  33.9 12.4 %collective-permute-start.6 = (bf16[2,4,128,256]{3,2,1,0:T(8,128)(2,1)}, bf16[2,4,128,256]{3,2,1,0:T(8,128)(2,1)}, u32[]{:S(2)}, u32[]{:S(2)}) collective-permute-start(bf16[2,4,128,256]{3,2,1,0:T(8,128)(2,1)} %collective-permute-done.5.refs_1_), channel_id=1, source_target_pairs={{0,1},{1,0},{2,3},{3,2},{4,5},{5,4},{6,7},{7,6},{8,9},{9,8},{10,11... | collective-permute-start | bytes 1572872 | tf_op jit(solution)/shard_map/ppermute | solution.py:220
  35.4 8.3 %collective-permute-start.12 = (bf16[256,512]{1,0:T(8,128)(2,1)S(1)}, bf16[256,512]{1,0:T(8,128)(2,1)S(1)}, u32[]{:S(2)}, u32[]{:S(2)}) collective-permute-start(bf16[256,512]{1,0:T(8,128)(2,1)S(1)} %fusion.3.refs_9_), channel_id=1, source_target_pairs={{0,16},{16,0},{1,17},{17,1},{2,18},{18,2},{3,19},{19,3},{4,20},{20... | collective-permute-start | bytes 786440 | tf_op jit(solution)/shard_map/ppermute | solution.py:220
  37.1 11.2 %collective-permute-start.4 = (bf16[2,4,128,256]{3,2,1,0:T(8,128)(2,1)S(1)}, bf16[2,4,128,256]{3,2,1,0:T(8,128)(2,1)S(1)}, u32[]{:S(2)}, u32[]{:S(2)}) collective-permute-start(bf16[2,4,128,256]{3,2,1,0:T(8,128)(2,1)S(1)} %collective-permute-done.3.refs_3_), channel_id=1, source_target_pairs={{0,4},{5,1},{4,8},{9,5},{8,12},{13,9},{12,14},{15,13},{14,10},{11,... | collective-permute-start | bytes 1572872 | tf_op jit(solution)/shard_map/ppermute | solution.py:246
  39.4 12.6 %collective-permute-start.8 = (bf16[2,4,128,256]{3,2,1,0:T(8,128)(2,1)}, bf16[2,4,128,256]{3,2,1,0:T(8,128)(2,1)S(1)}, u32[]{:S(2)}, u32[]{:S(2)}) collective-permute-start(bf16[2,4,128,256]{3,2,1,0:T(8,128)(2,1)} %collective-permute-done.7.refs_3_), channel_id=1, source_target_pairs={{0,1},{1,0},{2,3},{3,2},{4,5},{5,4},{6,7},{7,6},{8,9},{9,8},{10,11... | collective-permute-start | bytes 1572872 | tf_op jit(solution)/shard_map/ppermute | solution.py:220
  43.8 7.3 %collective-permute-start.13 = (bf16[2,2,128,256]{3,2,1,0:T(8,128)(2,1)S(1)}, bf16[2,2,128,256]{3,2,1,0:T(8,128)(2,1)S(1)}, u32[]{:S(2)}, u32[]{:S(2)}) collective-permute-start(bf16[2,2,128,256]{3,2,1,0:T(8,128)(2,1)S(1)} %constant_dynamic-slice_fusion.1), channel_id=1, source_target_pairs={{0,4},{5,1},{4,8},{9,5},{8,12},{13,9},{12,14},{15,13},{14,10},{11,... | collective-permute-start | bytes 786440 | tf_op jit(solution)/shard_map/ppermute | solution.py:246
  46.3 9.6 %collective-permute-start.10 = (bf16[2,4,128,256]{3,2,1,0:T(8,128)(2,1)S(1)}, bf16[2,4,128,256]{3,2,1,0:T(8,128)(2,1)S(1)}, u32[]{:S(2)}, u32[]{:S(2)}) collective-permute-start(bf16[2,4,128,256]{3,2,1,0:T(8,128)(2,1)S(1)} %collective-permute-done.9.refs_5_), channel_id=1, source_target_pairs={{0,1},{1,0},{2,3},{3,2},{4,5},{5,4},{6,7},{7,6},{8,9},{9,8},{10,11... | collective-permute-start | bytes 1572872 | tf_op jit(solution)/shard_map/ppermute | solution.py:220
  46.3 14.9 %collective-permute-start.16 = (bf16[2,4,128,256]{3,2,1,0:T(8,128)(2,1)S(1)}, bf16[2,4,128,256]{3,2,1,0:T(8,128)(2,1)S(1)}, u32[]{:S(2)}, u32[]{:S(2)}) collective-permute-start(bf16[2,4,128,256]{3,2,1,0:T(8,128)(2,1)S(1)} %collective-permute-done.2.refs_1_), channel_id=1, source_target_pairs={{0,1},{1,0},{2,3},{3,2},{4,5},{5,4},{6,7},{7,6},{8,9},{9,8},{10,11... | collective-permute-start | bytes 1572872 | tf_op jit(solution)/shard_map/ppermute | solution.py:220
  48.3 7.0 %collective-permute-start.15 = (bf16[256,512]{1,0:T(8,128)(2,1)S(1)}, bf16[256,512]{1,0:T(8,128)(2,1)S(1)}, u32[]{:S(2)}, u32[]{:S(2)}) collective-permute-start(bf16[256,512]{1,0:T(8,128)(2,1)S(1)} %collective-permute-done.12.refs_11_), channel_id=1, source_target_pairs={{0,1},{1,0},{2,3},{3,2},{4,5},{5,4},{6,7},{7,6},{8,9},{9,8},{10,11... | collective-permute-start | bytes 786440 | tf_op jit(solution)/shard_map/ppermute | solution.py:220
  51.1 4.2 %collective-permute-start.14 = (bf16[2,2,128,256]{3,2,1,0:T(8,128)(2,1)S(1)}, bf16[2,2,128,256]{3,2,1,0:T(8,128)(2,1)S(1)}, u32[]{:S(2)}, u32[]{:S(2)}) collective-permute-start(bf16[2,2,128,256]{3,2,1,0:T(8,128)(2,1)S(1)} %collective-permute-done.13.refs_7_), channel_id=1, source_target_pairs={{0,1},{1,0},{2,3},{3,2},{4,5},{5,4},{6,7},{7,6},{8,9},{9,8},{10,11... | collective-permute-start | bytes 786440 | tf_op jit(solution)/shard_map/ppermute | solution.py:220
  52.0 9.2 %copy-start = (bf16[3,256,256]{2,1,0:T(8,128)(2,1)S(1)}, bf16[3,256,256]{2,1,0:T(8,128)(2,1)}, u32[]{:S(2)}) copy-start(bf16[3,256,256]{2,1,0:T(8,128)(2,1)} %res_mine_ref.1) | copy-start | bytes 1179652
  52.0 9.3 %collective-permute-start.19 = (bf16[2,2,128,256]{3,2,1,0:T(8,128)(2,1)S(1)}, bf16[2,2,128,256]{3,2,1,0:T(8,128)(2,1)S(1)}, u32[]{:S(2)}, u32[]{:S(2)}) collective-permute-start(bf16[2,2,128,256]{3,2,1,0:T(8,128)(2,1)S(1)} %constant_dynamic-slice_fusion), channel_id=1, source_target_pairs={{0,4},{5,1},{4,8},{9,5},{8,12},{13,9},{12,14},{15,13},{14,10},{11,... | collective-permute-start | bytes 786440 | tf_op jit(solution)/shard_map/ppermute | solution.py:246
  55.3 8.8 %collective-permute-start.17 = (bf16[2,4,128,256]{3,2,1,0:T(8,128)(2,1)S(1)}, bf16[2,4,128,256]{3,2,1,0:T(8,128)(2,1)S(1)}, u32[]{:S(2)}, u32[]{:S(2)}) collective-permute-start(bf16[2,4,128,256]{3,2,1,0:T(8,128)(2,1)S(1)} %collective-permute-done.3.refs_3_), channel_id=1, source_target_pairs={{0,1},{1,0},{2,3},{3,2},{4,5},{5,4},{6,7},{7,6},{8,9},{9,8},{10,11... | collective-permute-start | bytes 1572872 | tf_op jit(solution)/shard_map/ppermute | solution.py:220
  55.3 8.8 %collective-permute-start.18 = (bf16[2,4,128,256]{3,2,1,0:T(8,128)(2,1)S(1)}, bf16[2,4,128,256]{3,2,1,0:T(8,128)(2,1)S(1)}, u32[]{:S(2)}, u32[]{:S(2)}) collective-permute-start(bf16[2,4,128,256]{3,2,1,0:T(8,128)(2,1)S(1)} %collective-permute-done.4.refs_5_), channel_id=1, source_target_pairs={{0,1},{1,0},{2,3},{3,2},{4,5},{5,4},{6,7},{7,6},{8,9},{9,8},{10,11... | collective-permute-start | bytes 1572872 | tf_op jit(solution)/shard_map/ppermute | solution.py:220
  58.8 14.0 %collective-permute-start.22 = (bf16[4,256,256]{2,1,0:T(8,128)(2,1)S(1)}, bf16[4,256,256]{2,1,0:T(8,128)(2,1)S(1)}, u32[]{:S(2)}, u32[]{:S(2)}) collective-permute-start(bf16[4,256,256]{2,1,0:T(8,128)(2,1)S(1)} %get-tuple-element.22), channel_id=1, source_target_pairs={{0,16},{16,0},{1,17},{17,1},{2,18},{18,2},{3,19},{19,3},{4,20},{20... | collective-permute-start | bytes 1572872 | tf_op jit(solution)/shard_map/ppermute | solution.py:220
  61.2 5.2 %collective-permute-start.21 = (bf16[3,256,256]{2,1,0:T(8,128)(2,1)S(1)}, bf16[3,256,256]{2,1,0:T(8,128)(2,1)S(1)}, u32[]{:S(2)}, u32[]{:S(2)}) collective-permute-start(bf16[3,256,256]{2,1,0:T(8,128)(2,1)S(1)} %copy-done), channel_id=1, source_target_pairs={{0,1},{1,0},{2,3},{3,2},{4,5},{5,4},{6,7},{7,6},{8,9},{9,8},{10,11... | collective-permute-start | bytes 1179656 | tf_op jit(solution)/shard_map/ppermute | solution.py:220
  61.3 2.8 %collective-permute-start.20 = (bf16[2,2,128,256]{3,2,1,0:T(8,128)(2,1)S(1)}, bf16[2,2,128,256]{3,2,1,0:T(8,128)(2,1)S(1)}, u32[]{:S(2)}, u32[]{:S(2)}) collective-permute-start(bf16[2,2,128,256]{3,2,1,0:T(8,128)(2,1)S(1)} %collective-permute-done.19.refs_7_), channel_id=1, source_target_pairs={{0,1},{1,0},{2,3},{3,2},{4,5},{5,4},{6,7},{7,6},{8,9},{9,8},{10,11... | collective-permute-start | bytes 786440 | tf_op jit(solution)/shard_map/ppermute | solution.py:220
  64.1 8.7 %copy-start.2 = (f32[256]{0:T(256)S(1)}, f32[256]{0:T(256)}, u32[]{:S(2)}) copy-start(f32[256]{0:T(256)} %param.12) | copy-start | bytes 3076
  72.8 3.8 %copy-start.1 = (bf16[256,256]{1,0:T(8,128)(2,1)S(1)}, bf16[256,256]{1,0:T(8,128)(2,1)}, u32[]{:S(2)}) copy-start(bf16[256,256]{1,0:T(8,128)(2,1)} %skip_ref.1) | copy-start | bytes 393220
  72.8 3.8 %copy-start.3 = (f32[256]{0:T(256)S(1)}, f32[256]{0:T(256)}, u32[]{:S(2)}) copy-start(f32[256]{0:T(256)} %param.17) | copy-start | bytes 3076
  72.8 3.8 %copy-start.4 = (f32[256]{0:T(256)S(1)}, f32[256]{0:T(256)}, u32[]{:S(2)}) copy-start(f32[256]{0:T(256)} %param.19) | copy-start | bytes 3076
  73.5 3.1 %collective-permute-start.23 = (bf16[10,256,256]{2,1,0:T(8,128)(2,1)S(1)}, bf16[10,256,256]{2,1,0:T(8,128)(2,1)S(1)}, u32[]{:S(2)}, u32[]{:S(2)}) collective-permute-start(bf16[10,256,256]{2,1,0:T(8,128)(2,1)S(1)} %shard_map.115.mine_ref), channel_id=1, source_target_pairs={{0,1},{1,0},{2,3},{3,2},{4,5},{5,4},{6,7},{7,6},{8,9},{9,8},{10,11... | collective-permute-start | bytes 3932168 | tf_op jit(solution)/shard_map/ppermute | solution.py:220
  73.6 14.3 %collective-permute-start.24 = (bf16[4,256,256]{2,1,0:T(8,128)(2,1)S(1)}, bf16[4,256,256]{2,1,0:T(8,128)(2,1)S(1)}, u32[]{:S(2)}, u32[]{:S(2)}) collective-permute-start(bf16[4,256,256]{2,1,0:T(8,128)(2,1)S(1)} %get-tuple-element.20), channel_id=1, source_target_pairs={{0,16},{16,0},{1,17},{17,1},{2,18},{18,2},{3,19},{19,3},{4,20},{20... | collective-permute-start | bytes 1572872 | tf_op jit(solution)/shard_map/ppermute | solution.py:220

commit v5 on v4

--- a/solution.py
+++ b/solution.py
@@ -104,7 +104,7 @@
             yield first + tap, source[tap].astype(F32)
 
 
-def excite_kernel(group_ref, own_ref, other_ref, prev_ref, bias_ref, window_ref):
+def excite_kernel(group_ref, own_ref, other_ref, prev_ref, bias_ref, window_ref, *part_refs):
     steps = 2 * own_ref.shape[0]
     history = prev_ref.shape[0] - steps
     for step in range(history):
@@ -112,35 +112,32 @@
     for step, value in each_step(group_ref[0], own_ref, other_ref):
         up = value + prev_ref[step].astype(F32) + bias_ref[...]
         window_ref[history + step] = apply_elu(up).astype(BF16)
+    first = 0
+    for part_ref in part_refs:
+        part_ref[...] = window_ref[first : first + part_ref.shape[0]]
+        first += part_ref.shape[0]
 
 
 def excite(group, own, other, prev, bias):
+    steps, *rest = prev.shape
+    sizes = (steps,) + tuple((steps + part) // 4 for part in range(4))
     return pl.pallas_call(
         excite_kernel,
-        out_shape=jax.ShapeDtypeStruct(prev.shape, BF16),
+        out_shape=[jax.ShapeDtypeStruct((size, *rest), BF16) for size in sizes],
         in_specs=[pl.BlockSpec(memory_space=pltpu.SMEM)] + [VMEM] * 4,
-        out_specs=VMEM,
+        out_specs=[VMEM] * len(sizes),
         compiler_params=pltpu.CompilerParams(vmem_limit_bytes=VMEM_LIMIT),
     )(group, own, other, prev, bias)
 
 
-def residual_kernel(
-    group_ref,
-    own_ref,
-    other_ref,
-    prev_ref,
-    mine_ref,
-    theirs_ref,
-    bias_ref,
-    res_mine_ref,
-    res_theirs_ref,
-    res_bias_ref,
-    skip_ref,
-    skip_bias_ref,
-    out_ref,
-    products,
-    frames,
-):
+def residual_kernel(group_ref, own_ref, other_ref, prev_ref, mine_ref, *refs):
+    parts, refs = refs[:4], refs[4:]
+    bias_ref, res_mine_ref, res_theirs_ref, res_bias_ref, skip_ref, skip_bias_ref = refs[:6]
+    out_ref, theirs_ref, products, frames = refs[6:]
+    first = 0
+    for part_ref in parts:
+        theirs_ref[first : first + part_ref.shape[0]] = part_ref[...]
+        first += part_ref.shape[0]
     taps, block, width = own_ref.shape
     steps = 2 * taps
     branch = None
@@ -173,7 +170,7 @@
     def blocks(array):
         return pl.BlockSpec((array.shape[0], block, width), lambda i: (0, i, 0))
 
-    arrays = (own, other, prev, mine, theirs)
+    arrays = (own, other, prev, mine, *theirs)
     return pl.pallas_call(
         residual_kernel,
         out_shape=jax.ShapeDtypeStruct((sessions * steps, width), BF16),
@@ -183,6 +180,7 @@
         + [VMEM] * len(parameters),
         out_specs=pl.BlockSpec((block * steps, width), lambda i: (i, 0)),
         scratch_shapes=[
+            pltpu.VMEM((mine.shape[0], block, width), BF16),
             pltpu.VMEM((steps, block, width), F32),
             pltpu.VMEM((width // 128, block * steps, 128), F32),
         ],
@@ -235,7 +233,7 @@
         self.item = jnp.stack([own, other])
         self.blocks, self.steps, self.rounds = [own], [(0, 0)], 0
 
-    def round(self, earlier=None):
+    def round(self, earlier=None, passed_after=None):
         self.rounds += 1
         item = self.item
         if 2 * self.rounds == self.count:
@@ -245,7 +243,8 @@
             item = after(item, earlier)
         item = lax.ppermute(item, ("streams", "segment"), self.pairs)
         self.item = item
-        self.blocks += [item, swap(item, "segment")]
+        given = item if passed_after is None else after(item, passed_after)
+        self.blocks += [item, swap(given, "segment")]
         self.steps += [(self.rounds, 0), (self.rounds, 1)]
         return item
 
@@ -310,26 +309,26 @@
     res_theirs = swap(res_weight, "segment")
 
     if use_ring:
-        for r in range(count // 2):
-            up_ring.round(far_half if r == count // 2 - 1 else None)
-            seen = tail_ring.round()
-            if r == count // 2 - 2:
-                nearly_done = seen
+        last = count // 2 - 1
+        for _ in range(last):
+            up_ring.round()
+            nearly_done = tail_ring.round()
+        up_ring.round(far_half)
         up_ring.blocks[0] = after(up_ring.blocks[0], nearly_done)
-        gathered = [(ring.blocks, ring.steps) for ring in (up_ring, tail_ring)]
+        own_up, away_up = spread_taps(sides, up_ring.blocks, up_ring.steps, count, F32)
+        tail_ring.round(passed_after=away_up)
+        own_tail, away_tail = spread_taps(sides, tail_ring.blocks, tail_ring.steps, count, BF16)
     else:
-        gathered = [
-            ([lax.all_gather(own, "streams", axis=1, tiled=True)], [None]) for own in halves
-        ]
-    own_up, away_up = spread_taps(sides, *gathered[0], count, F32)
-    own_tail, away_tail = spread_taps(sides, *gathered[1], count, BF16)
+        whole = [lax.all_gather(own, "streams", axis=1, tiled=True) for own in halves]
+        own_up, away_up = spread_taps(sides, whole[:1], [None], count, F32)
+        own_tail, away_tail = spread_taps(sides, whole[1:], [None], count, BF16)
     other_up = swap(away_up, "groups")
     other_tail = swap(away_tail, "groups")
 
     own_up = after(own_up, (away_tail, res_theirs))
     bias = conv_bias[None]
-    mine = excite(group_word, own_up, other_up, prev, bias)
-    theirs = swap(mine, "segment")
+    mine, *parts = excite(group_word, own_up, other_up, prev, bias)
+    theirs = [swap(part, "segment") for part in parts]
     decoded = residual(
         group_word,
         own_up,

time: 90.4 us -> 87.4 us (0.967)
  starting transfers between devices: 33.4 us -> 31.4 us
  waiting for transfers between devices: 36.7 us -> 34.7 us
    ppermute x17 -> x20, waiting for transfers between devices: 17.9 us -> 14.8 us  [swap(): return lax.ppermute(value, axis, [(0, 1), (1, 0)])]
    ppermute x17 -> x20, starting transfers between devices: 9.59 us -> 7.6 us  [swap(): return lax.ppermute(value, axis, [(0, 1), (1, 0)])]
    ppermute x8, waiting for transfers between devices: 18.8 us -> 19.9 us  [round(): item = lax.ppermute(item, ('streams', 'segment'), self.pairs)]
  transfers between devices with their start and end apart: 26 -> 29, of which waited for: 13 -> 14; matrix products, arithmetic and copies ran while one was open for 5% -> 5% of each run, Pallas kernels for 12% -> 13%
where the time goes in v5:
time: 87.4 us; the launch traced here: 86.8 us
  waiting for transfers between devices  34.7 us (40%)
  starting transfers between devices  31.4 us (36%)
  Pallas kernels  13.3 us (15%)
  local copies, waits for them, and re-layouts  4.75 us (5%)
  other arithmetic  1.17 us (1%)
  between operations  0.94 us (1%)
    ppermute x8, waiting for transfers between devices, round(): item = lax.ppermute(item, ('streams', 'segment'), self.pairs)  19.9 us
    ppermute x8, starting transfers between devices, round(): item = lax.ppermute(item, ('streams', 'segment'), self.pairs)  19 us
    ppermute x20, waiting for transfers between devices, swap(): return lax.ppermute(value, axis, [(0, 1), (1, 0)])  14.8 us
    ppermute x20, starting transfers between devices, swap(): return lax.ppermute(value, axis, [(0, 1), (1, 0)])  7.6 us
    pallas_call x2, Pallas kernels, spread_taps(): pl.pallas_call(functools.partial(spread_kernel, count, steps), out_shape=...  5.25 us
    pallas_call x1, Pallas kernels, residual(): pl.pallas_call(residual_kernel, out_shape=jax.ShapeDtypeStruct((sessions...  5.14 us
    all_to_all x1, starting transfers between devices, local(): lax.all_to_all(parcel, 'streams', split_axis=0, concat_axis=0, tiled=True)  4.79 us
    pallas_call x1, Pallas kernels, weave(): pl.pallas_call(weave_kernel, out_shape=jax.ShapeDtypeStruct((sessions * s...  1.99 us
  transfers between devices with their start and end apart: 29, of which 14 were waited for; matrix products, arithmetic and copies ran while one was open for 5% of the time, Pallas kernels for 13%

profile of v5, /device:TPU:0, one launch (start us, length us, event | category | flops | bytes accessed | tf_op | source)
XLA Modules:
  0.0 86.8 jit_solution(7008031864003960292)
XLA Ops:
  0.6 1.5 %constant_dynamic-slice_fusion.2 = (bf16[128,4,256]{2,1,0:T(4,128)(2,1)S(1)}, bf16[128,4,256]{2,1,0:T(4,128)(2,1)S(1)}) fusion(bf16[128,16,256]{2,1,0:T(8,128)(2,1)} %param.11, s32[]{:T(128)S(6)} %select_n.15, s32[]{:T(128)S(6)} %select_n.14), kind=kLoop, calls=%fused_computation.24 | loop fusion | bytes 1048584 | tf_op jit(solution)/shard_map/dynamic_slice | solution.py:273
  2.2 0.5 collective-permute-start
  2.7 1.2 %collective-permute-done = bf16[4,128,256]{2,1,0:T(8,128)(2,1)S(1)} collective-permute-done((bf16[4,128,256]{2,1,0:T(8,128)(2,1)S(1)}, bf16[4,128,256]{2,1,0:T(8,128)(2,1)S(1)}, u32[]{:S(2)}, u32[]{:S(2)}) %collective-permute-start) | collective-permute-done | bytes 262176 | tf_op jit(solution)/shard_map/ppermute | solution.py:218
  3.9 3.0 %collective-permute-start.5 = (bf16[2,4,128,256]{3,2,1,0:T(8,128)(2,1)S(1)}, bf16[2,4,128,256]{3,2,1,0:T(8,128)(2,1)S(1)}, u32[]{:S(2)}, u32[]{:S(2)}) collective-permute-start(bf16[2,4,128,256]{3,2,1,0:T(8,128)(2,1)S(1)} %pad_maximum_fusion.1), channel_id=1, source_target_pairs={{0,4},{5,1},{4,8},{9,5},{8,12},{13,9},{12,14},{15,13},{14,10},{11,... | collective-permute-start | bytes 1572872 | tf_op jit(solution)/shard_map/ppermute | solution.py:244
  7.2 0.8 maximum_maximum_fusion
  8.0 0.6 collective-permute-done.1
  8.6 4.8 %all-to-all-start = ((bf16[8,40,512]{2,1,0:T(8,128)(2,1)}), bf16[8,40,512]{2,1,0:T(8,128)(2,1)S(1)}, u32[]{:S(2)}, u32[]{:S(2)}) async-start(bf16[8,40,512]{2,1,0:T(8,128)(2,1)} %maximum_maximum_fusion), calls=%async_computation | async-start | bytes 655360 | tf_op jit(solution)/shard_map/all_to_all | solution.py:295
  13.4 2.1 %collective-permute-start.2 = (bf16[2,4,128,256]{3,2,1,0:T(8,128)(2,1)S(1)}, bf16[2,4,128,256]{3,2,1,0:T(8,128)(2,1)S(1)}, u32[]{:S(2)}, u32[]{:S(2)}) collective-permute-start(bf16[2,4,128,256]{3,2,1,0:T(8,128)(2,1)S(1)} %pad_maximum_fusion), channel_id=1, source_target_pairs={{0,4},{5,1},{4,8},{9,5},{8,12},{13,9},{12,14},{15,13},{14,10},{11,... | collective-permute-start | bytes 1572872 | tf_op jit(solution)/shard_map/ppermute | solution.py:244
  15.5 1.5 %collective-permute-start.7 = (bf16[2,4,128,256]{3,2,1,0:T(8,128)(2,1)S(1)}, bf16[2,4,128,256]{3,2,1,0:T(8,128)(2,1)}, u32[]{:S(2)}, u32[]{:S(2)}) collective-permute-start(bf16[2,4,128,256]{3,2,1,0:T(8,128)(2,1)S(1)} %collective-permute-done.5.refs_1_), channel_id=1, source_target_pairs={{0,4},{5,1},{4,8},{9,5},{8,12},{13,9},{12,14},{15,13},{14,10},{11,... | collective-permute-start | bytes 1572872 | tf_op jit(solution)/shard_map/ppermute | solution.py:244
  17.0 8.9 %collective-permute-done.2.refs_1_ = bf16[2,4,128,256]{3,2,1,0:T(8,128)(2,1)S(1)} collective-permute-done((bf16[2,4,128,256]{3,2,1,0:T(8,128)(2,1)S(1)}, bf16[2,4,128,256]{3,2,1,0:T(8,128)(2,1)S(1)}, u32[]{:S(2)}, u32[]{:S(2)}) %collective-permute-start.2) | collective-permute-done | bytes 524320 | tf_op jit(solution)/shard_map/ppermute | solution.py:244
  25.8 2.1 %collective-permute-start.3 = (bf16[2,4,128,256]{3,2,1,0:T(8,128)(2,1)S(1)}, bf16[2,4,128,256]{3,2,1,0:T(8,128)(2,1)S(1)}, u32[]{:S(2)}, u32[]{:S(2)}) collective-permute-start(bf16[2,4,128,256]{3,2,1,0:T(8,128)(2,1)S(1)} %collective-permute-done.2.refs_1_), channel_id=1, source_target_pairs={{0,4},{5,1},{4,8},{9,5},{8,12},{13,9},{12,14},{15,13},{14,10},{11,... | collective-permute-start | bytes 1572872 | tf_op jit(solution)/shard_map/ppermute | solution.py:244
  28.0 0.7 copy-done.5
  28.7 2.8 %collective-permute-done.7.refs_3_ = bf16[2,4,128,256]{3,2,1,0:T(8,128)(2,1)} collective-permute-done((bf16[2,4,128,256]{3,2,1,0:T(8,128)(2,1)S(1)}, bf16[2,4,128,256]{3,2,1,0:T(8,128)(2,1)}, u32[]{:S(2)}, u32[]{:S(2)}) %collective-permute-start.7) | collective-permute-done | bytes 524320 | tf_op jit(solution)/shard_map/ppermute | solution.py:244
  31.5 2.0 %collective-permute-start.9 = (bf16[2,4,128,256]{3,2,1,0:T(8,128)(2,1)}, bf16[2,4,128,256]{3,2,1,0:T(8,128)(2,1)S(1)}, u32[]{:S(2)}, u32[]{:S(2)}) collective-permute-start(bf16[2,4,128,256]{3,2,1,0:T(8,128)(2,1)} %collective-permute-done.7.refs_3_), channel_id=1, source_target_pairs={{0,4},{5,1},{4,8},{9,5},{8,12},{13,9},{12,14},{15,13},{14,10},{11,... | collective-permute-start | bytes 1572872 | tf_op jit(solution)/shard_map/ppermute | solution.py:244
  33.6 0.1 fusion.3.refs_9_
  33.8 1.5 %collective-permute-done.11.refs_10_ = bf16[256,512]{1,0:T(8,128)(2,1)S(1)} collective-permute-done((bf16[256,512]{1,0:T(8,128)(2,1)S(1)}, bf16[256,512]{1,0:T(8,128)(2,1)S(1)}, u32[]{:S(2)}, u32[]{:S(2)}) %collective-permute-start.11) | collective-permute-done | bytes 262176 | tf_op jit(solution)/shard_map/ppermute | solution.py:218
  35.3 1.5 %collective-permute-start.12 = (bf16[256,512]{1,0:T(8,128)(2,1)S(1)}, bf16[256,512]{1,0:T(8,128)(2,1)S(1)}, u32[]{:S(2)}, u32[]{:S(2)}) collective-permute-start(bf16[256,512]{1,0:T(8,128)(2,1)S(1)} %fusion.3.refs_9_), channel_id=1, source_target_pairs={{0,16},{16,0},{1,17},{17,1},{2,18},{18,2},{3,19},{19,3},{4,20},{20... | collective-permute-start | bytes 786440 | tf_op jit(solution)/shard_map/ppermute | solution.py:218
  36.9 0.2 collective-permute-done.3.refs_3_
  37.1 2.4 %collective-permute-start.4 = (bf16[2,4,128,256]{3,2,1,0:T(8,128)(2,1)S(1)}, bf16[2,4,128,256]{3,2,1,0:T(8,128)(2,1)S(1)}, u32[]{:S(2)}, u32[]{:S(2)}) collective-permute-start(bf16[2,4,128,256]{3,2,1,0:T(8,128)(2,1)S(1)} %collective-permute-done.3.refs_3_), channel_id=1, source_target_pairs={{0,4},{5,1},{4,8},{9,5},{8,12},{13,9},{12,14},{15,13},{14,10},{11,... | collective-permute-start | bytes 1572872 | tf_op jit(solution)/shard_map/ppermute | solution.py:244
  39.5 3.2 %collective-permute-done.9.refs_5_ = bf16[2,4,128,256]{3,2,1,0:T(8,128)(2,1)S(1)} collective-permute-done((bf16[2,4,128,256]{3,2,1,0:T(8,128)(2,1)}, bf16[2,4,128,256]{3,2,1,0:T(8,128)(2,1)S(1)}, u32[]{:S(2)}, u32[]{:S(2)}) %collective-permute-start.9) | collective-permute-done | bytes 524320 | tf_op jit(solution)/shard_map/ppermute | solution.py:244
  42.7 1.0 %collective-permute-done.12.refs_11_ = bf16[256,512]{1,0:T(8,128)(2,1)S(1)} collective-permute-done((bf16[256,512]{1,0:T(8,128)(2,1)S(1)}, bf16[256,512]{1,0:T(8,128)(2,1)S(1)}, u32[]{:S(2)}, u32[]{:S(2)}) %collective-permute-start.12) | collective-permute-done | bytes 262176 | tf_op jit(solution)/shard_map/ppermute | solution.py:218
  43.7 2.6 %collective-permute-start.13 = (bf16[2,2,128,256]{3,2,1,0:T(8,128)(2,1)S(1)}, bf16[2,2,128,256]{3,2,1,0:T(8,128)(2,1)S(1)}, u32[]{:S(2)}, u32[]{:S(2)}) collective-permute-start(bf16[2,2,128,256]{3,2,1,0:T(8,128)(2,1)S(1)} %constant_dynamic-slice_fusion.1), channel_id=1, source_target_pairs={{0,4},{5,1},{4,8},{9,5},{8,12},{13,9},{12,14},{15,13},{14,10},{11,... | collective-permute-start | bytes 786440 | tf_op jit(solution)/shard_map/ppermute | solution.py:244
  46.3 0.5 collective-permute-start.15
  46.8 4.3 %collective-permute-done.13.refs_7_ = bf16[2,2,128,256]{3,2,1,0:T(8,128)(2,1)S(1)} collective-permute-done((bf16[2,2,128,256]{3,2,1,0:T(8,128)(2,1)S(1)}, bf16[2,2,128,256]{3,2,1,0:T(8,128)(2,1)S(1)}, u32[]{:S(2)}, u32[]{:S(2)}) %collective-permute-start.13) | collective-permute-done | bytes 262176 | tf_op jit(solution)/shard_map/ppermute | solution.py:244
  51.1 0.9 %collective-permute-start.14 = (bf16[2,2,128,256]{3,2,1,0:T(8,128)(2,1)S(1)}, bf16[2,2,128,256]{3,2,1,0:T(8,128)(2,1)S(1)}, u32[]{:S(2)}, u32[]{:S(2)}) collective-permute-start(bf16[2,2,128,256]{3,2,1,0:T(8,128)(2,1)S(1)} %collective-permute-done.13.refs_7_), channel_id=1, source_target_pairs={{0,1},{1,0},{2,3},{3,2},{4,5},{5,4},{6,7},{7,6},{8,9},{9,8},{10,11... | collective-permute-start | bytes 786440 | tf_op jit(solution)/shard_map/ppermute | solution.py:218
  52.1 3.3 %collective-permute-start.19 = (bf16[2,2,128,256]{3,2,1,0:T(8,128)(2,1)S(1)}, bf16[2,2,128,256]{3,2,1,0:T(8,128)(2,1)S(1)}, u32[]{:S(2)}, u32[]{:S(2)}) collective-permute-start(bf16[2,2,128,256]{3,2,1,0:T(8,128)(2,1)S(1)} %constant_dynamic-slice_fusion), channel_id=1, source_target_pairs={{0,4},{5,1},{4,8},{9,5},{8,12},{13,9},{12,14},{15,13},{14,10},{11,... | collective-permute-start | bytes 786440 | tf_op jit(solution)/shard_map/ppermute | solution.py:244
  55.3 0.5 collective-permute-start.18
  55.8 2.9 %shard_map.113 = (f32[4,256,256]{2,1,0:T(8,128)S(1)}, bf16[4,256,256]{2,1,0:T(8,128)(2,1)S(1)}) custom-call(bf16[4,128,256]{2,1,0:T(8,128)(2,1)S(1)} %bitcast.37, bf16[2,4,128,256]{3,2,1,0:T(8,128)(2,1)S(1)} %collective-permute-done.5.refs_1_, bf16[2,4,128,256]{3,2,1,0:T(8,128)(2,1)} %collective-permute-done.6.refs_2_, ...), custom_call_target="tpu_custom_call" | custom-call | flops 1073741824 | bytes 4718592 | tf_op jit(solution)/shard_map/pallas_call | solution.py:77
  58.8 0.4 collective-permute-done.19.refs_7_
  59.2 0.1 collective-permute-start.20
  59.3 1.5 %collective-permute-start.22 = (bf16[4,256,256]{2,1,0:T(8,128)(2,1)S(1)}, bf16[4,256,256]{2,1,0:T(8,128)(2,1)S(1)}, u32[]{:S(2)}, u32[]{:S(2)}) collective-permute-start(bf16[4,256,256]{2,1,0:T(8,128)(2,1)S(1)} %get-tuple-element.26), channel_id=1, source_target_pairs={{0,16},{16,0},{1,17},{17,1},{2,18},{18,2},{3,19},{19,3},{4,20},{20... | collective-permute-start | bytes 1572872 | tf_op jit(solution)/shard_map/ppermute | solution.py:218
  60.8 0.8 slice.28
  61.6 0.2 collective-permute-start.21
  61.9 0.1 convert_reduce_fusion
  62.0 0.8 slice.26
  62.7 0.8 slice.27
  63.5 2.3 %shard_map.114 = (bf16[4,256,256]{2,1,0:T(8,128)(2,1)S(1)}, bf16[4,256,256]{2,1,0:T(8,128)(2,1)S(1)}) custom-call(bf16[4,128,256]{2,1,0:T(8,128)(2,1)S(1)} %bitcast.34, bf16[2,4,128,256]{3,2,1,0:T(8,128)(2,1)S(1)} %collective-permute-done.2.refs_1_, bf16[2,4,128,256]{3,2,1,0:T(8,128)(2,1)S(1)} %collective-permute-done.16.refs_2_, ...), custom_call_target="tpu_custom_call" | custom-call | flops 1073741824 | bytes 4718592 | tf_op jit(solution)/shard_map/pallas_call | solution.py:77
  65.9 0.6 collective-permute-start.27
  66.5 0.6 fusion.prev_ref
  67.1 6.9 %collective-permute-done.22.other_ref = bf16[4,256,256]{2,1,0:T(8,128)(2,1)S(1)} collective-permute-done((bf16[4,256,256]{2,1,0:T(8,128)(2,1)S(1)}, bf16[4,256,256]{2,1,0:T(8,128)(2,1)S(1)}, u32[]{:S(2)}, u32[]{:S(2)}) %collective-permute-start.22) | collective-permute-done | bytes 524320 | tf_op jit(solution)/shard_map/ppermute | solution.py:218
  74.1 0.9 %shard_map.115 = (bf16[10,256,256]{2,1,0:T(8,128)(2,1)S(1)}, bf16[2,256,256]{2,1,0:T(8,128)(2,1)S(1)}, bf16[2,256,256]{2,1,0:T(8,128)(2,1)S(1)}, bf16[3,256,256]...) custom-call(s32[1]{0:T(128)} %bitcast.group_ref, f32[4,256,256]{2,1,0:T(8,128)S(1)} %get-tuple-element.29.own_ref, ...), custom_call_target="tpu_custom_call" | custom-call | tf_op jit(solution)/shard_map/pallas_call | solution.py:124
  75.0 0.5 collective-permute-start.26
  75.6 0.4 collective-permute-start.24
  76.0 1.6 %collective-permute-done.23.refs_0_ = bf16[2,256,256]{2,1,0:T(8,128)(2,1)S(1)} collective-permute-done((bf16[2,256,256]{2,1,0:T(8,128)(2,1)S(1)}, bf16[2,256,256]{2,1,0:T(8,128)(2,1)S(1)}, u32[]{:S(2)}, u32[]{:S(2)}) %collective-permute-start.23) | collective-permute-done | bytes 262176 | tf_op jit(solution)/shard_map/ppermute | solution.py:218
  77.7 0.4 collective-permute-done.24.refs_1_
  78.1 5.1 %shard_map.116 = bf16[2048,256]{1,0:T(8,128)(2,1)} custom-call(s32[1]{0:T(128)} %bitcast.group_ref, f32[4,256,256]{2,1,0:T(8,128)S(1)} %get-tuple-element.29.own_ref, bf16[4,256,256]{2,1,0:T(8,128)(2,1)S(1)} %collective-permute-done.22.other_ref, bf16[10,256,256]{2,1,0:T(8,128)(2,1)S(1)} %fusion.prev_ref, ...), custom_call_target="tpu_custom_call" | custom-call | tf_op jit(solution)/shard_map/pallas_call | solution.py:174
  83.2 1.6 %collective-permute-done.27.other_ref = bf16[4,256,256]{2,1,0:T(8,128)(2,1)S(1)} collective-permute-done((bf16[4,256,256]{2,1,0:T(8,128)(2,1)S(1)}, bf16[4,256,256]{2,1,0:T(8,128)(2,1)S(1)}, u32[]{:S(2)}, u32[]{:S(2)}) %collective-permute-start.27) | collective-permute-done | bytes 524320 | tf_op jit(solution)/shard_map/ppermute | solution.py:218
  84.8 2.0 %shard_map.117 = bf16[2048,256]{1,0:T(8,128)(2,1)} custom-call(s32[1]{0:T(128)} %bitcast.group_ref, bf16[4,256,256]{2,1,0:T(8,128)(2,1)S(1)} %get-tuple-element.36.own_ref, bf16[4,256,256]{2,1,0:T(8,128)(2,1)S(1)} %collective-permute-done.27.other_ref), custom_call_target="tpu_custom_call" | custom-call | tf_op jit(solution)/shard_map/pallas_call | solution.py:206
  (57 shorter events, 0.7 us)
Async XLA Ops:
  2.1 4.9 %copy-start.9 = (s32[8]{0:T(128)S(1)}, s32[8]{0:T(128)}, u32[]{:S(2)}) copy-start(s32[8]{0:T(128)} %param.15) | copy-start | bytes 100
  2.1 5.0 %copy-start.6 = (bf16[256,512]{1,0:T(8,128)(2,1)S(1)}, bf16[256,512]{1,0:T(8,128)(2,1)}, u32[]{:S(2)}) copy-start(bf16[256,512]{1,0:T(8,128)(2,1)} %param.10) | copy-start | bytes 786436
  2.1 5.0 %copy-start.7 = (bf16[8,8,256]{2,1,0:T(8,128)(2,1)S(1)}, bf16[8,8,256]{2,1,0:T(8,128)(2,1)}, u32[]{:S(2)}) copy-start(bf16[8,8,256]{2,1,0:T(8,128)(2,1)} %param.13) | copy-start | bytes 98308
  2.2 5.0 %copy-start.8 = (bf16[8,2,256]{2,1,0:T(2,128)(2,1)S(1)}, bf16[8,2,256]{2,1,0:T(2,128)(2,1)}, u32[]{:S(2)}) copy-start(bf16[8,2,256]{2,1,0:T(2,128)(2,1)} %param.14) | copy-start | bytes 24580
  2.2 1.7 %collective-permute-start = (bf16[4,128,256]{2,1,0:T(8,128)(2,1)S(1)}, bf16[4,128,256]{2,1,0:T(8,128)(2,1)S(1)}, u32[]{:S(2)}, u32[]{:S(2)}) collective-permute-start(bf16[4,128,256]{2,1,0:T(8,128)(2,1)S(1)} %bitcast.35), channel_id=1, source_target_pairs={{0,1},{1,0},{2,3},{3,2},{4,5},{5,4},{6,7},{7,6},{8,9},{9,8},{10,11... | collective-permute-start | bytes 786440 | tf_op jit(solution)/shard_map/ppermute | solution.py:218
  3.9 11.6 %collective-permute-start.5 = (bf16[2,4,128,256]{3,2,1,0:T(8,128)(2,1)S(1)}, bf16[2,4,128,256]{3,2,1,0:T(8,128)(2,1)S(1)}, u32[]{:S(2)}, u32[]{:S(2)}) collective-permute-start(bf16[2,4,128,256]{3,2,1,0:T(8,128)(2,1)S(1)} %pad_maximum_fusion.1), channel_id=1, source_target_pairs={{0,4},{5,1},{4,8},{9,5},{8,12},{13,9},{12,14},{15,13},{14,10},{11,... | collective-permute-start | bytes 1572872 | tf_op jit(solution)/shard_map/ppermute | solution.py:244
  7.0 1.6 %collective-permute-start.1 = (bf16[4,128,256]{2,1,0:T(8,128)(2,1)S(1)}, bf16[4,128,256]{2,1,0:T(8,128)(2,1)S(1)}, u32[]{:S(2)}, u32[]{:S(2)}) collective-permute-start(bf16[4,128,256]{2,1,0:T(8,128)(2,1)S(1)} %bitcast.32), channel_id=1, source_target_pairs={{0,1},{1,0},{2,3},{3,2},{4,5},{5,4},{6,7},{7,6},{8,9},{9,8},{10,11... | collective-permute-start | bytes 786440 | tf_op jit(solution)/shard_map/ppermute | solution.py:218
  8.6 19.4 %all-to-all-start = ((bf16[8,40,512]{2,1,0:T(8,128)(2,1)}), bf16[8,40,512]{2,1,0:T(8,128)(2,1)S(1)}, u32[]{:S(2)}, u32[]{:S(2)}) async-start(bf16[8,40,512]{2,1,0:T(8,128)(2,1)} %maximum_maximum_fusion), calls=%async_computation | async-start | bytes 655360 | tf_op jit(solution)/shard_map/all_to_all | solution.py:295
  13.4 12.4 %collective-permute-start.2 = (bf16[2,4,128,256]{3,2,1,0:T(8,128)(2,1)S(1)}, bf16[2,4,128,256]{3,2,1,0:T(8,128)(2,1)S(1)}, u32[]{:S(2)}, u32[]{:S(2)}) collective-permute-start(bf16[2,4,128,256]{3,2,1,0:T(8,128)(2,1)S(1)} %pad_maximum_fusion), channel_id=1, source_target_pairs={{0,4},{5,1},{4,8},{9,5},{8,12},{13,9},{12,14},{15,13},{14,10},{11,... | collective-permute-start | bytes 1572872 | tf_op jit(solution)/shard_map/ppermute | solution.py:244
  15.5 16.0 %collective-permute-start.7 = (bf16[2,4,128,256]{3,2,1,0:T(8,128)(2,1)S(1)}, bf16[2,4,128,256]{3,2,1,0:T(8,128)(2,1)}, u32[]{:S(2)}, u32[]{:S(2)}) collective-permute-start(bf16[2,4,128,256]{3,2,1,0:T(8,128)(2,1)S(1)} %collective-permute-done.5.refs_1_), channel_id=1, source_target_pairs={{0,4},{5,1},{4,8},{9,5},{8,12},{13,9},{12,14},{15,13},{14,10},{11,... | collective-permute-start | bytes 1572872 | tf_op jit(solution)/shard_map/ppermute | solution.py:244
  25.8 11.2 %collective-permute-start.3 = (bf16[2,4,128,256]{3,2,1,0:T(8,128)(2,1)S(1)}, bf16[2,4,128,256]{3,2,1,0:T(8,128)(2,1)S(1)}, u32[]{:S(2)}, u32[]{:S(2)}) collective-permute-start(bf16[2,4,128,256]{3,2,1,0:T(8,128)(2,1)S(1)} %collective-permute-done.2.refs_1_), channel_id=1, source_target_pairs={{0,4},{5,1},{4,8},{9,5},{8,12},{13,9},{12,14},{15,13},{14,10},{11,... | collective-permute-start | bytes 1572872 | tf_op jit(solution)/shard_map/ppermute | solution.py:244
  28.0 0.7 copy-start.5
  31.5 11.1 %collective-permute-start.9 = (bf16[2,4,128,256]{3,2,1,0:T(8,128)(2,1)}, bf16[2,4,128,256]{3,2,1,0:T(8,128)(2,1)S(1)}, u32[]{:S(2)}, u32[]{:S(2)}) collective-permute-start(bf16[2,4,128,256]{3,2,1,0:T(8,128)(2,1)} %collective-permute-done.7.refs_3_), channel_id=1, source_target_pairs={{0,4},{5,1},{4,8},{9,5},{8,12},{13,9},{12,14},{15,13},{14,10},{11,... | collective-permute-start | bytes 1572872 | tf_op jit(solution)/shard_map/ppermute | solution.py:244
  33.7 1.6 %collective-permute-start.11 = (bf16[256,512]{1,0:T(8,128)(2,1)S(1)}, bf16[256,512]{1,0:T(8,128)(2,1)S(1)}, u32[]{:S(2)}, u32[]{:S(2)}) collective-permute-start(bf16[256,512]{1,0:T(8,128)(2,1)S(1)} %fusion.3.refs_9_), channel_id=1, source_target_pairs={{0,1},{1,0},{2,3},{3,2},{4,5},{5,4},{6,7},{7,6},{8,9},{9,8},{10,11... | collective-permute-start | bytes 786440 | tf_op jit(solution)/shard_map/ppermute | solution.py:218
  35.3 8.3 %collective-permute-start.12 = (bf16[256,512]{1,0:T(8,128)(2,1)S(1)}, bf16[256,512]{1,0:T(8,128)(2,1)S(1)}, u32[]{:S(2)}, u32[]{:S(2)}) collective-permute-start(bf16[256,512]{1,0:T(8,128)(2,1)S(1)} %fusion.3.refs_9_), channel_id=1, source_target_pairs={{0,16},{16,0},{1,17},{17,1},{2,18},{18,2},{3,19},{19,3},{4,20},{20... | collective-permute-start | bytes 786440 | tf_op jit(solution)/shard_map/ppermute | solution.py:218
  36.9 9.4 %collective-permute-start.6 = (bf16[2,4,128,256]{3,2,1,0:T(8,128)(2,1)S(1)}, bf16[2,4,128,256]{3,2,1,0:T(8,128)(2,1)}, u32[]{:S(2)}, u32[]{:S(2)}) collective-permute-start(bf16[2,4,128,256]{3,2,1,0:T(8,128)(2,1)S(1)} %collective-permute-done.5.refs_1_), channel_id=1, source_target_pairs={{0,1},{1,0},{2,3},{3,2},{4,5},{5,4},{6,7},{7,6},{8,9},{9,8},{10,11... | collective-permute-start | bytes 1572872 | tf_op jit(solution)/shard_map/ppermute | solution.py:218
  37.1 14.9 %collective-permute-start.4 = (bf16[2,4,128,256]{3,2,1,0:T(8,128)(2,1)S(1)}, bf16[2,4,128,256]{3,2,1,0:T(8,128)(2,1)S(1)}, u32[]{:S(2)}, u32[]{:S(2)}) collective-permute-start(bf16[2,4,128,256]{3,2,1,0:T(8,128)(2,1)S(1)} %collective-permute-done.3.refs_3_), channel_id=1, source_target_pairs={{0,4},{5,1},{4,8},{9,5},{8,12},{13,9},{12,14},{15,13},{14,10},{11,... | collective-permute-start | bytes 1572872 | tf_op jit(solution)/shard_map/ppermute | solution.py:244
  39.4 12.6 %collective-permute-start.8 = (bf16[2,4,128,256]{3,2,1,0:T(8,128)(2,1)}, bf16[2,4,128,256]{3,2,1,0:T(8,128)(2,1)S(1)}, u32[]{:S(2)}, u32[]{:S(2)}) collective-permute-start(bf16[2,4,128,256]{3,2,1,0:T(8,128)(2,1)} %collective-permute-done.7.refs_3_), channel_id=1, source_target_pairs={{0,1},{1,0},{2,3},{3,2},{4,5},{5,4},{6,7},{7,6},{8,9},{9,8},{10,11... | collective-permute-start | bytes 1572872 | tf_op jit(solution)/shard_map/ppermute | solution.py:218
  43.7 7.4 %collective-permute-start.13 = (bf16[2,2,128,256]{3,2,1,0:T(8,128)(2,1)S(1)}, bf16[2,2,128,256]{3,2,1,0:T(8,128)(2,1)S(1)}, u32[]{:S(2)}, u32[]{:S(2)}) collective-permute-start(bf16[2,2,128,256]{3,2,1,0:T(8,128)(2,1)S(1)} %constant_dynamic-slice_fusion.1), channel_id=1, source_target_pairs={{0,4},{5,1},{4,8},{9,5},{8,12},{13,9},{12,14},{15,13},{14,10},{11,... | collective-permute-start | bytes 786440 | tf_op jit(solution)/shard_map/ppermute | solution.py:244
  46.3 9.6 %collective-permute-start.10 = (bf16[2,4,128,256]{3,2,1,0:T(8,128)(2,1)S(1)}, bf16[2,4,128,256]{3,2,1,0:T(8,128)(2,1)S(1)}, u32[]{:S(2)}, u32[]{:S(2)}) collective-permute-start(bf16[2,4,128,256]{3,2,1,0:T(8,128)(2,1)S(1)} %collective-permute-done.9.refs_5_), channel_id=1, source_target_pairs={{0,1},{1,0},{2,3},{3,2},{4,5},{5,4},{6,7},{7,6},{8,9},{9,8},{10,11... | collective-permute-start | bytes 1572872 | tf_op jit(solution)/shard_map/ppermute | solution.py:218
  46.3 9.0 %collective-permute-start.15 = (bf16[256,512]{1,0:T(8,128)(2,1)S(1)}, bf16[256,512]{1,0:T(8,128)(2,1)S(1)}, u32[]{:S(2)}, u32[]{:S(2)}) collective-permute-start(bf16[256,512]{1,0:T(8,128)(2,1)S(1)} %collective-permute-done.12.refs_11_), channel_id=1, source_target_pairs={{0,1},{1,0},{2,3},{3,2},{4,5},{5,4},{6,7},{7,6},{8,9},{9,8},{10,11... | collective-permute-start | bytes 786440 | tf_op jit(solution)/shard_map/ppermute | solution.py:218
  51.1 4.2 %collective-permute-start.14 = (bf16[2,2,128,256]{3,2,1,0:T(8,128)(2,1)S(1)}, bf16[2,2,128,256]{3,2,1,0:T(8,128)(2,1)S(1)}, u32[]{:S(2)}, u32[]{:S(2)}) collective-permute-start(bf16[2,2,128,256]{3,2,1,0:T(8,128)(2,1)S(1)} %collective-permute-done.13.refs_7_), channel_id=1, source_target_pairs={{0,1},{1,0},{2,3},{3,2},{4,5},{5,4},{6,7},{7,6},{8,9},{9,8},{10,11... | collective-permute-start | bytes 786440 | tf_op jit(solution)/shard_map/ppermute | solution.py:218
  52.0 9.6 %collective-permute-start.16 = (bf16[2,4,128,256]{3,2,1,0:T(8,128)(2,1)S(1)}, bf16[2,4,128,256]{3,2,1,0:T(8,128)(2,1)S(1)}, u32[]{:S(2)}, u32[]{:S(2)}) collective-permute-start(bf16[2,4,128,256]{3,2,1,0:T(8,128)(2,1)S(1)} %collective-permute-done.2.refs_1_), channel_id=1, source_target_pairs={{0,1},{1,0},{2,3},{3,2},{4,5},{5,4},{6,7},{7,6},{8,9},{9,8},{10,11... | collective-permute-start | bytes 1572872 | tf_op jit(solution)/shard_map/ppermute | solution.py:218
  52.0 9.6 %copy-start = (bf16[3,256,256]{2,1,0:T(8,128)(2,1)S(1)}, bf16[3,256,256]{2,1,0:T(8,128)(2,1)}, u32[]{:S(2)}) copy-start(bf16[3,256,256]{2,1,0:T(8,128)(2,1)} %refs_5_.1) | copy-start | bytes 1179652
  52.1 7.2 %collective-permute-start.19 = (bf16[2,2,128,256]{3,2,1,0:T(8,128)(2,1)S(1)}, bf16[2,2,128,256]{3,2,1,0:T(8,128)(2,1)S(1)}, u32[]{:S(2)}, u32[]{:S(2)}) collective-permute-start(bf16[2,2,128,256]{3,2,1,0:T(8,128)(2,1)S(1)} %constant_dynamic-slice_fusion), channel_id=1, source_target_pairs={{0,4},{5,1},{4,8},{9,5},{8,12},{13,9},{12,14},{15,13},{14,10},{11,... | collective-permute-start | bytes 786440 | tf_op jit(solution)/shard_map/ppermute | solution.py:244
  55.3 8.2 %collective-permute-start.17 = (bf16[2,4,128,256]{3,2,1,0:T(8,128)(2,1)S(1)}, bf16[2,4,128,256]{3,2,1,0:T(8,128)(2,1)S(1)}, u32[]{:S(2)}, u32[]{:S(2)}) collective-permute-start(bf16[2,4,128,256]{3,2,1,0:T(8,128)(2,1)S(1)} %collective-permute-done.3.refs_3_), channel_id=1, source_target_pairs={{0,1},{1,0},{2,3},{3,2},{4,5},{5,4},{6,7},{7,6},{8,9},{9,8},{10,11... | collective-permute-start | bytes 1572872 | tf_op jit(solution)/shard_map/ppermute | solution.py:218
  55.3 8.2 %collective-permute-start.18 = (bf16[2,4,128,256]{3,2,1,0:T(8,128)(2,1)S(1)}, bf16[2,4,128,256]{3,2,1,0:T(8,128)(2,1)S(1)}, u32[]{:S(2)}, u32[]{:S(2)}) collective-permute-start(bf16[2,4,128,256]{3,2,1,0:T(8,128)(2,1)S(1)} %collective-permute-done.4.refs_5_), channel_id=1, source_target_pairs={{0,1},{1,0},{2,3},{3,2},{4,5},{5,4},{6,7},{7,6},{8,9},{9,8},{10,11... | collective-permute-start | bytes 1572872 | tf_op jit(solution)/shard_map/ppermute | solution.py:218
  59.2 4.3 %collective-permute-start.20 = (bf16[2,2,128,256]{3,2,1,0:T(8,128)(2,1)S(1)}, bf16[2,2,128,256]{3,2,1,0:T(8,128)(2,1)S(1)}, u32[]{:S(2)}, u32[]{:S(2)}) collective-permute-start(bf16[2,2,128,256]{3,2,1,0:T(8,128)(2,1)S(1)} %collective-permute-done.19.refs_7_), channel_id=1, source_target_pairs={{0,1},{1,0},{2,3},{3,2},{4,5},{5,4},{6,7},{7,6},{8,9},{9,8},{10,11... | collective-permute-start | bytes 786440 | tf_op jit(solution)/shard_map/ppermute | solution.py:218
  59.3 14.7 %collective-permute-start.22 = (bf16[4,256,256]{2,1,0:T(8,128)(2,1)S(1)}, bf16[4,256,256]{2,1,0:T(8,128)(2,1)S(1)}, u32[]{:S(2)}, u32[]{:S(2)}) collective-permute-start(bf16[4,256,256]{2,1,0:T(8,128)(2,1)S(1)} %get-tuple-element.26), channel_id=1, source_target_pairs={{0,16},{16,0},{1,17},{17,1},{2,18},{18,2},{3,19},{19,3},{4,20},{20... | collective-permute-start | bytes 1572872 | tf_op jit(solution)/shard_map/ppermute | solution.py:218
  61.6 5.5 %collective-permute-start.21 = (bf16[3,256,256]{2,1,0:T(8,128)(2,1)S(1)}, bf16[3,256,256]{2,1,0:T(8,128)(2,1)S(1)}, u32[]{:S(2)}, u32[]{:S(2)}) collective-permute-start(bf16[3,256,256]{2,1,0:T(8,128)(2,1)S(1)} %copy-done), channel_id=1, source_target_pairs={{0,1},{1,0},{2,3},{3,2},{4,5},{5,4},{6,7},{7,6},{8,9},{9,8},{10,11... | collective-permute-start | bytes 1179656 | tf_op jit(solution)/shard_map/ppermute | solution.py:218
  65.9 8.2 %copy-start.2 = (f32[256]{0:T(256)S(1)}, f32[256]{0:T(256)}, u32[]{:S(2)}) copy-start(f32[256]{0:T(256)} %param.12) | copy-start | bytes 3076
  65.9 18.9 %collective-permute-start.27 = (bf16[4,256,256]{2,1,0:T(8,128)(2,1)S(1)}, bf16[4,256,256]{2,1,0:T(8,128)(2,1)S(1)}, u32[]{:S(2)}, u32[]{:S(2)}) collective-permute-start(bf16[4,256,256]{2,1,0:T(8,128)(2,1)S(1)} %get-tuple-element.28), channel_id=1, source_target_pairs={{0,16},{16,0},{1,17},{17,1},{2,18},{18,2},{3,19},{19,3},{4,20},{20... | collective-permute-start | bytes 1572872 | tf_op jit(solution)/shard_map/ppermute | solution.py:218
  74.0 4.0 %copy-start.1 = (bf16[256,256]{1,0:T(8,128)(2,1)S(1)}, bf16[256,256]{1,0:T(8,128)(2,1)}, u32[]{:S(2)}) copy-start(bf16[256,256]{1,0:T(8,128)(2,1)} %refs_8_.1) | copy-start | bytes 393220
  74.0 4.0 %copy-start.3 = (f32[256]{0:T(256)S(1)}, f32[256]{0:T(256)}, u32[]{:S(2)}) copy-start(f32[256]{0:T(256)} %param.17) | copy-start | bytes 3076
  74.0 4.0 %copy-start.4 = (f32[256]{0:T(256)S(1)}, f32[256]{0:T(256)}, u32[]{:S(2)}) copy-start(f32[256]{0:T(256)} %param.19) | copy-start | bytes 3076
  74.9 3.1 %collective-permute-start.25 = (bf16[3,256,256]{2,1,0:T(8,128)(2,1)S(1)}, bf16[3,256,256]{2,1,0:T(8,128)(2,1)S(1)}, u32[]{:S(2)}, u32[]{:S(2)}) collective-permute-start(bf16[3,256,256]{2,1,0:T(8,128)(2,1)S(1)} %get-tuple-element.33), channel_id=1, source_target_pairs={{0,1},{1,0},{2,3},{3,2},{4,5},{5,4},{6,7},{7,6},{8,9},{9,8},{10,11... | collective-permute-start | bytes 1179656 | tf_op jit(solution)/shard_map/ppermute | solution.py:218
  75.0 3.0 %collective-permute-start.26 = (bf16[3,256,256]{2,1,0:T(8,128)(2,1)S(1)}, bf16[3,256,256]{2,1,0:T(8,128)(2,1)S(1)}, u32[]{:S(2)}, u32[]{:S(2)}) collective-permute-start(bf16[3,256,256]{2,1,0:T(8,128)(2,1)S(1)} %get-tuple-element.34), channel_id=1, source_target_pairs={{0,1},{1,0},{2,3},{3,2},{4,5},{5,4},{6,7},{7,6},{8,9},{9,8},{10,11... | collective-permute-start | bytes 1179656 | tf_op jit(solution)/shard_map/ppermute | solution.py:218
  75.5 2.1 %collective-permute-start.23 = (bf16[2,256,256]{2,1,0:T(8,128)(2,1)S(1)}, bf16[2,256,256]{2,1,0:T(8,128)(2,1)S(1)}, u32[]{:S(2)}, u32[]{:S(2)}) collective-permute-start(bf16[2,256,256]{2,1,0:T(8,128)(2,1)S(1)} %get-tuple-element.31), channel_id=1, source_target_pairs={{0,1},{1,0},{2,3},{3,2},{4,5},{5,4},{6,7},{7,6},{8,9},{9,8},{10,11... | collective-permute-start | bytes 786440 | tf_op jit(solution)/shard_map/ppermute | solution.py:218
  75.6 2.4 %collective-permute-start.24 = (bf16[2,256,256]{2,1,0:T(8,128)(2,1)S(1)}, bf16[2,256,256]{2,1,0:T(8,128)(2,1)S(1)}, u32[]{:S(2)}, u32[]{:S(2)}) collective-permute-start(bf16[2,256,256]{2,1,0:T(8,128)(2,1)S(1)} %get-tuple-element.32), channel_id=1, source_target_pairs={{0,1},{1,0},{2,3},{3,2},{4,5},{5,4},{6,7},{7,6},{8,9},{9,8},{10,11... | collective-permute-start | bytes 786440 | tf_op jit(solution)/shard_map/ppermute | solution.py:218

commit v6 on v5

--- a/solution.py
+++ b/solution.py
@@ -233,19 +233,21 @@
         self.item = jnp.stack([own, other])
         self.blocks, self.steps, self.rounds = [own], [(0, 0)], 0
 
-    def round(self, earlier=None, passed_after=None):
+    def round(self, earlier=None, whole=False):
         self.rounds += 1
         item = self.item
-        if 2 * self.rounds == self.count:
+        if 2 * self.rounds == self.count and not whole:
             part = item.shape[1] // 2
             item = lax.dynamic_slice_in_dim(item, lax.axis_index("segment") * part, part, axis=1)
         if earlier is not None:
             item = after(item, earlier)
         item = lax.ppermute(item, ("streams", "segment"), self.pairs)
         self.item = item
-        given = item if passed_after is None else after(item, passed_after)
-        self.blocks += [item, swap(given, "segment")]
-        self.steps += [(self.rounds, 0), (self.rounds, 1)]
+        self.blocks.append(item)
+        self.steps.append((self.rounds, 0))
+        if not whole:
+            self.blocks.append(swap(item, "segment"))
+            self.steps.append((self.rounds, 1))
         return item
 
 
@@ -316,7 +318,7 @@
         up_ring.round(far_half)
         up_ring.blocks[0] = after(up_ring.blocks[0], nearly_done)
         own_up, away_up = spread_taps(sides, up_ring.blocks, up_ring.steps, count, F32)
-        tail_ring.round(passed_after=away_up)
+        tail_ring.round(whole=True)
         own_tail, away_tail = spread_taps(sides, tail_ring.blocks, tail_ring.steps, count, BF16)
     else:
         whole = [lax.all_gather(own, "streams", axis=1, tiled=True) for own in halves]

time: 87.4 us -> 85.9 us (0.983)
  waiting for transfers between devices: 34.7 us -> 32.6 us
  starting transfers between devices: 31.4 us -> 32.3 us
    ppermute x20 -> x19, waiting for transfers between devices: 14.8 us -> 13.2 us  [swap(): return lax.ppermute(value, axis, [(0, 1), (1, 0)])]
    ppermute x20 -> x19, starting transfers between devices: 7.6 us -> 8.55 us  [swap(): return lax.ppermute(value, axis, [(0, 1), (1, 0)])]
  transfers between devices with their start and end apart: 29 -> 28, of which waited for: 14 -> 13; matrix products, arithmetic and copies ran while one was open for 5% -> 5% of each run, Pallas kernels for 13% -> 13%
where the time goes in v6:
time: 85.9 us; the launch traced here: 85.4 us
  waiting for transfers between devices  32.6 us (38%)
  starting transfers between devices  32.3 us (38%)
  Pallas kernels  13.1 us (15%)
  local copies, waits for them, and re-layouts  4.73 us (6%)
  other arithmetic  1.17 us (1%)
  between operations  0.93 us (1%)
    ppermute x8, waiting for transfers between devices, round(): item = lax.ppermute(item, ('streams', 'segment'), self.pairs)  19.4 us
    ppermute x8, starting transfers between devices, round(): item = lax.ppermute(item, ('streams', 'segment'), self.pairs)  18.9 us
    ppermute x19, waiting for transfers between devices, swap(): return lax.ppermute(value, axis, [(0, 1), (1, 0)])  13.2 us
    ppermute x19, starting transfers between devices, swap(): return lax.ppermute(value, axis, [(0, 1), (1, 0)])  8.55 us
    pallas_call x1, Pallas kernels, residual(): pl.pallas_call(residual_kernel, out_shape=jax.ShapeDtypeStruct((sessions...  5.12 us
    pallas_call x2, Pallas kernels, spread_taps(): pl.pallas_call(functools.partial(spread_kernel, count, steps), out_shape=...  5.07 us
    all_to_all x1, starting transfers between devices, local(): lax.all_to_all(parcel, 'streams', split_axis=0, concat_axis=0, tiled=True)  4.79 us
    pallas_call x1, Pallas kernels, weave(): pl.pallas_call(weave_kernel, out_shape=jax.ShapeDtypeStruct((sessions * s...  1.99 us
  transfers between devices with their start and end apart: 28, of which 13 were waited for; matrix products, arithmetic and copies ran while one was open for 5% of the time, Pallas kernels for 13%

profile of v6, /device:TPU:0, one launch (start us, length us, event | category | flops | bytes accessed | tf_op | source)
XLA Modules:
  0.0 85.4 jit_solution(6478510897453272646)
XLA Ops:
  0.6 1.5 %constant_dynamic-slice_fusion.1 = (bf16[128,4,256]{2,1,0:T(4,128)(2,1)S(1)}, bf16[128,4,256]{2,1,0:T(4,128)(2,1)S(1)}) fusion(bf16[128,16,256]{2,1,0:T(8,128)(2,1)} %param.11, s32[]{:T(128)S(6)} %select_n.14, s32[]{:T(128)S(6)} %select_n.13), kind=kLoop, calls=%fused_computation.23 | loop fusion | bytes 1048584 | tf_op jit(solution)/shard_map/dynamic_slice | solution.py:275
  2.2 0.5 collective-permute-start
  2.7 1.2 %collective-permute-done = bf16[4,128,256]{2,1,0:T(8,128)(2,1)S(1)} collective-permute-done((bf16[4,128,256]{2,1,0:T(8,128)(2,1)S(1)}, bf16[4,128,256]{2,1,0:T(8,128)(2,1)S(1)}, u32[]{:S(2)}, u32[]{:S(2)}) %collective-permute-start) | collective-permute-done | bytes 262176 | tf_op jit(solution)/shard_map/ppermute | solution.py:218
  3.9 3.0 %collective-permute-start.5 = (bf16[2,4,128,256]{3,2,1,0:T(8,128)(2,1)S(1)}, bf16[2,4,128,256]{3,2,1,0:T(8,128)(2,1)S(1)}, u32[]{:S(2)}, u32[]{:S(2)}) collective-permute-start(bf16[2,4,128,256]{3,2,1,0:T(8,128)(2,1)S(1)} %pad_maximum_fusion.1), channel_id=1, source_target_pairs={{0,4},{5,1},{4,8},{9,5},{8,12},{13,9},{12,14},{15,13},{14,10},{11,... | collective-permute-start | bytes 1572872 | tf_op jit(solution)/shard_map/ppermute | solution.py:244
  7.1 0.1 broadcast_in_dim.23
  7.2 0.8 maximum_maximum_fusion
  8.0 0.6 collective-permute-done.1
  8.6 4.8 %all-to-all-start = ((bf16[8,40,512]{2,1,0:T(8,128)(2,1)}), bf16[8,40,512]{2,1,0:T(8,128)(2,1)S(1)}, u32[]{:S(2)}, u32[]{:S(2)}) async-start(bf16[8,40,512]{2,1,0:T(8,128)(2,1)} %maximum_maximum_fusion), calls=%async_computation | async-start | bytes 655360 | tf_op jit(solution)/shard_map/all_to_all | solution.py:297
  13.4 2.1 %collective-permute-start.2 = (bf16[2,4,128,256]{3,2,1,0:T(8,128)(2,1)S(1)}, bf16[2,4,128,256]{3,2,1,0:T(8,128)(2,1)S(1)}, u32[]{:S(2)}, u32[]{:S(2)}) collective-permute-start(bf16[2,4,128,256]{3,2,1,0:T(8,128)(2,1)S(1)} %pad_maximum_fusion), channel_id=1, source_target_pairs={{0,4},{5,1},{4,8},{9,5},{8,12},{13,9},{12,14},{15,13},{14,10},{11,... | collective-permute-start | bytes 1572872 | tf_op jit(solution)/shard_map/ppermute | solution.py:244
  15.5 1.5 %collective-permute-start.7 = (bf16[2,4,128,256]{3,2,1,0:T(8,128)(2,1)S(1)}, bf16[2,4,128,256]{3,2,1,0:T(8,128)(2,1)}, u32[]{:S(2)}, u32[]{:S(2)}) collective-permute-start(bf16[2,4,128,256]{3,2,1,0:T(8,128)(2,1)S(1)} %collective-permute-done.5.refs_1_), channel_id=1, source_target_pairs={{0,4},{5,1},{4,8},{9,5},{8,12},{13,9},{12,14},{15,13},{14,10},{11,... | collective-permute-start | bytes 1572872 | tf_op jit(solution)/shard_map/ppermute | solution.py:244
  17.0 8.9 %collective-permute-done.2.refs_1_ = bf16[2,4,128,256]{3,2,1,0:T(8,128)(2,1)S(1)} collective-permute-done((bf16[2,4,128,256]{3,2,1,0:T(8,128)(2,1)S(1)}, bf16[2,4,128,256]{3,2,1,0:T(8,128)(2,1)S(1)}, u32[]{:S(2)}, u32[]{:S(2)}) %collective-permute-start.2) | collective-permute-done | bytes 524320 | tf_op jit(solution)/shard_map/ppermute | solution.py:244
  25.8 2.1 %collective-permute-start.3 = (bf16[2,4,128,256]{3,2,1,0:T(8,128)(2,1)S(1)}, bf16[2,4,128,256]{3,2,1,0:T(8,128)(2,1)S(1)}, u32[]{:S(2)}, u32[]{:S(2)}) collective-permute-start(bf16[2,4,128,256]{3,2,1,0:T(8,128)(2,1)S(1)} %collective-permute-done.2.refs_1_), channel_id=1, source_target_pairs={{0,4},{5,1},{4,8},{9,5},{8,12},{13,9},{12,14},{15,13},{14,10},{11,... | collective-permute-start | bytes 1572872 | tf_op jit(solution)/shard_map/ppermute | solution.py:244
  28.0 0.7 copy-done.5
  28.7 2.8 %collective-permute-done.7.refs_3_ = bf16[2,4,128,256]{3,2,1,0:T(8,128)(2,1)} collective-permute-done((bf16[2,4,128,256]{3,2,1,0:T(8,128)(2,1)S(1)}, bf16[2,4,128,256]{3,2,1,0:T(8,128)(2,1)}, u32[]{:S(2)}, u32[]{:S(2)}) %collective-permute-start.7) | collective-permute-done | bytes 524320 | tf_op jit(solution)/shard_map/ppermute | solution.py:244
  31.5 2.0 %collective-permute-start.9 = (bf16[2,4,128,256]{3,2,1,0:T(8,128)(2,1)}, bf16[2,4,128,256]{3,2,1,0:T(8,128)(2,1)S(1)}, u32[]{:S(2)}, u32[]{:S(2)}) collective-permute-start(bf16[2,4,128,256]{3,2,1,0:T(8,128)(2,1)} %collective-permute-done.7.refs_3_), channel_id=1, source_target_pairs={{0,4},{5,1},{4,8},{9,5},{8,12},{13,9},{12,14},{15,13},{14,10},{11,... | collective-permute-start | bytes 1572872 | tf_op jit(solution)/shard_map/ppermute | solution.py:244
  33.6 0.1 fusion.3.refs_9_.refs_8_
  33.8 0.5 collective-permute-start.6
  34.3 1.0 %collective-permute-done.11.refs_10_.refs_9_ = bf16[256,512]{1,0:T(8,128)(2,1)S(1)} collective-permute-done((bf16[256,512]{1,0:T(8,128)(2,1)S(1)}, bf16[256,512]{1,0:T(8,128)(2,1)S(1)}, u32[]{:S(2)}, u32[]{:S(2)}) %collective-permute-start.11) | collective-permute-done | bytes 262176 | tf_op jit(solution)/shard_map/ppermute | solution.py:218
  35.3 1.5 %collective-permute-start.12 = (bf16[256,512]{1,0:T(8,128)(2,1)S(1)}, bf16[256,512]{1,0:T(8,128)(2,1)S(1)}, u32[]{:S(2)}, u32[]{:S(2)}) collective-permute-start(bf16[256,512]{1,0:T(8,128)(2,1)S(1)} %fusion.3.refs_9_.refs_8_), channel_id=1, source_target_pairs={{0,16},{16,0},{1,17},{17,1},{2,18},{18,2},{3,19},{19,3},{4,20},{20... | collective-permute-start | bytes 786440 | tf_op jit(solution)/shard_map/ppermute | solution.py:218
  36.9 0.2 collective-permute-done.3.refs_3_
  37.1 2.4 %collective-permute-start.4 = (bf16[2,4,128,256]{3,2,1,0:T(8,128)(2,1)S(1)}, bf16[2,4,128,256]{3,2,1,0:T(8,128)(2,1)S(1)}, u32[]{:S(2)}, u32[]{:S(2)}) collective-permute-start(bf16[2,4,128,256]{3,2,1,0:T(8,128)(2,1)S(1)} %collective-permute-done.3.refs_3_), channel_id=1, source_target_pairs={{0,4},{5,1},{4,8},{9,5},{8,12},{13,9},{12,14},{15,13},{14,10},{11,... | collective-permute-start | bytes 1572872 | tf_op jit(solution)/shard_map/ppermute | solution.py:244
  39.4 3.2 %collective-permute-done.9.refs_5_ = bf16[2,4,128,256]{3,2,1,0:T(8,128)(2,1)S(1)} collective-permute-done((bf16[2,4,128,256]{3,2,1,0:T(8,128)(2,1)}, bf16[2,4,128,256]{3,2,1,0:T(8,128)(2,1)S(1)}, u32[]{:S(2)}, u32[]{:S(2)}) %collective-permute-start.9) | collective-permute-done | bytes 524320 | tf_op jit(solution)/shard_map/ppermute | solution.py:244
  42.7 1.0 %collective-permute-done.12.refs_11_.refs_10_ = bf16[256,512]{1,0:T(8,128)(2,1)S(1)} collective-permute-done((bf16[256,512]{1,0:T(8,128)(2,1)S(1)}, bf16[256,512]{1,0:T(8,128)(2,1)S(1)}, u32[]{:S(2)}, u32[]{:S(2)}) %collective-permute-start.12) | collective-permute-done | bytes 262176 | tf_op jit(solution)/shard_map/ppermute | solution.py:218
  43.7 2.6 %collective-permute-start.13 = (bf16[2,2,128,256]{3,2,1,0:T(8,128)(2,1)S(1)}, bf16[2,2,128,256]{3,2,1,0:T(8,128)(2,1)S(1)}, u32[]{:S(2)}, u32[]{:S(2)}) collective-permute-start(bf16[2,2,128,256]{3,2,1,0:T(8,128)(2,1)S(1)} %constant_dynamic-slice_fusion), channel_id=1, source_target_pairs={{0,4},{5,1},{4,8},{9,5},{8,12},{13,9},{12,14},{15,13},{14,10},{11,... | collective-permute-start | bytes 786440 | tf_op jit(solution)/shard_map/ppermute | solution.py:244
  46.3 0.5 collective-permute-start.15
  46.8 4.3 %collective-permute-done.13.refs_7_ = bf16[2,2,128,256]{3,2,1,0:T(8,128)(2,1)S(1)} collective-permute-done((bf16[2,2,128,256]{3,2,1,0:T(8,128)(2,1)S(1)}, bf16[2,2,128,256]{3,2,1,0:T(8,128)(2,1)S(1)}, u32[]{:S(2)}, u32[]{:S(2)}) %collective-permute-start.13) | collective-permute-done | bytes 262176 | tf_op jit(solution)/shard_map/ppermute | solution.py:244
  51.1 0.9 %collective-permute-start.14 = (bf16[2,2,128,256]{3,2,1,0:T(8,128)(2,1)S(1)}, bf16[2,2,128,256]{3,2,1,0:T(8,128)(2,1)S(1)}, u32[]{:S(2)}, u32[]{:S(2)}) collective-permute-start(bf16[2,2,128,256]{3,2,1,0:T(8,128)(2,1)S(1)} %collective-permute-done.13.refs_7_), channel_id=1, source_target_pairs={{0,1},{1,0},{2,3},{3,2},{4,5},{5,4},{6,7},{7,6},{8,9},{9,8},{10,11... | collective-permute-start | bytes 786440 | tf_op jit(solution)/shard_map/ppermute | solution.py:218
  52.0 0.5 collective-permute-start.17
  52.6 0.6 collective-permute-done.14.refs_8_
  53.2 3.2 %collective-permute-start.19 = (bf16[2,4,128,256]{3,2,1,0:T(8,128)(2,1)S(1)}, bf16[2,4,128,256]{3,2,1,0:T(8,128)(2,1)S(1)}, u32[]{:S(2)}, u32[]{:S(2)}) collective-permute-start(bf16[2,4,128,256]{3,2,1,0:T(8,128)(2,1)S(1)} %collective-permute-done.4.refs_5_), channel_id=1, source_target_pairs={{0,4},{5,1},{4,8},{9,5},{8,12},{13,9},{12,14},{15,13},{14,10},{11,... | collective-permute-start | bytes 1572872 | tf_op jit(solution)/shard_map/ppermute | solution.py:244
  56.4 2.9 %shard_map.113 = (f32[4,256,256]{2,1,0:T(8,128)S(1)}, bf16[4,256,256]{2,1,0:T(8,128)(2,1)S(1)}) custom-call(bf16[4,128,256]{2,1,0:T(8,128)(2,1)S(1)} %bitcast.37, bf16[2,4,128,256]{3,2,1,0:T(8,128)(2,1)S(1)} %collective-permute-done.5.refs_1_, bf16[2,4,128,256]{3,2,1,0:T(8,128)(2,1)} %collective-permute-done.6.refs_2_, ...), custom_call_target="tpu_custom_call" | custom-call | flops 1073741824 | bytes 4718592 | tf_op jit(solution)/shard_map/pallas_call | solution.py:77
  59.3 1.6 %collective-permute-start.21 = (bf16[4,256,256]{2,1,0:T(8,128)(2,1)S(1)}, bf16[4,256,256]{2,1,0:T(8,128)(2,1)S(1)}, u32[]{:S(2)}, u32[]{:S(2)}) collective-permute-start(bf16[4,256,256]{2,1,0:T(8,128)(2,1)S(1)} %get-tuple-element.27), channel_id=1, source_target_pairs={{0,16},{16,0},{1,17},{17,1},{2,18},{18,2},{3,19},{19,3},{4,20},{20... | collective-permute-start | bytes 1572872 | tf_op jit(solution)/shard_map/ppermute | solution.py:218
  60.9 0.8 slice.28
  61.8 0.1 convert_reduce_fusion
  61.9 0.8 slice.26
  62.7 0.8 slice.27
  63.5 2.1 %shard_map.114 = (bf16[4,256,256]{2,1,0:T(8,128)(2,1)S(1)}, bf16[4,256,256]{2,1,0:T(8,128)(2,1)S(1)}) custom-call(bf16[4,128,256]{2,1,0:T(8,128)(2,1)S(1)} %bitcast.34, bf16[2,4,128,256]{3,2,1,0:T(8,128)(2,1)S(1)} %collective-permute-done.2.refs_1_, bf16[2,4,128,256]{3,2,1,0:T(8,128)(2,1)S(1)} %collective-permute-done.16.refs_2_, ...), custom_call_target="tpu_custom_call" | custom-call | flops 1073741824 | bytes 4718592 | tf_op jit(solution)/shard_map/pallas_call | solution.py:77
  65.6 1.1 %collective-permute-start.26 = (bf16[4,256,256]{2,1,0:T(8,128)(2,1)S(1)}, bf16[4,256,256]{2,1,0:T(8,128)(2,1)S(1)}, u32[]{:S(2)}, u32[]{:S(2)}) collective-permute-start(bf16[4,256,256]{2,1,0:T(8,128)(2,1)S(1)} %get-tuple-element.25), channel_id=1, source_target_pairs={{0,16},{16,0},{1,17},{17,1},{2,18},{18,2},{3,19},{19,3},{4,20},{20... | collective-permute-start | bytes 1572872 | tf_op jit(solution)/shard_map/ppermute | solution.py:218
  66.8 0.6 fusion.prev_ref
  67.4 6.8 %collective-permute-done.21.other_ref = bf16[4,256,256]{2,1,0:T(8,128)(2,1)S(1)} collective-permute-done((bf16[4,256,256]{2,1,0:T(8,128)(2,1)S(1)}, bf16[4,256,256]{2,1,0:T(8,128)(2,1)S(1)}, u32[]{:S(2)}, u32[]{:S(2)}) %collective-permute-start.21) | collective-permute-done | bytes 524320 | tf_op jit(solution)/shard_map/ppermute | solution.py:218
  74.3 0.9 %shard_map.115 = (bf16[10,256,256]{2,1,0:T(8,128)(2,1)S(1)}, bf16[2,256,256]{2,1,0:T(8,128)(2,1)S(1)}, bf16[2,256,256]{2,1,0:T(8,128)(2,1)S(1)}, bf16[3,256,256]...) custom-call(s32[1]{0:T(128)} %bitcast.group_ref, f32[4,256,256]{2,1,0:T(8,128)S(1)} %get-tuple-element.26.own_ref, ...), custom_call_target="tpu_custom_call" | custom-call | tf_op jit(solution)/shard_map/pallas_call | solution.py:124
  75.2 0.5 collective-permute-start.25
  75.7 0.1 collective-permute-start.22
  75.8 0.4 collective-permute-start.23
  76.2 1.6 %collective-permute-done.22.refs_0_ = bf16[2,256,256]{2,1,0:T(8,128)(2,1)S(1)} collective-permute-done((bf16[2,256,256]{2,1,0:T(8,128)(2,1)S(1)}, bf16[2,256,256]{2,1,0:T(8,128)(2,1)S(1)}, u32[]{:S(2)}, u32[]{:S(2)}) %collective-permute-start.22) | collective-permute-done | bytes 262176 | tf_op jit(solution)/shard_map/ppermute | solution.py:218
  77.9 0.4 collective-permute-done.23.refs_1_
  78.3 5.1 %shard_map.116 = bf16[2048,256]{1,0:T(8,128)(2,1)} custom-call(s32[1]{0:T(128)} %bitcast.group_ref, f32[4,256,256]{2,1,0:T(8,128)S(1)} %get-tuple-element.26.own_ref, bf16[4,256,256]{2,1,0:T(8,128)(2,1)S(1)} %collective-permute-done.21.other_ref, bf16[10,256,256]{2,1,0:T(8,128)(2,1)S(1)} %fusion.prev_ref, ...), custom_call_target="tpu_custom_call" | custom-call | tf_op jit(solution)/shard_map/pallas_call | solution.py:174
  83.4 2.0 %shard_map.117 = bf16[2048,256]{1,0:T(8,128)(2,1)} custom-call(s32[1]{0:T(128)} %bitcast.group_ref, bf16[4,256,256]{2,1,0:T(8,128)(2,1)S(1)} %get-tuple-element.34.own_ref, bf16[4,256,256]{2,1,0:T(8,128)(2,1)S(1)} %collective-permute-done.26.other_ref), custom_call_target="tpu_custom_call" | custom-call | tf_op jit(solution)/shard_map/pallas_call | solution.py:206
  (54 shorter events, 0.7 us)
Async XLA Ops:
  2.1 4.9 %copy-start.9 = (s32[8]{0:T(128)S(1)}, s32[8]{0:T(128)}, u32[]{:S(2)}) copy-start(s32[8]{0:T(128)} %param.15) | copy-start | bytes 100
  2.1 5.0 %copy-start.6 = (bf16[256,512]{1,0:T(8,128)(2,1)S(1)}, bf16[256,512]{1,0:T(8,128)(2,1)}, u32[]{:S(2)}) copy-start(bf16[256,512]{1,0:T(8,128)(2,1)} %param.10) | copy-start | bytes 786436
  2.1 5.0 %copy-start.7 = (bf16[8,8,256]{2,1,0:T(8,128)(2,1)S(1)}, bf16[8,8,256]{2,1,0:T(8,128)(2,1)}, u32[]{:S(2)}) copy-start(bf16[8,8,256]{2,1,0:T(8,128)(2,1)} %param.13) | copy-start | bytes 98308
  2.2 5.0 %copy-start.8 = (bf16[8,2,256]{2,1,0:T(2,128)(2,1)S(1)}, bf16[8,2,256]{2,1,0:T(2,128)(2,1)}, u32[]{:S(2)}) copy-start(bf16[8,2,256]{2,1,0:T(2,128)(2,1)} %param.14) | copy-start | bytes 24580
  2.2 1.7 %collective-permute-start = (bf16[4,128,256]{2,1,0:T(8,128)(2,1)S(1)}, bf16[4,128,256]{2,1,0:T(8,128)(2,1)S(1)}, u32[]{:S(2)}, u32[]{:S(2)}) collective-permute-start(bf16[4,128,256]{2,1,0:T(8,128)(2,1)S(1)} %bitcast.35), channel_id=1, source_target_pairs={{0,1},{1,0},{2,3},{3,2},{4,5},{5,4},{6,7},{7,6},{8,9},{9,8},{10,11... | collective-permute-start | bytes 786440 | tf_op jit(solution)/shard_map/ppermute | solution.py:218
  3.9 11.6 %collective-permute-start.5 = (bf16[2,4,128,256]{3,2,1,0:T(8,128)(2,1)S(1)}, bf16[2,4,128,256]{3,2,1,0:T(8,128)(2,1)S(1)}, u32[]{:S(2)}, u32[]{:S(2)}) collective-permute-start(bf16[2,4,128,256]{3,2,1,0:T(8,128)(2,1)S(1)} %pad_maximum_fusion.1), channel_id=1, source_target_pairs={{0,4},{5,1},{4,8},{9,5},{8,12},{13,9},{12,14},{15,13},{14,10},{11,... | collective-permute-start | bytes 1572872 | tf_op jit(solution)/shard_map/ppermute | solution.py:244
  7.0 1.6 %collective-permute-start.1 = (bf16[4,128,256]{2,1,0:T(8,128)(2,1)S(1)}, bf16[4,128,256]{2,1,0:T(8,128)(2,1)S(1)}, u32[]{:S(2)}, u32[]{:S(2)}) collective-permute-start(bf16[4,128,256]{2,1,0:T(8,128)(2,1)S(1)} %bitcast.32), channel_id=1, source_target_pairs={{0,1},{1,0},{2,3},{3,2},{4,5},{5,4},{6,7},{7,6},{8,9},{9,8},{10,11... | collective-permute-start | bytes 786440 | tf_op jit(solution)/shard_map/ppermute | solution.py:218
  8.6 19.4 %all-to-all-start = ((bf16[8,40,512]{2,1,0:T(8,128)(2,1)}), bf16[8,40,512]{2,1,0:T(8,128)(2,1)S(1)}, u32[]{:S(2)}, u32[]{:S(2)}) async-start(bf16[8,40,512]{2,1,0:T(8,128)(2,1)} %maximum_maximum_fusion), calls=%async_computation | async-start | bytes 655360 | tf_op jit(solution)/shard_map/all_to_all | solution.py:297
  13.4 12.4 %collective-permute-start.2 = (bf16[2,4,128,256]{3,2,1,0:T(8,128)(2,1)S(1)}, bf16[2,4,128,256]{3,2,1,0:T(8,128)(2,1)S(1)}, u32[]{:S(2)}, u32[]{:S(2)}) collective-permute-start(bf16[2,4,128,256]{3,2,1,0:T(8,128)(2,1)S(1)} %pad_maximum_fusion), channel_id=1, source_target_pairs={{0,4},{5,1},{4,8},{9,5},{8,12},{13,9},{12,14},{15,13},{14,10},{11,... | collective-permute-start | bytes 1572872 | tf_op jit(solution)/shard_map/ppermute | solution.py:244
  15.5 16.0 %collective-permute-start.7 = (bf16[2,4,128,256]{3,2,1,0:T(8,128)(2,1)S(1)}, bf16[2,4,128,256]{3,2,1,0:T(8,128)(2,1)}, u32[]{:S(2)}, u32[]{:S(2)}) collective-permute-start(bf16[2,4,128,256]{3,2,1,0:T(8,128)(2,1)S(1)} %collective-permute-done.5.refs_1_), channel_id=1, source_target_pairs={{0,4},{5,1},{4,8},{9,5},{8,12},{13,9},{12,14},{15,13},{14,10},{11,... | collective-permute-start | bytes 1572872 | tf_op jit(solution)/shard_map/ppermute | solution.py:244
  25.8 11.2 %collective-permute-start.3 = (bf16[2,4,128,256]{3,2,1,0:T(8,128)(2,1)S(1)}, bf16[2,4,128,256]{3,2,1,0:T(8,128)(2,1)S(1)}, u32[]{:S(2)}, u32[]{:S(2)}) collective-permute-start(bf16[2,4,128,256]{3,2,1,0:T(8,128)(2,1)S(1)} %collective-permute-done.2.refs_1_), channel_id=1, source_target_pairs={{0,4},{5,1},{4,8},{9,5},{8,12},{13,9},{12,14},{15,13},{14,10},{11,... | collective-permute-start | bytes 1572872 | tf_op jit(solution)/shard_map/ppermute | solution.py:244
  28.0 0.7 copy-start.5
  31.5 11.1 %collective-permute-start.9 = (bf16[2,4,128,256]{3,2,1,0:T(8,128)(2,1)}, bf16[2,4,128,256]{3,2,1,0:T(8,128)(2,1)S(1)}, u32[]{:S(2)}, u32[]{:S(2)}) collective-permute-start(bf16[2,4,128,256]{3,2,1,0:T(8,128)(2,1)} %collective-permute-done.7.refs_3_), channel_id=1, source_target_pairs={{0,4},{5,1},{4,8},{9,5},{8,12},{13,9},{12,14},{15,13},{14,10},{11,... | collective-permute-start | bytes 1572872 | tf_op jit(solution)/shard_map/ppermute | solution.py:244
  33.7 1.6 %collective-permute-start.11 = (bf16[256,512]{1,0:T(8,128)(2,1)S(1)}, bf16[256,512]{1,0:T(8,128)(2,1)S(1)}, u32[]{:S(2)}, u32[]{:S(2)}) collective-permute-start(bf16[256,512]{1,0:T(8,128)(2,1)S(1)} %fusion.3.refs_9_.refs_8_), channel_id=1, source_target_pairs={{0,1},{1,0},{2,3},{3,2},{4,5},{5,4},{6,7},{7,6},{8,9},{9,8},{10,11... | collective-permute-start | bytes 786440 | tf_op jit(solution)/shard_map/ppermute | solution.py:218
  33.8 12.5 %collective-permute-start.6 = (bf16[2,4,128,256]{3,2,1,0:T(8,128)(2,1)S(1)}, bf16[2,4,128,256]{3,2,1,0:T(8,128)(2,1)}, u32[]{:S(2)}, u32[]{:S(2)}) collective-permute-start(bf16[2,4,128,256]{3,2,1,0:T(8,128)(2,1)S(1)} %collective-permute-done.5.refs_1_), channel_id=1, source_target_pairs={{0,1},{1,0},{2,3},{3,2},{4,5},{5,4},{6,7},{7,6},{8,9},{9,8},{10,11... | collective-permute-start | bytes 1572872 | tf_op jit(solution)/shard_map/ppermute | solution.py:218
  35.3 8.3 %collective-permute-start.12 = (bf16[256,512]{1,0:T(8,128)(2,1)S(1)}, bf16[256,512]{1,0:T(8,128)(2,1)S(1)}, u32[]{:S(2)}, u32[]{:S(2)}) collective-permute-start(bf16[256,512]{1,0:T(8,128)(2,1)S(1)} %fusion.3.refs_9_.refs_8_), channel_id=1, source_target_pairs={{0,16},{16,0},{1,17},{17,1},{2,18},{18,2},{3,19},{19,3},{4,20},{20... | collective-permute-start | bytes 786440 | tf_op jit(solution)/shard_map/ppermute | solution.py:218
  36.9 15.1 %collective-permute-start.8 = (bf16[2,4,128,256]{3,2,1,0:T(8,128)(2,1)}, bf16[2,4,128,256]{3,2,1,0:T(8,128)(2,1)S(1)}, u32[]{:S(2)}, u32[]{:S(2)}) collective-permute-start(bf16[2,4,128,256]{3,2,1,0:T(8,128)(2,1)} %collective-permute-done.7.refs_3_), channel_id=1, source_target_pairs={{0,1},{1,0},{2,3},{3,2},{4,5},{5,4},{6,7},{7,6},{8,9},{9,8},{10,11... | collective-permute-start | bytes 1572872 | tf_op jit(solution)/shard_map/ppermute | solution.py:218
  37.1 15.5 %collective-permute-start.4 = (bf16[2,4,128,256]{3,2,1,0:T(8,128)(2,1)S(1)}, bf16[2,4,128,256]{3,2,1,0:T(8,128)(2,1)S(1)}, u32[]{:S(2)}, u32[]{:S(2)}) collective-permute-start(bf16[2,4,128,256]{3,2,1,0:T(8,128)(2,1)S(1)} %collective-permute-done.3.refs_3_), channel_id=1, source_target_pairs={{0,4},{5,1},{4,8},{9,5},{8,12},{13,9},{12,14},{15,13},{14,10},{11,... | collective-permute-start | bytes 1572872 | tf_op jit(solution)/shard_map/ppermute | solution.py:244
  42.7 19.0 %copy-start = (bf16[3,256,256]{2,1,0:T(8,128)(2,1)S(1)}, bf16[3,256,256]{2,1,0:T(8,128)(2,1)}, u32[]{:S(2)}) copy-start(bf16[3,256,256]{2,1,0:T(8,128)(2,1)} %refs_5_.1) | copy-start | bytes 1179652
  43.7 7.4 %collective-permute-start.13 = (bf16[2,2,128,256]{3,2,1,0:T(8,128)(2,1)S(1)}, bf16[2,2,128,256]{3,2,1,0:T(8,128)(2,1)S(1)}, u32[]{:S(2)}, u32[]{:S(2)}) collective-permute-start(bf16[2,2,128,256]{3,2,1,0:T(8,128)(2,1)S(1)} %constant_dynamic-slice_fusion), channel_id=1, source_target_pairs={{0,4},{5,1},{4,8},{9,5},{8,12},{13,9},{12,14},{15,13},{14,10},{11,... | collective-permute-start | bytes 786440 | tf_op jit(solution)/shard_map/ppermute | solution.py:244
  46.3 10.1 %collective-permute-start.10 = (bf16[2,4,128,256]{3,2,1,0:T(8,128)(2,1)S(1)}, bf16[2,4,128,256]{3,2,1,0:T(8,128)(2,1)S(1)}, u32[]{:S(2)}, u32[]{:S(2)}) collective-permute-start(bf16[2,4,128,256]{3,2,1,0:T(8,128)(2,1)S(1)} %collective-permute-done.9.refs_5_), channel_id=1, source_target_pairs={{0,1},{1,0},{2,3},{3,2},{4,5},{5,4},{6,7},{7,6},{8,9},{9,8},{10,11... | collective-permute-start | bytes 1572872 | tf_op jit(solution)/shard_map/ppermute | solution.py:218
  46.3 5.7 %collective-permute-start.15 = (bf16[256,512]{1,0:T(8,128)(2,1)S(1)}, bf16[256,512]{1,0:T(8,128)(2,1)S(1)}, u32[]{:S(2)}, u32[]{:S(2)}) collective-permute-start(bf16[256,512]{1,0:T(8,128)(2,1)S(1)} %collective-permute-done.12.refs_11_.refs_10_), channel_id=1, source_target_pairs={{0,1},{1,0},{2,3},{3,2},{4,5},{5,4},{6,7},{7,6},{8,9},{9,8},{10,11... | collective-permute-start | bytes 786440 | tf_op jit(solution)/shard_map/ppermute | solution.py:218
  51.1 2.1 %collective-permute-start.14 = (bf16[2,2,128,256]{3,2,1,0:T(8,128)(2,1)S(1)}, bf16[2,2,128,256]{3,2,1,0:T(8,128)(2,1)S(1)}, u32[]{:S(2)}, u32[]{:S(2)}) collective-permute-start(bf16[2,2,128,256]{3,2,1,0:T(8,128)(2,1)S(1)} %collective-permute-done.13.refs_7_), channel_id=1, source_target_pairs={{0,1},{1,0},{2,3},{3,2},{4,5},{5,4},{6,7},{7,6},{8,9},{9,8},{10,11... | collective-permute-start | bytes 786440 | tf_op jit(solution)/shard_map/ppermute | solution.py:218
  52.0 9.7 %collective-permute-start.16 = (bf16[2,4,128,256]{3,2,1,0:T(8,128)(2,1)S(1)}, bf16[2,4,128,256]{3,2,1,0:T(8,128)(2,1)S(1)}, u32[]{:S(2)}, u32[]{:S(2)}) collective-permute-start(bf16[2,4,128,256]{3,2,1,0:T(8,128)(2,1)S(1)} %collective-permute-done.2.refs_1_), channel_id=1, source_target_pairs={{0,1},{1,0},{2,3},{3,2},{4,5},{5,4},{6,7},{7,6},{8,9},{9,8},{10,11... | collective-permute-start | bytes 1572872 | tf_op jit(solution)/shard_map/ppermute | solution.py:218
  52.0 11.4 %collective-permute-start.17 = (bf16[2,4,128,256]{3,2,1,0:T(8,128)(2,1)S(1)}, bf16[2,4,128,256]{3,2,1,0:T(8,128)(2,1)S(1)}, u32[]{:S(2)}, u32[]{:S(2)}) collective-permute-start(bf16[2,4,128,256]{3,2,1,0:T(8,128)(2,1)S(1)} %collective-permute-done.3.refs_3_), channel_id=1, source_target_pairs={{0,1},{1,0},{2,3},{3,2},{4,5},{5,4},{6,7},{7,6},{8,9},{9,8},{10,11... | collective-permute-start | bytes 1572872 | tf_op jit(solution)/shard_map/ppermute | solution.py:218
  52.5 10.9 %collective-permute-start.18 = (bf16[2,4,128,256]{3,2,1,0:T(8,128)(2,1)S(1)}, bf16[2,4,128,256]{3,2,1,0:T(8,128)(2,1)S(1)}, u32[]{:S(2)}, u32[]{:S(2)}) collective-permute-start(bf16[2,4,128,256]{3,2,1,0:T(8,128)(2,1)S(1)} %collective-permute-done.4.refs_5_), channel_id=1, source_target_pairs={{0,1},{1,0},{2,3},{3,2},{4,5},{5,4},{6,7},{7,6},{8,9},{9,8},{10,11... | collective-permute-start | bytes 1572872 | tf_op jit(solution)/shard_map/ppermute | solution.py:218
  53.2 10.3 %collective-permute-start.19 = (bf16[2,4,128,256]{3,2,1,0:T(8,128)(2,1)S(1)}, bf16[2,4,128,256]{3,2,1,0:T(8,128)(2,1)S(1)}, u32[]{:S(2)}, u32[]{:S(2)}) collective-permute-start(bf16[2,4,128,256]{3,2,1,0:T(8,128)(2,1)S(1)} %collective-permute-done.4.refs_5_), channel_id=1, source_target_pairs={{0,4},{5,1},{4,8},{9,5},{8,12},{13,9},{12,14},{15,13},{14,10},{11,... | collective-permute-start | bytes 1572872 | tf_op jit(solution)/shard_map/ppermute | solution.py:244
  59.3 14.9 %collective-permute-start.21 = (bf16[4,256,256]{2,1,0:T(8,128)(2,1)S(1)}, bf16[4,256,256]{2,1,0:T(8,128)(2,1)S(1)}, u32[]{:S(2)}, u32[]{:S(2)}) collective-permute-start(bf16[4,256,256]{2,1,0:T(8,128)(2,1)S(1)} %get-tuple-element.27), channel_id=1, source_target_pairs={{0,16},{16,0},{1,17},{17,1},{2,18},{18,2},{3,19},{19,3},{4,20},{20... | collective-permute-start | bytes 1572872 | tf_op jit(solution)/shard_map/ppermute | solution.py:218
  61.7 5.7 %collective-permute-start.20 = (bf16[3,256,256]{2,1,0:T(8,128)(2,1)S(1)}, bf16[3,256,256]{2,1,0:T(8,128)(2,1)S(1)}, u32[]{:S(2)}, u32[]{:S(2)}) collective-permute-start(bf16[3,256,256]{2,1,0:T(8,128)(2,1)S(1)} %copy-done), channel_id=1, source_target_pairs={{0,1},{1,0},{2,3},{3,2},{4,5},{5,4},{6,7},{7,6},{8,9},{9,8},{10,11... | collective-permute-start | bytes 1179656 | tf_op jit(solution)/shard_map/ppermute | solution.py:218
  65.6 8.6 %copy-start.2 = (f32[256]{0:T(256)S(1)}, f32[256]{0:T(256)}, u32[]{:S(2)}) copy-start(f32[256]{0:T(256)} %param.12) | copy-start | bytes 3076
  65.6 17.8 %collective-permute-start.26 = (bf16[4,256,256]{2,1,0:T(8,128)(2,1)S(1)}, bf16[4,256,256]{2,1,0:T(8,128)(2,1)S(1)}, u32[]{:S(2)}, u32[]{:S(2)}) collective-permute-start(bf16[4,256,256]{2,1,0:T(8,128)(2,1)S(1)} %get-tuple-element.25), channel_id=1, source_target_pairs={{0,16},{16,0},{1,17},{17,1},{2,18},{18,2},{3,19},{19,3},{4,20},{20... | collective-permute-start | bytes 1572872 | tf_op jit(solution)/shard_map/ppermute | solution.py:218
  74.2 4.0 %copy-start.1 = (bf16[256,256]{1,0:T(8,128)(2,1)S(1)}, bf16[256,256]{1,0:T(8,128)(2,1)}, u32[]{:S(2)}) copy-start(bf16[256,256]{1,0:T(8,128)(2,1)} %refs_8_.1) | copy-start | bytes 393220
  74.3 4.0 %copy-start.3 = (f32[256]{0:T(256)S(1)}, f32[256]{0:T(256)}, u32[]{:S(2)}) copy-start(f32[256]{0:T(256)} %param.17) | copy-start | bytes 3076
  74.3 4.0 %copy-start.4 = (f32[256]{0:T(256)S(1)}, f32[256]{0:T(256)}, u32[]{:S(2)}) copy-start(f32[256]{0:T(256)} %param.19) | copy-start | bytes 3076
  75.1 3.1 %collective-permute-start.24 = (bf16[3,256,256]{2,1,0:T(8,128)(2,1)S(1)}, bf16[3,256,256]{2,1,0:T(8,128)(2,1)S(1)}, u32[]{:S(2)}, u32[]{:S(2)}) collective-permute-start(bf16[3,256,256]{2,1,0:T(8,128)(2,1)S(1)} %get-tuple-element.31), channel_id=1, source_target_pairs={{0,1},{1,0},{2,3},{3,2},{4,5},{5,4},{6,7},{7,6},{8,9},{9,8},{10,11... | collective-permute-start | bytes 1179656 | tf_op jit(solution)/shard_map/ppermute | solution.py:218
  75.2 3.0 %collective-permute-start.25 = (bf16[3,256,256]{2,1,0:T(8,128)(2,1)S(1)}, bf16[3,256,256]{2,1,0:T(8,128)(2,1)S(1)}, u32[]{:S(2)}, u32[]{:S(2)}) collective-permute-start(bf16[3,256,256]{2,1,0:T(8,128)(2,1)S(1)} %get-tuple-element.32), channel_id=1, source_target_pairs={{0,1},{1,0},{2,3},{3,2},{4,5},{5,4},{6,7},{7,6},{8,9},{9,8},{10,11... | collective-permute-start | bytes 1179656 | tf_op jit(solution)/shard_map/ppermute | solution.py:218
  75.7 2.1 %collective-permute-start.22 = (bf16[2,256,256]{2,1,0:T(8,128)(2,1)S(1)}, bf16[2,256,256]{2,1,0:T(8,128)(2,1)S(1)}, u32[]{:S(2)}, u32[]{:S(2)}) collective-permute-start(bf16[2,256,256]{2,1,0:T(8,128)(2,1)S(1)} %get-tuple-element.29), channel_id=1, source_target_pairs={{0,1},{1,0},{2,3},{3,2},{4,5},{5,4},{6,7},{7,6},{8,9},{9,8},{10,11... | collective-permute-start | bytes 786440 | tf_op jit(solution)/shard_map/ppermute | solution.py:218
  75.8 2.4 %collective-permute-start.23 = (bf16[2,256,256]{2,1,0:T(8,128)(2,1)S(1)}, bf16[2,256,256]{2,1,0:T(8,128)(2,1)S(1)}, u32[]{:S(2)}, u32[]{:S(2)}) collective-permute-start(bf16[2,256,256]{2,1,0:T(8,128)(2,1)S(1)} %get-tuple-element.30), channel_id=1, source_target_pairs={{0,1},{1,0},{2,3},{3,2},{4,5},{5,4},{6,7},{7,6},{8,9},{9,8},{10,11... | collective-permute-start | bytes 786440 | tf_op jit(solution)/shard_map/ppermute | solution.py:218

commit v7 on v6

--- a/solution.py
+++ b/solution.py
@@ -318,7 +318,7 @@
         up_ring.round(far_half)
         up_ring.blocks[0] = after(up_ring.blocks[0], nearly_done)
         own_up, away_up = spread_taps(sides, up_ring.blocks, up_ring.steps, count, F32)
-        tail_ring.round(whole=True)
+        tail_ring.round(away_up, whole=True)
         own_tail, away_tail = spread_taps(sides, tail_ring.blocks, tail_ring.steps, count, BF16)
     else:
         whole = [lax.all_gather(own, "streams", axis=1, tiled=True) for own in halves]

time: 85.9 us -> 85.6 us (level)
  waiting for transfers between devices: 32.6 us -> 31.7 us
    ppermute x19, waiting for transfers between devices: 13.2 us -> 10.4 us  [swap(): return lax.ppermute(value, axis, [(0, 1), (1, 0)])]
    ppermute x8, waiting for transfers between devices: 19.4 us -> 21.4 us  [round(): item = lax.ppermute(item, ('streams', 'segment'), self.pairs)]
  transfers between devices with their start and end apart: 28 -> 28, of which waited for: 13 -> 14; matrix products, arithmetic and copies ran while one was open for 5% -> 5% of each run, Pallas kernels for 13% -> 13%
where the time goes in v7:
time: 85.6 us; the launch traced here: 85.1 us
  starting transfers between devices  32.9 us (38%)
  waiting for transfers between devices  31.7 us (37%)
  Pallas kernels  13 us (15%)
  local copies, waits for them, and re-layouts  4.73 us (6%)
  other arithmetic  1.17 us (1%)
  between operations  0.93 us (1%)
    ppermute x8, waiting for transfers between devices, round(): item = lax.ppermute(item, ('streams', 'segment'), self.pairs)  21.4 us
    ppermute x8, starting transfers between devices, round(): item = lax.ppermute(item, ('streams', 'segment'), self.pairs)  19.2 us
    ppermute x19, waiting for transfers between devices, swap(): return lax.ppermute(value, axis, [(0, 1), (1, 0)])  10.4 us
    ppermute x19, starting transfers between devices, swap(): return lax.ppermute(value, axis, [(0, 1), (1, 0)])  8.93 us
    pallas_call x1, Pallas kernels, residual(): pl.pallas_call(residual_kernel, out_shape=jax.ShapeDtypeStruct((sessions...  5.14 us
    pallas_call x2, Pallas kernels, spread_taps(): pl.pallas_call(functools.partial(spread_kernel, count, steps), out_shape=...  5.04 us
    all_to_all x1, starting transfers between devices, local(): lax.all_to_all(parcel, 'streams', split_axis=0, concat_axis=0, tiled=True)  4.79 us
    pallas_call x1, Pallas kernels, weave(): pl.pallas_call(weave_kernel, out_shape=jax.ShapeDtypeStruct((sessions * s...  1.99 us
  transfers between devices with their start and end apart: 28, of which 14 were waited for; matrix products, arithmetic and copies ran while one was open for 5% of the time, Pallas kernels for 13%

profile of v7, /device:TPU:0, one launch (start us, length us, event | category | flops | bytes accessed | tf_op | source)
XLA Modules:
  0.0 85.1 jit_solution(12832313157329559298)
XLA Ops:
  0.6 1.5 %constant_dynamic-slice_fusion.1 = (bf16[128,4,256]{2,1,0:T(4,128)(2,1)S(1)}, bf16[128,4,256]{2,1,0:T(4,128)(2,1)S(1)}) fusion(bf16[128,16,256]{2,1,0:T(8,128)(2,1)} %param.11, s32[]{:T(128)S(6)} %select_n.14, s32[]{:T(128)S(6)} %select_n.13), kind=kLoop, calls=%fused_computation.23 | loop fusion | bytes 1048584 | tf_op jit(solution)/shard_map/dynamic_slice | solution.py:275
  2.2 0.5 collective-permute-start
  2.7 1.2 %collective-permute-done = bf16[4,128,256]{2,1,0:T(8,128)(2,1)S(1)} collective-permute-done((bf16[4,128,256]{2,1,0:T(8,128)(2,1)S(1)}, bf16[4,128,256]{2,1,0:T(8,128)(2,1)S(1)}, u32[]{:S(2)}, u32[]{:S(2)}) %collective-permute-start) | collective-permute-done | bytes 262176 | tf_op jit(solution)/shard_map/ppermute | solution.py:218
  3.9 3.0 %collective-permute-start.5 = (bf16[2,4,128,256]{3,2,1,0:T(8,128)(2,1)S(1)}, bf16[2,4,128,256]{3,2,1,0:T(8,128)(2,1)S(1)}, u32[]{:S(2)}, u32[]{:S(2)}) collective-permute-start(bf16[2,4,128,256]{3,2,1,0:T(8,128)(2,1)S(1)} %pad_maximum_fusion.1), channel_id=1, source_target_pairs={{0,4},{5,1},{4,8},{9,5},{8,12},{13,9},{12,14},{15,13},{14,10},{11,... | collective-permute-start | bytes 1572872 | tf_op jit(solution)/shard_map/ppermute | solution.py:244
  7.2 0.8 maximum_maximum_fusion
  8.0 0.6 collective-permute-done.1
  8.6 4.8 %all-to-all-start = ((bf16[8,40,512]{2,1,0:T(8,128)(2,1)}), bf16[8,40,512]{2,1,0:T(8,128)(2,1)S(1)}, u32[]{:S(2)}, u32[]{:S(2)}) async-start(bf16[8,40,512]{2,1,0:T(8,128)(2,1)} %maximum_maximum_fusion), calls=%async_computation | async-start | bytes 655360 | tf_op jit(solution)/shard_map/all_to_all | solution.py:297
  13.4 2.1 %collective-permute-start.2 = (bf16[2,4,128,256]{3,2,1,0:T(8,128)(2,1)S(1)}, bf16[2,4,128,256]{3,2,1,0:T(8,128)(2,1)S(1)}, u32[]{:S(2)}, u32[]{:S(2)}) collective-permute-start(bf16[2,4,128,256]{3,2,1,0:T(8,128)(2,1)S(1)} %pad_maximum_fusion), channel_id=1, source_target_pairs={{0,4},{5,1},{4,8},{9,5},{8,12},{13,9},{12,14},{15,13},{14,10},{11,... | collective-permute-start | bytes 1572872 | tf_op jit(solution)/shard_map/ppermute | solution.py:244
  15.5 1.5 %collective-permute-start.7 = (bf16[2,4,128,256]{3,2,1,0:T(8,128)(2,1)S(1)}, bf16[2,4,128,256]{3,2,1,0:T(8,128)(2,1)}, u32[]{:S(2)}, u32[]{:S(2)}) collective-permute-start(bf16[2,4,128,256]{3,2,1,0:T(8,128)(2,1)S(1)} %collective-permute-done.5.refs_1_), channel_id=1, source_target_pairs={{0,4},{5,1},{4,8},{9,5},{8,12},{13,9},{12,14},{15,13},{14,10},{11,... | collective-permute-start | bytes 1572872 | tf_op jit(solution)/shard_map/ppermute | solution.py:244
  17.0 8.9 %collective-permute-done.2.refs_1_ = bf16[2,4,128,256]{3,2,1,0:T(8,128)(2,1)S(1)} collective-permute-done((bf16[2,4,128,256]{3,2,1,0:T(8,128)(2,1)S(1)}, bf16[2,4,128,256]{3,2,1,0:T(8,128)(2,1)S(1)}, u32[]{:S(2)}, u32[]{:S(2)}) %collective-permute-start.2) | collective-permute-done | bytes 524320 | tf_op jit(solution)/shard_map/ppermute | solution.py:244
  25.8 2.1 %collective-permute-start.3 = (bf16[2,4,128,256]{3,2,1,0:T(8,128)(2,1)S(1)}, bf16[2,4,128,256]{3,2,1,0:T(8,128)(2,1)S(1)}, u32[]{:S(2)}, u32[]{:S(2)}) collective-permute-start(bf16[2,4,128,256]{3,2,1,0:T(8,128)(2,1)S(1)} %collective-permute-done.2.refs_1_), channel_id=1, source_target_pairs={{0,4},{5,1},{4,8},{9,5},{8,12},{13,9},{12,14},{15,13},{14,10},{11,... | collective-permute-start | bytes 1572872 | tf_op jit(solution)/shard_map/ppermute | solution.py:244
  28.0 0.7 copy-done.5
  28.7 2.8 %collective-permute-done.7.refs_3_ = bf16[2,4,128,256]{3,2,1,0:T(8,128)(2,1)} collective-permute-done((bf16[2,4,128,256]{3,2,1,0:T(8,128)(2,1)S(1)}, bf16[2,4,128,256]{3,2,1,0:T(8,128)(2,1)}, u32[]{:S(2)}, u32[]{:S(2)}) %collective-permute-start.7) | collective-permute-done | bytes 524320 | tf_op jit(solution)/shard_map/ppermute | solution.py:244
  31.5 2.0 %collective-permute-start.9 = (bf16[2,4,128,256]{3,2,1,0:T(8,128)(2,1)}, bf16[2,4,128,256]{3,2,1,0:T(8,128)(2,1)S(1)}, u32[]{:S(2)}, u32[]{:S(2)}) collective-permute-start(bf16[2,4,128,256]{3,2,1,0:T(8,128)(2,1)} %collective-permute-done.7.refs_3_), channel_id=1, source_target_pairs={{0,4},{5,1},{4,8},{9,5},{8,12},{13,9},{12,14},{15,13},{14,10},{11,... | collective-permute-start | bytes 1572872 | tf_op jit(solution)/shard_map/ppermute | solution.py:244
  33.6 0.1 fusion.3.refs_9_.refs_8_
  33.8 1.5 %collective-permute-done.11.refs_10_.refs_9_ = bf16[256,512]{1,0:T(8,128)(2,1)S(1)} collective-permute-done((bf16[256,512]{1,0:T(8,128)(2,1)S(1)}, bf16[256,512]{1,0:T(8,128)(2,1)S(1)}, u32[]{:S(2)}, u32[]{:S(2)}) %collective-permute-start.11) | collective-permute-done | bytes 262176 | tf_op jit(solution)/shard_map/ppermute | solution.py:218
  35.3 1.5 %collective-permute-start.12 = (bf16[256,512]{1,0:T(8,128)(2,1)S(1)}, bf16[256,512]{1,0:T(8,128)(2,1)S(1)}, u32[]{:S(2)}, u32[]{:S(2)}) collective-permute-start(bf16[256,512]{1,0:T(8,128)(2,1)S(1)} %fusion.3.refs_9_.refs_8_), channel_id=1, source_target_pairs={{0,16},{16,0},{1,17},{17,1},{2,18},{18,2},{3,19},{19,3},{4,20},{20... | collective-permute-start | bytes 786440 | tf_op jit(solution)/shard_map/ppermute | solution.py:218
  36.9 0.5 collective-permute-start.8
  37.4 2.6 %collective-permute-start.4 = (bf16[2,4,128,256]{3,2,1,0:T(8,128)(2,1)S(1)}, bf16[2,4,128,256]{3,2,1,0:T(8,128)(2,1)S(1)}, u32[]{:S(2)}, u32[]{:S(2)}) collective-permute-start(bf16[2,4,128,256]{3,2,1,0:T(8,128)(2,1)S(1)} %collective-permute-done.3.refs_3_), channel_id=1, source_target_pairs={{0,4},{5,1},{4,8},{9,5},{8,12},{13,9},{12,14},{15,13},{14,10},{11,... | collective-permute-start | bytes 1572872 | tf_op jit(solution)/shard_map/ppermute | solution.py:244
  40.0 2.7 %collective-permute-done.9.refs_5_ = bf16[2,4,128,256]{3,2,1,0:T(8,128)(2,1)S(1)} collective-permute-done((bf16[2,4,128,256]{3,2,1,0:T(8,128)(2,1)}, bf16[2,4,128,256]{3,2,1,0:T(8,128)(2,1)S(1)}, u32[]{:S(2)}, u32[]{:S(2)}) %collective-permute-start.9) | collective-permute-done | bytes 524320 | tf_op jit(solution)/shard_map/ppermute | solution.py:244
  42.7 1.0 %collective-permute-done.12.refs_11_.refs_10_ = bf16[256,512]{1,0:T(8,128)(2,1)S(1)} collective-permute-done((bf16[256,512]{1,0:T(8,128)(2,1)S(1)}, bf16[256,512]{1,0:T(8,128)(2,1)S(1)}, u32[]{:S(2)}, u32[]{:S(2)}) %collective-permute-start.12) | collective-permute-done | bytes 262176 | tf_op jit(solution)/shard_map/ppermute | solution.py:218
  43.7 2.6 %collective-permute-start.13 = (bf16[2,2,128,256]{3,2,1,0:T(8,128)(2,1)S(1)}, bf16[2,2,128,256]{3,2,1,0:T(8,128)(2,1)S(1)}, u32[]{:S(2)}, u32[]{:S(2)}) collective-permute-start(bf16[2,2,128,256]{3,2,1,0:T(8,128)(2,1)S(1)} %constant_dynamic-slice_fusion), channel_id=1, source_target_pairs={{0,4},{5,1},{4,8},{9,5},{8,12},{13,9},{12,14},{15,13},{14,10},{11,... | collective-permute-start | bytes 786440 | tf_op jit(solution)/shard_map/ppermute | solution.py:244
  46.3 0.5 collective-permute-start.15
  46.8 4.3 %collective-permute-done.13.refs_7_ = bf16[2,2,128,256]{3,2,1,0:T(8,128)(2,1)S(1)} collective-permute-done((bf16[2,2,128,256]{3,2,1,0:T(8,128)(2,1)S(1)}, bf16[2,2,128,256]{3,2,1,0:T(8,128)(2,1)S(1)}, u32[]{:S(2)}, u32[]{:S(2)}) %collective-permute-start.13) | collective-permute-done | bytes 262176 | tf_op jit(solution)/shard_map/ppermute | solution.py:244
  51.1 0.9 %collective-permute-start.14 = (bf16[2,2,128,256]{3,2,1,0:T(8,128)(2,1)S(1)}, bf16[2,2,128,256]{3,2,1,0:T(8,128)(2,1)S(1)}, u32[]{:S(2)}, u32[]{:S(2)}) collective-permute-start(bf16[2,2,128,256]{3,2,1,0:T(8,128)(2,1)S(1)} %collective-permute-done.13.refs_7_), channel_id=1, source_target_pairs={{0,1},{1,0},{2,3},{3,2},{4,5},{5,4},{6,7},{7,6},{8,9},{9,8},{10,11... | collective-permute-start | bytes 786440 | tf_op jit(solution)/shard_map/ppermute | solution.py:218
  52.0 0.5 collective-permute-start.17
  52.6 0.6 collective-permute-done.14.refs_8_
  53.2 2.9 %shard_map.113 = (f32[4,256,256]{2,1,0:T(8,128)S(1)}, bf16[4,256,256]{2,1,0:T(8,128)(2,1)S(1)}) custom-call(bf16[4,128,256]{2,1,0:T(8,128)(2,1)S(1)} %bitcast.37, bf16[2,4,128,256]{3,2,1,0:T(8,128)(2,1)S(1)} %collective-permute-done.5.refs_1_, bf16[2,4,128,256]{3,2,1,0:T(8,128)(2,1)} %collective-permute-done.6.refs_2_, ...), custom_call_target="tpu_custom_call" | custom-call | flops 1073741824 | bytes 4718592 | tf_op jit(solution)/shard_map/pallas_call | solution.py:77
  56.1 3.3 %collective-permute-start.19 = (bf16[2,4,128,256]{3,2,1,0:T(8,128)(2,1)S(1)}, bf16[2,4,128,256]{3,2,1,0:T(8,128)(2,1)S(1)}, u32[]{:S(2)}, u32[]{:S(2)}) collective-permute-start(bf16[2,4,128,256]{3,2,1,0:T(8,128)(2,1)S(1)} %collective-permute-done.4.refs_5_), channel_id=1, source_target_pairs={{0,4},{5,1},{4,8},{9,5},{8,12},{13,9},{12,14},{15,13},{14,10},{11,... | collective-permute-start | bytes 1572872 | tf_op jit(solution)/shard_map/ppermute | solution.py:244
  59.4 1.5 %collective-permute-start.21 = (bf16[4,256,256]{2,1,0:T(8,128)(2,1)S(1)}, bf16[4,256,256]{2,1,0:T(8,128)(2,1)S(1)}, u32[]{:S(2)}, u32[]{:S(2)}) collective-permute-start(bf16[4,256,256]{2,1,0:T(8,128)(2,1)S(1)} %get-tuple-element.26), channel_id=1, source_target_pairs={{0,16},{16,0},{1,17},{17,1},{2,18},{18,2},{3,19},{19,3},{4,20},{20... | collective-permute-start | bytes 1572872 | tf_op jit(solution)/shard_map/ppermute | solution.py:218
  60.9 0.8 slice.28
  61.8 0.1 convert_reduce_fusion
  61.9 0.8 slice.26
  62.7 0.8 slice.27
  63.5 2.6 %collective-permute-done.19.refs_7_ = bf16[2,4,128,256]{3,2,1,0:T(8,128)(2,1)S(1)} collective-permute-done((bf16[2,4,128,256]{3,2,1,0:T(8,128)(2,1)S(1)}, bf16[2,4,128,256]{3,2,1,0:T(8,128)(2,1)S(1)}, u32[]{:S(2)}, u32[]{:S(2)}) %collective-permute-start.19) | collective-permute-done | bytes 524320 | tf_op jit(solution)/shard_map/ppermute | solution.py:244
  66.1 2.1 %shard_map.114 = (bf16[4,256,256]{2,1,0:T(8,128)(2,1)S(1)}, bf16[4,256,256]{2,1,0:T(8,128)(2,1)S(1)}) custom-call(bf16[4,128,256]{2,1,0:T(8,128)(2,1)S(1)} %bitcast.34, bf16[2,4,128,256]{3,2,1,0:T(8,128)(2,1)S(1)} %collective-permute-done.2.refs_1_, bf16[2,4,128,256]{3,2,1,0:T(8,128)(2,1)S(1)} %collective-permute-done.16.refs_2_, ...), custom_call_target="tpu_custom_call" | custom-call | flops 1073741824 | bytes 4718592 | tf_op jit(solution)/shard_map/pallas_call | solution.py:77
  68.2 1.6 %collective-permute-start.26 = (bf16[4,256,256]{2,1,0:T(8,128)(2,1)S(1)}, bf16[4,256,256]{2,1,0:T(8,128)(2,1)S(1)}, u32[]{:S(2)}, u32[]{:S(2)}) collective-permute-start(bf16[4,256,256]{2,1,0:T(8,128)(2,1)S(1)} %get-tuple-element.28), channel_id=1, source_target_pairs={{0,16},{16,0},{1,17},{17,1},{2,18},{18,2},{3,19},{19,3},{4,20},{20... | collective-permute-start | bytes 1572872 | tf_op jit(solution)/shard_map/ppermute | solution.py:218
  69.8 0.6 fusion.prev_ref
  70.4 2.1 %collective-permute-done.21.other_ref = bf16[4,256,256]{2,1,0:T(8,128)(2,1)S(1)} collective-permute-done((bf16[4,256,256]{2,1,0:T(8,128)(2,1)S(1)}, bf16[4,256,256]{2,1,0:T(8,128)(2,1)S(1)}, u32[]{:S(2)}, u32[]{:S(2)}) %collective-permute-start.21) | collective-permute-done | bytes 524320 | tf_op jit(solution)/shard_map/ppermute | solution.py:218
  72.6 0.9 %shard_map.115 = (bf16[10,256,256]{2,1,0:T(8,128)(2,1)S(1)}, bf16[2,256,256]{2,1,0:T(8,128)(2,1)S(1)}, bf16[2,256,256]{2,1,0:T(8,128)(2,1)S(1)}, bf16[3,256,256]...) custom-call(s32[1]{0:T(128)} %bitcast.group_ref, f32[4,256,256]{2,1,0:T(8,128)S(1)} %get-tuple-element.29.own_ref, ...), custom_call_target="tpu_custom_call" | custom-call | tf_op jit(solution)/shard_map/pallas_call | solution.py:124
  73.5 0.5 collective-permute-start.25
  74.0 0.1 collective-permute-start.22
  74.1 0.4 collective-permute-start.23
  74.6 1.6 %collective-permute-done.22.refs_0_ = bf16[2,256,256]{2,1,0:T(8,128)(2,1)S(1)} collective-permute-done((bf16[2,256,256]{2,1,0:T(8,128)(2,1)S(1)}, bf16[2,256,256]{2,1,0:T(8,128)(2,1)S(1)}, u32[]{:S(2)}, u32[]{:S(2)}) %collective-permute-start.22) | collective-permute-done | bytes 262176 | tf_op jit(solution)/shard_map/ppermute | solution.py:218
  76.2 0.4 collective-permute-done.23.refs_1_
  76.6 5.1 %shard_map.116 = bf16[2048,256]{1,0:T(8,128)(2,1)} custom-call(s32[1]{0:T(128)} %bitcast.group_ref, f32[4,256,256]{2,1,0:T(8,128)S(1)} %get-tuple-element.29.own_ref, bf16[4,256,256]{2,1,0:T(8,128)(2,1)S(1)} %collective-permute-done.21.other_ref, bf16[10,256,256]{2,1,0:T(8,128)(2,1)S(1)} %fusion.prev_ref, ...), custom_call_target="tpu_custom_call" | custom-call | tf_op jit(solution)/shard_map/pallas_call | solution.py:174
  81.7 1.4 %collective-permute-done.26.other_ref = bf16[4,256,256]{2,1,0:T(8,128)(2,1)S(1)} collective-permute-done((bf16[4,256,256]{2,1,0:T(8,128)(2,1)S(1)}, bf16[4,256,256]{2,1,0:T(8,128)(2,1)S(1)}, u32[]{:S(2)}, u32[]{:S(2)}) %collective-permute-start.26) | collective-permute-done | bytes 524320 | tf_op jit(solution)/shard_map/ppermute | solution.py:218
  83.1 2.0 %shard_map.117 = bf16[2048,256]{1,0:T(8,128)(2,1)} custom-call(s32[1]{0:T(128)} %bitcast.group_ref, bf16[4,256,256]{2,1,0:T(8,128)(2,1)S(1)} %get-tuple-element.36.own_ref, bf16[4,256,256]{2,1,0:T(8,128)(2,1)S(1)} %collective-permute-done.26.other_ref), custom_call_target="tpu_custom_call" | custom-call | tf_op jit(solution)/shard_map/pallas_call | solution.py:206
  (54 shorter events, 0.8 us)
Async XLA Ops:
  2.1 4.9 %copy-start.9 = (s32[8]{0:T(128)S(1)}, s32[8]{0:T(128)}, u32[]{:S(2)}) copy-start(s32[8]{0:T(128)} %param.15) | copy-start | bytes 100
  2.1 5.0 %copy-start.6 = (bf16[256,512]{1,0:T(8,128)(2,1)S(1)}, bf16[256,512]{1,0:T(8,128)(2,1)}, u32[]{:S(2)}) copy-start(bf16[256,512]{1,0:T(8,128)(2,1)} %param.10) | copy-start | bytes 786436
  2.1 5.0 %copy-start.7 = (bf16[8,8,256]{2,1,0:T(8,128)(2,1)S(1)}, bf16[8,8,256]{2,1,0:T(8,128)(2,1)}, u32[]{:S(2)}) copy-start(bf16[8,8,256]{2,1,0:T(8,128)(2,1)} %param.13) | copy-start | bytes 98308
  2.2 5.0 %copy-start.8 = (bf16[8,2,256]{2,1,0:T(2,128)(2,1)S(1)}, bf16[8,2,256]{2,1,0:T(2,128)(2,1)}, u32[]{:S(2)}) copy-start(bf16[8,2,256]{2,1,0:T(2,128)(2,1)} %param.14) | copy-start | bytes 24580
  2.2 1.7 %collective-permute-start = (bf16[4,128,256]{2,1,0:T(8,128)(2,1)S(1)}, bf16[4,128,256]{2,1,0:T(8,128)(2,1)S(1)}, u32[]{:S(2)}, u32[]{:S(2)}) collective-permute-start(bf16[4,128,256]{2,1,0:T(8,128)(2,1)S(1)} %bitcast.35), channel_id=1, source_target_pairs={{0,1},{1,0},{2,3},{3,2},{4,5},{5,4},{6,7},{7,6},{8,9},{9,8},{10,11... | collective-permute-start | bytes 786440 | tf_op jit(solution)/shard_map/ppermute | solution.py:218
  3.9 11.6 %collective-permute-start.5 = (bf16[2,4,128,256]{3,2,1,0:T(8,128)(2,1)S(1)}, bf16[2,4,128,256]{3,2,1,0:T(8,128)(2,1)S(1)}, u32[]{:S(2)}, u32[]{:S(2)}) collective-permute-start(bf16[2,4,128,256]{3,2,1,0:T(8,128)(2,1)S(1)} %pad_maximum_fusion.1), channel_id=1, source_target_pairs={{0,4},{5,1},{4,8},{9,5},{8,12},{13,9},{12,14},{15,13},{14,10},{11,... | collective-permute-start | bytes 1572872 | tf_op jit(solution)/shard_map/ppermute | solution.py:244
  7.0 1.6 %collective-permute-start.1 = (bf16[4,128,256]{2,1,0:T(8,128)(2,1)S(1)}, bf16[4,128,256]{2,1,0:T(8,128)(2,1)S(1)}, u32[]{:S(2)}, u32[]{:S(2)}) collective-permute-start(bf16[4,128,256]{2,1,0:T(8,128)(2,1)S(1)} %bitcast.32), channel_id=1, source_target_pairs={{0,1},{1,0},{2,3},{3,2},{4,5},{5,4},{6,7},{7,6},{8,9},{9,8},{10,11... | collective-permute-start | bytes 786440 | tf_op jit(solution)/shard_map/ppermute | solution.py:218
  8.6 19.4 %all-to-all-start = ((bf16[8,40,512]{2,1,0:T(8,128)(2,1)}), bf16[8,40,512]{2,1,0:T(8,128)(2,1)S(1)}, u32[]{:S(2)}, u32[]{:S(2)}) async-start(bf16[8,40,512]{2,1,0:T(8,128)(2,1)} %maximum_maximum_fusion), calls=%async_computation | async-start | bytes 655360 | tf_op jit(solution)/shard_map/all_to_all | solution.py:297
  13.4 12.4 %collective-permute-start.2 = (bf16[2,4,128,256]{3,2,1,0:T(8,128)(2,1)S(1)}, bf16[2,4,128,256]{3,2,1,0:T(8,128)(2,1)S(1)}, u32[]{:S(2)}, u32[]{:S(2)}) collective-permute-start(bf16[2,4,128,256]{3,2,1,0:T(8,128)(2,1)S(1)} %pad_maximum_fusion), channel_id=1, source_target_pairs={{0,4},{5,1},{4,8},{9,5},{8,12},{13,9},{12,14},{15,13},{14,10},{11,... | collective-permute-start | bytes 1572872 | tf_op jit(solution)/shard_map/ppermute | solution.py:244
  15.5 16.0 %collective-permute-start.7 = (bf16[2,4,128,256]{3,2,1,0:T(8,128)(2,1)S(1)}, bf16[2,4,128,256]{3,2,1,0:T(8,128)(2,1)}, u32[]{:S(2)}, u32[]{:S(2)}) collective-permute-start(bf16[2,4,128,256]{3,2,1,0:T(8,128)(2,1)S(1)} %collective-permute-done.5.refs_1_), channel_id=1, source_target_pairs={{0,4},{5,1},{4,8},{9,5},{8,12},{13,9},{12,14},{15,13},{14,10},{11,... | collective-permute-start | bytes 1572872 | tf_op jit(solution)/shard_map/ppermute | solution.py:244
  25.8 11.6 %collective-permute-start.3 = (bf16[2,4,128,256]{3,2,1,0:T(8,128)(2,1)S(1)}, bf16[2,4,128,256]{3,2,1,0:T(8,128)(2,1)S(1)}, u32[]{:S(2)}, u32[]{:S(2)}) collective-permute-start(bf16[2,4,128,256]{3,2,1,0:T(8,128)(2,1)S(1)} %collective-permute-done.2.refs_1_), channel_id=1, source_target_pairs={{0,4},{5,1},{4,8},{9,5},{8,12},{13,9},{12,14},{15,13},{14,10},{11,... | collective-permute-start | bytes 1572872 | tf_op jit(solution)/shard_map/ppermute | solution.py:244
  28.0 0.7 copy-start.5
  31.5 11.1 %collective-permute-start.9 = (bf16[2,4,128,256]{3,2,1,0:T(8,128)(2,1)}, bf16[2,4,128,256]{3,2,1,0:T(8,128)(2,1)S(1)}, u32[]{:S(2)}, u32[]{:S(2)}) collective-permute-start(bf16[2,4,128,256]{3,2,1,0:T(8,128)(2,1)} %collective-permute-done.7.refs_3_), channel_id=1, source_target_pairs={{0,4},{5,1},{4,8},{9,5},{8,12},{13,9},{12,14},{15,13},{14,10},{11,... | collective-permute-start | bytes 1572872 | tf_op jit(solution)/shard_map/ppermute | solution.py:244
  33.7 1.6 %collective-permute-start.11 = (bf16[256,512]{1,0:T(8,128)(2,1)S(1)}, bf16[256,512]{1,0:T(8,128)(2,1)S(1)}, u32[]{:S(2)}, u32[]{:S(2)}) collective-permute-start(bf16[256,512]{1,0:T(8,128)(2,1)S(1)} %fusion.3.refs_9_.refs_8_), channel_id=1, source_target_pairs={{0,1},{1,0},{2,3},{3,2},{4,5},{5,4},{6,7},{7,6},{8,9},{9,8},{10,11... | collective-permute-start | bytes 786440 | tf_op jit(solution)/shard_map/ppermute | solution.py:218
  35.3 8.3 %collective-permute-start.12 = (bf16[256,512]{1,0:T(8,128)(2,1)S(1)}, bf16[256,512]{1,0:T(8,128)(2,1)S(1)}, u32[]{:S(2)}, u32[]{:S(2)}) collective-permute-start(bf16[256,512]{1,0:T(8,128)(2,1)S(1)} %fusion.3.refs_9_.refs_8_), channel_id=1, source_target_pairs={{0,16},{16,0},{1,17},{17,1},{2,18},{18,2},{3,19},{19,3},{4,20},{20... | collective-permute-start | bytes 786440 | tf_op jit(solution)/shard_map/ppermute | solution.py:218
  36.9 9.4 %collective-permute-start.6 = (bf16[2,4,128,256]{3,2,1,0:T(8,128)(2,1)S(1)}, bf16[2,4,128,256]{3,2,1,0:T(8,128)(2,1)}, u32[]{:S(2)}, u32[]{:S(2)}) collective-permute-start(bf16[2,4,128,256]{3,2,1,0:T(8,128)(2,1)S(1)} %collective-permute-done.5.refs_1_), channel_id=1, source_target_pairs={{0,1},{1,0},{2,3},{3,2},{4,5},{5,4},{6,7},{7,6},{8,9},{9,8},{10,11... | collective-permute-start | bytes 1572872 | tf_op jit(solution)/shard_map/ppermute | solution.py:218
  36.9 15.2 %collective-permute-start.8 = (bf16[2,4,128,256]{3,2,1,0:T(8,128)(2,1)}, bf16[2,4,128,256]{3,2,1,0:T(8,128)(2,1)S(1)}, u32[]{:S(2)}, u32[]{:S(2)}) collective-permute-start(bf16[2,4,128,256]{3,2,1,0:T(8,128)(2,1)} %collective-permute-done.7.refs_3_), channel_id=1, source_target_pairs={{0,1},{1,0},{2,3},{3,2},{4,5},{5,4},{6,7},{7,6},{8,9},{9,8},{10,11... | collective-permute-start | bytes 1572872 | tf_op jit(solution)/shard_map/ppermute | solution.py:218
  37.4 14.6 %collective-permute-start.4 = (bf16[2,4,128,256]{3,2,1,0:T(8,128)(2,1)S(1)}, bf16[2,4,128,256]{3,2,1,0:T(8,128)(2,1)S(1)}, u32[]{:S(2)}, u32[]{:S(2)}) collective-permute-start(bf16[2,4,128,256]{3,2,1,0:T(8,128)(2,1)S(1)} %collective-permute-done.3.refs_3_), channel_id=1, source_target_pairs={{0,4},{5,1},{4,8},{9,5},{8,12},{13,9},{12,14},{15,13},{14,10},{11,... | collective-permute-start | bytes 1572872 | tf_op jit(solution)/shard_map/ppermute | solution.py:244
  42.7 19.0 %copy-start = (bf16[3,256,256]{2,1,0:T(8,128)(2,1)S(1)}, bf16[3,256,256]{2,1,0:T(8,128)(2,1)}, u32[]{:S(2)}) copy-start(bf16[3,256,256]{2,1,0:T(8,128)(2,1)} %refs_5_.1) | copy-start | bytes 1179652
  43.7 7.4 %collective-permute-start.13 = (bf16[2,2,128,256]{3,2,1,0:T(8,128)(2,1)S(1)}, bf16[2,2,128,256]{3,2,1,0:T(8,128)(2,1)S(1)}, u32[]{:S(2)}, u32[]{:S(2)}) collective-permute-start(bf16[2,2,128,256]{3,2,1,0:T(8,128)(2,1)S(1)} %constant_dynamic-slice_fusion), channel_id=1, source_target_pairs={{0,4},{5,1},{4,8},{9,5},{8,12},{13,9},{12,14},{15,13},{14,10},{11,... | collective-permute-start | bytes 786440 | tf_op jit(solution)/shard_map/ppermute | solution.py:244
  46.3 6.9 %collective-permute-start.10 = (bf16[2,4,128,256]{3,2,1,0:T(8,128)(2,1)S(1)}, bf16[2,4,128,256]{3,2,1,0:T(8,128)(2,1)S(1)}, u32[]{:S(2)}, u32[]{:S(2)}) collective-permute-start(bf16[2,4,128,256]{3,2,1,0:T(8,128)(2,1)S(1)} %collective-permute-done.9.refs_5_), channel_id=1, source_target_pairs={{0,1},{1,0},{2,3},{3,2},{4,5},{5,4},{6,7},{7,6},{8,9},{9,8},{10,11... | collective-permute-start | bytes 1572872 | tf_op jit(solution)/shard_map/ppermute | solution.py:218
  46.3 6.2 %collective-permute-start.15 = (bf16[256,512]{1,0:T(8,128)(2,1)S(1)}, bf16[256,512]{1,0:T(8,128)(2,1)S(1)}, u32[]{:S(2)}, u32[]{:S(2)}) collective-permute-start(bf16[256,512]{1,0:T(8,128)(2,1)S(1)} %collective-permute-done.12.refs_11_.refs_10_), channel_id=1, source_target_pairs={{0,1},{1,0},{2,3},{3,2},{4,5},{5,4},{6,7},{7,6},{8,9},{9,8},{10,11... | collective-permute-start | bytes 786440 | tf_op jit(solution)/shard_map/ppermute | solution.py:218
  51.1 2.1 %collective-permute-start.14 = (bf16[2,2,128,256]{3,2,1,0:T(8,128)(2,1)S(1)}, bf16[2,2,128,256]{3,2,1,0:T(8,128)(2,1)S(1)}, u32[]{:S(2)}, u32[]{:S(2)}) collective-permute-start(bf16[2,2,128,256]{3,2,1,0:T(8,128)(2,1)S(1)} %collective-permute-done.13.refs_7_), channel_id=1, source_target_pairs={{0,1},{1,0},{2,3},{3,2},{4,5},{5,4},{6,7},{7,6},{8,9},{9,8},{10,11... | collective-permute-start | bytes 786440 | tf_op jit(solution)/shard_map/ppermute | solution.py:218
  52.0 9.7 %collective-permute-start.16 = (bf16[2,4,128,256]{3,2,1,0:T(8,128)(2,1)S(1)}, bf16[2,4,128,256]{3,2,1,0:T(8,128)(2,1)S(1)}, u32[]{:S(2)}, u32[]{:S(2)}) collective-permute-start(bf16[2,4,128,256]{3,2,1,0:T(8,128)(2,1)S(1)} %collective-permute-done.2.refs_1_), channel_id=1, source_target_pairs={{0,1},{1,0},{2,3},{3,2},{4,5},{5,4},{6,7},{7,6},{8,9},{9,8},{10,11... | collective-permute-start | bytes 1572872 | tf_op jit(solution)/shard_map/ppermute | solution.py:218
  52.0 11.4 %collective-permute-start.17 = (bf16[2,4,128,256]{3,2,1,0:T(8,128)(2,1)S(1)}, bf16[2,4,128,256]{3,2,1,0:T(8,128)(2,1)S(1)}, u32[]{:S(2)}, u32[]{:S(2)}) collective-permute-start(bf16[2,4,128,256]{3,2,1,0:T(8,128)(2,1)S(1)} %collective-permute-done.3.refs_3_), channel_id=1, source_target_pairs={{0,1},{1,0},{2,3},{3,2},{4,5},{5,4},{6,7},{7,6},{8,9},{9,8},{10,11... | collective-permute-start | bytes 1572872 | tf_op jit(solution)/shard_map/ppermute | solution.py:218
  52.5 10.9 %collective-permute-start.18 = (bf16[2,4,128,256]{3,2,1,0:T(8,128)(2,1)S(1)}, bf16[2,4,128,256]{3,2,1,0:T(8,128)(2,1)S(1)}, u32[]{:S(2)}, u32[]{:S(2)}) collective-permute-start(bf16[2,4,128,256]{3,2,1,0:T(8,128)(2,1)S(1)} %collective-permute-done.4.refs_5_), channel_id=1, source_target_pairs={{0,1},{1,0},{2,3},{3,2},{4,5},{5,4},{6,7},{7,6},{8,9},{9,8},{10,11... | collective-permute-start | bytes 1572872 | tf_op jit(solution)/shard_map/ppermute | solution.py:218
  56.1 10.0 %collective-permute-start.19 = (bf16[2,4,128,256]{3,2,1,0:T(8,128)(2,1)S(1)}, bf16[2,4,128,256]{3,2,1,0:T(8,128)(2,1)S(1)}, u32[]{:S(2)}, u32[]{:S(2)}) collective-permute-start(bf16[2,4,128,256]{3,2,1,0:T(8,128)(2,1)S(1)} %collective-permute-done.4.refs_5_), channel_id=1, source_target_pairs={{0,4},{5,1},{4,8},{9,5},{8,12},{13,9},{12,14},{15,13},{14,10},{11,... | collective-permute-start | bytes 1572872 | tf_op jit(solution)/shard_map/ppermute | solution.py:244
  59.4 13.2 %collective-permute-start.21 = (bf16[4,256,256]{2,1,0:T(8,128)(2,1)S(1)}, bf16[4,256,256]{2,1,0:T(8,128)(2,1)S(1)}, u32[]{:S(2)}, u32[]{:S(2)}) collective-permute-start(bf16[4,256,256]{2,1,0:T(8,128)(2,1)S(1)} %get-tuple-element.26), channel_id=1, source_target_pairs={{0,16},{16,0},{1,17},{17,1},{2,18},{18,2},{3,19},{19,3},{4,20},{20... | collective-permute-start | bytes 1572872 | tf_op jit(solution)/shard_map/ppermute | solution.py:218
  61.7 8.7 %collective-permute-start.20 = (bf16[3,256,256]{2,1,0:T(8,128)(2,1)S(1)}, bf16[3,256,256]{2,1,0:T(8,128)(2,1)S(1)}, u32[]{:S(2)}, u32[]{:S(2)}) collective-permute-start(bf16[3,256,256]{2,1,0:T(8,128)(2,1)S(1)} %copy-done), channel_id=1, source_target_pairs={{0,1},{1,0},{2,3},{3,2},{4,5},{5,4},{6,7},{7,6},{8,9},{9,8},{10,11... | collective-permute-start | bytes 1179656 | tf_op jit(solution)/shard_map/ppermute | solution.py:218
  68.2 4.4 %copy-start.2 = (f32[256]{0:T(256)S(1)}, f32[256]{0:T(256)}, u32[]{:S(2)}) copy-start(f32[256]{0:T(256)} %param.12) | copy-start | bytes 3076
  68.2 14.9 %collective-permute-start.26 = (bf16[4,256,256]{2,1,0:T(8,128)(2,1)S(1)}, bf16[4,256,256]{2,1,0:T(8,128)(2,1)S(1)}, u32[]{:S(2)}, u32[]{:S(2)}) collective-permute-start(bf16[4,256,256]{2,1,0:T(8,128)(2,1)S(1)} %get-tuple-element.28), channel_id=1, source_target_pairs={{0,16},{16,0},{1,17},{17,1},{2,18},{18,2},{3,19},{19,3},{4,20},{20... | collective-permute-start | bytes 1572872 | tf_op jit(solution)/shard_map/ppermute | solution.py:218
  72.6 4.0 %copy-start.1 = (bf16[256,256]{1,0:T(8,128)(2,1)S(1)}, bf16[256,256]{1,0:T(8,128)(2,1)}, u32[]{:S(2)}) copy-start(bf16[256,256]{1,0:T(8,128)(2,1)} %refs_8_.1) | copy-start | bytes 393220
  72.6 4.0 %copy-start.3 = (f32[256]{0:T(256)S(1)}, f32[256]{0:T(256)}, u32[]{:S(2)}) copy-start(f32[256]{0:T(256)} %param.17) | copy-start | bytes 3076
  72.6 4.0 %copy-start.4 = (f32[256]{0:T(256)S(1)}, f32[256]{0:T(256)}, u32[]{:S(2)}) copy-start(f32[256]{0:T(256)} %param.19) | copy-start | bytes 3076
  73.5 3.1 %collective-permute-start.24 = (bf16[3,256,256]{2,1,0:T(8,128)(2,1)S(1)}, bf16[3,256,256]{2,1,0:T(8,128)(2,1)S(1)}, u32[]{:S(2)}, u32[]{:S(2)}) collective-permute-start(bf16[3,256,256]{2,1,0:T(8,128)(2,1)S(1)} %get-tuple-element.33), channel_id=1, source_target_pairs={{0,1},{1,0},{2,3},{3,2},{4,5},{5,4},{6,7},{7,6},{8,9},{9,8},{10,11... | collective-permute-start | bytes 1179656 | tf_op jit(solution)/shard_map/ppermute | solution.py:218
  73.5 3.0 %collective-permute-start.25 = (bf16[3,256,256]{2,1,0:T(8,128)(2,1)S(1)}, bf16[3,256,256]{2,1,0:T(8,128)(2,1)S(1)}, u32[]{:S(2)}, u32[]{:S(2)}) collective-permute-start(bf16[3,256,256]{2,1,0:T(8,128)(2,1)S(1)} %get-tuple-element.34), channel_id=1, source_target_pairs={{0,1},{1,0},{2,3},{3,2},{4,5},{5,4},{6,7},{7,6},{8,9},{9,8},{10,11... | collective-permute-start | bytes 1179656 | tf_op jit(solution)/shard_map/ppermute | solution.py:218
  74.0 2.1 %collective-permute-start.22 = (bf16[2,256,256]{2,1,0:T(8,128)(2,1)S(1)}, bf16[2,256,256]{2,1,0:T(8,128)(2,1)S(1)}, u32[]{:S(2)}, u32[]{:S(2)}) collective-permute-start(bf16[2,256,256]{2,1,0:T(8,128)(2,1)S(1)} %get-tuple-element.31), channel_id=1, source_target_pairs={{0,1},{1,0},{2,3},{3,2},{4,5},{5,4},{6,7},{7,6},{8,9},{9,8},{10,11... | collective-permute-start | bytes 786440 | tf_op jit(solution)/shard_map/ppermute | solution.py:218
  74.1 2.4 %collective-permute-start.23 = (bf16[2,256,256]{2,1,0:T(8,128)(2,1)S(1)}, bf16[2,256,256]{2,1,0:T(8,128)(2,1)S(1)}, u32[]{:S(2)}, u32[]{:S(2)}) collective-permute-start(bf16[2,256,256]{2,1,0:T(8,128)(2,1)S(1)} %get-tuple-element.32), channel_id=1, source_target_pairs={{0,1},{1,0},{2,3},{3,2},{4,5},{5,4},{6,7},{7,6},{8,9},{9,8},{10,11... | collective-permute-start | bytes 786440 | tf_op jit(solution)/shard_map/ppermute | solution.py:218

commit v8 on v6

--- a/solution.py
+++ b/solution.py
@@ -165,7 +165,7 @@
 
 def residual(group, own, other, prev, mine, theirs, *parameters):
     taps, sessions, width = own.shape
-    steps, block = 2 * taps, sessions // 4
+    steps, block = 2 * taps, sessions // 2
 
     def blocks(array):
         return pl.BlockSpec((array.shape[0], block, width), lambda i: (0, i, 0))
@@ -174,7 +174,7 @@
     return pl.pallas_call(
         residual_kernel,
         out_shape=jax.ShapeDtypeStruct((sessions * steps, width), BF16),
-        grid=(4,),
+        grid=(2,),
         in_specs=[pl.BlockSpec(memory_space=pltpu.SMEM)]
         + [blocks(array) for array in arrays]
         + [VMEM] * len(parameters),
@@ -201,12 +201,12 @@
 
 def weave(group, own, other):
     taps, sessions, width = own.shape
-    steps, block = 2 * taps, sessions // 4
+    steps, block = 2 * taps, sessions // 2
     taken = pl.BlockSpec((taps, block, width), lambda i: (0, i, 0))
     return pl.pallas_call(
         weave_kernel,
         out_shape=jax.ShapeDtypeStruct((sessions * steps, width), BF16),
-        grid=(4,),
+        grid=(2,),
         in_specs=[pl.BlockSpec(memory_space=pltpu.SMEM), taken, taken],
         out_specs=pl.BlockSpec((block * steps, width), lambda i: (i, 0)),
         scratch_shapes=[pltpu.VMEM((width // 128, block * steps, 128), F32)],

time: 85.9 us -> 85.2 us (level)
  Pallas kernels: 13.1 us -> 12.2 us
  transfers between devices with their start and end apart: 28 -> 28, of which waited for: 13 -> 14; matrix products, arithmetic and copies ran while one was open for 5% -> 5% of each run, Pallas kernels for 13% -> 13%
where the time goes in v8:
time: 85.2 us; the launch traced here: 84.7 us
  waiting for transfers between devices  32.8 us (38%)
  starting transfers between devices  32.3 us (38%)
  Pallas kernels  12.2 us (14%)
  local copies, waits for them, and re-layouts  4.73 us (6%)
  other arithmetic  1.17 us (1%)
  between operations  0.93 us (1%)
    ppermute x8, waiting for transfers between devices, round(): item = lax.ppermute(item, ('streams', 'segment'), self.pairs)  19.4 us
    ppermute x8, starting transfers between devices, round(): item = lax.ppermute(item, ('streams', 'segment'), self.pairs)  18.9 us
    ppermute x19, waiting for transfers between devices, swap(): return lax.ppermute(value, axis, [(0, 1), (1, 0)])  13.3 us
    ppermute x19, starting transfers between devices, swap(): return lax.ppermute(value, axis, [(0, 1), (1, 0)])  8.55 us
    pallas_call x2, Pallas kernels, spread_taps(): pl.pallas_call(functools.partial(spread_kernel, count, steps), out_shape=...  5.07 us
    all_to_all x1, starting transfers between devices, local(): lax.all_to_all(parcel, 'streams', split_axis=0, concat_axis=0, tiled=True)  4.79 us
    pallas_call x1, Pallas kernels, residual(): pl.pallas_call(residual_kernel, out_shape=jax.ShapeDtypeStruct((sessions...  4.68 us
  transfers between devices with their start and end apart: 28, of which 14 were waited for; matrix products, arithmetic and copies ran while one was open for 5% of the time, Pallas kernels for 13%

profile of v8, /device:TPU:0, one launch (start us, length us, event | category | flops | bytes accessed | tf_op | source)
XLA Modules:
  0.0 84.7 jit_solution(11116362495750008698)
XLA Ops:
  0.6 1.5 %constant_dynamic-slice_fusion.1 = (bf16[128,4,256]{2,1,0:T(4,128)(2,1)S(1)}, bf16[128,4,256]{2,1,0:T(4,128)(2,1)S(1)}) fusion(bf16[128,16,256]{2,1,0:T(8,128)(2,1)} %param.11, s32[]{:T(128)S(6)} %select_n.14, s32[]{:T(128)S(6)} %select_n.13), kind=kLoop, calls=%fused_computation.23 | loop fusion | bytes 1048584 | tf_op jit(solution)/shard_map/dynamic_slice | solution.py:275
  2.2 0.5 collective-permute-start
  2.7 1.2 %collective-permute-done = bf16[4,128,256]{2,1,0:T(8,128)(2,1)S(1)} collective-permute-done((bf16[4,128,256]{2,1,0:T(8,128)(2,1)S(1)}, bf16[4,128,256]{2,1,0:T(8,128)(2,1)S(1)}, u32[]{:S(2)}, u32[]{:S(2)}) %collective-permute-start) | collective-permute-done | bytes 262176 | tf_op jit(solution)/shard_map/ppermute | solution.py:218
  3.9 3.0 %collective-permute-start.5 = (bf16[2,4,128,256]{3,2,1,0:T(8,128)(2,1)S(1)}, bf16[2,4,128,256]{3,2,1,0:T(8,128)(2,1)S(1)}, u32[]{:S(2)}, u32[]{:S(2)}) collective-permute-start(bf16[2,4,128,256]{3,2,1,0:T(8,128)(2,1)S(1)} %pad_maximum_fusion.1), channel_id=1, source_target_pairs={{0,4},{5,1},{4,8},{9,5},{8,12},{13,9},{12,14},{15,13},{14,10},{11,... | collective-permute-start | bytes 1572872 | tf_op jit(solution)/shard_map/ppermute | solution.py:244
  7.2 0.8 maximum_maximum_fusion
  8.0 0.6 collective-permute-done.1
  8.6 4.8 %all-to-all-start = ((bf16[8,40,512]{2,1,0:T(8,128)(2,1)}), bf16[8,40,512]{2,1,0:T(8,128)(2,1)S(1)}, u32[]{:S(2)}, u32[]{:S(2)}) async-start(bf16[8,40,512]{2,1,0:T(8,128)(2,1)} %maximum_maximum_fusion), calls=%async_computation | async-start | bytes 655360 | tf_op jit(solution)/shard_map/all_to_all | solution.py:297
  13.4 2.1 %collective-permute-start.2 = (bf16[2,4,128,256]{3,2,1,0:T(8,128)(2,1)S(1)}, bf16[2,4,128,256]{3,2,1,0:T(8,128)(2,1)S(1)}, u32[]{:S(2)}, u32[]{:S(2)}) collective-permute-start(bf16[2,4,128,256]{3,2,1,0:T(8,128)(2,1)S(1)} %pad_maximum_fusion), channel_id=1, source_target_pairs={{0,4},{5,1},{4,8},{9,5},{8,12},{13,9},{12,14},{15,13},{14,10},{11,... | collective-permute-start | bytes 1572872 | tf_op jit(solution)/shard_map/ppermute | solution.py:244
  15.5 1.5 %collective-permute-start.7 = (bf16[2,4,128,256]{3,2,1,0:T(8,128)(2,1)S(1)}, bf16[2,4,128,256]{3,2,1,0:T(8,128)(2,1)}, u32[]{:S(2)}, u32[]{:S(2)}) collective-permute-start(bf16[2,4,128,256]{3,2,1,0:T(8,128)(2,1)S(1)} %collective-permute-done.5.refs_1_), channel_id=1, source_target_pairs={{0,4},{5,1},{4,8},{9,5},{8,12},{13,9},{12,14},{15,13},{14,10},{11,... | collective-permute-start | bytes 1572872 | tf_op jit(solution)/shard_map/ppermute | solution.py:244
  17.0 8.9 %collective-permute-done.2.refs_1_ = bf16[2,4,128,256]{3,2,1,0:T(8,128)(2,1)S(1)} collective-permute-done((bf16[2,4,128,256]{3,2,1,0:T(8,128)(2,1)S(1)}, bf16[2,4,128,256]{3,2,1,0:T(8,128)(2,1)S(1)}, u32[]{:S(2)}, u32[]{:S(2)}) %collective-permute-start.2) | collective-permute-done | bytes 524320 | tf_op jit(solution)/shard_map/ppermute | solution.py:244
  25.8 2.1 %collective-permute-start.3 = (bf16[2,4,128,256]{3,2,1,0:T(8,128)(2,1)S(1)}, bf16[2,4,128,256]{3,2,1,0:T(8,128)(2,1)S(1)}, u32[]{:S(2)}, u32[]{:S(2)}) collective-permute-start(bf16[2,4,128,256]{3,2,1,0:T(8,128)(2,1)S(1)} %collective-permute-done.2.refs_1_), channel_id=1, source_target_pairs={{0,4},{5,1},{4,8},{9,5},{8,12},{13,9},{12,14},{15,13},{14,10},{11,... | collective-permute-start | bytes 1572872 | tf_op jit(solution)/shard_map/ppermute | solution.py:244
  28.0 0.7 copy-done.5
  28.7 2.8 %collective-permute-done.7.refs_3_ = bf16[2,4,128,256]{3,2,1,0:T(8,128)(2,1)} collective-permute-done((bf16[2,4,128,256]{3,2,1,0:T(8,128)(2,1)S(1)}, bf16[2,4,128,256]{3,2,1,0:T(8,128)(2,1)}, u32[]{:S(2)}, u32[]{:S(2)}) %collective-permute-start.7) | collective-permute-done | bytes 524320 | tf_op jit(solution)/shard_map/ppermute | solution.py:244
  31.5 2.0 %collective-permute-start.9 = (bf16[2,4,128,256]{3,2,1,0:T(8,128)(2,1)}, bf16[2,4,128,256]{3,2,1,0:T(8,128)(2,1)S(1)}, u32[]{:S(2)}, u32[]{:S(2)}) collective-permute-start(bf16[2,4,128,256]{3,2,1,0:T(8,128)(2,1)} %collective-permute-done.7.refs_3_), channel_id=1, source_target_pairs={{0,4},{5,1},{4,8},{9,5},{8,12},{13,9},{12,14},{15,13},{14,10},{11,... | collective-permute-start | bytes 1572872 | tf_op jit(solution)/shard_map/ppermute | solution.py:244
  33.6 0.1 fusion.3.refs_9_.refs_8_
  33.8 0.5 collective-permute-start.6
  34.3 1.0 %collective-permute-done.11.refs_10_.refs_9_ = bf16[256,512]{1,0:T(8,128)(2,1)S(1)} collective-permute-done((bf16[256,512]{1,0:T(8,128)(2,1)S(1)}, bf16[256,512]{1,0:T(8,128)(2,1)S(1)}, u32[]{:S(2)}, u32[]{:S(2)}) %collective-permute-start.11) | collective-permute-done | bytes 262176 | tf_op jit(solution)/shard_map/ppermute | solution.py:218
  35.3 1.5 %collective-permute-start.12 = (bf16[256,512]{1,0:T(8,128)(2,1)S(1)}, bf16[256,512]{1,0:T(8,128)(2,1)S(1)}, u32[]{:S(2)}, u32[]{:S(2)}) collective-permute-start(bf16[256,512]{1,0:T(8,128)(2,1)S(1)} %fusion.3.refs_9_.refs_8_), channel_id=1, source_target_pairs={{0,16},{16,0},{1,17},{17,1},{2,18},{18,2},{3,19},{19,3},{4,20},{20... | collective-permute-start | bytes 786440 | tf_op jit(solution)/shard_map/ppermute | solution.py:218
  36.9 0.2 collective-permute-done.3.refs_3_
  37.1 2.4 %collective-permute-start.4 = (bf16[2,4,128,256]{3,2,1,0:T(8,128)(2,1)S(1)}, bf16[2,4,128,256]{3,2,1,0:T(8,128)(2,1)S(1)}, u32[]{:S(2)}, u32[]{:S(2)}) collective-permute-start(bf16[2,4,128,256]{3,2,1,0:T(8,128)(2,1)S(1)} %collective-permute-done.3.refs_3_), channel_id=1, source_target_pairs={{0,4},{5,1},{4,8},{9,5},{8,12},{13,9},{12,14},{15,13},{14,10},{11,... | collective-permute-start | bytes 1572872 | tf_op jit(solution)/shard_map/ppermute | solution.py:244
  39.4 3.2 %collective-permute-done.9.refs_5_ = bf16[2,4,128,256]{3,2,1,0:T(8,128)(2,1)S(1)} collective-permute-done((bf16[2,4,128,256]{3,2,1,0:T(8,128)(2,1)}, bf16[2,4,128,256]{3,2,1,0:T(8,128)(2,1)S(1)}, u32[]{:S(2)}, u32[]{:S(2)}) %collective-permute-start.9) | collective-permute-done | bytes 524320 | tf_op jit(solution)/shard_map/ppermute | solution.py:244
  42.7 1.0 %collective-permute-done.12.refs_11_.refs_10_ = bf16[256,512]{1,0:T(8,128)(2,1)S(1)} collective-permute-done((bf16[256,512]{1,0:T(8,128)(2,1)S(1)}, bf16[256,512]{1,0:T(8,128)(2,1)S(1)}, u32[]{:S(2)}, u32[]{:S(2)}) %collective-permute-start.12) | collective-permute-done | bytes 262176 | tf_op jit(solution)/shard_map/ppermute | solution.py:218
  43.7 2.6 %collective-permute-start.13 = (bf16[2,2,128,256]{3,2,1,0:T(8,128)(2,1)S(1)}, bf16[2,2,128,256]{3,2,1,0:T(8,128)(2,1)S(1)}, u32[]{:S(2)}, u32[]{:S(2)}) collective-permute-start(bf16[2,2,128,256]{3,2,1,0:T(8,128)(2,1)S(1)} %constant_dynamic-slice_fusion), channel_id=1, source_target_pairs={{0,4},{5,1},{4,8},{9,5},{8,12},{13,9},{12,14},{15,13},{14,10},{11,... | collective-permute-start | bytes 786440 | tf_op jit(solution)/shard_map/ppermute | solution.py:244
  46.3 0.5 collective-permute-start.15
  46.8 4.3 %collective-permute-done.13.refs_7_ = bf16[2,2,128,256]{3,2,1,0:T(8,128)(2,1)S(1)} collective-permute-done((bf16[2,2,128,256]{3,2,1,0:T(8,128)(2,1)S(1)}, bf16[2,2,128,256]{3,2,1,0:T(8,128)(2,1)S(1)}, u32[]{:S(2)}, u32[]{:S(2)}) %collective-permute-start.13) | collective-permute-done | bytes 262176 | tf_op jit(solution)/shard_map/ppermute | solution.py:244
  51.1 0.9 %collective-permute-start.14 = (bf16[2,2,128,256]{3,2,1,0:T(8,128)(2,1)S(1)}, bf16[2,2,128,256]{3,2,1,0:T(8,128)(2,1)S(1)}, u32[]{:S(2)}, u32[]{:S(2)}) collective-permute-start(bf16[2,2,128,256]{3,2,1,0:T(8,128)(2,1)S(1)} %collective-permute-done.13.refs_7_), channel_id=1, source_target_pairs={{0,1},{1,0},{2,3},{3,2},{4,5},{5,4},{6,7},{7,6},{8,9},{9,8},{10,11... | collective-permute-start | bytes 786440 | tf_op jit(solution)/shard_map/ppermute | solution.py:218
  52.0 0.5 collective-permute-start.17
  52.6 0.6 collective-permute-done.14.refs_8_
  53.2 3.2 %collective-permute-start.19 = (bf16[2,4,128,256]{3,2,1,0:T(8,128)(2,1)S(1)}, bf16[2,4,128,256]{3,2,1,0:T(8,128)(2,1)S(1)}, u32[]{:S(2)}, u32[]{:S(2)}) collective-permute-start(bf16[2,4,128,256]{3,2,1,0:T(8,128)(2,1)S(1)} %collective-permute-done.4.refs_5_), channel_id=1, source_target_pairs={{0,4},{5,1},{4,8},{9,5},{8,12},{13,9},{12,14},{15,13},{14,10},{11,... | collective-permute-start | bytes 1572872 | tf_op jit(solution)/shard_map/ppermute | solution.py:244
  56.4 2.9 %shard_map.113 = (f32[4,256,256]{2,1,0:T(8,128)S(1)}, bf16[4,256,256]{2,1,0:T(8,128)(2,1)S(1)}) custom-call(bf16[4,128,256]{2,1,0:T(8,128)(2,1)S(1)} %bitcast.37, bf16[2,4,128,256]{3,2,1,0:T(8,128)(2,1)S(1)} %collective-permute-done.5.refs_1_, bf16[2,4,128,256]{3,2,1,0:T(8,128)(2,1)} %collective-permute-done.6.refs_2_, ...), custom_call_target="tpu_custom_call" | custom-call | flops 1073741824 | bytes 4718592 | tf_op jit(solution)/shard_map/pallas_call | solution.py:77
  59.3 1.6 %collective-permute-start.21 = (bf16[4,256,256]{2,1,0:T(8,128)(2,1)S(1)}, bf16[4,256,256]{2,1,0:T(8,128)(2,1)S(1)}, u32[]{:S(2)}, u32[]{:S(2)}) collective-permute-start(bf16[4,256,256]{2,1,0:T(8,128)(2,1)S(1)} %get-tuple-element.27), channel_id=1, source_target_pairs={{0,16},{16,0},{1,17},{17,1},{2,18},{18,2},{3,19},{19,3},{4,20},{20... | collective-permute-start | bytes 1572872 | tf_op jit(solution)/shard_map/ppermute | solution.py:218
  60.9 0.8 slice.28
  61.8 0.1 convert_reduce_fusion
  61.9 0.8 slice.26
  62.7 0.8 slice.27
  63.5 2.1 %shard_map.114 = (bf16[4,256,256]{2,1,0:T(8,128)(2,1)S(1)}, bf16[4,256,256]{2,1,0:T(8,128)(2,1)S(1)}) custom-call(bf16[4,128,256]{2,1,0:T(8,128)(2,1)S(1)} %bitcast.34, bf16[2,4,128,256]{3,2,1,0:T(8,128)(2,1)S(1)} %collective-permute-done.2.refs_1_, bf16[2,4,128,256]{3,2,1,0:T(8,128)(2,1)S(1)} %collective-permute-done.16.refs_2_, ...), custom_call_target="tpu_custom_call" | custom-call | flops 1073741824 | bytes 4718592 | tf_op jit(solution)/shard_map/pallas_call | solution.py:77
  65.6 1.1 %collective-permute-start.26 = (bf16[4,256,256]{2,1,0:T(8,128)(2,1)S(1)}, bf16[4,256,256]{2,1,0:T(8,128)(2,1)S(1)}, u32[]{:S(2)}, u32[]{:S(2)}) collective-permute-start(bf16[4,256,256]{2,1,0:T(8,128)(2,1)S(1)} %get-tuple-element.25), channel_id=1, source_target_pairs={{0,16},{16,0},{1,17},{17,1},{2,18},{18,2},{3,19},{19,3},{4,20},{20... | collective-permute-start | bytes 1572872 | tf_op jit(solution)/shard_map/ppermute | solution.py:218
  66.8 0.6 fusion.prev_ref
  67.4 6.8 %collective-permute-done.21.other_ref = bf16[4,256,256]{2,1,0:T(8,128)(2,1)S(1)} collective-permute-done((bf16[4,256,256]{2,1,0:T(8,128)(2,1)S(1)}, bf16[4,256,256]{2,1,0:T(8,128)(2,1)S(1)}, u32[]{:S(2)}, u32[]{:S(2)}) %collective-permute-start.21) | collective-permute-done | bytes 524320 | tf_op jit(solution)/shard_map/ppermute | solution.py:218
  74.3 0.9 %shard_map.115 = (bf16[10,256,256]{2,1,0:T(8,128)(2,1)S(1)}, bf16[2,256,256]{2,1,0:T(8,128)(2,1)S(1)}, bf16[2,256,256]{2,1,0:T(8,128)(2,1)S(1)}, bf16[3,256,256]...) custom-call(s32[1]{0:T(128)} %bitcast.group_ref, f32[4,256,256]{2,1,0:T(8,128)S(1)} %get-tuple-element.26.own_ref, ...), custom_call_target="tpu_custom_call" | custom-call | tf_op jit(solution)/shard_map/pallas_call | solution.py:124
  75.2 0.5 collective-permute-start.25
  75.7 0.1 collective-permute-start.22
  75.8 0.4 collective-permute-start.23
  76.2 1.6 %collective-permute-done.22.refs_0_ = bf16[2,256,256]{2,1,0:T(8,128)(2,1)S(1)} collective-permute-done((bf16[2,256,256]{2,1,0:T(8,128)(2,1)S(1)}, bf16[2,256,256]{2,1,0:T(8,128)(2,1)S(1)}, u32[]{:S(2)}, u32[]{:S(2)}) %collective-permute-start.22) | collective-permute-done | bytes 262176 | tf_op jit(solution)/shard_map/ppermute | solution.py:218
  77.9 0.4 collective-permute-done.23.refs_1_
  78.3 4.7 %shard_map.116 = bf16[2048,256]{1,0:T(8,128)(2,1)} custom-call(s32[1]{0:T(128)} %bitcast.group_ref, f32[4,256,256]{2,1,0:T(8,128)S(1)} %get-tuple-element.26.own_ref, bf16[4,256,256]{2,1,0:T(8,128)(2,1)S(1)} %collective-permute-done.21.other_ref, bf16[10,256,256]{2,1,0:T(8,128)(2,1)S(1)} %fusion.prev_ref, ...), custom_call_target="tpu_custom_call" | custom-call | tf_op jit(solution)/shard_map/pallas_call | solution.py:174
  83.0 0.2 collective-permute-done.26.other_ref
  83.1 1.6 %shard_map.117 = bf16[2048,256]{1,0:T(8,128)(2,1)} custom-call(s32[1]{0:T(128)} %bitcast.group_ref, bf16[4,256,256]{2,1,0:T(8,128)(2,1)S(1)} %get-tuple-element.34.own_ref, bf16[4,256,256]{2,1,0:T(8,128)(2,1)S(1)} %collective-permute-done.26.other_ref), custom_call_target="tpu_custom_call" | custom-call | tf_op jit(solution)/shard_map/pallas_call | solution.py:206
  (54 shorter events, 0.8 us)
Async XLA Ops:
  2.1 4.9 %copy-start.9 = (s32[8]{0:T(128)S(1)}, s32[8]{0:T(128)}, u32[]{:S(2)}) copy-start(s32[8]{0:T(128)} %param.15) | copy-start | bytes 100
  2.1 5.0 %copy-start.6 = (bf16[256,512]{1,0:T(8,128)(2,1)S(1)}, bf16[256,512]{1,0:T(8,128)(2,1)}, u32[]{:S(2)}) copy-start(bf16[256,512]{1,0:T(8,128)(2,1)} %param.10) | copy-start | bytes 786436
  2.1 5.0 %copy-start.7 = (bf16[8,8,256]{2,1,0:T(8,128)(2,1)S(1)}, bf16[8,8,256]{2,1,0:T(8,128)(2,1)}, u32[]{:S(2)}) copy-start(bf16[8,8,256]{2,1,0:T(8,128)(2,1)} %param.13) | copy-start | bytes 98308
  2.2 5.0 %copy-start.8 = (bf16[8,2,256]{2,1,0:T(2,128)(2,1)S(1)}, bf16[8,2,256]{2,1,0:T(2,128)(2,1)}, u32[]{:S(2)}) copy-start(bf16[8,2,256]{2,1,0:T(2,128)(2,1)} %param.14) | copy-start | bytes 24580
  2.2 1.7 %collective-permute-start = (bf16[4,128,256]{2,1,0:T(8,128)(2,1)S(1)}, bf16[4,128,256]{2,1,0:T(8,128)(2,1)S(1)}, u32[]{:S(2)}, u32[]{:S(2)}) collective-permute-start(bf16[4,128,256]{2,1,0:T(8,128)(2,1)S(1)} %bitcast.35), channel_id=1, source_target_pairs={{0,1},{1,0},{2,3},{3,2},{4,5},{5,4},{6,7},{7,6},{8,9},{9,8},{10,11... | collective-permute-start | bytes 786440 | tf_op jit(solution)/shard_map/ppermute | solution.py:218
  3.9 11.6 %collective-permute-start.5 = (bf16[2,4,128,256]{3,2,1,0:T(8,128)(2,1)S(1)}, bf16[2,4,128,256]{3,2,1,0:T(8,128)(2,1)S(1)}, u32[]{:S(2)}, u32[]{:S(2)}) collective-permute-start(bf16[2,4,128,256]{3,2,1,0:T(8,128)(2,1)S(1)} %pad_maximum_fusion.1), channel_id=1, source_target_pairs={{0,4},{5,1},{4,8},{9,5},{8,12},{13,9},{12,14},{15,13},{14,10},{11,... | collective-permute-start | bytes 1572872 | tf_op jit(solution)/shard_map/ppermute | solution.py:244
  7.0 1.6 %collective-permute-start.1 = (bf16[4,128,256]{2,1,0:T(8,128)(2,1)S(1)}, bf16[4,128,256]{2,1,0:T(8,128)(2,1)S(1)}, u32[]{:S(2)}, u32[]{:S(2)}) collective-permute-start(bf16[4,128,256]{2,1,0:T(8,128)(2,1)S(1)} %bitcast.32), channel_id=1, source_target_pairs={{0,1},{1,0},{2,3},{3,2},{4,5},{5,4},{6,7},{7,6},{8,9},{9,8},{10,11... | collective-permute-start | bytes 786440 | tf_op jit(solution)/shard_map/ppermute | solution.py:218
  8.6 19.4 %all-to-all-start = ((bf16[8,40,512]{2,1,0:T(8,128)(2,1)}), bf16[8,40,512]{2,1,0:T(8,128)(2,1)S(1)}, u32[]{:S(2)}, u32[]{:S(2)}) async-start(bf16[8,40,512]{2,1,0:T(8,128)(2,1)} %maximum_maximum_fusion), calls=%async_computation | async-start | bytes 655360 | tf_op jit(solution)/shard_map/all_to_all | solution.py:297
  13.4 12.4 %collective-permute-start.2 = (bf16[2,4,128,256]{3,2,1,0:T(8,128)(2,1)S(1)}, bf16[2,4,128,256]{3,2,1,0:T(8,128)(2,1)S(1)}, u32[]{:S(2)}, u32[]{:S(2)}) collective-permute-start(bf16[2,4,128,256]{3,2,1,0:T(8,128)(2,1)S(1)} %pad_maximum_fusion), channel_id=1, source_target_pairs={{0,4},{5,1},{4,8},{9,5},{8,12},{13,9},{12,14},{15,13},{14,10},{11,... | collective-permute-start | bytes 1572872 | tf_op jit(solution)/shard_map/ppermute | solution.py:244
  15.5 16.0 %collective-permute-start.7 = (bf16[2,4,128,256]{3,2,1,0:T(8,128)(2,1)S(1)}, bf16[2,4,128,256]{3,2,1,0:T(8,128)(2,1)}, u32[]{:S(2)}, u32[]{:S(2)}) collective-permute-start(bf16[2,4,128,256]{3,2,1,0:T(8,128)(2,1)S(1)} %collective-permute-done.5.refs_1_), channel_id=1, source_target_pairs={{0,4},{5,1},{4,8},{9,5},{8,12},{13,9},{12,14},{15,13},{14,10},{11,... | collective-permute-start | bytes 1572872 | tf_op jit(solution)/shard_map/ppermute | solution.py:244
  25.8 11.2 %collective-permute-start.3 = (bf16[2,4,128,256]{3,2,1,0:T(8,128)(2,1)S(1)}, bf16[2,4,128,256]{3,2,1,0:T(8,128)(2,1)S(1)}, u32[]{:S(2)}, u32[]{:S(2)}) collective-permute-start(bf16[2,4,128,256]{3,2,1,0:T(8,128)(2,1)S(1)} %collective-permute-done.2.refs_1_), channel_id=1, source_target_pairs={{0,4},{5,1},{4,8},{9,5},{8,12},{13,9},{12,14},{15,13},{14,10},{11,... | collective-permute-start | bytes 1572872 | tf_op jit(solution)/shard_map/ppermute | solution.py:244
  28.0 0.7 copy-start.5
  31.5 11.1 %collective-permute-start.9 = (bf16[2,4,128,256]{3,2,1,0:T(8,128)(2,1)}, bf16[2,4,128,256]{3,2,1,0:T(8,128)(2,1)S(1)}, u32[]{:S(2)}, u32[]{:S(2)}) collective-permute-start(bf16[2,4,128,256]{3,2,1,0:T(8,128)(2,1)} %collective-permute-done.7.refs_3_), channel_id=1, source_target_pairs={{0,4},{5,1},{4,8},{9,5},{8,12},{13,9},{12,14},{15,13},{14,10},{11,... | collective-permute-start | bytes 1572872 | tf_op jit(solution)/shard_map/ppermute | solution.py:244
  33.7 1.6 %collective-permute-start.11 = (bf16[256,512]{1,0:T(8,128)(2,1)S(1)}, bf16[256,512]{1,0:T(8,128)(2,1)S(1)}, u32[]{:S(2)}, u32[]{:S(2)}) collective-permute-start(bf16[256,512]{1,0:T(8,128)(2,1)S(1)} %fusion.3.refs_9_.refs_8_), channel_id=1, source_target_pairs={{0,1},{1,0},{2,3},{3,2},{4,5},{5,4},{6,7},{7,6},{8,9},{9,8},{10,11... | collective-permute-start | bytes 786440 | tf_op jit(solution)/shard_map/ppermute | solution.py:218
  33.8 12.5 %collective-permute-start.6 = (bf16[2,4,128,256]{3,2,1,0:T(8,128)(2,1)S(1)}, bf16[2,4,128,256]{3,2,1,0:T(8,128)(2,1)}, u32[]{:S(2)}, u32[]{:S(2)}) collective-permute-start(bf16[2,4,128,256]{3,2,1,0:T(8,128)(2,1)S(1)} %collective-permute-done.5.refs_1_), channel_id=1, source_target_pairs={{0,1},{1,0},{2,3},{3,2},{4,5},{5,4},{6,7},{7,6},{8,9},{9,8},{10,11... | collective-permute-start | bytes 1572872 | tf_op jit(solution)/shard_map/ppermute | solution.py:218
  35.3 8.3 %collective-permute-start.12 = (bf16[256,512]{1,0:T(8,128)(2,1)S(1)}, bf16[256,512]{1,0:T(8,128)(2,1)S(1)}, u32[]{:S(2)}, u32[]{:S(2)}) collective-permute-start(bf16[256,512]{1,0:T(8,128)(2,1)S(1)} %fusion.3.refs_9_.refs_8_), channel_id=1, source_target_pairs={{0,16},{16,0},{1,17},{17,1},{2,18},{18,2},{3,19},{19,3},{4,20},{20... | collective-permute-start | bytes 786440 | tf_op jit(solution)/shard_map/ppermute | solution.py:218
  36.9 15.1 %collective-permute-start.8 = (bf16[2,4,128,256]{3,2,1,0:T(8,128)(2,1)}, bf16[2,4,128,256]{3,2,1,0:T(8,128)(2,1)S(1)}, u32[]{:S(2)}, u32[]{:S(2)}) collective-permute-start(bf16[2,4,128,256]{3,2,1,0:T(8,128)(2,1)} %collective-permute-done.7.refs_3_), channel_id=1, source_target_pairs={{0,1},{1,0},{2,3},{3,2},{4,5},{5,4},{6,7},{7,6},{8,9},{9,8},{10,11... | collective-permute-start | bytes 1572872 | tf_op jit(solution)/shard_map/ppermute | solution.py:218
  37.1 15.5 %collective-permute-start.4 = (bf16[2,4,128,256]{3,2,1,0:T(8,128)(2,1)S(1)}, bf16[2,4,128,256]{3,2,1,0:T(8,128)(2,1)S(1)}, u32[]{:S(2)}, u32[]{:S(2)}) collective-permute-start(bf16[2,4,128,256]{3,2,1,0:T(8,128)(2,1)S(1)} %collective-permute-done.3.refs_3_), channel_id=1, source_target_pairs={{0,4},{5,1},{4,8},{9,5},{8,12},{13,9},{12,14},{15,13},{14,10},{11,... | collective-permute-start | bytes 1572872 | tf_op jit(solution)/shard_map/ppermute | solution.py:244
  42.7 19.0 %copy-start = (bf16[3,256,256]{2,1,0:T(8,128)(2,1)S(1)}, bf16[3,256,256]{2,1,0:T(8,128)(2,1)}, u32[]{:S(2)}) copy-start(bf16[3,256,256]{2,1,0:T(8,128)(2,1)} %refs_5_.1) | copy-start | bytes 1179652
  43.7 7.4 %collective-permute-start.13 = (bf16[2,2,128,256]{3,2,1,0:T(8,128)(2,1)S(1)}, bf16[2,2,128,256]{3,2,1,0:T(8,128)(2,1)S(1)}, u32[]{:S(2)}, u32[]{:S(2)}) collective-permute-start(bf16[2,2,128,256]{3,2,1,0:T(8,128)(2,1)S(1)} %constant_dynamic-slice_fusion), channel_id=1, source_target_pairs={{0,4},{5,1},{4,8},{9,5},{8,12},{13,9},{12,14},{15,13},{14,10},{11,... | collective-permute-start | bytes 786440 | tf_op jit(solution)/shard_map/ppermute | solution.py:244
  46.3 10.1 %collective-permute-start.10 = (bf16[2,4,128,256]{3,2,1,0:T(8,128)(2,1)S(1)}, bf16[2,4,128,256]{3,2,1,0:T(8,128)(2,1)S(1)}, u32[]{:S(2)}, u32[]{:S(2)}) collective-permute-start(bf16[2,4,128,256]{3,2,1,0:T(8,128)(2,1)S(1)} %collective-permute-done.9.refs_5_), channel_id=1, source_target_pairs={{0,1},{1,0},{2,3},{3,2},{4,5},{5,4},{6,7},{7,6},{8,9},{9,8},{10,11... | collective-permute-start | bytes 1572872 | tf_op jit(solution)/shard_map/ppermute | solution.py:218
  46.3 5.7 %collective-permute-start.15 = (bf16[256,512]{1,0:T(8,128)(2,1)S(1)}, bf16[256,512]{1,0:T(8,128)(2,1)S(1)}, u32[]{:S(2)}, u32[]{:S(2)}) collective-permute-start(bf16[256,512]{1,0:T(8,128)(2,1)S(1)} %collective-permute-done.12.refs_11_.refs_10_), channel_id=1, source_target_pairs={{0,1},{1,0},{2,3},{3,2},{4,5},{5,4},{6,7},{7,6},{8,9},{9,8},{10,11... | collective-permute-start | bytes 786440 | tf_op jit(solution)/shard_map/ppermute | solution.py:218
  51.1 2.1 %collective-permute-start.14 = (bf16[2,2,128,256]{3,2,1,0:T(8,128)(2,1)S(1)}, bf16[2,2,128,256]{3,2,1,0:T(8,128)(2,1)S(1)}, u32[]{:S(2)}, u32[]{:S(2)}) collective-permute-start(bf16[2,2,128,256]{3,2,1,0:T(8,128)(2,1)S(1)} %collective-permute-done.13.refs_7_), channel_id=1, source_target_pairs={{0,1},{1,0},{2,3},{3,2},{4,5},{5,4},{6,7},{7,6},{8,9},{9,8},{10,11... | collective-permute-start | bytes 786440 | tf_op jit(solution)/shard_map/ppermute | solution.py:218
  52.0 9.7 %collective-permute-start.16 = (bf16[2,4,128,256]{3,2,1,0:T(8,128)(2,1)S(1)}, bf16[2,4,128,256]{3,2,1,0:T(8,128)(2,1)S(1)}, u32[]{:S(2)}, u32[]{:S(2)}) collective-permute-start(bf16[2,4,128,256]{3,2,1,0:T(8,128)(2,1)S(1)} %collective-permute-done.2.refs_1_), channel_id=1, source_target_pairs={{0,1},{1,0},{2,3},{3,2},{4,5},{5,4},{6,7},{7,6},{8,9},{9,8},{10,11... | collective-permute-start | bytes 1572872 | tf_op jit(solution)/shard_map/ppermute | solution.py:218
  52.0 11.4 %collective-permute-start.17 = (bf16[2,4,128,256]{3,2,1,0:T(8,128)(2,1)S(1)}, bf16[2,4,128,256]{3,2,1,0:T(8,128)(2,1)S(1)}, u32[]{:S(2)}, u32[]{:S(2)}) collective-permute-start(bf16[2,4,128,256]{3,2,1,0:T(8,128)(2,1)S(1)} %collective-permute-done.3.refs_3_), channel_id=1, source_target_pairs={{0,1},{1,0},{2,3},{3,2},{4,5},{5,4},{6,7},{7,6},{8,9},{9,8},{10,11... | collective-permute-start | bytes 1572872 | tf_op jit(solution)/shard_map/ppermute | solution.py:218
  52.5 10.9 %collective-permute-start.18 = (bf16[2,4,128,256]{3,2,1,0:T(8,128)(2,1)S(1)}, bf16[2,4,128,256]{3,2,1,0:T(8,128)(2,1)S(1)}, u32[]{:S(2)}, u32[]{:S(2)}) collective-permute-start(bf16[2,4,128,256]{3,2,1,0:T(8,128)(2,1)S(1)} %collective-permute-done.4.refs_5_), channel_id=1, source_target_pairs={{0,1},{1,0},{2,3},{3,2},{4,5},{5,4},{6,7},{7,6},{8,9},{9,8},{10,11... | collective-permute-start | bytes 1572872 | tf_op jit(solution)/shard_map/ppermute | solution.py:218
  53.2 10.3 %collective-permute-start.19 = (bf16[2,4,128,256]{3,2,1,0:T(8,128)(2,1)S(1)}, bf16[2,4,128,256]{3,2,1,0:T(8,128)(2,1)S(1)}, u32[]{:S(2)}, u32[]{:S(2)}) collective-permute-start(bf16[2,4,128,256]{3,2,1,0:T(8,128)(2,1)S(1)} %collective-permute-done.4.refs_5_), channel_id=1, source_target_pairs={{0,4},{5,1},{4,8},{9,5},{8,12},{13,9},{12,14},{15,13},{14,10},{11,... | collective-permute-start | bytes 1572872 | tf_op jit(solution)/shard_map/ppermute | solution.py:244
  59.3 14.9 %collective-permute-start.21 = (bf16[4,256,256]{2,1,0:T(8,128)(2,1)S(1)}, bf16[4,256,256]{2,1,0:T(8,128)(2,1)S(1)}, u32[]{:S(2)}, u32[]{:S(2)}) collective-permute-start(bf16[4,256,256]{2,1,0:T(8,128)(2,1)S(1)} %get-tuple-element.27), channel_id=1, source_target_pairs={{0,16},{16,0},{1,17},{17,1},{2,18},{18,2},{3,19},{19,3},{4,20},{20... | collective-permute-start | bytes 1572872 | tf_op jit(solution)/shard_map/ppermute | solution.py:218
  61.7 5.7 %collective-permute-start.20 = (bf16[3,256,256]{2,1,0:T(8,128)(2,1)S(1)}, bf16[3,256,256]{2,1,0:T(8,128)(2,1)S(1)}, u32[]{:S(2)}, u32[]{:S(2)}) collective-permute-start(bf16[3,256,256]{2,1,0:T(8,128)(2,1)S(1)} %copy-done), channel_id=1, source_target_pairs={{0,1},{1,0},{2,3},{3,2},{4,5},{5,4},{6,7},{7,6},{8,9},{9,8},{10,11... | collective-permute-start | bytes 1179656 | tf_op jit(solution)/shard_map/ppermute | solution.py:218
  65.6 8.6 %copy-start.2 = (f32[256]{0:T(256)S(1)}, f32[256]{0:T(256)}, u32[]{:S(2)}) copy-start(f32[256]{0:T(256)} %param.12) | copy-start | bytes 3076
  65.6 17.5 %collective-permute-start.26 = (bf16[4,256,256]{2,1,0:T(8,128)(2,1)S(1)}, bf16[4,256,256]{2,1,0:T(8,128)(2,1)S(1)}, u32[]{:S(2)}, u32[]{:S(2)}) collective-permute-start(bf16[4,256,256]{2,1,0:T(8,128)(2,1)S(1)} %get-tuple-element.25), channel_id=1, source_target_pairs={{0,16},{16,0},{1,17},{17,1},{2,18},{18,2},{3,19},{19,3},{4,20},{20... | collective-permute-start | bytes 1572872 | tf_op jit(solution)/shard_map/ppermute | solution.py:218
  74.2 4.0 %copy-start.1 = (bf16[256,256]{1,0:T(8,128)(2,1)S(1)}, bf16[256,256]{1,0:T(8,128)(2,1)}, u32[]{:S(2)}) copy-start(bf16[256,256]{1,0:T(8,128)(2,1)} %refs_8_.1) | copy-start | bytes 393220
  74.3 4.0 %copy-start.3 = (f32[256]{0:T(256)S(1)}, f32[256]{0:T(256)}, u32[]{:S(2)}) copy-start(f32[256]{0:T(256)} %param.17) | copy-start | bytes 3076
  74.3 4.0 %copy-start.4 = (f32[256]{0:T(256)S(1)}, f32[256]{0:T(256)}, u32[]{:S(2)}) copy-start(f32[256]{0:T(256)} %param.19) | copy-start | bytes 3076
  75.1 3.1 %collective-permute-start.24 = (bf16[3,256,256]{2,1,0:T(8,128)(2,1)S(1)}, bf16[3,256,256]{2,1,0:T(8,128)(2,1)S(1)}, u32[]{:S(2)}, u32[]{:S(2)}) collective-permute-start(bf16[3,256,256]{2,1,0:T(8,128)(2,1)S(1)} %get-tuple-element.31), channel_id=1, source_target_pairs={{0,1},{1,0},{2,3},{3,2},{4,5},{5,4},{6,7},{7,6},{8,9},{9,8},{10,11... | collective-permute-start | bytes 1179656 | tf_op jit(solution)/shard_map/ppermute | solution.py:218
  75.2 3.0 %collective-permute-start.25 = (bf16[3,256,256]{2,1,0:T(8,128)(2,1)S(1)}, bf16[3,256,256]{2,1,0:T(8,128)(2,1)S(1)}, u32[]{:S(2)}, u32[]{:S(2)}) collective-permute-start(bf16[3,256,256]{2,1,0:T(8,128)(2,1)S(1)} %get-tuple-element.32), channel_id=1, source_target_pairs={{0,1},{1,0},{2,3},{3,2},{4,5},{5,4},{6,7},{7,6},{8,9},{9,8},{10,11... | collective-permute-start | bytes 1179656 | tf_op jit(solution)/shard_map/ppermute | solution.py:218
  75.7 2.1 %collective-permute-start.22 = (bf16[2,256,256]{2,1,0:T(8,128)(2,1)S(1)}, bf16[2,256,256]{2,1,0:T(8,128)(2,1)S(1)}, u32[]{:S(2)}, u32[]{:S(2)}) collective-permute-start(bf16[2,256,256]{2,1,0:T(8,128)(2,1)S(1)} %get-tuple-element.29), channel_id=1, source_target_pairs={{0,1},{1,0},{2,3},{3,2},{4,5},{5,4},{6,7},{7,6},{8,9},{9,8},{10,11... | collective-permute-start | bytes 786440 | tf_op jit(solution)/shard_map/ppermute | solution.py:218
  75.8 2.4 %collective-permute-start.23 = (bf16[2,256,256]{2,1,0:T(8,128)(2,1)S(1)}, bf16[2,256,256]{2,1,0:T(8,128)(2,1)S(1)}, u32[]{:S(2)}, u32[]{:S(2)}) collective-permute-start(bf16[2,256,256]{2,1,0:T(8,128)(2,1)S(1)} %get-tuple-element.30), channel_id=1, source_target_pairs={{0,1},{1,0},{2,3},{3,2},{4,5},{5,4},{6,7},{7,6},{8,9},{9,8},{10,11... | collective-permute-start | bytes 786440 | tf_op jit(solution)/shard_map/ppermute | solution.py:218

commit v9 on v8

--- a/solution.py
+++ b/solution.py
@@ -201,12 +201,12 @@
 
 def weave(group, own, other):
     taps, sessions, width = own.shape
-    steps, block = 2 * taps, sessions // 2
+    steps, block = 2 * taps, sessions
     taken = pl.BlockSpec((taps, block, width), lambda i: (0, i, 0))
     return pl.pallas_call(
         weave_kernel,
         out_shape=jax.ShapeDtypeStruct((sessions * steps, width), BF16),
-        grid=(2,),
+        grid=(1,),
         in_specs=[pl.BlockSpec(memory_space=pltpu.SMEM), taken, taken],
         out_specs=pl.BlockSpec((block * steps, width), lambda i: (i, 0)),
         scratch_shapes=[pltpu.VMEM((width // 128, block * steps, 128), F32)],
@@ -318,7 +318,7 @@
         up_ring.round(far_half)
         up_ring.blocks[0] = after(up_ring.blocks[0], nearly_done)
         own_up, away_up = spread_taps(sides, up_ring.blocks, up_ring.steps, count, F32)
-        tail_ring.round(whole=True)
+        tail_ring.round(away_up, whole=True)
         own_tail, away_tail = spread_taps(sides, tail_ring.blocks, tail_ring.steps, count, BF16)
     else:
         whole = [lax.all_gather(own, "streams", axis=1, tiled=True) for own in halves]

time: 85.2 us -> 85.3 us (level)
    ppermute x19, waiting for transfers between devices: 13.3 us -> 10.8 us  [swap(): return lax.ppermute(value, axis, [(0, 1), (1, 0)])]
    ppermute x8, waiting for transfers between devices: 19.4 us -> 21.4 us  [round(): item = lax.ppermute(item, ('streams', 'segment'), self.pairs)]
where the time goes in v9:
time: 85.3 us; the launch traced here: 84.8 us
  starting transfers between devices  32.9 us (39%)
  waiting for transfers between devices  32.2 us (38%)
  Pallas kernels  12.3 us (14%)
  local copies, waits for them, and re-layouts  4.73 us (6%)
  other arithmetic  1.17 us (1%)
  between operations  0.93 us (1%)
    ppermute x8, waiting for transfers between devices, round(): item = lax.ppermute(item, ('streams', 'segment'), self.pairs)  21.4 us
    ppermute x8, starting transfers between devices, round(): item = lax.ppermute(item, ('streams', 'segment'), self.pairs)  19.2 us
    ppermute x19, waiting for transfers between devices, swap(): return lax.ppermute(value, axis, [(0, 1), (1, 0)])  10.8 us
    ppermute x19, starting transfers between devices, swap(): return lax.ppermute(value, axis, [(0, 1), (1, 0)])  8.93 us
    pallas_call x2, Pallas kernels, spread_taps(): pl.pallas_call(functools.partial(spread_kernel, count, steps), out_shape=...  5.04 us
    all_to_all x1, starting transfers between devices, local(): lax.all_to_all(parcel, 'streams', split_axis=0, concat_axis=0, tiled=True)  4.79 us
    pallas_call x1, Pallas kernels, residual(): pl.pallas_call(residual_kernel, out_shape=jax.ShapeDtypeStruct((sessions...  4.69 us
  transfers between devices with their start and end apart: 28, of which 14 were waited for; matrix products, arithmetic and copies ran while one was open for 5% of the time, Pallas kernels for 13%

profile of v9, /device:TPU:0, one launch (start us, length us, event | category | flops | bytes accessed | tf_op | source)
XLA Modules:
  0.0 84.8 jit_solution(14993126130733050341)
XLA Ops:
  0.6 1.5 %constant_dynamic-slice_fusion.1 = (bf16[128,4,256]{2,1,0:T(4,128)(2,1)S(1)}, bf16[128,4,256]{2,1,0:T(4,128)(2,1)S(1)}) fusion(bf16[128,16,256]{2,1,0:T(8,128)(2,1)} %param.11, s32[]{:T(128)S(6)} %select_n.14, s32[]{:T(128)S(6)} %select_n.13), kind=kLoop, calls=%fused_computation.23 | loop fusion | bytes 1048584 | tf_op jit(solution)/shard_map/dynamic_slice | solution.py:275
  2.2 0.5 collective-permute-start
  2.7 1.2 %collective-permute-done = bf16[4,128,256]{2,1,0:T(8,128)(2,1)S(1)} collective-permute-done((bf16[4,128,256]{2,1,0:T(8,128)(2,1)S(1)}, bf16[4,128,256]{2,1,0:T(8,128)(2,1)S(1)}, u32[]{:S(2)}, u32[]{:S(2)}) %collective-permute-start) | collective-permute-done | bytes 262176 | tf_op jit(solution)/shard_map/ppermute | solution.py:218
  3.9 3.0 %collective-permute-start.5 = (bf16[2,4,128,256]{3,2,1,0:T(8,128)(2,1)S(1)}, bf16[2,4,128,256]{3,2,1,0:T(8,128)(2,1)S(1)}, u32[]{:S(2)}, u32[]{:S(2)}) collective-permute-start(bf16[2,4,128,256]{3,2,1,0:T(8,128)(2,1)S(1)} %pad_maximum_fusion.1), channel_id=1, source_target_pairs={{0,4},{5,1},{4,8},{9,5},{8,12},{13,9},{12,14},{15,13},{14,10},{11,... | collective-permute-start | bytes 1572872 | tf_op jit(solution)/shard_map/ppermute | solution.py:244
  7.2 0.8 maximum_maximum_fusion
  8.0 0.6 collective-permute-done.1
  8.6 4.8 %all-to-all-start = ((bf16[8,40,512]{2,1,0:T(8,128)(2,1)}), bf16[8,40,512]{2,1,0:T(8,128)(2,1)S(1)}, u32[]{:S(2)}, u32[]{:S(2)}) async-start(bf16[8,40,512]{2,1,0:T(8,128)(2,1)} %maximum_maximum_fusion), calls=%async_computation | async-start | bytes 655360 | tf_op jit(solution)/shard_map/all_to_all | solution.py:297
  13.4 2.1 %collective-permute-start.2 = (bf16[2,4,128,256]{3,2,1,0:T(8,128)(2,1)S(1)}, bf16[2,4,128,256]{3,2,1,0:T(8,128)(2,1)S(1)}, u32[]{:S(2)}, u32[]{:S(2)}) collective-permute-start(bf16[2,4,128,256]{3,2,1,0:T(8,128)(2,1)S(1)} %pad_maximum_fusion), channel_id=1, source_target_pairs={{0,4},{5,1},{4,8},{9,5},{8,12},{13,9},{12,14},{15,13},{14,10},{11,... | collective-permute-start | bytes 1572872 | tf_op jit(solution)/shard_map/ppermute | solution.py:244
  15.5 1.5 %collective-permute-start.7 = (bf16[2,4,128,256]{3,2,1,0:T(8,128)(2,1)S(1)}, bf16[2,4,128,256]{3,2,1,0:T(8,128)(2,1)}, u32[]{:S(2)}, u32[]{:S(2)}) collective-permute-start(bf16[2,4,128,256]{3,2,1,0:T(8,128)(2,1)S(1)} %collective-permute-done.5.refs_1_), channel_id=1, source_target_pairs={{0,4},{5,1},{4,8},{9,5},{8,12},{13,9},{12,14},{15,13},{14,10},{11,... | collective-permute-start | bytes 1572872 | tf_op jit(solution)/shard_map/ppermute | solution.py:244
  17.0 8.9 %collective-permute-done.2.refs_1_ = bf16[2,4,128,256]{3,2,1,0:T(8,128)(2,1)S(1)} collective-permute-done((bf16[2,4,128,256]{3,2,1,0:T(8,128)(2,1)S(1)}, bf16[2,4,128,256]{3,2,1,0:T(8,128)(2,1)S(1)}, u32[]{:S(2)}, u32[]{:S(2)}) %collective-permute-start.2) | collective-permute-done | bytes 524320 | tf_op jit(solution)/shard_map/ppermute | solution.py:244
  25.8 2.1 %collective-permute-start.3 = (bf16[2,4,128,256]{3,2,1,0:T(8,128)(2,1)S(1)}, bf16[2,4,128,256]{3,2,1,0:T(8,128)(2,1)S(1)}, u32[]{:S(2)}, u32[]{:S(2)}) collective-permute-start(bf16[2,4,128,256]{3,2,1,0:T(8,128)(2,1)S(1)} %collective-permute-done.2.refs_1_), channel_id=1, source_target_pairs={{0,4},{5,1},{4,8},{9,5},{8,12},{13,9},{12,14},{15,13},{14,10},{11,... | collective-permute-start | bytes 1572872 | tf_op jit(solution)/shard_map/ppermute | solution.py:244
  28.0 0.7 copy-done.5
  28.7 2.8 %collective-permute-done.7.refs_3_ = bf16[2,4,128,256]{3,2,1,0:T(8,128)(2,1)} collective-permute-done((bf16[2,4,128,256]{3,2,1,0:T(8,128)(2,1)S(1)}, bf16[2,4,128,256]{3,2,1,0:T(8,128)(2,1)}, u32[]{:S(2)}, u32[]{:S(2)}) %collective-permute-start.7) | collective-permute-done | bytes 524320 | tf_op jit(solution)/shard_map/ppermute | solution.py:244
  31.5 2.0 %collective-permute-start.9 = (bf16[2,4,128,256]{3,2,1,0:T(8,128)(2,1)}, bf16[2,4,128,256]{3,2,1,0:T(8,128)(2,1)S(1)}, u32[]{:S(2)}, u32[]{:S(2)}) collective-permute-start(bf16[2,4,128,256]{3,2,1,0:T(8,128)(2,1)} %collective-permute-done.7.refs_3_), channel_id=1, source_target_pairs={{0,4},{5,1},{4,8},{9,5},{8,12},{13,9},{12,14},{15,13},{14,10},{11,... | collective-permute-start | bytes 1572872 | tf_op jit(solution)/shard_map/ppermute | solution.py:244
  33.6 0.1 fusion.3.refs_9_.refs_8_
  33.8 1.5 %collective-permute-done.11.refs_10_.refs_9_ = bf16[256,512]{1,0:T(8,128)(2,1)S(1)} collective-permute-done((bf16[256,512]{1,0:T(8,128)(2,1)S(1)}, bf16[256,512]{1,0:T(8,128)(2,1)S(1)}, u32[]{:S(2)}, u32[]{:S(2)}) %collective-permute-start.11) | collective-permute-done | bytes 262176 | tf_op jit(solution)/shard_map/ppermute | solution.py:218
  35.3 1.5 %collective-permute-start.12 = (bf16[256,512]{1,0:T(8,128)(2,1)S(1)}, bf16[256,512]{1,0:T(8,128)(2,1)S(1)}, u32[]{:S(2)}, u32[]{:S(2)}) collective-permute-start(bf16[256,512]{1,0:T(8,128)(2,1)S(1)} %fusion.3.refs_9_.refs_8_), channel_id=1, source_target_pairs={{0,16},{16,0},{1,17},{17,1},{2,18},{18,2},{3,19},{19,3},{4,20},{20... | collective-permute-start | bytes 786440 | tf_op jit(solution)/shard_map/ppermute | solution.py:218
  36.9 0.5 collective-permute-start.8
  37.4 2.6 %collective-permute-start.4 = (bf16[2,4,128,256]{3,2,1,0:T(8,128)(2,1)S(1)}, bf16[2,4,128,256]{3,2,1,0:T(8,128)(2,1)S(1)}, u32[]{:S(2)}, u32[]{:S(2)}) collective-permute-start(bf16[2,4,128,256]{3,2,1,0:T(8,128)(2,1)S(1)} %collective-permute-done.3.refs_3_), channel_id=1, source_target_pairs={{0,4},{5,1},{4,8},{9,5},{8,12},{13,9},{12,14},{15,13},{14,10},{11,... | collective-permute-start | bytes 1572872 | tf_op jit(solution)/shard_map/ppermute | solution.py:244
  40.0 2.7 %collective-permute-done.9.refs_5_ = bf16[2,4,128,256]{3,2,1,0:T(8,128)(2,1)S(1)} collective-permute-done((bf16[2,4,128,256]{3,2,1,0:T(8,128)(2,1)}, bf16[2,4,128,256]{3,2,1,0:T(8,128)(2,1)S(1)}, u32[]{:S(2)}, u32[]{:S(2)}) %collective-permute-start.9) | collective-permute-done | bytes 524320 | tf_op jit(solution)/shard_map/ppermute | solution.py:244
  42.7 1.0 %collective-permute-done.12.refs_11_.refs_10_ = bf16[256,512]{1,0:T(8,128)(2,1)S(1)} collective-permute-done((bf16[256,512]{1,0:T(8,128)(2,1)S(1)}, bf16[256,512]{1,0:T(8,128)(2,1)S(1)}, u32[]{:S(2)}, u32[]{:S(2)}) %collective-permute-start.12) | collective-permute-done | bytes 262176 | tf_op jit(solution)/shard_map/ppermute | solution.py:218
  43.7 2.6 %collective-permute-start.13 = (bf16[2,2,128,256]{3,2,1,0:T(8,128)(2,1)S(1)}, bf16[2,2,128,256]{3,2,1,0:T(8,128)(2,1)S(1)}, u32[]{:S(2)}, u32[]{:S(2)}) collective-permute-start(bf16[2,2,128,256]{3,2,1,0:T(8,128)(2,1)S(1)} %constant_dynamic-slice_fusion), channel_id=1, source_target_pairs={{0,4},{5,1},{4,8},{9,5},{8,12},{13,9},{12,14},{15,13},{14,10},{11,... | collective-permute-start | bytes 786440 | tf_op jit(solution)/shard_map/ppermute | solution.py:244
  46.3 0.5 collective-permute-start.15
  46.8 4.3 %collective-permute-done.13.refs_7_ = bf16[2,2,128,256]{3,2,1,0:T(8,128)(2,1)S(1)} collective-permute-done((bf16[2,2,128,256]{3,2,1,0:T(8,128)(2,1)S(1)}, bf16[2,2,128,256]{3,2,1,0:T(8,128)(2,1)S(1)}, u32[]{:S(2)}, u32[]{:S(2)}) %collective-permute-start.13) | collective-permute-done | bytes 262176 | tf_op jit(solution)/shard_map/ppermute | solution.py:244
  51.1 0.9 %collective-permute-start.14 = (bf16[2,2,128,256]{3,2,1,0:T(8,128)(2,1)S(1)}, bf16[2,2,128,256]{3,2,1,0:T(8,128)(2,1)S(1)}, u32[]{:S(2)}, u32[]{:S(2)}) collective-permute-start(bf16[2,2,128,256]{3,2,1,0:T(8,128)(2,1)S(1)} %collective-permute-done.13.refs_7_), channel_id=1, source_target_pairs={{0,1},{1,0},{2,3},{3,2},{4,5},{5,4},{6,7},{7,6},{8,9},{9,8},{10,11... | collective-permute-start | bytes 786440 | tf_op jit(solution)/shard_map/ppermute | solution.py:218
  52.0 0.5 collective-permute-start.17
  52.6 0.6 collective-permute-done.14.refs_8_
  53.2 2.9 %shard_map.113 = (f32[4,256,256]{2,1,0:T(8,128)S(1)}, bf16[4,256,256]{2,1,0:T(8,128)(2,1)S(1)}) custom-call(bf16[4,128,256]{2,1,0:T(8,128)(2,1)S(1)} %bitcast.37, bf16[2,4,128,256]{3,2,1,0:T(8,128)(2,1)S(1)} %collective-permute-done.5.refs_1_, bf16[2,4,128,256]{3,2,1,0:T(8,128)(2,1)} %collective-permute-done.6.refs_2_, ...), custom_call_target="tpu_custom_call" | custom-call | flops 1073741824 | bytes 4718592 | tf_op jit(solution)/shard_map/pallas_call | solution.py:77
  56.1 3.3 %collective-permute-start.19 = (bf16[2,4,128,256]{3,2,1,0:T(8,128)(2,1)S(1)}, bf16[2,4,128,256]{3,2,1,0:T(8,128)(2,1)S(1)}, u32[]{:S(2)}, u32[]{:S(2)}) collective-permute-start(bf16[2,4,128,256]{3,2,1,0:T(8,128)(2,1)S(1)} %collective-permute-done.4.refs_5_), channel_id=1, source_target_pairs={{0,4},{5,1},{4,8},{9,5},{8,12},{13,9},{12,14},{15,13},{14,10},{11,... | collective-permute-start | bytes 1572872 | tf_op jit(solution)/shard_map/ppermute | solution.py:244
  59.4 1.5 %collective-permute-start.21 = (bf16[4,256,256]{2,1,0:T(8,128)(2,1)S(1)}, bf16[4,256,256]{2,1,0:T(8,128)(2,1)S(1)}, u32[]{:S(2)}, u32[]{:S(2)}) collective-permute-start(bf16[4,256,256]{2,1,0:T(8,128)(2,1)S(1)} %get-tuple-element.26), channel_id=1, source_target_pairs={{0,16},{16,0},{1,17},{17,1},{2,18},{18,2},{3,19},{19,3},{4,20},{20... | collective-permute-start | bytes 1572872 | tf_op jit(solution)/shard_map/ppermute | solution.py:218
  60.9 0.8 slice.28
  61.8 0.1 convert_reduce_fusion
  61.9 0.8 slice.26
  62.7 0.8 slice.27
  63.5 2.6 %collective-permute-done.19.refs_7_ = bf16[2,4,128,256]{3,2,1,0:T(8,128)(2,1)S(1)} collective-permute-done((bf16[2,4,128,256]{3,2,1,0:T(8,128)(2,1)S(1)}, bf16[2,4,128,256]{3,2,1,0:T(8,128)(2,1)S(1)}, u32[]{:S(2)}, u32[]{:S(2)}) %collective-permute-start.19) | collective-permute-done | bytes 524320 | tf_op jit(solution)/shard_map/ppermute | solution.py:244
  66.1 2.1 %shard_map.114 = (bf16[4,256,256]{2,1,0:T(8,128)(2,1)S(1)}, bf16[4,256,256]{2,1,0:T(8,128)(2,1)S(1)}) custom-call(bf16[4,128,256]{2,1,0:T(8,128)(2,1)S(1)} %bitcast.34, bf16[2,4,128,256]{3,2,1,0:T(8,128)(2,1)S(1)} %collective-permute-done.2.refs_1_, bf16[2,4,128,256]{3,2,1,0:T(8,128)(2,1)S(1)} %collective-permute-done.16.refs_2_, ...), custom_call_target="tpu_custom_call" | custom-call | flops 1073741824 | bytes 4718592 | tf_op jit(solution)/shard_map/pallas_call | solution.py:77
  68.2 1.6 %collective-permute-start.26 = (bf16[4,256,256]{2,1,0:T(8,128)(2,1)S(1)}, bf16[4,256,256]{2,1,0:T(8,128)(2,1)S(1)}, u32[]{:S(2)}, u32[]{:S(2)}) collective-permute-start(bf16[4,256,256]{2,1,0:T(8,128)(2,1)S(1)} %get-tuple-element.28), channel_id=1, source_target_pairs={{0,16},{16,0},{1,17},{17,1},{2,18},{18,2},{3,19},{19,3},{4,20},{20... | collective-permute-start | bytes 1572872 | tf_op jit(solution)/shard_map/ppermute | solution.py:218
  69.8 0.6 fusion.prev_ref
  70.4 2.1 %collective-permute-done.21.other_ref = bf16[4,256,256]{2,1,0:T(8,128)(2,1)S(1)} collective-permute-done((bf16[4,256,256]{2,1,0:T(8,128)(2,1)S(1)}, bf16[4,256,256]{2,1,0:T(8,128)(2,1)S(1)}, u32[]{:S(2)}, u32[]{:S(2)}) %collective-permute-start.21) | collective-permute-done | bytes 524320 | tf_op jit(solution)/shard_map/ppermute | solution.py:218
  72.6 0.9 %shard_map.115 = (bf16[10,256,256]{2,1,0:T(8,128)(2,1)S(1)}, bf16[2,256,256]{2,1,0:T(8,128)(2,1)S(1)}, bf16[2,256,256]{2,1,0:T(8,128)(2,1)S(1)}, bf16[3,256,256]...) custom-call(s32[1]{0:T(128)} %bitcast.group_ref, f32[4,256,256]{2,1,0:T(8,128)S(1)} %get-tuple-element.29.own_ref, ...), custom_call_target="tpu_custom_call" | custom-call | tf_op jit(solution)/shard_map/pallas_call | solution.py:124
  73.5 0.5 collective-permute-start.25
  74.0 0.1 collective-permute-start.22
  74.1 0.4 collective-permute-start.23
  74.6 1.6 %collective-permute-done.22.refs_0_ = bf16[2,256,256]{2,1,0:T(8,128)(2,1)S(1)} collective-permute-done((bf16[2,256,256]{2,1,0:T(8,128)(2,1)S(1)}, bf16[2,256,256]{2,1,0:T(8,128)(2,1)S(1)}, u32[]{:S(2)}, u32[]{:S(2)}) %collective-permute-start.22) | collective-permute-done | bytes 262176 | tf_op jit(solution)/shard_map/ppermute | solution.py:218
  76.2 0.4 collective-permute-done.23.refs_1_
  76.6 4.7 %shard_map.116 = bf16[2048,256]{1,0:T(8,128)(2,1)} custom-call(s32[1]{0:T(128)} %bitcast.group_ref, f32[4,256,256]{2,1,0:T(8,128)S(1)} %get-tuple-element.29.own_ref, bf16[4,256,256]{2,1,0:T(8,128)(2,1)S(1)} %collective-permute-done.21.other_ref, bf16[10,256,256]{2,1,0:T(8,128)(2,1)S(1)} %fusion.prev_ref, ...), custom_call_target="tpu_custom_call" | custom-call | tf_op jit(solution)/shard_map/pallas_call | solution.py:174
  81.3 1.8 %collective-permute-done.26.other_ref = bf16[4,256,256]{2,1,0:T(8,128)(2,1)S(1)} collective-permute-done((bf16[4,256,256]{2,1,0:T(8,128)(2,1)S(1)}, bf16[4,256,256]{2,1,0:T(8,128)(2,1)S(1)}, u32[]{:S(2)}, u32[]{:S(2)}) %collective-permute-start.26) | collective-permute-done | bytes 524320 | tf_op jit(solution)/shard_map/ppermute | solution.py:218
  83.1 1.7 %shard_map.117 = bf16[2048,256]{1,0:T(8,128)(2,1)} custom-call(s32[1]{0:T(128)} %bitcast.group_ref, bf16[4,256,256]{2,1,0:T(8,128)(2,1)S(1)} %get-tuple-element.36.own_ref, bf16[4,256,256]{2,1,0:T(8,128)(2,1)S(1)} %collective-permute-done.26.other_ref), custom_call_target="tpu_custom_call" | custom-call | tf_op jit(solution)/shard_map/pallas_call | solution.py:206
  (54 shorter events, 0.8 us)
Async XLA Ops:
  2.1 4.9 %copy-start.9 = (s32[8]{0:T(128)S(1)}, s32[8]{0:T(128)}, u32[]{:S(2)}) copy-start(s32[8]{0:T(128)} %param.15) | copy-start | bytes 100
  2.1 5.0 %copy-start.6 = (bf16[256,512]{1,0:T(8,128)(2,1)S(1)}, bf16[256,512]{1,0:T(8,128)(2,1)}, u32[]{:S(2)}) copy-start(bf16[256,512]{1,0:T(8,128)(2,1)} %param.10) | copy-start | bytes 786436
  2.1 5.0 %copy-start.7 = (bf16[8,8,256]{2,1,0:T(8,128)(2,1)S(1)}, bf16[8,8,256]{2,1,0:T(8,128)(2,1)}, u32[]{:S(2)}) copy-start(bf16[8,8,256]{2,1,0:T(8,128)(2,1)} %param.13) | copy-start | bytes 98308
  2.2 5.0 %copy-start.8 = (bf16[8,2,256]{2,1,0:T(2,128)(2,1)S(1)}, bf16[8,2,256]{2,1,0:T(2,128)(2,1)}, u32[]{:S(2)}) copy-start(bf16[8,2,256]{2,1,0:T(2,128)(2,1)} %param.14) | copy-start | bytes 24580
  2.2 1.7 %collective-permute-start = (bf16[4,128,256]{2,1,0:T(8,128)(2,1)S(1)}, bf16[4,128,256]{2,1,0:T(8,128)(2,1)S(1)}, u32[]{:S(2)}, u32[]{:S(2)}) collective-permute-start(bf16[4,128,256]{2,1,0:T(8,128)(2,1)S(1)} %bitcast.35), channel_id=1, source_target_pairs={{0,1},{1,0},{2,3},{3,2},{4,5},{5,4},{6,7},{7,6},{8,9},{9,8},{10,11... | collective-permute-start | bytes 786440 | tf_op jit(solution)/shard_map/ppermute | solution.py:218
  3.9 11.6 %collective-permute-start.5 = (bf16[2,4,128,256]{3,2,1,0:T(8,128)(2,1)S(1)}, bf16[2,4,128,256]{3,2,1,0:T(8,128)(2,1)S(1)}, u32[]{:S(2)}, u32[]{:S(2)}) collective-permute-start(bf16[2,4,128,256]{3,2,1,0:T(8,128)(2,1)S(1)} %pad_maximum_fusion.1), channel_id=1, source_target_pairs={{0,4},{5,1},{4,8},{9,5},{8,12},{13,9},{12,14},{15,13},{14,10},{11,... | collective-permute-start | bytes 1572872 | tf_op jit(solution)/shard_map/ppermute | solution.py:244
  7.0 1.6 %collective-permute-start.1 = (bf16[4,128,256]{2,1,0:T(8,128)(2,1)S(1)}, bf16[4,128,256]{2,1,0:T(8,128)(2,1)S(1)}, u32[]{:S(2)}, u32[]{:S(2)}) collective-permute-start(bf16[4,128,256]{2,1,0:T(8,128)(2,1)S(1)} %bitcast.32), channel_id=1, source_target_pairs={{0,1},{1,0},{2,3},{3,2},{4,5},{5,4},{6,7},{7,6},{8,9},{9,8},{10,11... | collective-permute-start | bytes 786440 | tf_op jit(solution)/shard_map/ppermute | solution.py:218
  8.6 19.4 %all-to-all-start = ((bf16[8,40,512]{2,1,0:T(8,128)(2,1)}), bf16[8,40,512]{2,1,0:T(8,128)(2,1)S(1)}, u32[]{:S(2)}, u32[]{:S(2)}) async-start(bf16[8,40,512]{2,1,0:T(8,128)(2,1)} %maximum_maximum_fusion), calls=%async_computation | async-start | bytes 655360 | tf_op jit(solution)/shard_map/all_to_all | solution.py:297
  13.4 12.4 %collective-permute-start.2 = (bf16[2,4,128,256]{3,2,1,0:T(8,128)(2,1)S(1)}, bf16[2,4,128,256]{3,2,1,0:T(8,128)(2,1)S(1)}, u32[]{:S(2)}, u32[]{:S(2)}) collective-permute-start(bf16[2,4,128,256]{3,2,1,0:T(8,128)(2,1)S(1)} %pad_maximum_fusion), channel_id=1, source_target_pairs={{0,4},{5,1},{4,8},{9,5},{8,12},{13,9},{12,14},{15,13},{14,10},{11,... | collective-permute-start | bytes 1572872 | tf_op jit(solution)/shard_map/ppermute | solution.py:244
  15.5 16.0 %collective-permute-start.7 = (bf16[2,4,128,256]{3,2,1,0:T(8,128)(2,1)S(1)}, bf16[2,4,128,256]{3,2,1,0:T(8,128)(2,1)}, u32[]{:S(2)}, u32[]{:S(2)}) collective-permute-start(bf16[2,4,128,256]{3,2,1,0:T(8,128)(2,1)S(1)} %collective-permute-done.5.refs_1_), channel_id=1, source_target_pairs={{0,4},{5,1},{4,8},{9,5},{8,12},{13,9},{12,14},{15,13},{14,10},{11,... | collective-permute-start | bytes 1572872 | tf_op jit(solution)/shard_map/ppermute | solution.py:244
  25.8 11.6 %collective-permute-start.3 = (bf16[2,4,128,256]{3,2,1,0:T(8,128)(2,1)S(1)}, bf16[2,4,128,256]{3,2,1,0:T(8,128)(2,1)S(1)}, u32[]{:S(2)}, u32[]{:S(2)}) collective-permute-start(bf16[2,4,128,256]{3,2,1,0:T(8,128)(2,1)S(1)} %collective-permute-done.2.refs_1_), channel_id=1, source_target_pairs={{0,4},{5,1},{4,8},{9,5},{8,12},{13,9},{12,14},{15,13},{14,10},{11,... | collective-permute-start | bytes 1572872 | tf_op jit(solution)/shard_map/ppermute | solution.py:244
  28.0 0.7 copy-start.5
  31.5 11.1 %collective-permute-start.9 = (bf16[2,4,128,256]{3,2,1,0:T(8,128)(2,1)}, bf16[2,4,128,256]{3,2,1,0:T(8,128)(2,1)S(1)}, u32[]{:S(2)}, u32[]{:S(2)}) collective-permute-start(bf16[2,4,128,256]{3,2,1,0:T(8,128)(2,1)} %collective-permute-done.7.refs_3_), channel_id=1, source_target_pairs={{0,4},{5,1},{4,8},{9,5},{8,12},{13,9},{12,14},{15,13},{14,10},{11,... | collective-permute-start | bytes 1572872 | tf_op jit(solution)/shard_map/ppermute | solution.py:244
  33.7 1.6 %collective-permute-start.11 = (bf16[256,512]{1,0:T(8,128)(2,1)S(1)}, bf16[256,512]{1,0:T(8,128)(2,1)S(1)}, u32[]{:S(2)}, u32[]{:S(2)}) collective-permute-start(bf16[256,512]{1,0:T(8,128)(2,1)S(1)} %fusion.3.refs_9_.refs_8_), channel_id=1, source_target_pairs={{0,1},{1,0},{2,3},{3,2},{4,5},{5,4},{6,7},{7,6},{8,9},{9,8},{10,11... | collective-permute-start | bytes 786440 | tf_op jit(solution)/shard_map/ppermute | solution.py:218
  35.3 8.3 %collective-permute-start.12 = (bf16[256,512]{1,0:T(8,128)(2,1)S(1)}, bf16[256,512]{1,0:T(8,128)(2,1)S(1)}, u32[]{:S(2)}, u32[]{:S(2)}) collective-permute-start(bf16[256,512]{1,0:T(8,128)(2,1)S(1)} %fusion.3.refs_9_.refs_8_), channel_id=1, source_target_pairs={{0,16},{16,0},{1,17},{17,1},{2,18},{18,2},{3,19},{19,3},{4,20},{20... | collective-permute-start | bytes 786440 | tf_op jit(solution)/shard_map/ppermute | solution.py:218
  36.9 9.4 %collective-permute-start.6 = (bf16[2,4,128,256]{3,2,1,0:T(8,128)(2,1)S(1)}, bf16[2,4,128,256]{3,2,1,0:T(8,128)(2,1)}, u32[]{:S(2)}, u32[]{:S(2)}) collective-permute-start(bf16[2,4,128,256]{3,2,1,0:T(8,128)(2,1)S(1)} %collective-permute-done.5.refs_1_), channel_id=1, source_target_pairs={{0,1},{1,0},{2,3},{3,2},{4,5},{5,4},{6,7},{7,6},{8,9},{9,8},{10,11... | collective-permute-start | bytes 1572872 | tf_op jit(solution)/shard_map/ppermute | solution.py:218
  36.9 15.2 %collective-permute-start.8 = (bf16[2,4,128,256]{3,2,1,0:T(8,128)(2,1)}, bf16[2,4,128,256]{3,2,1,0:T(8,128)(2,1)S(1)}, u32[]{:S(2)}, u32[]{:S(2)}) collective-permute-start(bf16[2,4,128,256]{3,2,1,0:T(8,128)(2,1)} %collective-permute-done.7.refs_3_), channel_id=1, source_target_pairs={{0,1},{1,0},{2,3},{3,2},{4,5},{5,4},{6,7},{7,6},{8,9},{9,8},{10,11... | collective-permute-start | bytes 1572872 | tf_op jit(solution)/shard_map/ppermute | solution.py:218
  37.4 14.6 %collective-permute-start.4 = (bf16[2,4,128,256]{3,2,1,0:T(8,128)(2,1)S(1)}, bf16[2,4,128,256]{3,2,1,0:T(8,128)(2,1)S(1)}, u32[]{:S(2)}, u32[]{:S(2)}) collective-permute-start(bf16[2,4,128,256]{3,2,1,0:T(8,128)(2,1)S(1)} %collective-permute-done.3.refs_3_), channel_id=1, source_target_pairs={{0,4},{5,1},{4,8},{9,5},{8,12},{13,9},{12,14},{15,13},{14,10},{11,... | collective-permute-start | bytes 1572872 | tf_op jit(solution)/shard_map/ppermute | solution.py:244
  42.7 19.0 %copy-start = (bf16[3,256,256]{2,1,0:T(8,128)(2,1)S(1)}, bf16[3,256,256]{2,1,0:T(8,128)(2,1)}, u32[]{:S(2)}) copy-start(bf16[3,256,256]{2,1,0:T(8,128)(2,1)} %refs_5_.1) | copy-start | bytes 1179652
  43.7 7.4 %collective-permute-start.13 = (bf16[2,2,128,256]{3,2,1,0:T(8,128)(2,1)S(1)}, bf16[2,2,128,256]{3,2,1,0:T(8,128)(2,1)S(1)}, u32[]{:S(2)}, u32[]{:S(2)}) collective-permute-start(bf16[2,2,128,256]{3,2,1,0:T(8,128)(2,1)S(1)} %constant_dynamic-slice_fusion), channel_id=1, source_target_pairs={{0,4},{5,1},{4,8},{9,5},{8,12},{13,9},{12,14},{15,13},{14,10},{11,... | collective-permute-start | bytes 786440 | tf_op jit(solution)/shard_map/ppermute | solution.py:244
  46.3 6.9 %collective-permute-start.10 = (bf16[2,4,128,256]{3,2,1,0:T(8,128)(2,1)S(1)}, bf16[2,4,128,256]{3,2,1,0:T(8,128)(2,1)S(1)}, u32[]{:S(2)}, u32[]{:S(2)}) collective-permute-start(bf16[2,4,128,256]{3,2,1,0:T(8,128)(2,1)S(1)} %collective-permute-done.9.refs_5_), channel_id=1, source_target_pairs={{0,1},{1,0},{2,3},{3,2},{4,5},{5,4},{6,7},{7,6},{8,9},{9,8},{10,11... | collective-permute-start | bytes 1572872 | tf_op jit(solution)/shard_map/ppermute | solution.py:218
  46.3 6.2 %collective-permute-start.15 = (bf16[256,512]{1,0:T(8,128)(2,1)S(1)}, bf16[256,512]{1,0:T(8,128)(2,1)S(1)}, u32[]{:S(2)}, u32[]{:S(2)}) collective-permute-start(bf16[256,512]{1,0:T(8,128)(2,1)S(1)} %collective-permute-done.12.refs_11_.refs_10_), channel_id=1, source_target_pairs={{0,1},{1,0},{2,3},{3,2},{4,5},{5,4},{6,7},{7,6},{8,9},{9,8},{10,11... | collective-permute-start | bytes 786440 | tf_op jit(solution)/shard_map/ppermute | solution.py:218
  51.1 2.1 %collective-permute-start.14 = (bf16[2,2,128,256]{3,2,1,0:T(8,128)(2,1)S(1)}, bf16[2,2,128,256]{3,2,1,0:T(8,128)(2,1)S(1)}, u32[]{:S(2)}, u32[]{:S(2)}) collective-permute-start(bf16[2,2,128,256]{3,2,1,0:T(8,128)(2,1)S(1)} %collective-permute-done.13.refs_7_), channel_id=1, source_target_pairs={{0,1},{1,0},{2,3},{3,2},{4,5},{5,4},{6,7},{7,6},{8,9},{9,8},{10,11... | collective-permute-start | bytes 786440 | tf_op jit(solution)/shard_map/ppermute | solution.py:218
  52.0 9.7 %collective-permute-start.16 = (bf16[2,4,128,256]{3,2,1,0:T(8,128)(2,1)S(1)}, bf16[2,4,128,256]{3,2,1,0:T(8,128)(2,1)S(1)}, u32[]{:S(2)}, u32[]{:S(2)}) collective-permute-start(bf16[2,4,128,256]{3,2,1,0:T(8,128)(2,1)S(1)} %collective-permute-done.2.refs_1_), channel_id=1, source_target_pairs={{0,1},{1,0},{2,3},{3,2},{4,5},{5,4},{6,7},{7,6},{8,9},{9,8},{10,11... | collective-permute-start | bytes 1572872 | tf_op jit(solution)/shard_map/ppermute | solution.py:218
  52.0 11.4 %collective-permute-start.17 = (bf16[2,4,128,256]{3,2,1,0:T(8,128)(2,1)S(1)}, bf16[2,4,128,256]{3,2,1,0:T(8,128)(2,1)S(1)}, u32[]{:S(2)}, u32[]{:S(2)}) collective-permute-start(bf16[2,4,128,256]{3,2,1,0:T(8,128)(2,1)S(1)} %collective-permute-done.3.refs_3_), channel_id=1, source_target_pairs={{0,1},{1,0},{2,3},{3,2},{4,5},{5,4},{6,7},{7,6},{8,9},{9,8},{10,11... | collective-permute-start | bytes 1572872 | tf_op jit(solution)/shard_map/ppermute | solution.py:218
  52.5 10.9 %collective-permute-start.18 = (bf16[2,4,128,256]{3,2,1,0:T(8,128)(2,1)S(1)}, bf16[2,4,128,256]{3,2,1,0:T(8,128)(2,1)S(1)}, u32[]{:S(2)}, u32[]{:S(2)}) collective-permute-start(bf16[2,4,128,256]{3,2,1,0:T(8,128)(2,1)S(1)} %collective-permute-done.4.refs_5_), channel_id=1, source_target_pairs={{0,1},{1,0},{2,3},{3,2},{4,5},{5,4},{6,7},{7,6},{8,9},{9,8},{10,11... | collective-permute-start | bytes 1572872 | tf_op jit(solution)/shard_map/ppermute | solution.py:218
  56.1 10.0 %collective-permute-start.19 = (bf16[2,4,128,256]{3,2,1,0:T(8,128)(2,1)S(1)}, bf16[2,4,128,256]{3,2,1,0:T(8,128)(2,1)S(1)}, u32[]{:S(2)}, u32[]{:S(2)}) collective-permute-start(bf16[2,4,128,256]{3,2,1,0:T(8,128)(2,1)S(1)} %collective-permute-done.4.refs_5_), channel_id=1, source_target_pairs={{0,4},{5,1},{4,8},{9,5},{8,12},{13,9},{12,14},{15,13},{14,10},{11,... | collective-permute-start | bytes 1572872 | tf_op jit(solution)/shard_map/ppermute | solution.py:244
  59.4 13.2 %collective-permute-start.21 = (bf16[4,256,256]{2,1,0:T(8,128)(2,1)S(1)}, bf16[4,256,256]{2,1,0:T(8,128)(2,1)S(1)}, u32[]{:S(2)}, u32[]{:S(2)}) collective-permute-start(bf16[4,256,256]{2,1,0:T(8,128)(2,1)S(1)} %get-tuple-element.26), channel_id=1, source_target_pairs={{0,16},{16,0},{1,17},{17,1},{2,18},{18,2},{3,19},{19,3},{4,20},{20... | collective-permute-start | bytes 1572872 | tf_op jit(solution)/shard_map/ppermute | solution.py:218
  61.7 8.7 %collective-permute-start.20 = (bf16[3,256,256]{2,1,0:T(8,128)(2,1)S(1)}, bf16[3,256,256]{2,1,0:T(8,128)(2,1)S(1)}, u32[]{:S(2)}, u32[]{:S(2)}) collective-permute-start(bf16[3,256,256]{2,1,0:T(8,128)(2,1)S(1)} %copy-done), channel_id=1, source_target_pairs={{0,1},{1,0},{2,3},{3,2},{4,5},{5,4},{6,7},{7,6},{8,9},{9,8},{10,11... | collective-permute-start | bytes 1179656 | tf_op jit(solution)/shard_map/ppermute | solution.py:218
  68.2 4.4 %copy-start.2 = (f32[256]{0:T(256)S(1)}, f32[256]{0:T(256)}, u32[]{:S(2)}) copy-start(f32[256]{0:T(256)} %param.12) | copy-start | bytes 3076
  68.2 14.9 %collective-permute-start.26 = (bf16[4,256,256]{2,1,0:T(8,128)(2,1)S(1)}, bf16[4,256,256]{2,1,0:T(8,128)(2,1)S(1)}, u32[]{:S(2)}, u32[]{:S(2)}) collective-permute-start(bf16[4,256,256]{2,1,0:T(8,128)(2,1)S(1)} %get-tuple-element.28), channel_id=1, source_target_pairs={{0,16},{16,0},{1,17},{17,1},{2,18},{18,2},{3,19},{19,3},{4,20},{20... | collective-permute-start | bytes 1572872 | tf_op jit(solution)/shard_map/ppermute | solution.py:218
  72.6 4.0 %copy-start.1 = (bf16[256,256]{1,0:T(8,128)(2,1)S(1)}, bf16[256,256]{1,0:T(8,128)(2,1)}, u32[]{:S(2)}) copy-start(bf16[256,256]{1,0:T(8,128)(2,1)} %refs_8_.1) | copy-start | bytes 393220
  72.6 4.0 %copy-start.3 = (f32[256]{0:T(256)S(1)}, f32[256]{0:T(256)}, u32[]{:S(2)}) copy-start(f32[256]{0:T(256)} %param.17) | copy-start | bytes 3076
  72.6 4.0 %copy-start.4 = (f32[256]{0:T(256)S(1)}, f32[256]{0:T(256)}, u32[]{:S(2)}) copy-start(f32[256]{0:T(256)} %param.19) | copy-start | bytes 3076
  73.5 3.1 %collective-permute-start.24 = (bf16[3,256,256]{2,1,0:T(8,128)(2,1)S(1)}, bf16[3,256,256]{2,1,0:T(8,128)(2,1)S(1)}, u32[]{:S(2)}, u32[]{:S(2)}) collective-permute-start(bf16[3,256,256]{2,1,0:T(8,128)(2,1)S(1)} %get-tuple-element.33), channel_id=1, source_target_pairs={{0,1},{1,0},{2,3},{3,2},{4,5},{5,4},{6,7},{7,6},{8,9},{9,8},{10,11... | collective-permute-start | bytes 1179656 | tf_op jit(solution)/shard_map/ppermute | solution.py:218
  73.5 3.0 %collective-permute-start.25 = (bf16[3,256,256]{2,1,0:T(8,128)(2,1)S(1)}, bf16[3,256,256]{2,1,0:T(8,128)(2,1)S(1)}, u32[]{:S(2)}, u32[]{:S(2)}) collective-permute-start(bf16[3,256,256]{2,1,0:T(8,128)(2,1)S(1)} %get-tuple-element.34), channel_id=1, source_target_pairs={{0,1},{1,0},{2,3},{3,2},{4,5},{5,4},{6,7},{7,6},{8,9},{9,8},{10,11... | collective-permute-start | bytes 1179656 | tf_op jit(solution)/shard_map/ppermute | solution.py:218
  74.0 2.1 %collective-permute-start.22 = (bf16[2,256,256]{2,1,0:T(8,128)(2,1)S(1)}, bf16[2,256,256]{2,1,0:T(8,128)(2,1)S(1)}, u32[]{:S(2)}, u32[]{:S(2)}) collective-permute-start(bf16[2,256,256]{2,1,0:T(8,128)(2,1)S(1)} %get-tuple-element.31), channel_id=1, source_target_pairs={{0,1},{1,0},{2,3},{3,2},{4,5},{5,4},{6,7},{7,6},{8,9},{9,8},{10,11... | collective-permute-start | bytes 786440 | tf_op jit(solution)/shard_map/ppermute | solution.py:218
  74.1 2.4 %collective-permute-start.23 = (bf16[2,256,256]{2,1,0:T(8,128)(2,1)S(1)}, bf16[2,256,256]{2,1,0:T(8,128)(2,1)S(1)}, u32[]{:S(2)}, u32[]{:S(2)}) collective-permute-start(bf16[2,256,256]{2,1,0:T(8,128)(2,1)S(1)} %get-tuple-element.32), channel_id=1, source_target_pairs={{0,1},{1,0},{2,3},{3,2},{4,5},{5,4},{6,7},{7,6},{8,9},{9,8},{10,11... | collective-permute-start | bytes 786440 | tf_op jit(solution)/shard_map/ppermute | solution.py:218
